TPU v7x, 32 devices: a whole 2x2x4 slice. The times are simulated.
32 devices in a mesh: grp: 2 (over x), wide: 4 (over y, core), head: 4 (over z).
Axes of the slice: x: 2, y: 2, z: 4, core: 2. Of those that a mesh axis runs over, the one named last changes fastest.
Arguments:
- tokens: bfloat16 [64, 8192], P('grp'), parts along dimension 0, may hold values from -30 to 30
- attn_gain: bfloat16 [8192], replicated, may hold values from 0.25 to 1.75
- ffn_gain: bfloat16 [8192], P('wide'), may hold values from 0.25 to 1.75
- w_query: bfloat16 [8192, 8192], P('wide', 'head'), may hold values from -0.0625 to 0.0625
- key_matrix: bfloat16 [8192, 1024], P('wide', 'head'), may hold values from -0.0625 to 0.0625
- value_matrix: bfloat16 [8192, 1024], P('wide', 'head'), may hold values from -0.0625 to 0.0625
- w_out: bfloat16 [8192, 8192], P('head', 'wide'), may hold values from -0.0625 to 0.0625
- w_gate: bfloat16 [8192, 14336], P('wide', 'head'), may hold values from -0.0625 to 0.0625
- w_up: bfloat16 [8192, 14336], P('wide', 'head'), may hold values from -0.0625 to 0.0625
- w_down: bfloat16 [14336, 8192], P('head', 'wide'), may hold values from -0.046875 to 0.046875
- kv_cache: bfloat16 [2, 16, 2048, 1024], P(None, 'grp', 'wide', 'head'), parts along dimension 1, may hold values from -250 to 250
- lengths: int32 [16], P('grp'), parts along dimension 0, may hold values from 1 to 2048, 8192 in all
- slots: int32 [16], P('grp'), parts along dimension 0, may hold values from 0 to 7, each once
Outputs:
- layer_out: bfloat16 [64, 8192], P(('grp', 'head'), 'wide'), parts along dimension 0
There are 2 independent parts, one for each index of `grp`. A program takes and returns all parts, laid end to end along the dimension named above; an argument that names none is the same for every part. Nothing has to cross between parts.
Inputs may be any that keep to these rules, and one draw needn't show every extreme that they name: `lengths`: they sum to 8192, and the longest is exactly 2048. `slots`: each slot belongs to exactly one request.
All inputs are finite; a program needn't handle non-finite values.
Results may differ from a plain program's by a relative error of at most 0.0057.
Values may be sent and summed in bfloat16 or wider, within the bound.
No kernel may reach another device: no remote copies, remote signals or barrier semaphores. Data moves between devices by JAX's collectives and lax.ppermute only.
A program may use at most 128 MiB of HBM per device.

v0:
```python
import jax
import jax.numpy as jnp
from jax import lax
from jax.sharding import PartitionSpec as P

MODEL_WIDTH = 8192
HEAD_WIDTH = 128
DRAFT_TOKENS = 4


epsilon = 1e-05
theta_base = 500000.0
neg_large = -1e30


def rotary_tables(values, token_positions):
    half_width = values.shape[-1] // 2
    exponent = jnp.arange(half_width, dtype=jnp.float32) * (2.0 / values.shape[-1])
    angles = token_positions[:, None] * (theta_base ** (-exponent))[None, :]
    cosine = jnp.cos(angles)[:, None, :]
    sine_part = jnp.sin(angles)[:, None, :]
    front_half = values[..., :half_width]
    back_half = values[..., half_width:]
    return jnp.concatenate(
        [front_half * cosine - back_half * sine_part, back_half * cosine + front_half * sine_part],
        axis=-1,
    )


def finish(query_sum, key_total, value_total, token_positions):
    row_count = query_sum.shape[0]
    rotated_queries = rotary_tables(
        query_sum.reshape(row_count, -1, HEAD_WIDTH), token_positions
    ) * HEAD_WIDTH ** (-0.5)
    rotated_keys = rotary_tables(key_total.reshape(row_count, -1, HEAD_WIDTH), token_positions)
    return (
        rotated_queries.reshape(row_count, -1).astype(jnp.bfloat16),
        rotated_keys.reshape(row_count, -1).astype(jnp.bfloat16),
        value_total.astype(jnp.bfloat16),
    )


def per_device(
    tokens,
    attn_gain,
    ffn_gain,
    w_query,
    key_matrix,
    value_matrix,
    w_out,
    w_gate,
    w_up,
    w_down,
    kv_cache,
    lengths,
    slots,
):
    token_row_count = tokens.shape[0]
    col_width = w_query.shape[0]
    head_size = lax.axis_size("head")
    wide_at = lax.axis_index("wide")
    head_at = lax.axis_index("head")
    tokens_f = tokens.astype(jnp.float32)
    scale_in = lax.rsqrt(jnp.mean(tokens_f * tokens_f, axis=1, keepdims=True) + epsilon)
    normed = (tokens_f * scale_in * attn_gain.astype(jnp.float32)[None, :]).astype(jnp.bfloat16)
    own_cols = lax.dynamic_slice_in_dim(normed, wide_at * col_width, col_width, 1)
    query_part = jnp.dot(own_cols, w_query, preferred_element_type=jnp.float32)
    key_part = jnp.dot(own_cols, key_matrix, preferred_element_type=jnp.float32)
    value_part = jnp.dot(own_cols, value_matrix, preferred_element_type=jnp.float32)
    token_positions = (
        jnp.repeat(lengths, DRAFT_TOKENS)
        + jnp.arange(token_row_count, dtype=jnp.int32) % DRAFT_TOKENS
    ).astype(jnp.float32)
    query_sum, key_total, value_total = lax.psum((query_part, key_part, value_part), "wide")
    query_all, key_new, fresh_value = finish(query_sum, key_total, value_total, token_positions)
    requests = lengths.shape[0]
    kv_local = key_matrix.shape[1] // HEAD_WIDTH
    heads_per_group = w_query.shape[1] // HEAD_WIDTH // kv_local
    ctx_local = kv_cache.shape[2]
    ordered = jnp.take(kv_cache, slots, axis=1)
    keys_local = ordered[0].reshape(requests, ctx_local, kv_local, HEAD_WIDTH)
    vals_local = ordered[1].reshape(requests, ctx_local, kv_local, HEAD_WIDTH)
    query_blocks = query_all.reshape(requests, DRAFT_TOKENS, kv_local, heads_per_group, HEAD_WIDTH)
    scores = jnp.einsum(
        "rjkgd,rpkd->rkgjp", query_blocks, keys_local, preferred_element_type=jnp.float32
    )
    live_mask = (wide_at * ctx_local + jnp.arange(ctx_local, dtype=jnp.int32))[None, :] < lengths[
        :, None
    ]
    live_full = live_mask[:, None, None, None, :]
    masked = jnp.where(live_full, scores, neg_large)
    local_top = jnp.max(masked, axis=-1)
    draft_keys = key_new.reshape(requests, DRAFT_TOKENS, kv_local, HEAD_WIDTH)
    draft_vals = fresh_value.reshape(requests, DRAFT_TOKENS, kv_local, HEAD_WIDTH)
    draft_scores = jnp.einsum(
        "rjkgd,rikd->rkgji", query_blocks, draft_keys, preferred_element_type=jnp.float32
    )
    causal = (
        jnp.arange(DRAFT_TOKENS, dtype=jnp.int32)[None, :]
        <= jnp.arange(DRAFT_TOKENS, dtype=jnp.int32)[:, None]
    )
    draft_masked = jnp.where(causal, draft_scores, neg_large)
    cache_top = lax.pmax(local_top, "wide")
    top_all = jnp.maximum(cache_top, jnp.max(draft_masked, axis=-1))
    weights = jnp.where(live_full, jnp.exp(masked - top_all[..., None]), 0.0)
    partial_acc = jnp.einsum(
        "rkgjp,rpkd->rkgjd",
        weights.astype(jnp.bfloat16),
        vals_local,
        preferred_element_type=jnp.float32,
    )
    cache_total, cache_acc = lax.psum((jnp.sum(weights, axis=-1), partial_acc), "wide")
    draft_weights = jnp.where(causal, jnp.exp(draft_masked - top_all[..., None]), 0.0)
    denominator = cache_total + jnp.sum(draft_weights, axis=-1)
    draft_acc = jnp.einsum(
        "rkgji,rikd->rkgjd",
        draft_weights.astype(jnp.bfloat16),
        draft_vals,
        preferred_element_type=jnp.float32,
    )
    attended = (
        ((cache_acc + draft_acc) / denominator[..., None])
        .transpose(0, 3, 1, 2, 4)
        .reshape(token_row_count, -1)
        .astype(jnp.bfloat16)
    )
    out_part = jnp.dot(attended, w_out, preferred_element_type=jnp.float32)
    own_tokens = lax.dynamic_slice_in_dim(tokens_f, wide_at * col_width, col_width, 1)
    gain_f = ffn_gain.astype(jnp.float32)[None, :]
    share_head = token_row_count // head_size
    attn_share = lax.psum_scatter(out_part, "head", scatter_dimension=0, tiled=True)
    token_rows = lax.dynamic_slice_in_dim(own_tokens, head_at * share_head, share_head, 0)
    resid_rows = (token_rows + attn_share).astype(jnp.bfloat16)
    resid_f = resid_rows.astype(jnp.float32)
    square_sum = lax.psum(jnp.sum(resid_f * resid_f, axis=1), "wide")
    normed_share = (
        resid_f * lax.rsqrt(square_sum / MODEL_WIDTH + epsilon)[:, None] * gain_f
    ).astype(jnp.bfloat16)
    ffn_in = lax.all_gather(normed_share, "head", axis=0, tiled=True)
    gate_part = jnp.dot(ffn_in, w_gate, preferred_element_type=jnp.float32)
    up_part = jnp.dot(ffn_in, w_up, preferred_element_type=jnp.float32)
    gate_sum, up_sum = lax.psum((gate_part, up_part), "wide")
    hidden = (jax.nn.silu(gate_sum) * up_sum).astype(jnp.bfloat16)
    ffn_out = lax.psum_scatter(
        jnp.dot(hidden, w_down, preferred_element_type=jnp.float32),
        "head",
        scatter_dimension=0,
        tiled=True,
    )
    return (resid_rows.astype(jnp.float32) + ffn_out).astype(jnp.bfloat16)


def solution(mesh):
    in_specs = (
        P("grp", None),
        P(),
        P("wide"),
        P("wide", "head"),
        P("wide", "head"),
        P("wide", "head"),
        P("head", "wide"),
        P("wide", "head"),
        P("wide", "head"),
        P("head", "wide"),
        P(None, "grp", "wide", "head"),
        P("grp"),
        P("grp"),
    )
    out_specs = P(("grp", "head"), "wide")
    return jax.shard_map(
        per_device, mesh=mesh, in_specs=in_specs, out_specs=out_specs, check_vma=False
    )
```

profile of v0, /device:TPU:0, one launch (start us, length us, event | category | flops | bytes accessed | tf_op | source)
XLA Modules:
  0.0 234.2 jit_solution(7514440644843655939)
XLA Ops:
  6.5 0.0 copy-start
  6.5 0.0 all-reduce.6.cloned.1.call-start
  6.5 1.2 convert_element_type.65
  7.7 0.0 copy-start.2
  7.8 1.6 multiply_reduce_fusion
  9.4 0.7 dynamic-slice
  10.1 5.0 %convolution_bitcast_fusion = f32[4,8,16,128]{3,1,2,0:T(8,128)S(1)} fusion(bf16[2048,2048]{1,0:T(8,128)(2,1)} %param.16, f32[32,8192]{1,0:T(8,128)S(1)} %convert_element_type.65, s32[]{:T(128)S(6)} %select_n.50, f32[2048]{0:T(1024)S(1)} %dynamic-slice, f32[32]{0:T(128)S(1)} %add_rsqrt_fusion.1), kind=kOutput, calls=%fused_computation.4 | convolution fusion | flops 268632064 | bytes 8921604 | tf_op jit(solution)/shard_map/dot_general | solution.py:67
  15.1 0.8 copy.46
  15.9 0.0 all-reduce.6.cloned.1.call-update
  15.9 0.0 all-reduce.8.cloned.1.call-start
  15.9 0.0 copy-done.6
  16.0 4.9 %gather_fusion = bf16[8,2,512,256]{3,2,1,0:T(8,128)(2,1)} fusion(bf16[2,8,512,256]{3,2,1,0:T(8,128)(2,1)} %param.23, s32[1024]{0:T(1024)S(1)} %pad_clamp_fusion), kind=kCustom, calls=%fused_computation | custom fusion | bytes 8388640 | tf_op jit(solution)/shard_map/jit(_take)/gather | solution.py:80
  20.9 2.7 %select_bitcast_fusion = bf16[2,8,512,256]{3,2,0,1:T(8,128)(2,1)S(1)} fusion(bf16[8,2,512,256]{3,2,1,0:T(8,128)(2,1)} %gather_fusion, pred[8]{0:T(512)(128)(4,1)S(1)} %compare_and_fusion), kind=kLoop, calls=%fused_computation.1 | loop fusion | flops 2097152 | bytes 8388616 | tf_op jit(solution)/shard_map/jit(_take)/select_n | solution.py:80
  23.6 0.0 copy-start.5
  23.6 0.0 copy-start.3
  23.6 2.3 fusion.36
  25.9 0.0 copy-done.5
  25.9 0.1 broadcast_in_dim.74
  26.0 0.1 reshape.139
  26.1 0.1 broadcast_compare_fusion
  26.1 0.0 copy-done
  26.1 0.3 convolution_bitcast_fusion.2
  26.5 12.9 %psum.57 = f32[32,2,128]{2,0,1:T(8,128)S(1)} all-reduce(f32[32,2,128]{2,0,1:T(8,128)S(1)} %bitcast.52), channel_id=1, replica_groups=mesh['grp'=2,'wide'=4,'head'=4] {'wide'}, use_global_device_ids=true, to_apply=%region_4.5 | all-reduce | flops 8192 | bytes 65536 | tf_op jit(solution)/shard_map/psum | solution.py:74
  39.4 0.0 copy-done.2
  39.4 0.0 copy-done.3
  39.5 0.3 fusion.41
  39.8 0.1 multiply_cosine_fusion
  39.9 0.1 subtract_convert_fusion
  40.0 2.9 %copy.29 = bf16[1,8,512,256]{2,3,1,0:T(8,128)(2,1)S(1)} copy(bf16[1,8,512,256]{3,2,0,1:T(8,128)(2,1)} %get-tuple-element.12) | data formatting | bytes 4194304 | tf_op jit(solution)/shard_map/slice | solution.py:82
  42.9 3.9 %copy.23 = bf16[1,8,512,256]{2,3,1,0:T(8,128)(2,1)} copy(bf16[1,8,512,256]{3,2,0,1:T(8,128)(2,1)} %get-tuple-element.11) | data formatting | bytes 4194304 | tf_op jit(solution)/shard_map/slice | solution.py:81
  46.9 0.1 pad_maximum_fusion
  46.9 3.8 %all-reduce.6.cloned.1.call-done = f32[32,16,128]{2,1,0:T(8,128)} async-done(((f32[32,16,128]{2,1,0:T(8,128)}), f32[32,16,128]{2,1,0:T(8,128)}) %all-reduce.6.cloned.1.call-update) | async-done | bytes 262160 | tf_op jit(solution)/shard_map/psum | solution.py:74
  50.8 1.2 multiply_subtract_fusion
  52.0 0.1 fusion.14
  52.1 2.1 fusion.37
  54.2 10.3 %pmax.7 = f32[8,2,8,4]{2,3,1,0:T(4,128)S(1)} all-reduce(f32[8,2,8,4]{2,3,1,0:T(4,128)S(1)} %get-tuple-element.19), channel_id=1, replica_groups=mesh['grp'=2,'wide'=4,'head'=4] {'wide'}, use_global_device_ids=true, to_apply=%region_3.4 | all-reduce | flops 512 | bytes 4096 | tf_op jit(solution)/shard_map/pmax | solution.py:103
  64.5 0.7 fusion.38
  65.2 1.5 fusion.7
  66.7 0.0 all-reduce.8.cloned.1.call-update
  66.8 0.0 reduce-scatter.3.cloned.1.call-start
  66.8 0.4 fusion.5
  67.2 10.7 %all-reduce = (f32[8,2,8,4]{2,3,1,0:T(4,128)S(1)}, bf16[32,256]{1,0:T(8,128)(2,1)S(1)}) all-reduce(f32[8,2,8,4]{2,3,1,0:T(4,128)S(1)} %fusion.5, f32[32,256]{1,0:T(8,128)S(1)} %fusion.41), channel_id=1, replica_groups=mesh['grp'=2,'wide'=4,'head'=4] {'wide'}, use_global_device_ids=true, to_apply=%region_9.10 | all-reduce | flops 8704 | bytes 53248 | tf_op jit(solution)/shard_map/psum | solution.py:112
  77.9 0.2 fusion.19
  78.1 20.8 %all-reduce.8.cloned.1.call-done = f32[8,2,8,4,128]{4,2,3,1,0:T(8,128)} async-done(((f32[8,2,8,4,128]{4,2,3,1,0:T(8,128)}), f32[8,2,8,4,128]{4,2,3,1,0:T(8,128)}) %all-reduce.8.cloned.1.call-update) | async-done | bytes 262160 | tf_op jit(solution)/shard_map/psum | solution.py:112
  98.9 1.3 fusion.3
  100.2 0.1 convert_element_type.77
  100.3 0.0 copy-start.4
  100.3 5.6 %fusion.43 = f32[32,2048]{1,0:T(8,128)} fusion(bf16[32,2048]{1,0:T(8,128)(2,1)S(1)} %convert_element_type.77, bf16[2048,2048]{1,0:T(8,128)(2,1)} %param.19), kind=kOutput, calls=%fused_computation.73 | convolution fusion | flops 268435456 | bytes 8781824 | tf_op jit(solution)/shard_map/dot_general | solution.py:127
  105.9 0.0 reduce-scatter.3.cloned.1.call-update
  106.0 0.0 all-reduce.10.cloned.1.call-start
  106.0 19.7 %reduce-scatter.3.cloned.1.call-done = f32[8,2048]{1,0:T(8,128)} async-done(((f32[32,2048]{1,0:T(8,128)}), f32[8,2048]{1,0:T(8,128)}) %reduce-scatter.3.cloned.1.call-update) | async-done | bytes 65552 | tf_op jit(solution)/shard_map/reduce_scatter | solution.py:131
  125.8 1.1 fusion.22
  126.9 5.7 %psum.61 = f32[8]{0:T(128)S(1)} all-reduce(f32[8]{0:T(128)S(1)} %get-tuple-element.9), channel_id=1, replica_groups=mesh['grp'=2,'wide'=4,'head'=4] {'wide'}, use_global_device_ids=true, to_apply=%region_13.14 | all-reduce | flops 8 | bytes 64 | tf_op jit(solution)/shard_map/psum | solution.py:135
  132.6 0.1 fusion.24
  132.7 13.5 %all_gather.3 = bf16[32,2048]{1,0:T(8,128)(2,1)S(1)} all-gather(bf16[8,2048]{1,0:T(8,128)(2,1)S(1)} %fusion.24), channel_id=1, replica_groups=mesh['grp'=2,'wide'=4,'head'=4] {'head'}, dimensions={0}, use_global_device_ids=true | all-gather | bytes 163840 | tf_op jit(solution)/shard_map/all_gather | solution.py:139
  146.2 8.5 %fusion.45 = f32[32,3584]{1,0:T(8,128)} fusion(bf16[32,2048]{1,0:T(8,128)(2,1)S(1)} %all_gather.3, bf16[2048,3584]{1,0:T(8,128)(2,1)} %param.21), kind=kOutput, calls=%fused_computation.75 | convolution fusion | flops 469762048 | bytes 15269888 | tf_op jit(solution)/shard_map/dot_general | solution.py:141
  154.7 8.6 %fusion.44 = f32[32,3584]{1,0:T(8,128)} fusion(bf16[32,2048]{1,0:T(8,128)(2,1)S(1)} %all_gather.3, bf16[2048,3584]{1,0:T(8,128)(2,1)} %param.20), kind=kOutput, calls=%fused_computation.74 | convolution fusion | flops 469762048 | bytes 15269888 | tf_op jit(solution)/shard_map/dot_general | solution.py:140
  163.3 0.0 all-reduce.10.cloned.1.call-update
  163.3 0.0 reduce-scatter.5.cloned.1.call-start
  163.4 33.9 %all-reduce.10.cloned.1.call-done = (f32[32,3584]{1,0:T(8,128)}, f32[32,3584]{1,0:T(8,128)}) async-done(((f32[32,3584]{1,0:T(8,128)}, f32[32,3584]{1,0:T(8,128)}), (f32[32,3584]{1,0:T(8,128)}, f32[32,3584]{1,0:T(8,128)})) %all-reduce.10.cloned.1.call-update) | async-done | bytes 917520 | tf_op jit(solution)/shard_map/psum | solution.py:142
  197.3 8.9 %fusion.15 = f32[32,2048]{1,0:T(8,128)} fusion(bf16[3584,2048]{1,0:T(8,128)(2,1)} %param.22, f32[32,3584]{1,0:T(8,128)} %get-tuple-element.7, f32[32,3584]{1,0:T(8,128)} %get-tuple-element.8), kind=kOutput, calls=%fused_computation.28 | convolution fusion | flops 470450176 | bytes 15859712 | tf_op jit(solution)/shard_map/dot_general | solution.py:145
  206.1 0.0 reduce-scatter.5.cloned.1.call-update
  206.2 20.0 %reduce-scatter.5.cloned.1.call-done = f32[8,2048]{1,0:T(8,128)} async-done(((f32[32,2048]{1,0:T(8,128)}), f32[8,2048]{1,0:T(8,128)}) %reduce-scatter.5.cloned.1.call-update) | async-done | bytes 65552 | tf_op jit(solution)/shard_map/reduce_scatter | solution.py:144
  226.2 1.5 fusion.25
  (19 shorter events, 0.1 us)
Async XLA Ops:
  6.5 19.6 %copy-start = (bf16[2048,256]{1,0:T(8,128)(2,1)S(1)}, bf16[2048,256]{1,0:T(8,128)(2,1)}, u32[]{:S(2)}) copy-start(bf16[2048,256]{1,0:T(8,128)(2,1)} %param.17) | copy-start | bytes 3145732
  6.5 44.2 %all-reduce.6.cloned.1.call-start = ((), (), s32[]{:S(2)}) async-start(), calls=%async_computation.2 | async-start | bytes 524288 | tf_op jit(solution)/shard_map/psum | solution.py:74
  7.7 31.7 %copy-start.2 = (f32[32,8192]{1,0:T(8,128)}, f32[32,8192]{1,0:T(8,128)S(1)}, u32[]{:S(2)}) copy-start(f32[32,8192]{1,0:T(8,128)S(1)} %convert_element_type.65) | copy-start | bytes 3145732
  10.1 5.8 %copy-start.6 = (s32[8]{0:T(128)S(1)}, s32[8]{0:T(128)}, u32[]{:S(2)}) copy-start(s32[8]{0:T(128)} %param.25) | copy-start | bytes 100
  15.9 83.0 %all-reduce.8.cloned.1.call-start = ((), (), s32[]{:S(2)}) async-start(), calls=%async_computation.3 | async-start | bytes 524288 | tf_op jit(solution)/shard_map/psum | solution.py:112
  23.6 2.3 copy-start.5
  23.6 15.8 %copy-start.3 = (bf16[2048,256]{1,0:T(8,128)(2,1)S(1)}, bf16[2048,256]{1,0:T(8,128)(2,1)}, u32[]{:S(2)}) copy-start(bf16[2048,256]{1,0:T(8,128)(2,1)} %param.18) | copy-start | bytes 3145732
  66.8 59.0 %reduce-scatter.3.cloned.1.call-start = ((), (), s32[]{:S(2)}) async-start(), calls=%async_computation.4 | async-start | bytes 327680 | tf_op jit(solution)/shard_map/reduce_scatter | solution.py:131
  100.3 5.7 %copy-start.4 = (bf16[2048]{0:T(1024)(128)(2,1)S(1)}, bf16[2048]{0:T(1024)(128)(2,1)}, u32[]{:S(2)}) copy-start(bf16[2048]{0:T(1024)(128)(2,1)} %param.15) | copy-start | bytes 12292
  106.0 91.3 %all-reduce.10.cloned.1.call-start = ((), (), s32[]{:S(2)}) async-start(), calls=%async_computation.6 | async-start | bytes 1835008 | tf_op jit(solution)/shard_map/psum | solution.py:142
  163.3 62.8 %reduce-scatter.5.cloned.1.call-start = ((), (), s32[]{:S(2)}) async-start(), calls=%async_computation.5 | async-start | bytes 327680 | tf_op jit(solution)/shard_map/reduce_scatter | solution.py:144
  197.3 30.4 %copy-start.1 = (bf16[2048,256]{1,0:T(8,128)(2,1)S(1)}, bf16[2048,256]{1,0:T(8,128)(2,1)}, u32[]{:S(2)}) copy-start(bf16[2048,256]{1,0:T(8,128)(2,1)} %param.17) | copy-start | bytes 3145732
Sparse Core Ops, SparseCore 0:
  16.0 34.7 all-reduce.5
  66.9 31.9 all-reduce.7
  106.1 19.6 reduce-scatter.2
  163.4 33.7 all-reduce.9
  206.3 19.8 reduce-scatter.4
where the time goes:
time: 235 us; the launch traced here: 234 us
  waiting for transfers between devices  98.4 us (42%)
  blocking collectives  53.1 us (23%)
  matrix products  42.8 us (18%)
  local copies, waits for them, and re-layouts  15.8 us (7%)
  between operations  13.4 us (6%)
  other arithmetic  10.5 us (4%)
    psum x1, waiting for transfers between devices, per_device(): gate_sum, up_sum = lax.psum((gate_part, up_part), 'wide')  33.9 us
    psum x1, waiting for transfers between devices, per_device(): lax.psum((jnp.sum(weights, axis=-1), partial_acc), 'wide')  20.8 us
    reduce_scatter x1, waiting for transfers between devices, per_device(): lax.psum_scatter(jnp.dot(hidden, w_down, preferred_element_type=jnp.float...  20 us
    reduce_scatter x1, waiting for transfers between devices, per_device(): lax.psum_scatter(out_part, 'head', scatter_dimension=0, tiled=True)  19.7 us
    all_gather x1, blocking collectives, per_device(): ffn_in = lax.all_gather(normed_share, 'head', axis=0, tiled=True)  13.5 us
    psum x1, blocking collectives, per_device(): lax.psum((query_part, key_part, value_part), 'wide')  12.9 us
    psum x1, blocking collectives, per_device(): lax.psum((jnp.sum(weights, axis=-1), partial_acc), 'wide')  10.7 us
    pmax x1, blocking collectives, per_device(): cache_top = lax.pmax(local_top, 'wide')  10.3 us
  transfers between devices with their start and end apart: 5, of which 5 were waited for; matrix products, arithmetic and copies ran while one was open for 8% of the time, Pallas kernels for 0%

commit v1 on v0

v1 whole, which is shorter than its diff:
```python
import jax
import jax.numpy as jnp
from jax import lax
from jax.experimental import pallas as pl
from jax.experimental.pallas import tpu as pltpu
from jax.sharding import PartitionSpec as P

HEAD_WIDTH = 128
DRAFT_TOKENS = 4
LANES = 128
MIB = 1 << 20

epsilon = 1e-05
theta_base = 500000.0
neg_large = -1e30

f32 = jnp.float32
bf16 = jnp.bfloat16
VMEM = pl.BlockSpec(memory_space=pltpu.VMEM)
SMEM = pl.BlockSpec(memory_space=pltpu.SMEM)
ANY = pl.BlockSpec(memory_space=pl.ANY)


def in_vmem(x):
    return pltpu.with_memory_space_constraint(x, pltpu.VMEM)


def cost(rows, *weights):
    size = sum(w.size for w in weights)
    return pl.CostEstimate(flops=2 * rows * size, bytes_accessed=2 * size, transcendentals=0)


def params(mib):
    return pltpu.CompilerParams(vmem_limit_bytes=mib * MIB)


def blocks_of(width, most):
    step = max(b for b in range(LANES, most + 1, LANES) if width % b == 0)
    return [(at, step) for at in range(0, width, step)]


def lanes(at):
    return slice(at * LANES, (at + 1) * LANES)


def project_kernel(chunks, at, tokens, gain, wq, wk, wv, out, own, tok, gain_f, norm, bq, bk, bv, acc, sems):
    rows, model = tok.shape
    depth, q_cols = bq.shape
    kv_cols = bk.shape[1]
    step = depth // chunks
    copies = [
        pltpu.make_async_copy(tokens, tok, sems.at[0]),
        pltpu.make_async_copy(wk, bk, sems.at[1]),
        pltpu.make_async_copy(wv, bv, sems.at[2]),
    ] + [
        pltpu.make_async_copy(
            wq.at[pl.ds(c * step, step)], bq.at[pl.ds(c * step, step)], sems.at[3 + c]
        )
        for c in range(chunks)
    ]
    for copy in copies:
        copy.start()
    gain_f[...] = gain[...].astype(f32)
    copies[0].wait()
    squares = jnp.zeros((rows, LANES), f32)
    for c in range(model // LANES):
        part = tok[:, lanes(c)].astype(f32)
        squares = squares + part * part
    scale = lax.rsqrt(jnp.sum(squares, axis=1, keepdims=True) / model + epsilon)
    count = depth // LANES
    for c in range(count):
        index = at[0] * count + c
        part = tok[:, pl.ds(pl.multiple_of(index * LANES, LANES), LANES)]
        own[:, lanes(c)] = part
        norm[:, lanes(c)] = (part.astype(f32) * scale * gain_f[pl.ds(index, 1), :]).astype(bf16)
    for copy, held, base in ((copies[1], bk, q_cols), (copies[2], bv, q_cols + kv_cols)):
        copy.wait()
        out[:, base : base + kv_cols] = jnp.dot(
            norm[...], held[...], preferred_element_type=f32
        ).astype(out.dtype)
    for c in range(chunks):
        copies[3 + c].wait()
        for start, size in blocks_of(q_cols, 512):
            cols = slice(start, start + size)
            term = jnp.dot(
                norm[:, c * step : (c + 1) * step],
                bq[c * step : (c + 1) * step, cols],
                preferred_element_type=f32,
            )
            if c:
                term = acc[:, cols] + term
            if c < chunks - 1:
                acc[:, cols] = term
            else:
                out[:, cols] = term.astype(out.dtype)


def project(at, tokens, gain, wq, wk, wv):
    rows, model = tokens.shape
    depth, q_cols = wq.shape
    kv_cols = wk.shape[1]
    chunks = max(1, min(8, depth // 256))
    return pl.pallas_call(
        lambda *refs: project_kernel(chunks, *refs),
        in_specs=[SMEM, ANY, VMEM, ANY, ANY, ANY],
        out_specs=[VMEM, VMEM],
        out_shape=[
            jax.ShapeDtypeStruct((rows, q_cols + 2 * kv_cols), bf16),
            jax.ShapeDtypeStruct((rows, depth), bf16),
        ],
        scratch_shapes=[
            pltpu.VMEM((rows, model), bf16),
            pltpu.VMEM((model // LANES, LANES), f32),
            pltpu.VMEM((rows, depth), bf16),
            pltpu.VMEM(wq.shape, bf16),
            pltpu.VMEM(wk.shape, bf16),
            pltpu.VMEM(wv.shape, bf16),
            pltpu.VMEM((rows, q_cols), f32),
            pltpu.SemaphoreType.DMA((3 + chunks,)),
        ],
        compiler_params=params(16),
        cost_estimate=cost(rows, wq, wk, wv),
        name="project",
    )(at, tokens, gain.reshape(model // LANES, LANES), wq, wk, wv)


def attend_kernel(n, at, lengths, slots, cos, sin, cache, *rest):
    parts, (out, lse_out, queries, total) = rest[:n], rest[n:]
    rows, q_cols = queries.shape
    context, kv_cols = cache.shape[2:]
    kv_heads = kv_cols // HEAD_WIDTH
    heads = q_cols // HEAD_WIDTH
    group = heads // kv_heads
    tile = 2 * DRAFT_TOKENS
    last = at[1]
    base = at[0] * context

    def column(c):
        return sum(p[:, lanes(c)].astype(f32) for p in parts)

    def rotated(x):
        return x * cos[...] + pltpu.roll(x, HEAD_WIDTH // 2, 1) * sin[...]

    for h in range(heads):
        queries[:, lanes(h)] = (rotated(column(h)) * HEAD_WIDTH ** (-0.5)).astype(bf16).astype(f32)
    new_keys = [rotated(column(heads + k)).astype(bf16) for k in range(kv_heads)]
    new_values = [column(heads + kv_heads + k).astype(bf16) for k in range(kv_heads)]

    high = group * tile
    row = lax.broadcasted_iota(jnp.int32, (high, 1), 0) % tile
    first = row < DRAFT_TOKENS
    position = lax.broadcasted_iota(jnp.int32, (high, context), 1) + base
    draft_col = lax.broadcasted_iota(jnp.int32, (high, rows), 1)
    lane = lax.broadcasted_iota(jnp.int32, (tile, LANES), 1)
    nt = (((1,), (1,)), ((), ()))
    for i in range(rows // tile):
        request = 2 * i
        limit = jnp.where(first, lengths[request], lengths[request + 1])
        live = position < limit
        own_at = tile * i + jnp.where(first, 0, DRAFT_TOKENS)
        seen = (draft_col >= own_at) & (draft_col <= tile * i + row) & (last > 0)
        stats = jnp.zeros((tile, LANES), f32)
        for k in range(kv_heads):
            q = jnp.concatenate(
                [queries[tile * i : tile * (i + 1), lanes(k * group + g)] for g in range(group)], axis=0
            ).astype(bf16)
            scores = [
                lax.dot_general(q, cache[0, slots[request + s], :, lanes(k)], nt, preferred_element_type=f32)
                for s in range(2)
            ]
            score = jnp.where(live, jnp.where(first, scores[0], scores[1]), neg_large)
            draft = lax.dot_general(q, new_keys[k], nt, preferred_element_type=f32)
            draft = jnp.where(seen, draft, neg_large)
            top = jnp.maximum(
                jnp.max(score, axis=1, keepdims=True), jnp.max(draft, axis=1, keepdims=True)
            )
            weight = jnp.where(live, jnp.exp(score - top), 0.0)
            draft_weight = jnp.where(seen, jnp.exp(draft - top), 0.0)
            mass = jnp.sum(weight, axis=1, keepdims=True) + jnp.sum(draft_weight, axis=1, keepdims=True)
            weight = weight.astype(bf16)
            sums = [
                jnp.dot(weight, cache[1, slots[request + s], :, lanes(k)], preferred_element_type=f32)
                for s in range(2)
            ]
            value = jnp.where(first, sums[0], sums[1]) + jnp.dot(
                draft_weight.astype(bf16), new_values[k], preferred_element_type=f32
            )
            some = mass > 0.0
            safe = jnp.where(some, mass, 1.0)
            value = value / safe
            lse = jnp.where(some, top + jnp.log(safe), neg_large)
            for g in range(group):
                at_rows = slice(tile * g, tile * (g + 1))
                total[tile * i : tile * (i + 1), lanes(k * group + g)] = value[at_rows]
                stats = jnp.where(lane == k * group + g, lse[at_rows], stats)
        lse_out[tile * i : tile * (i + 1), :] = stats
    out[...] = total[...].astype(bf16)


def attend(at, lengths, slots, cos, sin, cache, parts):
    rows, width = parts[0].shape
    q_cols = width - 2 * cache.shape[3]
    return pl.pallas_call(
        lambda *refs: attend_kernel(len(parts), *refs),
        in_specs=[SMEM] * 3 + [VMEM] * (3 + len(parts)),
        out_specs=[VMEM, VMEM],
        out_shape=[
            jax.ShapeDtypeStruct((rows, q_cols), bf16),
            jax.ShapeDtypeStruct((rows, LANES), f32),
        ],
        scratch_shapes=[pltpu.VMEM((rows, q_cols), f32), pltpu.VMEM((rows, q_cols), f32)],
        compiler_params=params(6),
        cost_estimate=cost(rows, cache),
        name="attend",
    )(at, lengths, slots, cos, sin, in_vmem(cache), *parts)


def output_kernel(n, w, *rest):
    values, stats, (out, attended) = rest[:n], rest[n : 2 * n], rest[2 * n :]
    heads = attended.shape[1] // HEAD_WIDTH
    top = stats[0][...]
    for s in stats[1:]:
        top = jnp.maximum(top, s[...])
    shares = [jnp.exp(s[...] - top) for s in stats]
    whole = sum(shares)
    shares = [s / whole for s in shares]
    for h in range(heads):
        attended[:, lanes(h)] = sum(
            v[:, lanes(h)].astype(f32) * s[:, h : h + 1] for v, s in zip(values, shares)
        ).astype(bf16)
    for start, size in blocks_of(w.shape[1], 512):
        cols = slice(start, start + size)
        out[:, cols] = jnp.dot(attended[...], w[:, cols], preferred_element_type=f32).astype(out.dtype)


def output(values, stats, w):
    rows = values[0].shape[0]
    return pl.pallas_call(
        lambda *refs: output_kernel(len(values), *refs),
        in_specs=[VMEM] * (1 + 2 * len(values)),
        out_specs=VMEM,
        out_shape=jax.ShapeDtypeStruct((rows, w.shape[1]), bf16),
        scratch_shapes=[pltpu.VMEM((rows, w.shape[0]), bf16)],
        compiler_params=params(4),
        cost_estimate=cost(rows, w),
        name="output",
    )(in_vmem(w), *values, *stats)


def half_of(side, x, wg, wu, out):
    half = wg.shape[1] // 2
    for base, w in ((0, wg), (half, wu)):
        for start, size in blocks_of(half, 512):
            cols = pl.ds(pl.multiple_of(side * half + start, LANES), size)
            out[:, base + start : base + start + size] = jnp.dot(
                x[...], w[:, cols], preferred_element_type=f32
            ).astype(out.dtype)


def expand_send_kernel(n, at, own, gain, wg, wu, *rest):
    parts, (out, resid, x, squares, gain_f) = rest[:n], rest[n:]
    rows = own.shape[0]
    gain_f[...] = gain[...].astype(f32)
    square = jnp.zeros((rows, LANES), f32)
    for c in range(own.shape[1] // LANES):
        value = own[:, lanes(c)].astype(f32) + sum(p[:, lanes(c)].astype(f32) for p in parts)
        value = value.astype(bf16)
        resid[:, lanes(c)] = value
        value = value.astype(f32)
        square = square + value * value
        x[:, lanes(c)] = (value * gain_f[c : c + 1, :]).astype(bf16)
    squares[...] = jnp.broadcast_to(jnp.sum(square, axis=1, keepdims=True), squares.shape)
    half_of(1 - at[2], x, wg, wu, out)


def expand_send(at, own, gain, parts, wg, wu):
    rows, depth = own.shape
    return pl.pallas_call(
        lambda *refs: expand_send_kernel(len(parts), *refs),
        in_specs=[SMEM] + [VMEM] * (4 + len(parts)),
        out_specs=[VMEM] * 4,
        out_shape=[
            jax.ShapeDtypeStruct((rows, wg.shape[1]), bf16),
            jax.ShapeDtypeStruct((rows, depth), bf16),
            jax.ShapeDtypeStruct((rows, depth), bf16),
            jax.ShapeDtypeStruct((rows, LANES), f32),
        ],
        scratch_shapes=[pltpu.VMEM((depth // LANES, LANES), f32)],
        compiler_params=params(4),
        cost_estimate=cost(rows, wg),
        name="expand_send",
    )(at, own, gain.reshape(depth // LANES, LANES), in_vmem(wg), in_vmem(wu), *parts)


def expand_keep_kernel(at, x, wg, wu, out):
    half_of(at[2], x, wg, wu, out)


def expand_keep(at, x, wg, wu):
    rows = x.shape[0]
    return pl.pallas_call(
        expand_keep_kernel,
        in_specs=[SMEM] + [VMEM] * 3,
        out_specs=VMEM,
        out_shape=jax.ShapeDtypeStruct((rows, wg.shape[1]), bf16),
        compiler_params=params(4),
        cost_estimate=cost(rows, wg),
        name="expand_keep",
    )(at, x, in_vmem(wg), in_vmem(wu))


def gated_kernel(n, model, squares_n, *rest):
    parts, squares, out = rest[:n], rest[n : n + squares_n], rest[-1]
    half = out.shape[1]
    scale = lax.rsqrt(sum(s[...] for s in squares) / model + epsilon)
    for c in range(half // LANES):
        gate = scale * sum(p[:, lanes(c)].astype(f32) for p in parts)
        up = scale * sum(p[:, half + c * LANES : half + (c + 1) * LANES].astype(f32) for p in parts)
        out[:, lanes(c)] = (gate / (1.0 + jnp.exp(-gate)) * up).astype(bf16)


def gated(model, parts, squares):
    rows, width = parts[0].shape
    return pl.pallas_call(
        lambda *refs: gated_kernel(len(parts), model, len(squares), *refs),
        in_specs=[VMEM] * (len(parts) + len(squares)),
        out_specs=VMEM,
        out_shape=jax.ShapeDtypeStruct((rows, width // 2), bf16),
        compiler_params=params(4),
        name="gated",
    )(*parts, *squares)


def contract_kernel(side, at, hidden, w, *rest):
    out = rest[-1]
    half = hidden.shape[1]
    from_row = pl.multiple_of((at[2] if side == 0 else 1 - at[2]) * half, LANES)
    for start, size in blocks_of(w.shape[1], 512):
        cols = slice(start, start + size)
        term = jnp.dot(hidden[...], w[pl.ds(from_row, half), cols], preferred_element_type=f32)
        if side:
            term = term + rest[0][:, cols]
        out[:, cols] = term.astype(out.dtype)


def contract(side, at, hidden, w, *before):
    rows = hidden.shape[0]
    return pl.pallas_call(
        lambda *refs: contract_kernel(side, *refs),
        in_specs=[SMEM] + [VMEM] * (2 + len(before)),
        out_specs=VMEM,
        out_shape=jax.ShapeDtypeStruct((rows, w.shape[1]), bf16 if side else f32),
        compiler_params=params(4),
        cost_estimate=cost(rows, w),
        name="contract",
    )(at, hidden, in_vmem(w), *before)


def swap(x, axis, bit):
    n = lax.axis_size(axis)
    return lax.ppermute(x, axis, [(i, i ^ bit) for i in range(n)])


def bits_of(axis):
    n = lax.axis_size(axis)
    return [1 << b for b in range(n.bit_length() - 1)]


def gathered(x, axis):
    parts = [x]
    for bit in reversed(bits_of(axis)):
        parts = parts + [swap(p, axis, bit) for p in parts]
    return parts


def summed(x, axis, bits):
    for bit in bits[:-1]:
        x = (x.astype(f32) + swap(x, axis, bit).astype(f32)).astype(bf16)
    return [x] + [swap(x, axis, bit) for bit in bits[-1:]]


def per_device(tokens, attn_gain, ffn_gain, w_query, key_matrix, value_matrix, w_out, w_gate, w_up, w_down, kv_cache, lengths, slots):
    rows, model = tokens.shape
    wide_at, head_at = lax.axis_index("wide"), lax.axis_index("head")
    wide_size, head_size = lax.axis_size("wide"), lax.axis_size("head")
    at = jnp.stack([wide_at, (wide_at == wide_size - 1).astype(jnp.int32), wide_at % 2]).astype(jnp.int32)

    half = HEAD_WIDTH // 2
    positions = (
        jnp.broadcast_to(lengths[:, None], (lengths.shape[0], DRAFT_TOKENS))
        + jnp.arange(DRAFT_TOKENS, dtype=jnp.int32)[None, :]
    ).reshape(rows).astype(f32)
    exponent = jnp.arange(half, dtype=f32) * (2.0 / HEAD_WIDTH)
    angles = positions[:, None] * (theta_base ** (-exponent))[None, :]
    cos, sin = jnp.cos(angles), jnp.sin(angles)
    cos = jnp.concatenate([cos, cos], axis=1)
    sin = jnp.concatenate([-sin, sin], axis=1)

    qkv, own = project(at, tokens, attn_gain, w_query, key_matrix, value_matrix)
    value, stats = attend(at, lengths, slots, cos, sin, kv_cache, gathered(qkv, "wide"))
    out_part = output(gathered(value, "wide"), gathered(stats, "wide"), w_out)
    parts = summed(out_part, "head", bits_of("head"))
    send, resid, x, squares = expand_send(at, own, ffn_gain, parts, w_gate, w_up)
    received = swap(send, "wide", 1)
    keep = expand_keep(at, x, w_gate, w_up)
    pair = (keep.astype(f32) + received.astype(f32)).astype(bf16)
    hidden = gated(model, summed(pair, "wide", bits_of("wide")[1:]), gathered(squares, "wide"))
    other = swap(hidden, "wide", 1)
    down = contract(0, at, hidden, w_down)
    down = contract(1, at, other, w_down, down)

    share = rows // head_size
    cols = down.shape[1]
    blocks = down.reshape(head_size, share, cols)

    def block(index):
        return lax.dynamic_index_in_dim(blocks, index, 0, keepdims=False)

    total = block(head_at).astype(f32)
    for s in range(1, head_size):
        total = total + swap(block(head_at ^ s), "head", s).astype(f32)
    resid_rows = lax.dynamic_slice_in_dim(resid, head_at * share, share, 0)
    return (resid_rows.astype(f32) + total).astype(bf16)


def solution(mesh):
    in_specs = (
        P("grp", None),
        P(),
        P("wide"),
        P("wide", "head"),
        P("wide", "head"),
        P("wide", "head"),
        P("head", "wide"),
        P("wide", "head"),
        P("wide", "head"),
        P("head", "wide"),
        P(None, "grp", "wide", "head"),
        P("grp"),
        P("grp"),
    )
    out_specs = P(("grp", "head"), "wide")
    return jax.shard_map(
        per_device, mesh=mesh, in_specs=in_specs, out_specs=out_specs, check_vma=False
    )
```

time: 235 us -> 110 us (0.47)
  waiting for transfers between devices: 98.4 us -> 31 us
  blocking collectives: 53.1 us -> 0 us
  matrix products: 42.8 us -> 0 us
  local copies, waits for them, and re-layouts: 15.8 us -> 38.5 us
  Pallas kernels: 0 us -> 19.4 us
  starting transfers between devices: 0.17 us -> 19.1 us
  between operations: 13.4 us -> 0.16 us
  other arithmetic: 10.5 us -> 1.76 us
    psum x3 -> x0, waiting for transfers between devices: 58.5 us -> none  [the longest x1 33.9 us: per_device(): gate_sum, up_sum = lax.psum((gate_part, up_part), 'wide')]
    dot_general x11 -> x0, matrix products: 42.8 us -> none  [the longest x1 8.86 us: per_device(): jnp.dot(hidden, w_down, preferred_element_type=jnp.float32)]
    reduce_scatter x2 -> x0, waiting for transfers between devices: 39.7 us -> none  [the longest x1 20 us: per_device(): lax.psum_scatter(jnp.dot(hidden, w_down, preferred_element_type=jnp.float...]
    unnamed x15 -> x44, local copies, waits for them, and re-layouts: 0.81 us -> 38.4 us
    ppermute x0 -> x20, waiting for transfers between devices: none -> 31 us  [swap(): return lax.ppermute(x, axis, [(i, i ^ bit) for i in range(n)])]
    psum x3 -> x0, blocking collectives: 29.3 us -> none  [the longest x1 12.9 us: per_device(): lax.psum((query_part, key_part, value_part), 'wide')]
    pallas_call x0 -> x8, Pallas kernels: none -> 19.4 us  [the longest x1 4.01 us: project(): pl.pallas_call(lambda *refs: project_kernel(chunks, *refs), in_specs=[SME...]
    ppermute x0 -> x20, starting transfers between devices: none -> 19.1 us  [swap(): return lax.ppermute(x, axis, [(i, i ^ bit) for i in range(n)])]
  transfers between devices with their start and end apart: 5 -> 20, of which waited for: 5 -> 11; matrix products, arithmetic and copies ran while one was open for 8% -> 1% of each run, Pallas kernels for 0% -> 5%
where the time goes in v1:
time: 110 us
  local copies, waits for them, and re-layouts  38.5 us (35%)
  waiting for transfers between devices  31 us (28%)
  Pallas kernels  19.4 us (18%)
  starting transfers between devices  19.1 us (17%)
  other arithmetic  1.76 us (2%)
    unnamed x44, local copies, waits for them, and re-layouts  38.4 us
    ppermute x20, waiting for transfers between devices, swap(): return lax.ppermute(x, axis, [(i, i ^ bit) for i in range(n)])  31 us
    ppermute x20, starting transfers between devices, swap(): return lax.ppermute(x, axis, [(i, i ^ bit) for i in range(n)])  19.1 us
    pallas_call x1, Pallas kernels, project(): pl.pallas_call(lambda *refs: project_kernel(chunks, *refs), in_specs=[SME...  4.01 us
    pallas_call x2, Pallas kernels, contract(): pl.pallas_call(lambda *refs: contract_kernel(side, *refs), in_specs=[SMEM...  3.8 us
    pallas_call x1, Pallas kernels, attend(): pl.pallas_call(lambda *refs: attend_kernel(len(parts), *refs), in_specs=[...  3.48 us
    pallas_call x1, Pallas kernels, expand_keep(): pl.pallas_call(expand_keep_kernel, in_specs=[SMEM] + [VMEM] * 3, out_spec...  3.15 us
    pallas_call x1, Pallas kernels, expand_send(): pl.pallas_call(lambda *refs: expand_send_kernel(len(parts), *refs), in_sp...  3.13 us
  transfers between devices with their start and end apart: 20, of which 11 were waited for; matrix products, arithmetic and copies ran while one was open for 1% of the time, Pallas kernels for 5%

profile of v1, /device:TPU:0, one launch (start us, length us, event | category | flops | bytes accessed | tf_op | source)
XLA Modules:
  0.0 109.9 jit_solution(12244878752239980736)
XLA Ops:
  0.0 0.1 pad_add_fusion.refs_0_.at
  0.1 3.4 %copy-done.4 = bf16[2048,2048]{1,0:T(8,128)(2,1)S(1)} copy-done((bf16[2048,2048]{1,0:T(8,128)(2,1)S(1)}, bf16[2048,2048]{1,0:T(8,128)(2,1)}, u32[]{:S(2)}) %copy-start.4) | copy-done | bytes 8388632
  3.5 1.2 %copy-done.7 = bf16[2048,256]{1,0:T(8,128)(2,1)S(1)} copy-done((bf16[2048,256]{1,0:T(8,128)(2,1)S(1)}, bf16[2048,256]{1,0:T(8,128)(2,1)}, u32[]{:S(2)}) %copy-start.7) | copy-done | bytes 1048600
  4.7 1.2 %copy-done.8 = bf16[2048,256]{1,0:T(8,128)(2,1)S(1)} copy-done((bf16[2048,256]{1,0:T(8,128)(2,1)S(1)}, bf16[2048,256]{1,0:T(8,128)(2,1)}, u32[]{:S(2)}) %copy-start.8) | copy-done | bytes 1048600
  5.9 1.0 copy-done.9
  7.0 0.7 copy-done.10
  7.7 4.0 %project.1 = (bf16[32,2560]{1,0:T(8,128)(2,1)S(1)}, bf16[32,2048]{1,0:T(8,128)(2,1)S(1)}) custom-call(s32[3]{0:T(128)S(1)} %pad_add_fusion.refs_0_.at, bf16[32,8192]{1,0:T(8,128)(2,1)S(1)} %copy-done.9, bf16[64,128]{1,0:T(8,128)(2,1)S(1)} %bitcast.21, bf16[2048,2048]{1,0:T(8,128)(2,1)S(1)} %copy-done.4, bf16[2048,256]{1,0:T(8,128)(2,1)S(1)} %copy-done.7, ...), custom_call_target="tpu_custom_call" | custom-call | flops 335544320 | bytes 10485760 | tf_op jit(solution)/shard_map/project/pallas_call | solution.py:103
  11.7 3.0 %collective-permute-start = (bf16[32,2560]{1,0:T(8,128)(2,1)S(1)}, bf16[32,2560]{1,0:T(8,128)(2,1)S(1)}, u32[]{:S(2)}, u32[]{:S(2)}) collective-permute-start(bf16[32,2560]{1,0:T(8,128)(2,1)S(1)} %get-tuple-element.14.refs_6_), channel_id=1, source_target_pairs={{0,8},{4,12},{8,0},{12,4},{1,9},{5,13},{9,1},{13,5},{2,10},{6,14},... | collective-permute-start | bytes 491528 | tf_op jit(solution)/shard_map/ppermute | solution.py:361
  14.7 0.0 collective-permute-start.1
  14.7 0.7 add_convert_fusion.2
  15.5 0.1 convert_element_type.51
  15.5 3.4 %collective-permute-done.refs_7_ = bf16[32,2560]{1,0:T(8,128)(2,1)S(1)} collective-permute-done((bf16[32,2560]{1,0:T(8,128)(2,1)S(1)}, bf16[32,2560]{1,0:T(8,128)(2,1)S(1)}, u32[]{:S(2)}, u32[]{:S(2)}) %collective-permute-start) | collective-permute-done | bytes 163872 | tf_op jit(solution)/shard_map/ppermute | solution.py:361
  18.9 0.1 fusion.4
  19.1 0.1 pad_maximum_fusion
  19.1 0.0 collective-permute-done.1.refs_8_
  19.2 1.2 %collective-permute-done.2.refs_9_ = bf16[32,2560]{1,0:T(8,128)(2,1)S(1)} collective-permute-done((bf16[32,2560]{1,0:T(8,128)(2,1)S(1)}, bf16[32,2560]{1,0:T(8,128)(2,1)S(1)}, u32[]{:S(2)}, u32[]{:S(2)}) %collective-permute-start.2) | collective-permute-done | bytes 163872 | tf_op jit(solution)/shard_map/ppermute | solution.py:361
  20.3 2.2 %copy-done.6 = bf16[2,8,512,256]{3,2,1,0:T(8,128)(2,1)S(1)} copy-done((bf16[2,8,512,256]{3,2,1,0:T(8,128)(2,1)S(1)}, bf16[2,8,512,256]{3,2,1,0:T(8,128)(2,1)}, u32[]{:S(2)}) %copy-start.6) | copy-done | bytes 4194328
  22.5 0.7 copy-done.12
  23.2 0.7 copy-done.13
  23.8 3.5 %attend.1 = (bf16[32,2048]{1,0:T(8,128)(2,1)S(1)}, f32[32,128]{1,0:T(8,128)S(1)}) custom-call(s32[3]{0:T(128)S(1)} %pad_add_fusion.refs_0_.at, s32[8]{0:T(128)S(1)} %copy-done.12, s32[8]{0:T(128)S(1)} %copy-done.13, f32[32,128]{1,0:T(8,128)S(1)} %get-tuple-element.27.refs_3_, f32[32,128]{1,0:T(8,128)S(1)} %get-tuple-element.28.refs_4_, ...), custom_call_target="tpu_custom_call" | custom-call | flops 134217728 | bytes 4194304 | tf_op jit(solution)/shard_map/attend/pallas_call | solution.py:203
  27.3 1.8 %collective-permute-start.3 = (bf16[32,2048]{1,0:T(8,128)(2,1)S(1)}, bf16[32,2048]{1,0:T(8,128)(2,1)S(1)}, u32[]{:S(2)}, u32[]{:S(2)}) collective-permute-start(bf16[32,2048]{1,0:T(8,128)(2,1)S(1)} %get-tuple-element.15.refs_1_), channel_id=1, source_target_pairs={{0,8},{4,12},{8,0},{12,4},{1,9},{5,13},{9,1},{13,5},{2,10},{6,14},... | collective-permute-start | bytes 393224 | tf_op jit(solution)/shard_map/ppermute | solution.py:361
  29.1 0.0 collective-permute-start.4
  29.1 3.8 %collective-permute-done.3.refs_2_ = bf16[32,2048]{1,0:T(8,128)(2,1)S(1)} collective-permute-done((bf16[32,2048]{1,0:T(8,128)(2,1)S(1)}, bf16[32,2048]{1,0:T(8,128)(2,1)S(1)}, u32[]{:S(2)}, u32[]{:S(2)}) %collective-permute-start.3) | collective-permute-done | bytes 131104 | tf_op jit(solution)/shard_map/ppermute | solution.py:361
  32.9 0.0 collective-permute-start.5
  32.9 1.7 %collective-permute-start.6 = (f32[32,128]{1,0:T(8,128)S(1)}, f32[32,128]{1,0:T(8,128)S(1)}, u32[]{:S(2)}, u32[]{:S(2)}) collective-permute-start(f32[32,128]{1,0:T(8,128)S(1)} %get-tuple-element.16.refs_5_), channel_id=1, source_target_pairs={{0,8},{4,12},{8,0},{12,4},{1,9},{5,13},{9,1},{13,5},{2,10},{6,14},... | collective-permute-start | bytes 49160 | tf_op jit(solution)/shard_map/ppermute | solution.py:361
  34.7 0.2 collective-permute-start.7
  34.9 1.8 %collective-permute-done.6.refs_6_ = f32[32,128]{1,0:T(8,128)S(1)} collective-permute-done((f32[32,128]{1,0:T(8,128)S(1)}, f32[32,128]{1,0:T(8,128)S(1)}, u32[]{:S(2)}, u32[]{:S(2)}) %collective-permute-start.6) | collective-permute-done | bytes 16416 | tf_op jit(solution)/shard_map/ppermute | solution.py:361
  36.7 0.0 collective-permute-start.8
  36.7 0.0 collective-permute-done.7.refs_7_
  36.7 1.2 %collective-permute-done.8.refs_8_ = f32[32,128]{1,0:T(8,128)S(1)} collective-permute-done((f32[32,128]{1,0:T(8,128)S(1)}, f32[32,128]{1,0:T(8,128)S(1)}, u32[]{:S(2)}, u32[]{:S(2)}) %collective-permute-start.8) | collective-permute-done | bytes 16416 | tf_op jit(solution)/shard_map/ppermute | solution.py:361
  37.9 3.4 %copy-done.5 = bf16[2048,2048]{1,0:T(8,128)(2,1)S(1)} copy-done((bf16[2048,2048]{1,0:T(8,128)(2,1)S(1)}, bf16[2048,2048]{1,0:T(8,128)(2,1)}, u32[]{:S(2)}) %copy-start.5) | copy-done | bytes 8388632
  41.2 1.7 %output.1 = bf16[32,2048]{1,0:T(8,128)(2,1)S(1)} custom-call(bf16[2048,2048]{1,0:T(8,128)(2,1)S(1)} %copy-done.5, bf16[32,2048]{1,0:T(8,128)(2,1)S(1)} %get-tuple-element.15.refs_1_, bf16[32,2048]{1,0:T(8,128)(2,1)S(1)} %collective-permute-done.3.refs_2_, bf16[32,2048]{1,0:T(8,128)(2,1)S(1)} %collective-permute-done.4.refs_3_, ...), custom_call_target="tpu_custom_call" | custom-call | flops 268435456 | bytes 8388608 | tf_op jit(solution)/shard_map/output/pallas_call | solution.py:238
  42.9 1.8 %collective-permute-start.9 = (bf16[32,2048]{1,0:T(8,128)(2,1)S(1)}, bf16[32,2048]{1,0:T(8,128)(2,1)S(1)}, u32[]{:S(2)}, u32[]{:S(2)}) collective-permute-start(bf16[32,2048]{1,0:T(8,128)(2,1)S(1)} %output.1), channel_id=1, source_target_pairs={{0,1},{1,0},{2,3},{3,2},{4,5},{5,4},{6,7},{7,6},{8,9},{9,8},{10,11... | collective-permute-start | bytes 393224 | tf_op jit(solution)/shard_map/ppermute | solution.py:361
  44.7 3.8 %collective-permute-done.9 = bf16[32,2048]{1,0:T(8,128)(2,1)S(1)} collective-permute-done((bf16[32,2048]{1,0:T(8,128)(2,1)S(1)}, bf16[32,2048]{1,0:T(8,128)(2,1)S(1)}, u32[]{:S(2)}, u32[]{:S(2)}) %collective-permute-start.9) | collective-permute-done | bytes 131104 | tf_op jit(solution)/shard_map/ppermute | solution.py:361
  48.6 2.8 %collective-permute-start.10 = (bf16[32,2048]{1,0:T(8,128)(2,1)S(1)}, bf16[32,2048]{1,0:T(8,128)(2,1)S(1)}, u32[]{:S(2)}, u32[]{:S(2)}) collective-permute-start(bf16[32,2048]{1,0:T(8,128)(2,1)S(1)} %add_convert_fusion.1.refs_5_), channel_id=1, source_target_pairs={{0,2},{1,3},{2,0},{3,1},{4,6},{5,7},{6,4},{7,5},{8,10},{9,11},{10,... | collective-permute-start | bytes 393224 | tf_op jit(solution)/shard_map/ppermute | solution.py:361
  51.4 5.8 %collective-permute-done.10.refs_6_ = bf16[32,2048]{1,0:T(8,128)(2,1)S(1)} collective-permute-done((bf16[32,2048]{1,0:T(8,128)(2,1)S(1)}, bf16[32,2048]{1,0:T(8,128)(2,1)S(1)}, u32[]{:S(2)}, u32[]{:S(2)}) %collective-permute-start.10) | collective-permute-done | bytes 131104 | tf_op jit(solution)/shard_map/ppermute | solution.py:361
  57.2 5.2 %copy-done = bf16[2048,3584]{1,0:T(8,128)(2,1)S(1)} copy-done((bf16[2048,3584]{1,0:T(8,128)(2,1)S(1)}, bf16[2048,3584]{1,0:T(8,128)(2,1)}, u32[]{:S(2)}) %copy-start) | copy-done | bytes 14680088
  62.4 5.2 %copy-done.1 = bf16[2048,3584]{1,0:T(8,128)(2,1)S(1)} copy-done((bf16[2048,3584]{1,0:T(8,128)(2,1)S(1)}, bf16[2048,3584]{1,0:T(8,128)(2,1)}, u32[]{:S(2)}) %copy-start.1) | copy-done | bytes 14680088
  67.6 0.0 slice-start.7
  67.6 3.1 %expand_send.1 = (bf16[32,3584]{1,0:T(8,128)(2,1)S(1)}, bf16[32,2048]{1,0:T(8,128)(2,1)S(1)}, bf16[32,2048]{1,0:T(8,128)(2,1)S(1)}, f32[32,128]{1,0:T(8,128)S(1)}) custom-call(s32[3]{0:T(128)S(1)} %pad_add_fusion.refs_0_.at, bf16[32,2048]{1,0:T(8,128)(2,1)S(1)} %get-tuple-element.13.refs_1_, bf16[16,128]{1,0:T(8,128)(2,1)S(1)} %bitcast.22, ...), custom_call_target="tpu_custom_call" | custom-call | flops 469762048 | bytes 14680064 | tf_op jit(solution)/shard_map/expand_send/pallas_call | solution.py:278
  70.7 0.1 collective-permute-start.11
  70.9 0.2 slice-done.2
  71.0 0.6 slice-done.3
  71.6 1.2 %slice-done.6 = s8[4194304]{0:T(1024)(128)(4,1)S(1)} async-done(((s8[14680064]{0:T(1024)(128)(4,1)}), s8[4194304]{0:T(1024)(128)(4,1)S(1)}, s32[]{:S(2)}) %slice-start.6) | async-done | bytes 4194328
  72.8 1.2 %slice-done.7 = s8[4194304]{0:T(1024)(128)(4,1)S(1)} async-done(((s8[14680064]{0:T(1024)(128)(4,1)}), s8[4194304]{0:T(1024)(128)(4,1)S(1)}, s32[]{:S(2)}) %slice-start.7) | async-done | bytes 4194328
  74.0 3.1 %expand_keep.1 = bf16[32,3584]{1,0:T(8,128)(2,1)S(1)} custom-call(s32[3]{0:T(128)S(1)} %pad_add_fusion.refs_0_.at, bf16[32,2048]{1,0:T(8,128)(2,1)S(1)} %get-tuple-element.18.x, bf16[2048,3584]{1,0:T(8,128)(2,1)S(1)} %bitcast.16, bf16[2048,3584]{1,0:T(8,128)(2,1)S(1)} %bitcast.18), custom_call_target="tpu_custom_call" | custom-call | flops 469762048 | bytes 14680064 | tf_op jit(solution)/shard_map/expand_keep/pallas_call | solution.py:301
  77.2 0.0 collective-permute-done.11
  77.2 0.1 add_convert_fusion.refs_0_
  77.3 1.6 %collective-permute-start.12 = (bf16[32,3584]{1,0:T(8,128)(2,1)S(1)}, bf16[32,3584]{1,0:T(8,128)(2,1)S(1)}, u32[]{:S(2)}, u32[]{:S(2)}) collective-permute-start(bf16[32,3584]{1,0:T(8,128)(2,1)S(1)} %add_convert_fusion.refs_0_), channel_id=1, source_target_pairs={{0,8},{4,12},{8,0},{12,4},{1,9},{5,13},{9,1},{13,5},{2,10},{6,14},... | collective-permute-start | bytes 688136 | tf_op jit(solution)/shard_map/ppermute | solution.py:361
  78.9 0.5 collective-permute-start.13
  79.4 4.7 %collective-permute-done.13.refs_3_ = f32[32,128]{1,0:T(8,128)S(1)} collective-permute-done((f32[32,128]{1,0:T(8,128)S(1)}, f32[32,128]{1,0:T(8,128)S(1)}, u32[]{:S(2)}, u32[]{:S(2)}) %collective-permute-start.13) | collective-permute-done | bytes 16416 | tf_op jit(solution)/shard_map/ppermute | solution.py:361
  84.1 1.2 %collective-permute-done.15.refs_5_ = f32[32,128]{1,0:T(8,128)S(1)} collective-permute-done((f32[32,128]{1,0:T(8,128)S(1)}, f32[32,128]{1,0:T(8,128)S(1)}, u32[]{:S(2)}, u32[]{:S(2)}) %collective-permute-start.15) | collective-permute-done | bytes 16416 | tf_op jit(solution)/shard_map/ppermute | solution.py:361
  85.3 0.1 gated.1.refs_1_
  85.4 0.2 collective-permute-start.16
  85.6 5.2 %copy-done.2 = bf16[3584,2048]{1,0:T(8,128)(2,1)S(1)} copy-done((bf16[3584,2048]{1,0:T(8,128)(2,1)S(1)}, bf16[3584,2048]{1,0:T(8,128)(2,1)}, u32[]{:S(2)}) %copy-start.2) | copy-done | bytes 14680088
  90.8 1.9 %contract.2.refs_3_ = f32[32,2048]{1,0:T(8,128)S(1)} custom-call(s32[3]{0:T(128)S(1)} %pad_add_fusion.refs_0_.at, bf16[32,1792]{1,0:T(8,128)(2,1)S(1)} %gated.1.refs_1_, bf16[3584,2048]{1,0:T(8,128)(2,1)S(1)} %copy-done.2), custom_call_target="tpu_custom_call" | custom-call | flops 469762048 | bytes 14680064 | tf_op jit(solution)/shard_map/contract/pallas_call | solution.py:348
  92.7 0.0 copy-start.3
  92.7 5.2 %copy-done.3 = bf16[3584,2048]{1,0:T(8,128)(2,1)S(1)} copy-done((bf16[3584,2048]{1,0:T(8,128)(2,1)S(1)}, bf16[3584,2048]{1,0:T(8,128)(2,1)}, u32[]{:S(2)}) %copy-start.3) | copy-done | bytes 14680088
  97.9 1.9 %contract.3 = bf16[32,2048]{1,0:T(8,128)(2,1)S(1)} custom-call(s32[3]{0:T(128)S(1)} %pad_add_fusion.refs_0_.at, bf16[32,1792]{1,0:T(8,128)(2,1)S(1)} %collective-permute-done.16.refs_1_, bf16[3584,2048]{1,0:T(8,128)(2,1)S(1)} %copy-done.3, f32[32,2048]{1,0:T(8,128)S(1)} %contract.2.refs_3_), custom_call_target="tpu_custom_call" | custom-call | flops 469762048 | bytes 14680064 | tf_op jit(solution)/shard_map/contract/pallas_call | solution.py:348
  99.8 4.6 %collective-permute-start.19 = (bf16[8,2048]{1,0:T(8,128)(2,1)S(1)}, bf16[8,2048]{1,0:T(8,128)(2,1)S(1)}, u32[]{:S(2)}, u32[]{:S(2)}) collective-permute-start(bf16[8,2048]{1,0:T(8,128)(2,1)S(1)} %get-tuple-element.22), channel_id=1, source_target_pairs={{0,3},{1,2},{2,1},{3,0},{4,7},{5,6},{6,5},{7,4},{8,11},{9,10},{10,... | collective-permute-start | bytes 98312 | tf_op jit(solution)/shard_map/ppermute | solution.py:361
  104.4 0.6 collective-permute-start.17
  105.1 1.5 %collective-permute-done.19 = bf16[8,2048]{1,0:T(8,128)(2,1)S(1)} collective-permute-done((bf16[8,2048]{1,0:T(8,128)(2,1)S(1)}, bf16[8,2048]{1,0:T(8,128)(2,1)S(1)}, u32[]{:S(2)}, u32[]{:S(2)}) %collective-permute-start.19) | collective-permute-done | bytes 32800 | tf_op jit(solution)/shard_map/ppermute | solution.py:361
  106.6 2.7 %collective-permute-done.18 = bf16[8,2048]{1,0:T(8,128)(2,1)S(1)} collective-permute-done((bf16[8,2048]{1,0:T(8,128)(2,1)S(1)}, bf16[8,2048]{1,0:T(8,128)(2,1)S(1)}, u32[]{:S(2)}, u32[]{:S(2)}) %collective-permute-start.18) | collective-permute-done | bytes 32800 | tf_op jit(solution)/shard_map/ppermute | solution.py:361
  109.2 0.6 fusion.3
  (40 shorter events, 0.1 us)
Async XLA Ops:
  0.0 57.2 %copy-start.11 = (bf16[2048]{0:T(1024)(128)(2,1)S(1)}, bf16[2048]{0:T(1024)(128)(2,1)}, u32[]{:S(2)}) copy-start(bf16[2048]{0:T(1024)(128)(2,1)} %param.15) | copy-start | bytes 12292
  0.1 3.4 %copy-start.4 = (bf16[2048,2048]{1,0:T(8,128)(2,1)S(1)}, bf16[2048,2048]{1,0:T(8,128)(2,1)}, u32[]{:S(2)}) copy-start(bf16[2048,2048]{1,0:T(8,128)(2,1)} %refs_3_.2) | copy-start | bytes 25165828
  3.5 1.2 %copy-start.7 = (bf16[2048,256]{1,0:T(8,128)(2,1)S(1)}, bf16[2048,256]{1,0:T(8,128)(2,1)}, u32[]{:S(2)}) copy-start(bf16[2048,256]{1,0:T(8,128)(2,1)} %refs_4_.2) | copy-start | bytes 3145732
  4.7 1.2 %copy-start.8 = (bf16[2048,256]{1,0:T(8,128)(2,1)S(1)}, bf16[2048,256]{1,0:T(8,128)(2,1)}, u32[]{:S(2)}) copy-start(bf16[2048,256]{1,0:T(8,128)(2,1)} %refs_5_.2) | copy-start | bytes 3145732
  5.9 1.0 copy-start.9
  7.0 0.7 copy-start.10
  7.7 63.1 %slice-start.4 = ((s8[14680064]{0:T(1024)(128)(4,1)}), s8[2097152]{0:T(1024)(128)(4,1)S(1)}, s32[]{:S(2)}) async-start(s8[14680064]{0:T(1024)(128)(4,1)} %bitcast.17), calls=%async_computation.4 | async-start | bytes 4194304
  11.7 7.2 %collective-permute-start = (bf16[32,2560]{1,0:T(8,128)(2,1)S(1)}, bf16[32,2560]{1,0:T(8,128)(2,1)S(1)}, u32[]{:S(2)}, u32[]{:S(2)}) collective-permute-start(bf16[32,2560]{1,0:T(8,128)(2,1)S(1)} %get-tuple-element.14.refs_6_), channel_id=1, source_target_pairs={{0,8},{4,12},{8,0},{12,4},{1,9},{5,13},{9,1},{13,5},{2,10},{6,14},... | collective-permute-start | bytes 491528 | tf_op jit(solution)/shard_map/ppermute | solution.py:361
  14.7 4.4 %collective-permute-start.1 = (bf16[32,2560]{1,0:T(8,128)(2,1)S(1)}, bf16[32,2560]{1,0:T(8,128)(2,1)S(1)}, u32[]{:S(2)}, u32[]{:S(2)}) collective-permute-start(bf16[32,2560]{1,0:T(8,128)(2,1)S(1)} %get-tuple-element.14.refs_6_), channel_id=1, source_target_pairs={{0,4},{4,0},{8,12},{12,8},{1,5},{5,1},{9,13},{13,9},{2,6},{6,2},{1... | collective-permute-start | bytes 491528 | tf_op jit(solution)/shard_map/ppermute | solution.py:361
  18.9 1.4 %collective-permute-start.2 = (bf16[32,2560]{1,0:T(8,128)(2,1)S(1)}, bf16[32,2560]{1,0:T(8,128)(2,1)S(1)}, u32[]{:S(2)}, u32[]{:S(2)}) collective-permute-start(bf16[32,2560]{1,0:T(8,128)(2,1)S(1)} %collective-permute-done.refs_7_), channel_id=1, source_target_pairs={{0,4},{4,0},{8,12},{12,8},{1,5},{5,1},{9,13},{13,9},{2,6},{6,2},{1... | collective-permute-start | bytes 491528 | tf_op jit(solution)/shard_map/ppermute | solution.py:361
  20.3 2.2 %copy-start.6 = (bf16[2,8,512,256]{3,2,1,0:T(8,128)(2,1)S(1)}, bf16[2,8,512,256]{3,2,1,0:T(8,128)(2,1)}, u32[]{:S(2)}) copy-start(bf16[2,8,512,256]{3,2,1,0:T(8,128)(2,1)} %refs_5_.3) | copy-start | bytes 12582916
  22.5 0.7 copy-start.12
  23.2 0.7 copy-start.13
  23.8 47.0 %slice-start.5 = ((s8[14680064]{0:T(1024)(128)(4,1)}), s8[4194304]{0:T(1024)(128)(4,1)S(1)}, s32[]{:S(2)}) async-start(s8[14680064]{0:T(1024)(128)(4,1)} %bitcast.17), calls=%async_computation.5 | async-start | bytes 8388608
  27.3 5.6 %collective-permute-start.3 = (bf16[32,2048]{1,0:T(8,128)(2,1)S(1)}, bf16[32,2048]{1,0:T(8,128)(2,1)S(1)}, u32[]{:S(2)}, u32[]{:S(2)}) collective-permute-start(bf16[32,2048]{1,0:T(8,128)(2,1)S(1)} %get-tuple-element.15.refs_1_), channel_id=1, source_target_pairs={{0,8},{4,12},{8,0},{12,4},{1,9},{5,13},{9,1},{13,5},{2,10},{6,14},... | collective-permute-start | bytes 393224 | tf_op jit(solution)/shard_map/ppermute | solution.py:361
  29.1 8.7 %collective-permute-start.4 = (bf16[32,2048]{1,0:T(8,128)(2,1)S(1)}, bf16[32,2048]{1,0:T(8,128)(2,1)S(1)}, u32[]{:S(2)}, u32[]{:S(2)}) collective-permute-start(bf16[32,2048]{1,0:T(8,128)(2,1)S(1)} %get-tuple-element.15.refs_1_), channel_id=1, source_target_pairs={{0,4},{4,0},{8,12},{12,8},{1,5},{5,1},{9,13},{13,9},{2,6},{6,2},{1... | collective-permute-start | bytes 393224 | tf_op jit(solution)/shard_map/ppermute | solution.py:361
  32.9 4.9 %collective-permute-start.5 = (bf16[32,2048]{1,0:T(8,128)(2,1)S(1)}, bf16[32,2048]{1,0:T(8,128)(2,1)S(1)}, u32[]{:S(2)}, u32[]{:S(2)}) collective-permute-start(bf16[32,2048]{1,0:T(8,128)(2,1)S(1)} %collective-permute-done.3.refs_2_), channel_id=1, source_target_pairs={{0,4},{4,0},{8,12},{12,8},{1,5},{5,1},{9,13},{13,9},{2,6},{6,2},{1... | collective-permute-start | bytes 393224 | tf_op jit(solution)/shard_map/ppermute | solution.py:361
  32.9 3.7 %collective-permute-start.6 = (f32[32,128]{1,0:T(8,128)S(1)}, f32[32,128]{1,0:T(8,128)S(1)}, u32[]{:S(2)}, u32[]{:S(2)}) collective-permute-start(f32[32,128]{1,0:T(8,128)S(1)} %get-tuple-element.16.refs_5_), channel_id=1, source_target_pairs={{0,8},{4,12},{8,0},{12,4},{1,9},{5,13},{9,1},{13,5},{2,10},{6,14},... | collective-permute-start | bytes 49160 | tf_op jit(solution)/shard_map/ppermute | solution.py:361
  34.7 2.0 %collective-permute-start.7 = (f32[32,128]{1,0:T(8,128)S(1)}, f32[32,128]{1,0:T(8,128)S(1)}, u32[]{:S(2)}, u32[]{:S(2)}) collective-permute-start(f32[32,128]{1,0:T(8,128)S(1)} %get-tuple-element.16.refs_5_), channel_id=1, source_target_pairs={{0,4},{4,0},{8,12},{12,8},{1,5},{5,1},{9,13},{13,9},{2,6},{6,2},{1... | collective-permute-start | bytes 49160 | tf_op jit(solution)/shard_map/ppermute | solution.py:361
  36.7 1.2 %collective-permute-start.8 = (f32[32,128]{1,0:T(8,128)S(1)}, f32[32,128]{1,0:T(8,128)S(1)}, u32[]{:S(2)}, u32[]{:S(2)}) collective-permute-start(f32[32,128]{1,0:T(8,128)S(1)} %collective-permute-done.6.refs_6_), channel_id=1, source_target_pairs={{0,4},{4,0},{8,12},{12,8},{1,5},{5,1},{9,13},{13,9},{2,6},{6,2},{1... | collective-permute-start | bytes 49160 | tf_op jit(solution)/shard_map/ppermute | solution.py:361
  37.9 3.4 %copy-start.5 = (bf16[2048,2048]{1,0:T(8,128)(2,1)S(1)}, bf16[2048,2048]{1,0:T(8,128)(2,1)}, u32[]{:S(2)}) copy-start(bf16[2048,2048]{1,0:T(8,128)(2,1)} %refs_0_.1) | copy-start | bytes 25165828
  41.2 29.6 %slice-start = ((s8[14680064]{0:T(1024)(128)(4,1)}), s8[4194304]{0:T(1024)(128)(4,1)S(1)}, s32[]{:S(2)}) async-start(s8[14680064]{0:T(1024)(128)(4,1)} %bitcast.15), calls=%async_computation | async-start | bytes 8388608
  42.9 5.6 %collective-permute-start.9 = (bf16[32,2048]{1,0:T(8,128)(2,1)S(1)}, bf16[32,2048]{1,0:T(8,128)(2,1)S(1)}, u32[]{:S(2)}, u32[]{:S(2)}) collective-permute-start(bf16[32,2048]{1,0:T(8,128)(2,1)S(1)} %output.1), channel_id=1, source_target_pairs={{0,1},{1,0},{2,3},{3,2},{4,5},{5,4},{6,7},{7,6},{8,9},{9,8},{10,11... | collective-permute-start | bytes 393224 | tf_op jit(solution)/shard_map/ppermute | solution.py:361
  48.6 8.6 %collective-permute-start.10 = (bf16[32,2048]{1,0:T(8,128)(2,1)S(1)}, bf16[32,2048]{1,0:T(8,128)(2,1)S(1)}, u32[]{:S(2)}, u32[]{:S(2)}) collective-permute-start(bf16[32,2048]{1,0:T(8,128)(2,1)S(1)} %add_convert_fusion.1.refs_5_), channel_id=1, source_target_pairs={{0,2},{1,3},{2,0},{3,1},{4,6},{5,7},{6,4},{7,5},{8,10},{9,11},{10,... | collective-permute-start | bytes 393224 | tf_op jit(solution)/shard_map/ppermute | solution.py:361
  57.2 5.2 %copy-start = (bf16[2048,3584]{1,0:T(8,128)(2,1)S(1)}, bf16[2048,3584]{1,0:T(8,128)(2,1)}, u32[]{:S(2)}) copy-start(bf16[2048,3584]{1,0:T(8,128)(2,1)} %wg.1) | copy-start | bytes 44040196
  62.4 5.2 %copy-start.1 = (bf16[2048,3584]{1,0:T(8,128)(2,1)S(1)}, bf16[2048,3584]{1,0:T(8,128)(2,1)}, u32[]{:S(2)}) copy-start(bf16[2048,3584]{1,0:T(8,128)(2,1)} %wu.1) | copy-start | bytes 44040196
  67.6 3.3 %slice-start.1 = ((s8[14680064]{0:T(1024)(128)(4,1)}), s8[4194304]{0:T(1024)(128)(4,1)S(1)}, s32[]{:S(2)}) async-start(s8[14680064]{0:T(1024)(128)(4,1)} %bitcast.15), calls=%async_computation.1 | async-start | bytes 8388608
  67.6 3.5 %slice-start.2 = ((s8[14680064]{0:T(1024)(128)(4,1)}), s8[4194304]{0:T(1024)(128)(4,1)S(1)}, s32[]{:S(2)}) async-start(s8[14680064]{0:T(1024)(128)(4,1)} %bitcast.15), calls=%async_computation.2 | async-start | bytes 8388608
  67.6 4.1 %slice-start.3 = ((s8[14680064]{0:T(1024)(128)(4,1)}), s8[2097152]{0:T(1024)(128)(4,1)S(1)}, s32[]{:S(2)}) async-start(s8[14680064]{0:T(1024)(128)(4,1)} %bitcast.15), calls=%async_computation.3 | async-start | bytes 4194304
  67.6 5.3 %slice-start.6 = ((s8[14680064]{0:T(1024)(128)(4,1)}), s8[4194304]{0:T(1024)(128)(4,1)S(1)}, s32[]{:S(2)}) async-start(s8[14680064]{0:T(1024)(128)(4,1)} %bitcast.17), calls=%async_computation.6 | async-start | bytes 8388608
  67.6 6.4 %slice-start.7 = ((s8[14680064]{0:T(1024)(128)(4,1)}), s8[4194304]{0:T(1024)(128)(4,1)S(1)}, s32[]{:S(2)}) async-start(s8[14680064]{0:T(1024)(128)(4,1)} %bitcast.17), calls=%async_computation.7 | async-start | bytes 8388608
  70.7 6.4 %collective-permute-start.11 = (bf16[32,3584]{1,0:T(8,128)(2,1)S(1)}, bf16[32,3584]{1,0:T(8,128)(2,1)S(1)}, u32[]{:S(2)}, u32[]{:S(2)}) collective-permute-start(bf16[32,3584]{1,0:T(8,128)(2,1)S(1)} %get-tuple-element.19), channel_id=1, source_target_pairs={{0,4},{4,0},{8,12},{12,8},{1,5},{5,1},{9,13},{13,9},{2,6},{6,2},{1... | collective-permute-start | bytes 688136 | tf_op jit(solution)/shard_map/ppermute | solution.py:361
  77.3 8.0 %collective-permute-start.12 = (bf16[32,3584]{1,0:T(8,128)(2,1)S(1)}, bf16[32,3584]{1,0:T(8,128)(2,1)S(1)}, u32[]{:S(2)}, u32[]{:S(2)}) collective-permute-start(bf16[32,3584]{1,0:T(8,128)(2,1)S(1)} %add_convert_fusion.refs_0_), channel_id=1, source_target_pairs={{0,8},{4,12},{8,0},{12,4},{1,9},{5,13},{9,1},{13,5},{2,10},{6,14},... | collective-permute-start | bytes 688136 | tf_op jit(solution)/shard_map/ppermute | solution.py:361
  78.9 5.2 %collective-permute-start.13 = (f32[32,128]{1,0:T(8,128)S(1)}, f32[32,128]{1,0:T(8,128)S(1)}, u32[]{:S(2)}, u32[]{:S(2)}) collective-permute-start(f32[32,128]{1,0:T(8,128)S(1)} %get-tuple-element.20.refs_2_), channel_id=1, source_target_pairs={{0,8},{4,12},{8,0},{12,4},{1,9},{5,13},{9,1},{13,5},{2,10},{6,14},... | collective-permute-start | bytes 49160 | tf_op jit(solution)/shard_map/ppermute | solution.py:361
  79.4 4.7 %collective-permute-start.14 = (f32[32,128]{1,0:T(8,128)S(1)}, f32[32,128]{1,0:T(8,128)S(1)}, u32[]{:S(2)}, u32[]{:S(2)}) collective-permute-start(f32[32,128]{1,0:T(8,128)S(1)} %get-tuple-element.20.refs_2_), channel_id=1, source_target_pairs={{0,4},{4,0},{8,12},{12,8},{1,5},{5,1},{9,13},{13,9},{2,6},{6,2},{1... | collective-permute-start | bytes 49160 | tf_op jit(solution)/shard_map/ppermute | solution.py:361
  84.1 1.2 %collective-permute-start.15 = (f32[32,128]{1,0:T(8,128)S(1)}, f32[32,128]{1,0:T(8,128)S(1)}, u32[]{:S(2)}, u32[]{:S(2)}) collective-permute-start(f32[32,128]{1,0:T(8,128)S(1)} %collective-permute-done.13.refs_3_), channel_id=1, source_target_pairs={{0,4},{4,0},{8,12},{12,8},{1,5},{5,1},{9,13},{13,9},{2,6},{6,2},{1... | collective-permute-start | bytes 49160 | tf_op jit(solution)/shard_map/ppermute | solution.py:361
  85.4 7.3 %collective-permute-start.16 = (bf16[32,1792]{1,0:T(8,128)(2,1)S(1)}, bf16[32,1792]{1,0:T(8,128)(2,1)S(1)}, u32[]{:S(2)}, u32[]{:S(2)}) collective-permute-start(bf16[32,1792]{1,0:T(8,128)(2,1)S(1)} %gated.1.refs_1_), channel_id=1, source_target_pairs={{0,4},{4,0},{8,12},{12,8},{1,5},{5,1},{9,13},{13,9},{2,6},{6,2},{1... | collective-permute-start | bytes 344072 | tf_op jit(solution)/shard_map/ppermute | solution.py:361
  85.6 5.2 %copy-start.2 = (bf16[3584,2048]{1,0:T(8,128)(2,1)S(1)}, bf16[3584,2048]{1,0:T(8,128)(2,1)}, u32[]{:S(2)}) copy-start(bf16[3584,2048]{1,0:T(8,128)(2,1)} %refs_2_.5) | copy-start | bytes 44040196
  92.7 5.2 %copy-start.3 = (bf16[3584,2048]{1,0:T(8,128)(2,1)S(1)}, bf16[3584,2048]{1,0:T(8,128)(2,1)}, u32[]{:S(2)}) copy-start(bf16[3584,2048]{1,0:T(8,128)(2,1)} %refs_2_.5) | copy-start | bytes 44040196
  99.8 6.8 %collective-permute-start.19 = (bf16[8,2048]{1,0:T(8,128)(2,1)S(1)}, bf16[8,2048]{1,0:T(8,128)(2,1)S(1)}, u32[]{:S(2)}, u32[]{:S(2)}) collective-permute-start(bf16[8,2048]{1,0:T(8,128)(2,1)S(1)} %get-tuple-element.22), channel_id=1, source_target_pairs={{0,3},{1,2},{2,1},{3,0},{4,7},{5,6},{6,5},{7,4},{8,11},{9,10},{10,... | collective-permute-start | bytes 98312 | tf_op jit(solution)/shard_map/ppermute | solution.py:361
  104.4 4.8 %collective-permute-start.18 = (bf16[8,2048]{1,0:T(8,128)(2,1)S(1)}, bf16[8,2048]{1,0:T(8,128)(2,1)S(1)}, u32[]{:S(2)}, u32[]{:S(2)}) collective-permute-start(bf16[8,2048]{1,0:T(8,128)(2,1)S(1)} %get-tuple-element.23), channel_id=1, source_target_pairs={{0,2},{1,3},{2,0},{3,1},{4,6},{5,7},{6,4},{7,5},{8,10},{9,11},{10,... | collective-permute-start | bytes 98312 | tf_op jit(solution)/shard_map/ppermute | solution.py:361
  104.4 4.8 %collective-permute-start.17 = (bf16[8,2048]{1,0:T(8,128)(2,1)S(1)}, bf16[8,2048]{1,0:T(8,128)(2,1)S(1)}, u32[]{:S(2)}, u32[]{:S(2)}) collective-permute-start(bf16[8,2048]{1,0:T(8,128)(2,1)S(1)} %get-tuple-element.21), channel_id=1, source_target_pairs={{0,1},{1,0},{2,3},{3,2},{4,5},{5,4},{6,7},{7,6},{8,9},{9,8},{10,11... | collective-permute-start | bytes 98312 | tf_op jit(solution)/shard_map/ppermute | solution.py:361

commit v2 on v1

--- a/solution.py
+++ b/solution.py
@@ -16,13 +16,14 @@
 
 f32 = jnp.float32
 bf16 = jnp.bfloat16
+ANY = pl.BlockSpec(memory_space=pl.ANY)
 VMEM = pl.BlockSpec(memory_space=pltpu.VMEM)
 SMEM = pl.BlockSpec(memory_space=pltpu.SMEM)
-ANY = pl.BlockSpec(memory_space=pl.ANY)
-
-
-def in_vmem(x):
-    return pltpu.with_memory_space_constraint(x, pltpu.VMEM)
+HBM = pl.BlockSpec(memory_space=pltpu.HBM)
+
+
+def in_hbm(x):
+    return pltpu.with_memory_space_constraint(x, pltpu.HBM)
 
 
 def cost(rows, *weights):
@@ -39,15 +40,69 @@
     return [(at, step) for at in range(0, width, step)]
 
 
+def thirds(x):
+    high = x.astype(bf16)
+    rest = x - high.astype(f32)
+    middle = rest.astype(bf16)
+    return high, middle, (rest - middle.astype(f32)).astype(bf16)
+
+
 def lanes(at):
     return slice(at * LANES, (at + 1) * LANES)
 
 
-def project_kernel(chunks, at, tokens, gain, wq, wk, wv, out, own, tok, gain_f, norm, bq, bk, bv, acc, sems):
+def fetch_kernel(pieces, sides, at, _, *refs):
+    n = len(sides)
+    sources, held, token, sems = refs[:n], refs[n : 2 * n], refs[-2], refs[-1]
+    copies = []
+    for source, to, side in zip(sources, held, sides):
+        step = max(1, to.shape[0] // pieces)
+        base = 0
+        if side is not None:
+            base = pl.multiple_of((at[2] if side == 0 else 1 - at[2]) * to.shape[0], LANES)
+        for p in range(to.shape[0] // step):
+            copies.append(
+                pltpu.make_async_copy(
+                    source.at[pl.ds(base + p * step, step)],
+                    to.at[pl.ds(p * step, step)],
+                    sems.at[len(copies)],
+                )
+            )
+    for copy in copies:
+        copy.start()
+    token[...] = jnp.zeros_like(token)
+    for copy in copies:
+        copy.wait()
+
+
+def fetch(at, after, *wanted):
+    pieces = 8
+    sides = [w[1] if isinstance(w, tuple) else None for w in wanted]
+    wanted = [w[0] if isinstance(w, tuple) else w for w in wanted]
+    shapes = [
+        w.shape if side is None else (w.shape[0] // 2,) + w.shape[1:] for w, side in zip(wanted, sides)
+    ]
+    size = sum(w.size // (1 if side is None else 2) for w, side in zip(wanted, sides))
+    return pl.pallas_call(
+        lambda *refs: fetch_kernel(pieces, sides, *refs),
+        in_specs=[SMEM, ANY] + [HBM] * len(wanted),
+        out_specs=[VMEM] * (len(wanted) + 1),
+        out_shape=[pltpu.VMEM(shape, w.dtype) for shape, w in zip(shapes, wanted)]
+        + [pltpu.VMEM((8, LANES), f32)],
+        scratch_shapes=[pltpu.SemaphoreType.DMA((2 * pieces * len(wanted),))],
+        compiler_params=params(2),
+        cost_estimate=pl.CostEstimate(flops=0, bytes_accessed=4 * size, transcendentals=0),
+        name="fetch",
+    )(at, after, *[in_hbm(w) for w in wanted])
+
+
+def project_kernel(chunks, at, tokens, gain, wq, wk, wv, out, own, tok, gain_f, norm, bq, bk, bv, acc, gain_b, sems):
     rows, model = tok.shape
     depth, q_cols = bq.shape
     kv_cols = bk.shape[1]
     step = depth // chunks
+    gain_copy = pltpu.make_async_copy(gain, gain_b, sems.at[3 + chunks])
+    gain_copy.start()
     copies = [
         pltpu.make_async_copy(tokens, tok, sems.at[0]),
         pltpu.make_async_copy(wk, bk, sems.at[1]),
@@ -60,7 +115,8 @@
     ]
     for copy in copies:
         copy.start()
-    gain_f[...] = gain[...].astype(f32)
+    gain_copy.wait()
+    gain_f[...] = gain_b[...].astype(f32)
     copies[0].wait()
     squares = jnp.zeros((rows, LANES), f32)
     for c in range(model // LANES):
@@ -102,7 +158,7 @@
     chunks = max(1, min(8, depth // 256))
     return pl.pallas_call(
         lambda *refs: project_kernel(chunks, *refs),
-        in_specs=[SMEM, ANY, VMEM, ANY, ANY, ANY],
+        in_specs=[SMEM] + [HBM] * 5,
         out_specs=[VMEM, VMEM],
         out_shape=[
             jax.ShapeDtypeStruct((rows, q_cols + 2 * kv_cols), bf16),
@@ -116,22 +172,31 @@
             pltpu.VMEM(wk.shape, bf16),
             pltpu.VMEM(wv.shape, bf16),
             pltpu.VMEM((rows, q_cols), f32),
-            pltpu.SemaphoreType.DMA((3 + chunks,)),
+            pltpu.VMEM((model // LANES, LANES), bf16),
+            pltpu.SemaphoreType.DMA((4 + chunks,)),
         ],
         compiler_params=params(16),
         cost_estimate=cost(rows, wq, wk, wv),
         name="project",
-    )(at, tokens, gain.reshape(model // LANES, LANES), wq, wk, wv)
-
-
-def attend_kernel(n, at, lengths, slots, cos, sin, cache, *rest):
-    parts, (out, lse_out, queries, total) = rest[:n], rest[n:]
+    )(at, in_hbm(tokens), in_hbm(gain.reshape(model // LANES, LANES)), in_hbm(wq), in_hbm(wk), in_hbm(wv))
+
+
+def attend_kernel(n, at, cos, sin, cache, *rest):
+    parts, (out, queries, total, stats_f) = rest[:n], rest[n:]
     rows, q_cols = queries.shape
     context, kv_cols = cache.shape[2:]
     kv_heads = kv_cols // HEAD_WIDTH
     heads = q_cols // HEAD_WIDTH
     group = heads // kv_heads
     tile = 2 * DRAFT_TOKENS
+    requests = rows // DRAFT_TOKENS
+
+    def length(r):
+        return at[4 + r]
+
+    def slot(r):
+        return at[4 + requests + r]
+
     last = at[1]
     base = at[0] * context
 
@@ -155,7 +220,7 @@
     nt = (((1,), (1,)), ((), ()))
     for i in range(rows // tile):
         request = 2 * i
-        limit = jnp.where(first, lengths[request], lengths[request + 1])
+        limit = jnp.where(first, length(request), length(request + 1))
         live = position < limit
         own_at = tile * i + jnp.where(first, 0, DRAFT_TOKENS)
         seen = (draft_col >= own_at) & (draft_col <= tile * i + row) & (last > 0)
@@ -165,7 +230,7 @@
                 [queries[tile * i : tile * (i + 1), lanes(k * group + g)] for g in range(group)], axis=0
             ).astype(bf16)
             scores = [
-                lax.dot_general(q, cache[0, slots[request + s], :, lanes(k)], nt, preferred_element_type=f32)
+                lax.dot_general(q, cache[0, slot(request + s), :, lanes(k)], nt, preferred_element_type=f32)
                 for s in range(2)
             ]
             score = jnp.where(live, jnp.where(first, scores[0], scores[1]), neg_large)
@@ -179,7 +244,7 @@
             mass = jnp.sum(weight, axis=1, keepdims=True) + jnp.sum(draft_weight, axis=1, keepdims=True)
             weight = weight.astype(bf16)
             sums = [
-                jnp.dot(weight, cache[1, slots[request + s], :, lanes(k)], preferred_element_type=f32)
+                jnp.dot(weight, cache[1, slot(request + s), :, lanes(k)], preferred_element_type=f32)
                 for s in range(2)
             ]
             value = jnp.where(first, sums[0], sums[1]) + jnp.dot(
@@ -193,35 +258,43 @@
                 at_rows = slice(tile * g, tile * (g + 1))
                 total[tile * i : tile * (i + 1), lanes(k * group + g)] = value[at_rows]
                 stats = jnp.where(lane == k * group + g, lse[at_rows], stats)
-        lse_out[tile * i : tile * (i + 1), :] = stats
-    out[...] = total[...].astype(bf16)
-
-
-def attend(at, lengths, slots, cos, sin, cache, parts):
+        stats_f[tile * i : tile * (i + 1), :] = stats
+    out[:, :q_cols] = total[...].astype(bf16)
+    for p, term in enumerate(thirds(stats_f[...])):
+        out[:, q_cols + p * LANES : q_cols + (p + 1) * LANES] = term
+
+
+def attend(at, cos, sin, cache, parts):
     rows, width = parts[0].shape
     q_cols = width - 2 * cache.shape[3]
     return pl.pallas_call(
         lambda *refs: attend_kernel(len(parts), *refs),
-        in_specs=[SMEM] * 3 + [VMEM] * (3 + len(parts)),
-        out_specs=[VMEM, VMEM],
-        out_shape=[
-            jax.ShapeDtypeStruct((rows, q_cols), bf16),
-            jax.ShapeDtypeStruct((rows, LANES), f32),
+        in_specs=[SMEM] + [VMEM] * (3 + len(parts)),
+        out_specs=VMEM,
+        out_shape=jax.ShapeDtypeStruct((rows, q_cols + 3 * LANES), bf16),
+        scratch_shapes=[
+            pltpu.VMEM((rows, q_cols), f32),
+            pltpu.VMEM((rows, q_cols), f32),
+            pltpu.VMEM((rows, LANES), f32),
         ],
-        scratch_shapes=[pltpu.VMEM((rows, q_cols), f32), pltpu.VMEM((rows, q_cols), f32)],
         compiler_params=params(6),
         cost_estimate=cost(rows, cache),
         name="attend",
-    )(at, lengths, slots, cos, sin, in_vmem(cache), *parts)
+    )(at, cos, sin, cache, *parts)
+
+
+def joined(ref, start):
+    return sum(ref[:, start + p * LANES : start + (p + 1) * LANES].astype(f32) for p in range(3))
 
 
 def output_kernel(n, w, *rest):
-    values, stats, (out, attended) = rest[:n], rest[n : 2 * n], rest[2 * n :]
+    values, (out, attended) = rest[:n], rest[n:]
     heads = attended.shape[1] // HEAD_WIDTH
-    top = stats[0][...]
+    stats = [joined(v, attended.shape[1]) for v in values]
+    top = stats[0]
     for s in stats[1:]:
-        top = jnp.maximum(top, s[...])
-    shares = [jnp.exp(s[...] - top) for s in stats]
+        top = jnp.maximum(top, s)
+    shares = [jnp.exp(s - top) for s in stats]
     whole = sum(shares)
     shares = [s / whole for s in shares]
     for h in range(heads):
@@ -233,18 +306,18 @@
         out[:, cols] = jnp.dot(attended[...], w[:, cols], preferred_element_type=f32).astype(out.dtype)
 
 
-def output(values, stats, w):
+def output(values, w, after):
     rows = values[0].shape[0]
     return pl.pallas_call(
-        lambda *refs: output_kernel(len(values), *refs),
-        in_specs=[VMEM] * (1 + 2 * len(values)),
+        lambda _, *refs: output_kernel(len(values), *refs),
+        in_specs=[ANY] + [VMEM] * (1 + len(values)),
         out_specs=VMEM,
         out_shape=jax.ShapeDtypeStruct((rows, w.shape[1]), bf16),
         scratch_shapes=[pltpu.VMEM((rows, w.shape[0]), bf16)],
         compiler_params=params(4),
         cost_estimate=cost(rows, w),
         name="output",
-    )(in_vmem(w), *values, *stats)
+    )(after, w, *values)
 
 
 def half_of(side, x, wg, wu, out):
@@ -258,18 +331,20 @@
 
 
 def expand_send_kernel(n, at, own, gain, wg, wu, *rest):
-    parts, (out, resid, x, squares, gain_f) = rest[:n], rest[n:]
+    parts, (out, resid, x, gain_f) = rest[:n], rest[n:]
     rows = own.shape[0]
     gain_f[...] = gain[...].astype(f32)
     square = jnp.zeros((rows, LANES), f32)
     for c in range(own.shape[1] // LANES):
         value = own[:, lanes(c)].astype(f32) + sum(p[:, lanes(c)].astype(f32) for p in parts)
         value = value.astype(bf16)
+        value = value.astype(f32)
         resid[:, lanes(c)] = value
-        value = value.astype(f32)
         square = square + value * value
         x[:, lanes(c)] = (value * gain_f[c : c + 1, :]).astype(bf16)
-    squares[...] = jnp.broadcast_to(jnp.sum(square, axis=1, keepdims=True), squares.shape)
+    square = jnp.broadcast_to(jnp.sum(square, axis=1, keepdims=True), square.shape)
+    for p, term in enumerate(thirds(square)):
+        out[:, wg.shape[1] + p * LANES : wg.shape[1] + (p + 1) * LANES] = term
     half_of(1 - at[2], x, wg, wu, out)
 
 
@@ -278,18 +353,17 @@
     return pl.pallas_call(
         lambda *refs: expand_send_kernel(len(parts), *refs),
         in_specs=[SMEM] + [VMEM] * (4 + len(parts)),
-        out_specs=[VMEM] * 4,
+        out_specs=[VMEM] * 3,
         out_shape=[
-            jax.ShapeDtypeStruct((rows, wg.shape[1]), bf16),
+            jax.ShapeDtypeStruct((rows, wg.shape[1] + 3 * LANES), bf16),
+            jax.ShapeDtypeStruct((rows, depth), f32),
             jax.ShapeDtypeStruct((rows, depth), bf16),
-            jax.ShapeDtypeStruct((rows, depth), bf16),
-            jax.ShapeDtypeStruct((rows, LANES), f32),
         ],
         scratch_shapes=[pltpu.VMEM((depth // LANES, LANES), f32)],
         compiler_params=params(4),
         cost_estimate=cost(rows, wg),
         name="expand_send",
-    )(at, own, gain.reshape(depth // LANES, LANES), in_vmem(wg), in_vmem(wu), *parts)
+    )(at, own, gain.reshape(depth // LANES, LANES), wg, wu, *parts)
 
 
 def expand_keep_kernel(at, x, wg, wu, out):
@@ -306,54 +380,122 @@
         compiler_params=params(4),
         cost_estimate=cost(rows, wg),
         name="expand_keep",
-    )(at, x, in_vmem(wg), in_vmem(wu))
-
-
-def gated_kernel(n, model, squares_n, *rest):
-    parts, squares, out = rest[:n], rest[n : n + squares_n], rest[-1]
+    )(at, x, wg, wu)
+
+
+def pair_kernel(keep, received, stats, out):
+    width = out.shape[1] - 3 * LANES
+    for start, size in blocks_of(width, 512):
+        cols = slice(start, start + size)
+        out[:, cols] = (keep[:, cols].astype(f32) + received[:, cols].astype(f32)).astype(bf16)
+    for p, term in enumerate(thirds(joined(stats, width) + joined(received, width))):
+        out[:, width + p * LANES : width + (p + 1) * LANES] = term
+
+
+def pair(keep, received, stats):
+    return pl.pallas_call(
+        pair_kernel,
+        in_specs=[VMEM] * 3,
+        out_specs=VMEM,
+        out_shape=jax.ShapeDtypeStruct(received.shape, bf16),
+        compiler_params=params(4),
+        name="pair",
+    )(keep, received, stats)
+
+
+def gated_kernel(model, one, two, out):
     half = out.shape[1]
-    scale = lax.rsqrt(sum(s[...] for s in squares) / model + epsilon)
+    scale = lax.rsqrt((joined(one, 2 * half) + joined(two, 2 * half)) / model + epsilon)
     for c in range(half // LANES):
-        gate = scale * sum(p[:, lanes(c)].astype(f32) for p in parts)
-        up = scale * sum(p[:, half + c * LANES : half + (c + 1) * LANES].astype(f32) for p in parts)
+        gate, up = (
+            scale * (one[:, lanes(at)].astype(f32) + two[:, lanes(at)].astype(f32))
+            for at in (c, half // LANES + c)
+        )
         out[:, lanes(c)] = (gate / (1.0 + jnp.exp(-gate)) * up).astype(bf16)
 
 
-def gated(model, parts, squares):
-    rows, width = parts[0].shape
-    return pl.pallas_call(
-        lambda *refs: gated_kernel(len(parts), model, len(squares), *refs),
-        in_specs=[VMEM] * (len(parts) + len(squares)),
-        out_specs=VMEM,
-        out_shape=jax.ShapeDtypeStruct((rows, width // 2), bf16),
+def gated(model, one, two, after):
+    rows, width = one.shape
+    return pl.pallas_call(
+        lambda _, *refs: gated_kernel(model, *refs),
+        in_specs=[ANY] + [VMEM] * 2,
+        out_specs=VMEM,
+        out_shape=jax.ShapeDtypeStruct((rows, (width - 3 * LANES) // 2), bf16),
         compiler_params=params(4),
         name="gated",
-    )(*parts, *squares)
-
-
-def contract_kernel(side, at, hidden, w, *rest):
-    out = rest[-1]
-    half = hidden.shape[1]
-    from_row = pl.multiple_of((at[2] if side == 0 else 1 - at[2]) * half, LANES)
+    )(after, one, two)
+
+
+def contract_kernel(hidden, w, out):
     for start, size in blocks_of(w.shape[1], 512):
         cols = slice(start, start + size)
-        term = jnp.dot(hidden[...], w[pl.ds(from_row, half), cols], preferred_element_type=f32)
-        if side:
-            term = term + rest[0][:, cols]
-        out[:, cols] = term.astype(out.dtype)
-
-
-def contract(side, at, hidden, w, *before):
+        out[:, cols] = jnp.dot(hidden[...], w[:, cols], preferred_element_type=f32)
+
+
+def contract(hidden, w):
     rows = hidden.shape[0]
     return pl.pallas_call(
-        lambda *refs: contract_kernel(side, *refs),
-        in_specs=[SMEM] + [VMEM] * (2 + len(before)),
-        out_specs=VMEM,
-        out_shape=jax.ShapeDtypeStruct((rows, w.shape[1]), bf16 if side else f32),
+        contract_kernel,
+        in_specs=[VMEM] * 2,
+        out_specs=VMEM,
+        out_shape=jax.ShapeDtypeStruct((rows, w.shape[1]), f32),
         compiler_params=params(4),
         cost_estimate=cost(rows, w),
         name="contract",
-    )(at, hidden, in_vmem(w), *before)
+    )(hidden, w)
+
+
+def contract_last_kernel(n, at, hidden, w, before, resid, own, *rest):
+    sends, acc = rest[:-1], rest[-1]
+    share = own.shape[0]
+    for start, size in blocks_of(w.shape[1], 512):
+        cols = slice(start, start + size)
+        acc[:, cols] = before[:, cols] + jnp.dot(hidden[...], w[:, cols], preferred_element_type=f32)
+
+    def block(ref, index):
+        if share % 8 == 0:
+            return ref[pl.ds(pl.multiple_of(index * share, share), share), :]
+        chosen = ref[:share, :]
+        for b in range(1, n):
+            chosen = jnp.where(index == b, ref[b * share : (b + 1) * share, :], chosen)
+        return chosen
+
+    own[...] = block(acc, at[3]) + block(resid, at[3])
+    for s in range(1, n):
+        sends[s - 1][...] = block(acc, at[3] ^ s).astype(bf16)
+
+
+def contract_last(n, at, hidden, w, before, resid):
+    rows, cols = before.shape
+    share = rows // n
+    return pl.pallas_call(
+        lambda *refs: contract_last_kernel(n, *refs),
+        in_specs=[SMEM] + [VMEM] * 4,
+        out_specs=[VMEM] * n,
+        out_shape=[jax.ShapeDtypeStruct((share, cols), f32)]
+        + [jax.ShapeDtypeStruct((share, cols), bf16)] * (n - 1),
+        scratch_shapes=[pltpu.VMEM((rows, cols), f32)],
+        compiler_params=params(4),
+        cost_estimate=cost(rows, w),
+        name="contract_last",
+    )(at, hidden, w, before, resid)
+
+
+def add_kernel(_, one, two, out):
+    for start, size in blocks_of(out.shape[1], 512):
+        cols = slice(start, start + size)
+        out[:, cols] = (one[:, cols].astype(f32) + two[:, cols].astype(f32)).astype(bf16)
+
+
+def add(one, two, after):
+    return pl.pallas_call(
+        add_kernel,
+        in_specs=[ANY] + [VMEM] * 2,
+        out_specs=VMEM,
+        out_shape=jax.ShapeDtypeStruct(one.shape, bf16),
+        compiler_params=params(4),
+        name="add",
+    )(after, one, two)
 
 
 def swap(x, axis, bit):
@@ -373,17 +515,12 @@
     return parts
 
 
-def summed(x, axis, bits):
-    for bit in bits[:-1]:
-        x = (x.astype(f32) + swap(x, axis, bit).astype(f32)).astype(bf16)
-    return [x] + [swap(x, axis, bit) for bit in bits[-1:]]
-
-
 def per_device(tokens, attn_gain, ffn_gain, w_query, key_matrix, value_matrix, w_out, w_gate, w_up, w_down, kv_cache, lengths, slots):
     rows, model = tokens.shape
     wide_at, head_at = lax.axis_index("wide"), lax.axis_index("head")
     wide_size, head_size = lax.axis_size("wide"), lax.axis_size("head")
-    at = jnp.stack([wide_at, (wide_at == wide_size - 1).astype(jnp.int32), wide_at % 2]).astype(jnp.int32)
+    places = jnp.stack([wide_at, (wide_at == wide_size - 1).astype(jnp.int32), wide_at & 1, head_at])
+    at = jnp.concatenate([places.astype(jnp.int32), lengths, slots])
 
     half = HEAD_WIDTH // 2
     positions = (
@@ -397,30 +534,30 @@
     sin = jnp.concatenate([-sin, sin], axis=1)
 
     qkv, own = project(at, tokens, attn_gain, w_query, key_matrix, value_matrix)
-    value, stats = attend(at, lengths, slots, cos, sin, kv_cache, gathered(qkv, "wide"))
-    out_part = output(gathered(value, "wide"), gathered(stats, "wide"), w_out)
-    parts = summed(out_part, "head", bits_of("head"))
-    send, resid, x, squares = expand_send(at, own, ffn_gain, parts, w_gate, w_up)
+    cache, w_out, _ = fetch(at, qkv, kv_cache.reshape((-1,) + kv_cache.shape[2:]), w_out)
+    cache = cache.reshape(kv_cache.shape)
+    value = attend(at, cos, sin, cache, gathered(qkv, "wide"))
+    w_gate, have_gate = fetch(at, value, w_gate)
+    out_part = output(gathered(value, "wide"), w_out, have_gate)
+    w_down_own, have_own = fetch(at, out_part, (w_down, 0))
+    for bit in bits_of("head")[:-1]:
+        out_part = add(out_part, swap(out_part, "head", bit), have_own)
+    w_up, _ = fetch(at, out_part, w_up)
+    parts = [out_part, swap(out_part, "head", bits_of("head")[-1])]
+    send, resid, x = expand_send(at, own, ffn_gain, parts, w_gate, w_up)
     received = swap(send, "wide", 1)
     keep = expand_keep(at, x, w_gate, w_up)
-    pair = (keep.astype(f32) + received.astype(f32)).astype(bf16)
-    hidden = gated(model, summed(pair, "wide", bits_of("wide")[1:]), gathered(squares, "wide"))
+    total = pair(keep, received, send)
+    w_down_other, have_other = fetch(at, total, (w_down, 1))
+    for bit in bits_of("wide")[1:-1]:
+        there = swap(total, "wide", bit)
+        total = pair(total, there, total)
+    hidden = gated(model, total, swap(total, "wide", bits_of("wide")[-1]), have_other)
     other = swap(hidden, "wide", 1)
-    down = contract(0, at, hidden, w_down)
-    down = contract(1, at, other, w_down, down)
-
-    share = rows // head_size
-    cols = down.shape[1]
-    blocks = down.reshape(head_size, share, cols)
-
-    def block(index):
-        return lax.dynamic_index_in_dim(blocks, index, 0, keepdims=False)
-
-    total = block(head_at).astype(f32)
-    for s in range(1, head_size):
-        total = total + swap(block(head_at ^ s), "head", s).astype(f32)
-    resid_rows = lax.dynamic_slice_in_dim(resid, head_at * share, share, 0)
-    return (resid_rows.astype(f32) + total).astype(bf16)
+    total, *sends = contract_last(head_size, at, other, w_down_other, contract(hidden, w_down_own), resid)
+    for s, send in enumerate(sends, 1):
+        total = total + swap(send, "head", s).astype(f32)
+    return total.astype(bf16)
 
 
 def solution(mesh):

time: 110 us -> 82.1 us (0.75)
  local copies, waits for them, and re-layouts: 38.5 us -> 0.9 us
  Pallas kernels: 19.4 us -> 46.1 us
  waiting for transfers between devices: 31 us -> 17.8 us
  starting transfers between devices: 19.1 us -> 15.9 us
    unnamed x44 -> x4, local copies, waits for them, and re-layouts: 38.4 us -> 0.01 us
    pallas_call x4 -> x11, Pallas kernels: 5.62 us -> 31.3 us  [the longest x5 26 us: fetch(): pl.pallas_call(lambda *refs: fetch_kernel(pieces, sides, *refs), in_specs...]
    ppermute x20 -> x14, waiting for transfers between devices: 31 us -> 17.8 us  [swap(): return lax.ppermute(x, axis, [(i, i ^ bit) for i in range(n)])]
    ppermute x20 -> x14, starting transfers between devices: 19.1 us -> 15.9 us  [swap(): return lax.ppermute(x, axis, [(i, i ^ bit) for i in range(n)])]
  transfers between devices with their start and end apart: 20 -> 14, of which waited for: 11 -> 6; matrix products, arithmetic and copies ran while one was open for 1% -> 0% of each run, Pallas kernels for 5% -> 37%
where the time goes in v2:
time: 82.1 us; the launch traced here: 81.8 us
  Pallas kernels  46.1 us (56%)
  waiting for transfers between devices  17.8 us (22%)
  starting transfers between devices  15.9 us (19%)
  other arithmetic  0.93 us (1%)
  local copies, waits for them, and re-layouts  0.9 us (1%)
    pallas_call x5, Pallas kernels, fetch(): pl.pallas_call(lambda *refs: fetch_kernel(pieces, sides, *refs), in_specs...  26 us
    ppermute x14, waiting for transfers between devices, swap(): return lax.ppermute(x, axis, [(i, i ^ bit) for i in range(n)])  17.8 us
    ppermute x14, starting transfers between devices, swap(): return lax.ppermute(x, axis, [(i, i ^ bit) for i in range(n)])  15.9 us
    pallas_call x1, Pallas kernels, project(): pl.pallas_call(lambda *refs: project_kernel(chunks, *refs), in_specs=[SME...  5.11 us
    pallas_call x1, Pallas kernels, attend(): pl.pallas_call(lambda *refs: attend_kernel(len(parts), *refs), in_specs=[...  3.44 us
    pallas_call x1, Pallas kernels, expand_send(): pl.pallas_call(lambda *refs: expand_send_kernel(len(parts), *refs), in_sp...  3.17 us
    pallas_call x1, Pallas kernels, expand_keep(): pl.pallas_call(expand_keep_kernel, in_specs=[SMEM] + [VMEM] * 3, out_spec...  3.15 us
    pallas_call x1, Pallas kernels, contract_last(): pl.pallas_call(lambda *refs: contract_last_kernel(n, *refs), in_specs=[SM...  1.94 us
  transfers between devices with their start and end apart: 14, of which 6 were waited for; matrix products, arithmetic and copies ran while one was open for 0% of the time, Pallas kernels for 37%

profile of v2, /device:TPU:0, one launch (start us, length us, event | category | flops | bytes accessed | tf_op | source)
XLA Modules:
  0.0 81.8 jit_solution(6889278885607310768)
XLA Ops:
  0.0 0.0 copy-start.1
  0.0 0.8 concatenate.9.refs_0_.at
  0.8 5.1 %project.1 = (bf16[32,2560]{1,0:T(8,128)(2,1)S(1)}, bf16[32,2048]{1,0:T(8,128)(2,1)S(1)}) custom-call(s32[20]{0:T(128)S(1)} %concatenate.9.refs_0_.at, bf16[32,8192]{1,0:T(8,128)(2,1)} %refs_1_.1, bf16[64,128]{1,0:T(8,128)(2,1)} %bitcast.11, bf16[2048,2048]{1,0:T(8,128)(2,1)} %refs_3_.2, bf16[2048,256]{1,0:T(8,128)(2,1)} %refs_4_.1, bf16[2048,256]{1,0:T(8,128)(2,1)} %refs_5_.1), custom_call_target="tpu_custom_call" | custom-call | flops 335544320 | bytes 10485760 | tf_op jit(solution)/shard_map/project/pallas_call | solution.py:159
  5.9 0.5 collective-permute-start.1
  6.4 2.6 %collective-permute-start = (bf16[32,2560]{1,0:T(8,128)(2,1)S(1)}, bf16[32,2560]{1,0:T(8,128)(2,1)S(1)}, u32[]{:S(2)}, u32[]{:S(2)}) collective-permute-start(bf16[32,2560]{1,0:T(8,128)(2,1)S(1)} %get-tuple-element.24.refs_1_.refs_4_), channel_id=1, source_target_pairs={{0,8},{4,12},{8,0},{12,4},{1,9},{5,13},{9,1},{13,5},{2,10},{6,14},... | collective-permute-start | bytes 491528 | tf_op jit(solution)/shard_map/ppermute | solution.py:503
  9.0 0.0 copy-done.1
  9.0 0.1 add_convert_fusion.1
  9.1 0.1 convert_element_type.24
  9.2 4.6 %collective-permute-done.refs_5_ = bf16[32,2560]{1,0:T(8,128)(2,1)S(1)} collective-permute-done((bf16[32,2560]{1,0:T(8,128)(2,1)S(1)}, bf16[32,2560]{1,0:T(8,128)(2,1)S(1)}, u32[]{:S(2)}, u32[]{:S(2)}) %collective-permute-start) | collective-permute-done | bytes 163872 | tf_op jit(solution)/shard_map/ppermute | solution.py:503
  13.8 0.0 collective-permute-start.2
  13.8 0.1 fusion
  14.0 6.0 %fetch.5 = (bf16[16,512,256]{2,1,0:T(8,128)(2,1)S(1)}, bf16[2048,2048]{1,0:T(8,128)(2,1)S(1)}, f32[8,128]{1,0:T(8,128)}) custom-call(s32[20]{0:T(128)S(1)} %concatenate.9.refs_0_.at, bf16[32,2560]{1,0:T(8,128)(2,1)S(1)} %get-tuple-element.24.refs_1_.refs_4_, bf16[16,512,256]{2,1,0:T(8,128)(2,1)} %bitcast.10, bf16[2048,2048]{1,0:T(8,128)(2,1)} %refs_3_.3), custom_call_target="tpu_custom_call" | custom-call | bytes 25165824 | tf_op jit(solution)/shard_map/fetch/pallas_call | solution.py:86
  20.0 0.1 pad_maximum_fusion
  20.1 0.0 collective-permute-done.1.refs_6_
  20.1 0.0 collective-permute-done.2.refs_7_
  20.1 3.4 %attend.1.refs_1_ = bf16[32,2432]{1,0:T(8,128)(2,1)S(1)} custom-call(s32[20]{0:T(128)S(1)} %concatenate.9.refs_0_.at, f32[32,128]{1,0:T(8,128)S(1)} %get-tuple-element.44.refs_1_, f32[32,128]{1,0:T(8,128)S(1)} %get-tuple-element.45.refs_2_, bf16[2,8,512,256]{3,2,1,0:T(8,128)(2,1)S(1)} %bitcast.8, bf16[32,2560]{1,0:T(8,128)(2,1)S(1)} %get-tuple-element.24.refs_1_.refs_4_, ...), custom_call_target="tpu_custom_call" | custom-call | flops 134217728 | bytes 4194304 | tf_op jit(solution)/shard_map/attend/pallas_call | solution.py:270
  23.5 1.8 %collective-permute-start.3 = (bf16[32,2432]{1,0:T(8,128)(2,1)S(1)}, bf16[32,2432]{1,0:T(8,128)(2,1)S(1)}, u32[]{:S(2)}, u32[]{:S(2)}) collective-permute-start(bf16[32,2432]{1,0:T(8,128)(2,1)S(1)} %attend.1.refs_1_), channel_id=1, source_target_pairs={{0,8},{4,12},{8,0},{12,4},{1,9},{5,13},{9,1},{13,5},{2,10},{6,14},... | collective-permute-start | bytes 466952 | tf_op jit(solution)/shard_map/ppermute | solution.py:503
  25.4 0.2 collective-permute-start.4
  25.6 4.5 %collective-permute-done.3.refs_2_ = bf16[32,2432]{1,0:T(8,128)(2,1)S(1)} collective-permute-done((bf16[32,2432]{1,0:T(8,128)(2,1)S(1)}, bf16[32,2432]{1,0:T(8,128)(2,1)S(1)}, u32[]{:S(2)}, u32[]{:S(2)}) %collective-permute-start.3) | collective-permute-done | bytes 155680 | tf_op jit(solution)/shard_map/ppermute | solution.py:503
  30.1 0.0 collective-permute-start.5
  30.1 5.9 %fetch.6 = (bf16[2048,3584]{1,0:T(8,128)(2,1)S(1)}, f32[8,128]{1,0:T(8,128)S(1)}) custom-call(s32[20]{0:T(128)S(1)} %concatenate.9.refs_0_.at, bf16[32,2432]{1,0:T(8,128)(2,1)S(1)} %attend.1.refs_1_, bf16[2048,3584]{1,0:T(8,128)(2,1)} %refs_2_.4), custom_call_target="tpu_custom_call" | custom-call | bytes 29360128 | tf_op jit(solution)/shard_map/fetch/pallas_call | solution.py:86
  36.0 0.0 collective-permute-done.4.refs_3_
  36.0 0.0 collective-permute-done.5.refs_4_
  36.0 1.7 %output.1.refs_1_.one = bf16[32,2048]{1,0:T(8,128)(2,1)S(1)} custom-call(f32[8,128]{1,0:T(8,128)S(1)} %get-tuple-element.27._, bf16[2048,2048]{1,0:T(8,128)(2,1)S(1)} %get-tuple-element.28.refs_0_, bf16[32,2432]{1,0:T(8,128)(2,1)S(1)} %attend.1.refs_1_, bf16[32,2432]{1,0:T(8,128)(2,1)S(1)} %collective-permute-done.3.refs_2_, ...), custom_call_target="tpu_custom_call" | custom-call | flops 268435456 | bytes 8388608 | tf_op jit(solution)/shard_map/output/pallas_call | solution.py:311
  37.7 1.8 %collective-permute-start.6 = (bf16[32,2048]{1,0:T(8,128)(2,1)S(1)}, bf16[32,2048]{1,0:T(8,128)(2,1)S(1)}, u32[]{:S(2)}, u32[]{:S(2)}) collective-permute-start(bf16[32,2048]{1,0:T(8,128)(2,1)S(1)} %output.1.refs_1_.one), channel_id=1, source_target_pairs={{0,1},{1,0},{2,3},{3,2},{4,5},{5,4},{6,7},{7,6},{8,9},{9,8},{10,11... | collective-permute-start | bytes 393224 | tf_op jit(solution)/shard_map/ppermute | solution.py:503
  39.5 3.8 %fetch.7 = (bf16[1792,2048]{1,0:T(8,128)(2,1)S(1)}, f32[8,128]{1,0:T(8,128)S(1)}) custom-call(s32[20]{0:T(128)S(1)} %concatenate.9.refs_0_.at, bf16[32,2048]{1,0:T(8,128)(2,1)S(1)} %output.1.refs_1_.one, bf16[3584,2048]{1,0:T(8,128)(2,1)} %refs_2_.7), custom_call_target="tpu_custom_call" | custom-call | bytes 14680064 | tf_op jit(solution)/shard_map/fetch/pallas_call | solution.py:86
  43.3 0.0 copy-start
  43.3 0.4 collective-permute-done.6.two
  43.7 2.8 %collective-permute-start.7 = (bf16[32,2048]{1,0:T(8,128)(2,1)S(1)}, bf16[32,2048]{1,0:T(8,128)(2,1)S(1)}, u32[]{:S(2)}, u32[]{:S(2)}) collective-permute-start(bf16[32,2048]{1,0:T(8,128)(2,1)S(1)} %add.34.refs_1_.refs_5_), channel_id=1, source_target_pairs={{0,2},{1,3},{2,0},{3,1},{4,6},{5,7},{6,4},{7,5},{8,10},{9,11},{10,... | collective-permute-start | bytes 393224 | tf_op jit(solution)/shard_map/ppermute | solution.py:503
  46.6 6.5 %fetch.8 = (bf16[2048,3584]{1,0:T(8,128)(2,1)S(1)}, f32[8,128]{1,0:T(8,128)}) custom-call(s32[20]{0:T(128)S(1)} %concatenate.9.refs_0_.at, bf16[32,2048]{1,0:T(8,128)(2,1)S(1)} %add.34.refs_1_.refs_5_, bf16[2048,3584]{1,0:T(8,128)(2,1)} %refs_2_.6), custom_call_target="tpu_custom_call" | custom-call | bytes 29360128 | tf_op jit(solution)/shard_map/fetch/pallas_call | solution.py:86
  53.1 0.0 collective-permute-done.7.refs_6_
  53.1 0.0 copy-done
  53.1 3.2 %expand_send.1 = (bf16[32,3968]{1,0:T(8,128)(2,1)S(1)}, f32[32,2048]{1,0:T(8,128)S(1)}, bf16[32,2048]{1,0:T(8,128)(2,1)S(1)}) custom-call(s32[20]{0:T(128)S(1)} %concatenate.9.refs_0_.at, bf16[32,2048]{1,0:T(8,128)(2,1)S(1)} %get-tuple-element.23.refs_1_, bf16[16,128]{1,0:T(8,128)(2,1)S(1)} %bitcast.9, bf16[2048,3584]{1,0:T(8,128)(2,1)S(1)} %get-tuple-element.26.refs_3_.wg, ...), custom_call_target="tpu_custom_call" | custom-call | flops 469762048 | bytes 14680064 | tf_op jit(solution)/shard_map/expand_send/pallas_call | solution.py:353
  56.3 0.0 collective-permute-start.8
  56.3 3.1 %expand_keep.1.keep = bf16[32,3584]{1,0:T(8,128)(2,1)S(1)} custom-call(s32[20]{0:T(128)S(1)} %concatenate.9.refs_0_.at, bf16[32,2048]{1,0:T(8,128)(2,1)S(1)} %get-tuple-element.31.x, bf16[2048,3584]{1,0:T(8,128)(2,1)S(1)} %get-tuple-element.26.refs_3_.wg, bf16[2048,3584]{1,0:T(8,128)(2,1)S(1)} %get-tuple-element.30.refs_4_.wu), custom_call_target="tpu_custom_call" | custom-call | flops 469762048 | bytes 14680064 | tf_op jit(solution)/shard_map/expand_keep/pallas_call | solution.py:375
  59.4 0.0 collective-permute-done.8.received
  59.5 0.1 pair.1.refs_1_.refs_0_
  59.5 1.6 %collective-permute-start.9 = (bf16[32,3968]{1,0:T(8,128)(2,1)S(1)}, bf16[32,3968]{1,0:T(8,128)(2,1)S(1)}, u32[]{:S(2)}, u32[]{:S(2)}) collective-permute-start(bf16[32,3968]{1,0:T(8,128)(2,1)S(1)} %pair.1.refs_1_.refs_0_), channel_id=1, source_target_pairs={{0,8},{4,12},{8,0},{12,4},{1,9},{5,13},{9,1},{13,5},{2,10},{6,14},... | collective-permute-start | bytes 761864 | tf_op jit(solution)/shard_map/ppermute | solution.py:503
  61.1 3.8 %fetch.9 = (bf16[1792,2048]{1,0:T(8,128)(2,1)S(1)}, f32[8,128]{1,0:T(8,128)S(1)}) custom-call(s32[20]{0:T(128)S(1)} %concatenate.9.refs_0_.at, bf16[32,3968]{1,0:T(8,128)(2,1)S(1)} %pair.1.refs_1_.refs_0_, bf16[3584,2048]{1,0:T(8,128)(2,1)} %refs_2_.7), custom_call_target="tpu_custom_call" | custom-call | bytes 14680064 | tf_op jit(solution)/shard_map/fetch/pallas_call | solution.py:86
  64.9 3.2 %collective-permute-done.9.refs_1_ = bf16[32,3968]{1,0:T(8,128)(2,1)S(1)} collective-permute-done((bf16[32,3968]{1,0:T(8,128)(2,1)S(1)}, bf16[32,3968]{1,0:T(8,128)(2,1)S(1)}, u32[]{:S(2)}, u32[]{:S(2)}) %collective-permute-start.9) | collective-permute-done | bytes 253984 | tf_op jit(solution)/shard_map/ppermute | solution.py:503
  68.1 0.1 gated.1.hidden
  68.3 0.1 collective-permute-start.10
  68.4 1.3 %contract.1.refs_3_ = f32[32,2048]{1,0:T(8,128)S(1)} custom-call(bf16[32,1792]{1,0:T(8,128)(2,1)S(1)} %gated.1.hidden, bf16[1792,2048]{1,0:T(8,128)(2,1)S(1)} %get-tuple-element.35.w), custom_call_target="tpu_custom_call" | custom-call | flops 234881024 | bytes 7340032 | tf_op jit(solution)/shard_map/contract/pallas_call | solution.py:437
  69.7 0.0 collective-permute-done.10.refs_1_
  69.7 1.9 %contract_last.1 = (f32[8,2048]{1,0:T(8,128)S(1)}, bf16[8,2048]{1,0:T(8,128)(2,1)S(1)}, bf16[8,2048]{1,0:T(8,128)(2,1)S(1)}, bf16[8,2048]{1,0:T(8,128)(2,1)S(1)}) custom-call(s32[20]{0:T(128)S(1)} %concatenate.9.refs_0_.at, bf16[32,1792]{1,0:T(8,128)(2,1)S(1)} %collective-permute-done.10.refs_1_, bf16[1792,2048]{1,0:T(8,128)(2,1)S(1)} %get-tuple-element.34.refs_2_, ...), custom_call_target="tpu_custom_call" | custom-call | flops 234881024 | bytes 7340032 | tf_op jit(solution)/shard_map/contract_last/pallas_call | solution.py:471
  71.6 1.6 %collective-permute-start.11 = (bf16[8,2048]{1,0:T(8,128)(2,1)S(1)}, bf16[8,2048]{1,0:T(8,128)(2,1)S(1)}, u32[]{:S(2)}, u32[]{:S(2)}) collective-permute-start(bf16[8,2048]{1,0:T(8,128)(2,1)S(1)} %get-tuple-element.38), channel_id=1, source_target_pairs={{0,1},{1,0},{2,3},{3,2},{4,5},{5,4},{6,7},{7,6},{8,9},{9,8},{10,11... | collective-permute-start | bytes 98312 | tf_op jit(solution)/shard_map/ppermute | solution.py:503
  73.3 2.2 %collective-permute-start.12 = (bf16[8,2048]{1,0:T(8,128)(2,1)S(1)}, bf16[8,2048]{1,0:T(8,128)(2,1)S(1)}, u32[]{:S(2)}, u32[]{:S(2)}) collective-permute-start(bf16[8,2048]{1,0:T(8,128)(2,1)S(1)} %get-tuple-element.39), channel_id=1, source_target_pairs={{0,2},{1,3},{2,0},{3,1},{4,6},{5,7},{6,4},{7,5},{8,10},{9,11},{10,... | collective-permute-start | bytes 98312 | tf_op jit(solution)/shard_map/ppermute | solution.py:503
  75.5 0.6 collective-permute-start.13
  76.1 0.0 collective-permute-done.11
  76.1 2.6 %collective-permute-done.12 = bf16[8,2048]{1,0:T(8,128)(2,1)S(1)} collective-permute-done((bf16[8,2048]{1,0:T(8,128)(2,1)S(1)}, bf16[8,2048]{1,0:T(8,128)(2,1)S(1)}, u32[]{:S(2)}, u32[]{:S(2)}) %collective-permute-start.12) | collective-permute-done | bytes 32800 | tf_op jit(solution)/shard_map/ppermute | solution.py:503
  78.7 2.5 %collective-permute-done.13 = bf16[8,2048]{1,0:T(8,128)(2,1)S(1)} collective-permute-done((bf16[8,2048]{1,0:T(8,128)(2,1)S(1)}, bf16[8,2048]{1,0:T(8,128)(2,1)S(1)}, u32[]{:S(2)}, u32[]{:S(2)}) %collective-permute-start.13) | collective-permute-done | bytes 32800 | tf_op jit(solution)/shard_map/ppermute | solution.py:503
  81.2 0.6 add_convert_fusion
  (2 shorter events, 0.0 us)
Async XLA Ops:
  0.0 9.0 %copy-start.1 = (s32[8]{0:T(128)S(1)}, s32[8]{0:T(128)}, u32[]{:S(2)}) copy-start(s32[8]{0:T(128)} %param.24) | copy-start | bytes 100
  5.9 14.2 %collective-permute-start.1 = (bf16[32,2560]{1,0:T(8,128)(2,1)S(1)}, bf16[32,2560]{1,0:T(8,128)(2,1)S(1)}, u32[]{:S(2)}, u32[]{:S(2)}) collective-permute-start(bf16[32,2560]{1,0:T(8,128)(2,1)S(1)} %get-tuple-element.24.refs_1_.refs_4_), channel_id=1, source_target_pairs={{0,4},{4,0},{8,12},{12,8},{1,5},{5,1},{9,13},{13,9},{2,6},{6,2},{1... | collective-permute-start | bytes 491528 | tf_op jit(solution)/shard_map/ppermute | solution.py:503
  6.4 7.4 %collective-permute-start = (bf16[32,2560]{1,0:T(8,128)(2,1)S(1)}, bf16[32,2560]{1,0:T(8,128)(2,1)S(1)}, u32[]{:S(2)}, u32[]{:S(2)}) collective-permute-start(bf16[32,2560]{1,0:T(8,128)(2,1)S(1)} %get-tuple-element.24.refs_1_.refs_4_), channel_id=1, source_target_pairs={{0,8},{4,12},{8,0},{12,4},{1,9},{5,13},{9,1},{13,5},{2,10},{6,14},... | collective-permute-start | bytes 491528 | tf_op jit(solution)/shard_map/ppermute | solution.py:503
  13.8 6.3 %collective-permute-start.2 = (bf16[32,2560]{1,0:T(8,128)(2,1)S(1)}, bf16[32,2560]{1,0:T(8,128)(2,1)S(1)}, u32[]{:S(2)}, u32[]{:S(2)}) collective-permute-start(bf16[32,2560]{1,0:T(8,128)(2,1)S(1)} %collective-permute-done.refs_5_), channel_id=1, source_target_pairs={{0,4},{4,0},{8,12},{12,8},{1,5},{5,1},{9,13},{13,9},{2,6},{6,2},{1... | collective-permute-start | bytes 491528 | tf_op jit(solution)/shard_map/ppermute | solution.py:503
  23.5 6.5 %collective-permute-start.3 = (bf16[32,2432]{1,0:T(8,128)(2,1)S(1)}, bf16[32,2432]{1,0:T(8,128)(2,1)S(1)}, u32[]{:S(2)}, u32[]{:S(2)}) collective-permute-start(bf16[32,2432]{1,0:T(8,128)(2,1)S(1)} %attend.1.refs_1_), channel_id=1, source_target_pairs={{0,8},{4,12},{8,0},{12,4},{1,9},{5,13},{9,1},{13,5},{2,10},{6,14},... | collective-permute-start | bytes 466952 | tf_op jit(solution)/shard_map/ppermute | solution.py:503
  25.4 10.6 %collective-permute-start.4 = (bf16[32,2432]{1,0:T(8,128)(2,1)S(1)}, bf16[32,2432]{1,0:T(8,128)(2,1)S(1)}, u32[]{:S(2)}, u32[]{:S(2)}) collective-permute-start(bf16[32,2432]{1,0:T(8,128)(2,1)S(1)} %attend.1.refs_1_), channel_id=1, source_target_pairs={{0,4},{4,0},{8,12},{12,8},{1,5},{5,1},{9,13},{13,9},{2,6},{6,2},{1... | collective-permute-start | bytes 466952 | tf_op jit(solution)/shard_map/ppermute | solution.py:503
  30.1 5.9 %collective-permute-start.5 = (bf16[32,2432]{1,0:T(8,128)(2,1)S(1)}, bf16[32,2432]{1,0:T(8,128)(2,1)S(1)}, u32[]{:S(2)}, u32[]{:S(2)}) collective-permute-start(bf16[32,2432]{1,0:T(8,128)(2,1)S(1)} %collective-permute-done.3.refs_2_), channel_id=1, source_target_pairs={{0,4},{4,0},{8,12},{12,8},{1,5},{5,1},{9,13},{13,9},{2,6},{6,2},{1... | collective-permute-start | bytes 466952 | tf_op jit(solution)/shard_map/ppermute | solution.py:503
  37.7 6.0 %collective-permute-start.6 = (bf16[32,2048]{1,0:T(8,128)(2,1)S(1)}, bf16[32,2048]{1,0:T(8,128)(2,1)S(1)}, u32[]{:S(2)}, u32[]{:S(2)}) collective-permute-start(bf16[32,2048]{1,0:T(8,128)(2,1)S(1)} %output.1.refs_1_.one), channel_id=1, source_target_pairs={{0,1},{1,0},{2,3},{3,2},{4,5},{5,4},{6,7},{7,6},{8,9},{9,8},{10,11... | collective-permute-start | bytes 393224 | tf_op jit(solution)/shard_map/ppermute | solution.py:503
  43.3 9.8 %copy-start = (bf16[2048]{0:T(1024)(128)(2,1)S(1)}, bf16[2048]{0:T(1024)(128)(2,1)}, u32[]{:S(2)}) copy-start(bf16[2048]{0:T(1024)(128)(2,1)} %param.15) | copy-start | bytes 12292
  43.7 9.3 %collective-permute-start.7 = (bf16[32,2048]{1,0:T(8,128)(2,1)S(1)}, bf16[32,2048]{1,0:T(8,128)(2,1)S(1)}, u32[]{:S(2)}, u32[]{:S(2)}) collective-permute-start(bf16[32,2048]{1,0:T(8,128)(2,1)S(1)} %add.34.refs_1_.refs_5_), channel_id=1, source_target_pairs={{0,2},{1,3},{2,0},{3,1},{4,6},{5,7},{6,4},{7,5},{8,10},{9,11},{10,... | collective-permute-start | bytes 393224 | tf_op jit(solution)/shard_map/ppermute | solution.py:503
  56.3 3.2 %collective-permute-start.8 = (bf16[32,3968]{1,0:T(8,128)(2,1)S(1)}, bf16[32,3968]{1,0:T(8,128)(2,1)S(1)}, u32[]{:S(2)}, u32[]{:S(2)}) collective-permute-start(bf16[32,3968]{1,0:T(8,128)(2,1)S(1)} %get-tuple-element.32.stats), channel_id=1, source_target_pairs={{0,4},{4,0},{8,12},{12,8},{1,5},{5,1},{9,13},{13,9},{2,6},{6,2},{1... | collective-permute-start | bytes 761864 | tf_op jit(solution)/shard_map/ppermute | solution.py:503
  59.5 8.6 %collective-permute-start.9 = (bf16[32,3968]{1,0:T(8,128)(2,1)S(1)}, bf16[32,3968]{1,0:T(8,128)(2,1)S(1)}, u32[]{:S(2)}, u32[]{:S(2)}) collective-permute-start(bf16[32,3968]{1,0:T(8,128)(2,1)S(1)} %pair.1.refs_1_.refs_0_), channel_id=1, source_target_pairs={{0,8},{4,12},{8,0},{12,4},{1,9},{5,13},{9,1},{13,5},{2,10},{6,14},... | collective-permute-start | bytes 761864 | tf_op jit(solution)/shard_map/ppermute | solution.py:503
  68.3 1.4 %collective-permute-start.10 = (bf16[32,1792]{1,0:T(8,128)(2,1)S(1)}, bf16[32,1792]{1,0:T(8,128)(2,1)S(1)}, u32[]{:S(2)}, u32[]{:S(2)}) collective-permute-start(bf16[32,1792]{1,0:T(8,128)(2,1)S(1)} %gated.1.hidden), channel_id=1, source_target_pairs={{0,4},{4,0},{8,12},{12,8},{1,5},{5,1},{9,13},{13,9},{2,6},{6,2},{1... | collective-permute-start | bytes 344072 | tf_op jit(solution)/shard_map/ppermute | solution.py:503
  71.6 4.5 %collective-permute-start.11 = (bf16[8,2048]{1,0:T(8,128)(2,1)S(1)}, bf16[8,2048]{1,0:T(8,128)(2,1)S(1)}, u32[]{:S(2)}, u32[]{:S(2)}) collective-permute-start(bf16[8,2048]{1,0:T(8,128)(2,1)S(1)} %get-tuple-element.38), channel_id=1, source_target_pairs={{0,1},{1,0},{2,3},{3,2},{4,5},{5,4},{6,7},{7,6},{8,9},{9,8},{10,11... | collective-permute-start | bytes 98312 | tf_op jit(solution)/shard_map/ppermute | solution.py:503
  73.3 5.4 %collective-permute-start.12 = (bf16[8,2048]{1,0:T(8,128)(2,1)S(1)}, bf16[8,2048]{1,0:T(8,128)(2,1)S(1)}, u32[]{:S(2)}, u32[]{:S(2)}) collective-permute-start(bf16[8,2048]{1,0:T(8,128)(2,1)S(1)} %get-tuple-element.39), channel_id=1, source_target_pairs={{0,2},{1,3},{2,0},{3,1},{4,6},{5,7},{6,4},{7,5},{8,10},{9,11},{10,... | collective-permute-start | bytes 98312 | tf_op jit(solution)/shard_map/ppermute | solution.py:503
  75.5 5.7 %collective-permute-start.13 = (bf16[8,2048]{1,0:T(8,128)(2,1)S(1)}, bf16[8,2048]{1,0:T(8,128)(2,1)S(1)}, u32[]{:S(2)}, u32[]{:S(2)}) collective-permute-start(bf16[8,2048]{1,0:T(8,128)(2,1)S(1)} %get-tuple-element.40), channel_id=1, source_target_pairs={{0,3},{1,2},{2,1},{3,0},{4,7},{5,6},{6,5},{7,4},{8,11},{9,10},{10,... | collective-permute-start | bytes 98312 | tf_op jit(solution)/shard_map/ppermute | solution.py:503

commit v3 on v2

--- a/solution.py
+++ b/solution.py
@@ -1,3 +1,5 @@
+import math
+
 import jax
 import jax.numpy as jnp
 from jax import lax
@@ -51,23 +53,34 @@
     return slice(at * LANES, (at + 1) * LANES)
 
 
-def fetch_kernel(pieces, sides, at, _, *refs):
-    n = len(sides)
-    sources, held, token, sems = refs[:n], refs[n : 2 * n], refs[-2], refs[-1]
-    copies = []
-    for source, to, side in zip(sources, held, sides):
-        step = max(1, to.shape[0] // pieces)
-        base = 0
-        if side is not None:
-            base = pl.multiple_of((at[2] if side == 0 else 1 - at[2]) * to.shape[0], LANES)
-        for p in range(to.shape[0] // step):
-            copies.append(
-                pltpu.make_async_copy(
-                    source.at[pl.ds(base + p * step, step)],
-                    to.at[pl.ds(p * step, step)],
-                    sems.at[len(copies)],
-                )
+PIECES = 8
+
+
+class Part:
+    def __init__(self, array, first=0, count=None, side=None):
+        rows = array.shape[0]
+        self.array, self.first, self.side = array, first, side
+        self.count = rows // 2 if side is not None else rows if count is None else count
+        self.shape = (self.count,) + array.shape[1:]
+        self.out = pltpu.VMEM(self.shape, array.dtype)
+
+    def copies(self, at, source, held, sems):
+        step = max(1, self.count // PIECES)
+        base = self.first
+        if self.side is not None:
+            base = pl.multiple_of((at[2] if self.side == 0 else 1 - at[2]) * self.count, LANES)
+        return [
+            pltpu.make_async_copy(
+                source.at[pl.ds(base + p * step, step)], held.at[pl.ds(p * step, step)], sems.at[p]
             )
+            for p in range(self.count // step)
+        ]
+
+
+def fetch_kernel(wanted, skip, at, *refs):
+    n, refs = len(wanted), refs[skip:]
+    sources, held, token, sems = refs[:n], refs[n : 2 * n], refs[2 * n], refs[2 * n + 1 :]
+    copies = sum([w.copies(at, *refs) for w, *refs in zip(wanted, sources, held, sems)], [])
     for copy in copies:
         copy.start()
     token[...] = jnp.zeros_like(token)
@@ -76,24 +89,30 @@
 
 
 def fetch(at, after, *wanted):
-    pieces = 8
-    sides = [w[1] if isinstance(w, tuple) else None for w in wanted]
-    wanted = [w[0] if isinstance(w, tuple) else w for w in wanted]
-    shapes = [
-        w.shape if side is None else (w.shape[0] // 2,) + w.shape[1:] for w, side in zip(wanted, sides)
-    ]
-    size = sum(w.size // (1 if side is None else 2) for w, side in zip(wanted, sides))
-    return pl.pallas_call(
-        lambda *refs: fetch_kernel(pieces, sides, *refs),
-        in_specs=[SMEM, ANY] + [HBM] * len(wanted),
+    after = after if isinstance(after, (list, tuple)) else [after]
+    size = sum(math.prod(w.shape) for w in wanted)
+    return pl.pallas_call(
+        lambda *refs: fetch_kernel(wanted, len(after), *refs),
+        in_specs=[SMEM] + [ANY] * len(after) + [HBM] * len(wanted),
         out_specs=[VMEM] * (len(wanted) + 1),
-        out_shape=[pltpu.VMEM(shape, w.dtype) for shape, w in zip(shapes, wanted)]
-        + [pltpu.VMEM((8, LANES), f32)],
-        scratch_shapes=[pltpu.SemaphoreType.DMA((2 * pieces * len(wanted),))],
+        out_shape=[w.out for w in wanted] + [pltpu.VMEM((8, LANES), f32)],
+        scratch_shapes=[pltpu.SemaphoreType.DMA((2 * PIECES,))] * len(wanted),
         compiler_params=params(2),
         cost_estimate=pl.CostEstimate(flops=0, bytes_accessed=4 * size, transcendentals=0),
         name="fetch",
-    )(at, after, *[in_hbm(w) for w in wanted])
+    )(at, *after, *[in_hbm(w.array) for w in wanted])
+
+
+def hold(x, token):
+    return pl.pallas_call(
+        lambda *_: None,
+        in_specs=[VMEM, ANY],
+        out_specs=VMEM,
+        out_shape=jax.ShapeDtypeStruct(x.shape, x.dtype),
+        input_output_aliases={0: 0},
+        compiler_params=params(1),
+        name="hold",
+    )(x, token)
 
 
 def project_kernel(chunks, at, tokens, gain, wq, wk, wv, out, own, tok, gain_f, norm, bq, bk, bv, acc, gain_b, sems):
@@ -181,8 +200,11 @@
     )(at, in_hbm(tokens), in_hbm(gain.reshape(model // LANES, LANES)), in_hbm(wq), in_hbm(wk), in_hbm(wv))
 
 
-def attend_kernel(n, at, cos, sin, cache, *rest):
-    parts, (out, queries, total, stats_f) = rest[:n], rest[n:]
+def attend_kernel(n, part, at, cos, sin, cache, source, *rest):
+    parts, (out, held, queries, total, stats_f, sems) = rest[:n], rest[n:]
+    copies = part.copies(at, source, held, sems)
+    for copy in copies:
+        copy.start()
     rows, q_cols = queries.shape
     context, kv_cols = cache.shape[2:]
     kv_heads = kv_cols // HEAD_WIDTH
@@ -262,32 +284,42 @@
     out[:, :q_cols] = total[...].astype(bf16)
     for p, term in enumerate(thirds(stats_f[...])):
         out[:, q_cols + p * LANES : q_cols + (p + 1) * LANES] = term
-
-
-def attend(at, cos, sin, cache, parts):
+    for copy in copies:
+        copy.wait()
+
+
+def attend(at, cos, sin, cache, parts, part):
     rows, width = parts[0].shape
     q_cols = width - 2 * cache.shape[3]
     return pl.pallas_call(
-        lambda *refs: attend_kernel(len(parts), *refs),
-        in_specs=[SMEM] + [VMEM] * (3 + len(parts)),
-        out_specs=VMEM,
-        out_shape=jax.ShapeDtypeStruct((rows, q_cols + 3 * LANES), bf16),
+        lambda *refs: attend_kernel(len(parts), part, *refs),
+        in_specs=[SMEM] + [VMEM] * 3 + [HBM] + [VMEM] * len(parts),
+        out_specs=[VMEM, VMEM],
+        out_shape=[jax.ShapeDtypeStruct((rows, q_cols + 3 * LANES), bf16), part.out],
         scratch_shapes=[
             pltpu.VMEM((rows, q_cols), f32),
             pltpu.VMEM((rows, q_cols), f32),
             pltpu.VMEM((rows, LANES), f32),
+            pltpu.SemaphoreType.DMA((2 * PIECES,)),
         ],
         compiler_params=params(6),
         cost_estimate=cost(rows, cache),
         name="attend",
-    )(at, cos, sin, cache, *parts)
+    )(at, cos, sin, cache, in_hbm(part.array), *parts)
 
 
 def joined(ref, start):
     return sum(ref[:, start + p * LANES : start + (p + 1) * LANES].astype(f32) for p in range(3))
 
 
-def output_kernel(n, w, *rest):
+def product(x, w, out, base, width):
+    for start, size in blocks_of(width, 512):
+        out[:, start : start + size] = jnp.dot(
+            x[...], w[:, base + start : base + start + size], preferred_element_type=f32
+        ).astype(out.dtype)
+
+
+def output_first_kernel(n, w, *rest):
     values, (out, attended) = rest[:n], rest[n:]
     heads = attended.shape[1] // HEAD_WIDTH
     stats = [joined(v, attended.shape[1]) for v in values]
@@ -301,86 +333,140 @@
         attended[:, lanes(h)] = sum(
             v[:, lanes(h)].astype(f32) * s[:, h : h + 1] for v, s in zip(values, shares)
         ).astype(bf16)
-    for start, size in blocks_of(w.shape[1], 512):
-        cols = slice(start, start + size)
-        out[:, cols] = jnp.dot(attended[...], w[:, cols], preferred_element_type=f32).astype(out.dtype)
-
-
-def output(values, w, after):
-    rows = values[0].shape[0]
-    return pl.pallas_call(
-        lambda _, *refs: output_kernel(len(values), *refs),
-        in_specs=[ANY] + [VMEM] * (1 + len(values)),
+    product(attended, w, out, 0, out.shape[1])
+
+
+def output_first(values, w):
+    rows, half = values[0].shape[0], w.shape[1] // 2
+    return pl.pallas_call(
+        lambda *refs: output_first_kernel(len(values), *refs),
+        in_specs=[VMEM] * (1 + len(values)),
+        out_specs=[VMEM, VMEM],
+        out_shape=[
+            jax.ShapeDtypeStruct((rows, half), bf16),
+            jax.ShapeDtypeStruct((rows, w.shape[0]), bf16),
+        ],
+        compiler_params=params(4),
+        cost_estimate=cost(rows, w),
+        name="output_first",
+    )(w, *values)
+
+
+def output_second(attended, w):
+    rows, half = attended.shape[0], w.shape[1] // 2
+    return pl.pallas_call(
+        lambda x, w, out: product(x, w, out, half, half),
+        in_specs=[VMEM] * 2,
         out_specs=VMEM,
-        out_shape=jax.ShapeDtypeStruct((rows, w.shape[1]), bf16),
-        scratch_shapes=[pltpu.VMEM((rows, w.shape[0]), bf16)],
+        out_shape=jax.ShapeDtypeStruct((rows, half), bf16),
         compiler_params=params(4),
         cost_estimate=cost(rows, w),
-        name="output",
-    )(after, w, *values)
-
-
-def half_of(side, x, wg, wu, out):
+        name="output_second",
+    )(attended, w)
+
+
+def half_of(side, x, wg, wu, out, before=None):
     half = wg.shape[1] // 2
     for base, w in ((0, wg), (half, wu)):
         for start, size in blocks_of(half, 512):
             cols = pl.ds(pl.multiple_of(side * half + start, LANES), size)
-            out[:, base + start : base + start + size] = jnp.dot(
-                x[...], w[:, cols], preferred_element_type=f32
-            ).astype(out.dtype)
-
-
-def expand_send_kernel(n, at, own, gain, wg, wu, *rest):
-    parts, (out, resid, x, gain_f) = rest[:n], rest[n:]
-    rows = own.shape[0]
+            to = slice(base + start, base + start + size)
+            term = jnp.dot(x[...], w[:, cols], preferred_element_type=f32)
+            if before is not None:
+                term = before[:, to] + term
+            out[:, to] = term.astype(out.dtype)
+
+
+def residual(which, own, gain, parts, resid, x, gain_f):
     gain_f[...] = gain[...].astype(f32)
-    square = jnp.zeros((rows, LANES), f32)
-    for c in range(own.shape[1] // LANES):
-        value = own[:, lanes(c)].astype(f32) + sum(p[:, lanes(c)].astype(f32) for p in parts)
-        value = value.astype(bf16)
-        value = value.astype(f32)
+    count = resid.shape[1] // LANES
+    square = jnp.zeros((own.shape[0], LANES), f32)
+    for c in range(count):
+        at = which * count + c
+        value = own[:, lanes(at)].astype(f32) + sum(p[:, lanes(c)].astype(f32) for p in parts)
+        value = value.astype(bf16).astype(f32)
         resid[:, lanes(c)] = value
         square = square + value * value
-        x[:, lanes(c)] = (value * gain_f[c : c + 1, :]).astype(bf16)
+        x[:, lanes(c)] = (value * gain_f[at : at + 1, :]).astype(bf16)
+    return square
+
+
+def expand_first_kernel(n, part, at, own, gain, wg, wu, _, source, *rest):
+    parts, (send, keep, resid, squares, held, x, gain_f, sems) = rest[:n], rest[n:]
+    copies = part.copies(at, source, held, sems)
+    for copy in copies:
+        copy.start()
+    squares[...] = residual(0, own, gain, parts, resid, x, gain_f)
+    half_of(1 - at[2], x, wg, wu, send)
+    half_of(at[2], x, wg, wu, keep)
+    for copy in copies:
+        copy.wait()
+
+
+def expand_first(at, own, gain, parts, wg, wu, part, after):
+    rows, depth = own.shape
+    width = wg.shape[1]
+    return pl.pallas_call(
+        lambda *refs: expand_first_kernel(len(parts), part, *refs),
+        in_specs=[SMEM] + [VMEM] * 4 + [ANY, HBM] + [VMEM] * len(parts),
+        out_specs=[VMEM] * 5,
+        out_shape=[
+            jax.ShapeDtypeStruct((rows, width), f32),
+            jax.ShapeDtypeStruct((rows, width), f32),
+            jax.ShapeDtypeStruct((rows, depth // 2), f32),
+            jax.ShapeDtypeStruct((rows, LANES), f32),
+            part.out,
+        ],
+        scratch_shapes=[
+            pltpu.VMEM((rows, depth // 2), bf16),
+            pltpu.VMEM((depth // LANES, LANES), f32),
+            pltpu.SemaphoreType.DMA((2 * PIECES,)),
+        ],
+        compiler_params=params(4),
+        cost_estimate=cost(rows, wg, wu),
+        name="expand_first",
+    )(at, own, gain, wg, wu, after, in_hbm(part.array), *parts)
+
+
+def expand_send_kernel(n, at, own, gain, wg, wu, before, squares, *rest):
+    parts, (out, resid, x, gain_f) = rest[:n], rest[n:]
+    square = squares[...] + residual(1, own, gain, parts, resid, x, gain_f)
     square = jnp.broadcast_to(jnp.sum(square, axis=1, keepdims=True), square.shape)
+    width = wg.shape[1]
     for p, term in enumerate(thirds(square)):
-        out[:, wg.shape[1] + p * LANES : wg.shape[1] + (p + 1) * LANES] = term
-    half_of(1 - at[2], x, wg, wu, out)
-
-
-def expand_send(at, own, gain, parts, wg, wu):
+        out[:, width + p * LANES : width + (p + 1) * LANES] = term
+    half_of(1 - at[2], x, wg, wu, out, before)
+
+
+def expand_send(at, own, gain, parts, wg, wu, before, squares):
     rows, depth = own.shape
     return pl.pallas_call(
         lambda *refs: expand_send_kernel(len(parts), *refs),
-        in_specs=[SMEM] + [VMEM] * (4 + len(parts)),
+        in_specs=[SMEM] + [VMEM] * (6 + len(parts)),
         out_specs=[VMEM] * 3,
         out_shape=[
             jax.ShapeDtypeStruct((rows, wg.shape[1] + 3 * LANES), bf16),
-            jax.ShapeDtypeStruct((rows, depth), f32),
-            jax.ShapeDtypeStruct((rows, depth), bf16),
+            jax.ShapeDtypeStruct((rows, depth // 2), f32),
+            jax.ShapeDtypeStruct((rows, depth // 2), bf16),
         ],
         scratch_shapes=[pltpu.VMEM((depth // LANES, LANES), f32)],
         compiler_params=params(4),
         cost_estimate=cost(rows, wg),
         name="expand_send",
-    )(at, own, gain.reshape(depth // LANES, LANES), wg, wu, *parts)
-
-
-def expand_keep_kernel(at, x, wg, wu, out):
-    half_of(at[2], x, wg, wu, out)
-
-
-def expand_keep(at, x, wg, wu):
+    )(at, own, gain, wg, wu, before, squares, *parts)
+
+
+def expand_keep(at, x, wg, wu, before):
     rows = x.shape[0]
     return pl.pallas_call(
-        expand_keep_kernel,
-        in_specs=[SMEM] + [VMEM] * 3,
+        lambda at, x, wg, wu, before, out: half_of(at[2], x, wg, wu, out, before),
+        in_specs=[SMEM] + [VMEM] * 4,
         out_specs=VMEM,
         out_shape=jax.ShapeDtypeStruct((rows, wg.shape[1]), bf16),
         compiler_params=params(4),
         cost_estimate=cost(rows, wg),
         name="expand_keep",
-    )(at, x, wg, wu)
+    )(at, x, wg, wu, before)
 
 
 def pair_kernel(keep, received, stats, out):
@@ -445,7 +531,7 @@
     )(hidden, w)
 
 
-def contract_last_kernel(n, at, hidden, w, before, resid, own, *rest):
+def contract_last_kernel(n, at, hidden, w, before, resid_0, resid_1, own, *rest):
     sends, acc = rest[:-1], rest[-1]
     share = own.shape[0]
     for start, size in blocks_of(w.shape[1], 512):
@@ -460,17 +546,20 @@
             chosen = jnp.where(index == b, ref[b * share : (b + 1) * share, :], chosen)
         return chosen
 
-    own[...] = block(acc, at[3]) + block(resid, at[3])
+    half = resid_0.shape[1]
+    mine = block(acc, at[3])
+    own[:, :half] = mine[:, :half] + block(resid_0, at[3])
+    own[:, half:] = mine[:, half:] + block(resid_1, at[3])
     for s in range(1, n):
         sends[s - 1][...] = block(acc, at[3] ^ s).astype(bf16)
 
 
-def contract_last(n, at, hidden, w, before, resid):
+def contract_last(n, at, hidden, w, before, *resid):
     rows, cols = before.shape
     share = rows // n
     return pl.pallas_call(
         lambda *refs: contract_last_kernel(n, *refs),
-        in_specs=[SMEM] + [VMEM] * 4,
+        in_specs=[SMEM] + [VMEM] * 5,
         out_specs=[VMEM] * n,
         out_shape=[jax.ShapeDtypeStruct((share, cols), f32)]
         + [jax.ShapeDtypeStruct((share, cols), bf16)] * (n - 1),
@@ -478,24 +567,24 @@
         compiler_params=params(4),
         cost_estimate=cost(rows, w),
         name="contract_last",
-    )(at, hidden, w, before, resid)
-
-
-def add_kernel(_, one, two, out):
+    )(at, hidden, w, before, *resid)
+
+
+def add_kernel(one, two, out):
     for start, size in blocks_of(out.shape[1], 512):
         cols = slice(start, start + size)
         out[:, cols] = (one[:, cols].astype(f32) + two[:, cols].astype(f32)).astype(bf16)
 
 
-def add(one, two, after):
+def add(one, two):
     return pl.pallas_call(
         add_kernel,
-        in_specs=[ANY] + [VMEM] * 2,
+        in_specs=[VMEM] * 2,
         out_specs=VMEM,
         out_shape=jax.ShapeDtypeStruct(one.shape, bf16),
         compiler_params=params(4),
         name="add",
-    )(after, one, two)
+    )(one, two)
 
 
 def swap(x, axis, bit):
@@ -508,11 +597,20 @@
     return [1 << b for b in range(n.bit_length() - 1)]
 
 
-def gathered(x, axis):
+def gathered(x, axis, token):
     parts = [x]
     for bit in reversed(bits_of(axis)):
         parts = parts + [swap(p, axis, bit) for p in parts]
+        if bit > 1:
+            parts = parts[:-1] + [hold(parts[-1], token)]
     return parts
+
+
+def summed(x, axis):
+    *bits, last = bits_of(axis)
+    for bit in bits:
+        x = add(x, swap(x, axis, bit))
+    return x, swap(x, axis, last)
 
 
 def per_device(tokens, attn_gain, ffn_gain, w_query, key_matrix, value_matrix, w_out, w_gate, w_up, w_down, kv_cache, lengths, slots):
@@ -520,7 +618,7 @@
     wide_at, head_at = lax.axis_index("wide"), lax.axis_index("head")
     wide_size, head_size = lax.axis_size("wide"), lax.axis_size("head")
     places = jnp.stack([wide_at, (wide_at == wide_size - 1).astype(jnp.int32), wide_at & 1, head_at])
-    at = jnp.concatenate([places.astype(jnp.int32), lengths, slots])
+    at = places.astype(jnp.int32)
 
     half = HEAD_WIDTH // 2
     positions = (
@@ -534,27 +632,36 @@
     sin = jnp.concatenate([-sin, sin], axis=1)
 
     qkv, own = project(at, tokens, attn_gain, w_query, key_matrix, value_matrix)
-    cache, w_out, _ = fetch(at, qkv, kv_cache.reshape((-1,) + kv_cache.shape[2:]), w_out)
+    depth = own.shape[1]
+    half = depth // 2
+    gain = ffn_gain.reshape(depth // LANES, LANES)
+
+    flat_cache = kv_cache.reshape((-1,) + kv_cache.shape[2:])
+    meta = jnp.concatenate([at, lengths, slots])
+    cache, gate_0, token = fetch(at, (qkv, meta, cos, sin), Part(flat_cache), Part(w_gate, 0, half))
     cache = cache.reshape(kv_cache.shape)
-    value = attend(at, cos, sin, cache, gathered(qkv, "wide"))
-    w_gate, have_gate = fetch(at, value, w_gate)
-    out_part = output(gathered(value, "wide"), w_out, have_gate)
-    w_down_own, have_own = fetch(at, out_part, (w_down, 0))
-    for bit in bits_of("head")[:-1]:
-        out_part = add(out_part, swap(out_part, "head", bit), have_own)
-    w_up, _ = fetch(at, out_part, w_up)
-    parts = [out_part, swap(out_part, "head", bits_of("head")[-1])]
-    send, resid, x = expand_send(at, own, ffn_gain, parts, w_gate, w_up)
+    value, w_out = attend(meta, cos, sin, cache, gathered(qkv, "wide", token), Part(w_out))
+
+    up_0, token = fetch(at, value, Part(w_up, 0, half))
+    out_0, attended = output_first(gathered(value, "wide", token), w_out)
+    out_1 = output_second(attended, w_out)
+    parts_0, parts_1 = summed(out_0, "head"), summed(out_1, "head")
+    gate_1, token = fetch(at, parts_1[0], Part(w_gate, half, half))
+    send, keep, resid_0, squares, up_1 = expand_first(
+        at, own, gain, parts_0, gate_0, up_0, Part(w_up, half, half), token
+    )
+    send, resid_1, x = expand_send(at, own, gain, parts_1, gate_1, up_1, send, squares)
     received = swap(send, "wide", 1)
-    keep = expand_keep(at, x, w_gate, w_up)
-    total = pair(keep, received, send)
-    w_down_other, have_other = fetch(at, total, (w_down, 1))
+    total = pair(expand_keep(at, x, gate_1, up_1, keep), received, send)
+    down_own, down_other, token = fetch(at, total, Part(w_down, side=0), Part(w_down, side=1))
     for bit in bits_of("wide")[1:-1]:
         there = swap(total, "wide", bit)
         total = pair(total, there, total)
-    hidden = gated(model, total, swap(total, "wide", bits_of("wide")[-1]), have_other)
+    hidden = gated(model, total, swap(total, "wide", bits_of("wide")[-1]), token)
     other = swap(hidden, "wide", 1)
-    total, *sends = contract_last(head_size, at, other, w_down_other, contract(hidden, w_down_own), resid)
+    total, *sends = contract_last(
+        head_size, at, other, down_other, contract(hidden, down_own), resid_0, resid_1
+    )
     for s, send in enumerate(sends, 1):
         total = total + swap(send, "head", s).astype(f32)
     return total.astype(bf16)

time: 82.1 us -> 74.6 us (0.909)
  waiting for transfers between devices: 17.8 us -> 10.5 us
  starting transfers between devices: 15.9 us -> 16.9 us
    ppermute x14 -> x16, waiting for transfers between devices: 17.8 us -> 10.5 us  [swap(): return lax.ppermute(x, axis, [(i, i ^ bit) for i in range(n)])]
    pallas_call x1, Pallas kernels: 3.17 us -> 1.91 us  [expand_send(): pl.pallas_call(lambda *refs: expand_send_kernel(len(parts), *refs), in_sp...]
    ppermute x14 -> x16, starting transfers between devices: 15.9 us -> 16.9 us  [swap(): return lax.ppermute(x, axis, [(i, i ^ bit) for i in range(n)])]
    pallas_call x9 -> x13, Pallas kernels: 34.3 us -> 35.1 us  [the longest x4 18.7 us: fetch(): pl.pallas_call(lambda *refs: fetch_kernel(wanted, len(after), *refs), in_...]
  transfers between devices with their start and end apart: 14 -> 16, of which waited for: 6 -> 7; matrix products, arithmetic and copies ran while one was open for 0% -> 1% of each run, Pallas kernels for 37% -> 39%
where the time goes in v3:
time: 74.6 us; the launch traced here: 74.5 us
  Pallas kernels  45.7 us (61%)
  starting transfers between devices  16.9 us (23%)
  waiting for transfers between devices  10.5 us (14%)
  other arithmetic  1.01 us (1%)
    pallas_call x4, Pallas kernels, fetch(): pl.pallas_call(lambda *refs: fetch_kernel(wanted, len(after), *refs), in_...  18.7 us
    ppermute x16, starting transfers between devices, swap(): return lax.ppermute(x, axis, [(i, i ^ bit) for i in range(n)])  16.9 us
    ppermute x16, waiting for transfers between devices, swap(): return lax.ppermute(x, axis, [(i, i ^ bit) for i in range(n)])  10.5 us
    pallas_call x1, Pallas kernels, attend(): pl.pallas_call(lambda *refs: attend_kernel(len(parts), part, *refs), in_s...  6.45 us
    pallas_call x1, Pallas kernels, expand_first(): pl.pallas_call(lambda *refs: expand_first_kernel(len(parts), part, *refs)...  6.26 us
    pallas_call x1, Pallas kernels, project(): pl.pallas_call(lambda *refs: project_kernel(chunks, *refs), in_specs=[SME...  5.11 us
    pallas_call x1, Pallas kernels, contract_last(): pl.pallas_call(lambda *refs: contract_last_kernel(n, *refs), in_specs=[SM...  1.93 us
    pallas_call x1, Pallas kernels, expand_keep(): pl.pallas_call(lambda at, x, wg, wu, before, out: half_of(at[2], x, wg, w...  1.91 us
  transfers between devices with their start and end apart: 16, of which 7 were waited for; matrix products, arithmetic and copies ran while one was open for 1% of the time, Pallas kernels for 39%

profile of v3, /device:TPU:0, one launch (start us, length us, event | category | flops | bytes accessed | tf_op | source)
XLA Modules:
  0.0 74.5 jit_solution(15320636783160087680)
XLA Ops:
  0.0 0.0 copy-start.1
  0.0 0.0 copy-start.2
  0.0 0.1 pad_add_fusion.refs_0_.at
  0.1 5.1 %project.1 = (bf16[32,2560]{1,0:T(8,128)(2,1)S(1)}, bf16[32,2048]{1,0:T(8,128)(2,1)S(1)}) custom-call(s32[4]{0:T(128)S(1)} %pad_add_fusion.refs_0_.at, bf16[32,8192]{1,0:T(8,128)(2,1)} %refs_1_.1, bf16[64,128]{1,0:T(8,128)(2,1)} %bitcast.12, bf16[2048,2048]{1,0:T(8,128)(2,1)} %refs_3_.2, bf16[2048,256]{1,0:T(8,128)(2,1)} %refs_4_.2, bf16[2048,256]{1,0:T(8,128)(2,1)} %refs_5_.1), custom_call_target="tpu_custom_call" | custom-call | flops 335544320 | bytes 10485760 | tf_op jit(solution)/shard_map/project/pallas_call | solution.py:178
  5.2 3.0 %collective-permute-start = (bf16[32,2560]{1,0:T(8,128)(2,1)S(1)}, bf16[32,2560]{1,0:T(8,128)(2,1)S(1)}, u32[]{:S(2)}, u32[]{:S(2)}) collective-permute-start(bf16[32,2560]{1,0:T(8,128)(2,1)S(1)} %get-tuple-element.34.refs_1_.refs_5_), channel_id=1, source_target_pairs={{0,8},{4,12},{8,0},{12,4},{1,9},{5,13},{9,1},{13,5},{2,10},{6,14},... | collective-permute-start | bytes 491528 | tf_op jit(solution)/shard_map/ppermute | solution.py:592
  8.2 0.0 collective-permute-start.1
  8.2 0.0 copy-done.1
  8.3 0.1 add_convert_fusion.1
  8.3 0.1 convert_element_type.24
  8.4 0.1 fusion
  8.6 0.0 copy-done.2
  8.6 0.1 concatenate.10.refs_2_.refs_0_
  8.7 0.1 pad_maximum_fusion
  8.7 5.1 %fetch.4 = (bf16[16,512,256]{2,1,0:T(8,128)(2,1)S(1)}, bf16[1024,3584]{1,0:T(8,128)(2,1)S(1)}, f32[8,128]{1,0:T(8,128)S(1)}) custom-call(s32[4]{0:T(128)S(1)} %pad_add_fusion.refs_0_.at, bf16[32,2560]{1,0:T(8,128)(2,1)S(1)} %get-tuple-element.34.refs_1_.refs_5_, s32[20]{0:T(128)S(1)} %concatenate.10.refs_2_.refs_0_, ...), custom_call_target="tpu_custom_call" | custom-call | bytes 23068672 | tf_op jit(solution)/shard_map/fetch/pallas_call | solution.py:94
  13.9 0.0 collective-permute-done.__0_
  13.9 0.6 collective-permute-start.2
  14.5 0.0 collective-permute-done.1.refs_7_
  14.5 1.0 %collective-permute-done.2.refs_8_ = bf16[32,2560]{1,0:T(8,128)(2,1)S(1)} collective-permute-done((bf16[32,2560]{1,0:T(8,128)(2,1)S(1)}, bf16[32,2560]{1,0:T(8,128)(2,1)S(1)}, u32[]{:S(2)}, u32[]{:S(2)}) %collective-permute-start.2) | collective-permute-done | bytes 163872 | tf_op jit(solution)/shard_map/ppermute | solution.py:592
  15.5 6.5 %attend.1 = (bf16[32,2432]{1,0:T(8,128)(2,1)S(1)}, bf16[2048,2048]{1,0:T(8,128)(2,1)S(1)}) custom-call(s32[20]{0:T(128)S(1)} %concatenate.10.refs_2_.refs_0_, f32[32,128]{1,0:T(8,128)S(1)} %get-tuple-element.64.refs_3_.refs_1_, f32[32,128]{1,0:T(8,128)S(1)} %get-tuple-element.65.refs_4_.refs_2_, bf16[2,8,512,256]{3,2,1,0:T(8,128)(2,1)S(1)} %bitcast.8, ...), custom_call_target="tpu_custom_call" | custom-call | flops 134217728 | bytes 4194304 | tf_op jit(solution)/shard_map/attend/pallas_call | solution.py:294
  21.9 0.2 collective-permute-start.3
  22.1 0.4 collective-permute-start.4
  22.5 3.8 %fetch.5 = (bf16[1024,3584]{1,0:T(8,128)(2,1)S(1)}, f32[8,128]{1,0:T(8,128)S(1)}) custom-call(s32[4]{0:T(128)S(1)} %pad_add_fusion.refs_0_.at, bf16[32,2432]{1,0:T(8,128)(2,1)S(1)} %get-tuple-element.38.refs_1_, bf16[2048,3584]{1,0:T(8,128)(2,1)} %refs_6_.3), custom_call_target="tpu_custom_call" | custom-call | bytes 14680064 | tf_op jit(solution)/shard_map/fetch/pallas_call | solution.py:94
  26.2 2.1 %collective-permute-done.3.__0_ = bf16[32,2432]{1,0:T(8,128)(2,1)S(1)} collective-permute-done((bf16[32,2432]{1,0:T(8,128)(2,1)S(1)}, bf16[32,2432]{1,0:T(8,128)(2,1)S(1)}, u32[]{:S(2)}, u32[]{:S(2)}) %collective-permute-start.3) | collective-permute-done | bytes 155680 | tf_op jit(solution)/shard_map/ppermute | solution.py:592
  28.3 0.0 collective-permute-start.5
  28.3 0.0 collective-permute-done.4.refs_3_
  28.3 1.4 %collective-permute-done.5.refs_4_ = bf16[32,2432]{1,0:T(8,128)(2,1)S(1)} collective-permute-done((bf16[32,2432]{1,0:T(8,128)(2,1)S(1)}, bf16[32,2432]{1,0:T(8,128)(2,1)S(1)}, u32[]{:S(2)}, u32[]{:S(2)}) %collective-permute-start.5) | collective-permute-done | bytes 155680 | tf_op jit(solution)/shard_map/ppermute | solution.py:592
  29.7 1.0 %output_first.1 = (bf16[32,1024]{1,0:T(8,128)(2,1)S(1)}, bf16[32,2048]{1,0:T(8,128)(2,1)S(1)}) custom-call(bf16[2048,2048]{1,0:T(8,128)(2,1)S(1)} %get-tuple-element.37.refs_0_.w, bf16[32,2432]{1,0:T(8,128)(2,1)S(1)} %get-tuple-element.38.refs_1_, bf16[32,2432]{1,0:T(8,128)(2,1)S(1)} %hold.3.refs_2_, bf16[32,2432]{1,0:T(8,128)(2,1)S(1)} %collective-permute-done.4.refs_3_, ...), custom_call_target="tpu_custom_call" | custom-call | flops 268435456 | bytes 8388608 | tf_op jit(solution)/shard_map/output_first/pallas_call | solution.py:341
  30.7 1.6 %collective-permute-start.7 = (bf16[32,1024]{1,0:T(8,128)(2,1)S(1)}, bf16[32,1024]{1,0:T(8,128)(2,1)S(1)}, u32[]{:S(2)}, u32[]{:S(2)}) collective-permute-start(bf16[32,1024]{1,0:T(8,128)(2,1)S(1)} %get-tuple-element.45.one), channel_id=1, source_target_pairs={{0,1},{1,0},{2,3},{3,2},{4,5},{5,4},{6,7},{7,6},{8,9},{9,8},{10,11... | collective-permute-start | bytes 196616 | tf_op jit(solution)/shard_map/ppermute | solution.py:592
  32.3 0.8 %output_second.1.one = bf16[32,1024]{1,0:T(8,128)(2,1)S(1)} custom-call(bf16[32,2048]{1,0:T(8,128)(2,1)S(1)} %get-tuple-element.40.x, bf16[2048,2048]{1,0:T(8,128)(2,1)S(1)} %get-tuple-element.37.refs_0_.w), custom_call_target="tpu_custom_call" | custom-call | flops 268435456 | bytes 8388608 | tf_op jit(solution)/shard_map/output_second/pallas_call | solution.py:357
  33.1 0.5 collective-permute-start.6
  33.5 1.4 %collective-permute-done.7.two = bf16[32,1024]{1,0:T(8,128)(2,1)S(1)} collective-permute-done((bf16[32,1024]{1,0:T(8,128)(2,1)S(1)}, bf16[32,1024]{1,0:T(8,128)(2,1)S(1)}, u32[]{:S(2)}, u32[]{:S(2)}) %collective-permute-start.7) | collective-permute-done | bytes 65568 | tf_op jit(solution)/shard_map/ppermute | solution.py:592
  35.0 2.7 %collective-permute-start.8 = (bf16[32,1024]{1,0:T(8,128)(2,1)S(1)}, bf16[32,1024]{1,0:T(8,128)(2,1)S(1)}, u32[]{:S(2)}, u32[]{:S(2)}) collective-permute-start(bf16[32,1024]{1,0:T(8,128)(2,1)S(1)} %add.42.refs_7_), channel_id=1, source_target_pairs={{0,2},{1,3},{2,0},{3,1},{4,6},{5,7},{6,4},{7,5},{8,10},{9,11},{10,... | collective-permute-start | bytes 196616 | tf_op jit(solution)/shard_map/ppermute | solution.py:592
  37.6 0.0 collective-permute-done.6.two
  37.7 0.0 copy-start
  37.7 2.9 %collective-permute-start.9 = (bf16[32,1024]{1,0:T(8,128)(2,1)S(1)}, bf16[32,1024]{1,0:T(8,128)(2,1)S(1)}, u32[]{:S(2)}, u32[]{:S(2)}) collective-permute-start(bf16[32,1024]{1,0:T(8,128)(2,1)S(1)} %add.41.refs_1_.refs_7_), channel_id=1, source_target_pairs={{0,2},{1,3},{2,0},{3,1},{4,6},{5,7},{6,4},{7,5},{8,10},{9,11},{10,... | collective-permute-start | bytes 196616 | tf_op jit(solution)/shard_map/ppermute | solution.py:592
  40.6 3.8 %fetch.6 = (bf16[1024,3584]{1,0:T(8,128)(2,1)S(1)}, f32[8,128]{1,0:T(8,128)S(1)}) custom-call(s32[4]{0:T(128)S(1)} %pad_add_fusion.refs_0_.at, bf16[32,1024]{1,0:T(8,128)(2,1)S(1)} %add.41.refs_1_.refs_7_, bf16[2048,3584]{1,0:T(8,128)(2,1)} %refs_2_.4), custom_call_target="tpu_custom_call" | custom-call | bytes 14680064 | tf_op jit(solution)/shard_map/fetch/pallas_call | solution.py:94
  44.4 0.0 collective-permute-done.8.refs_8_
  44.4 0.0 copy-done
  44.4 6.3 %expand_first.1 = (f32[32,3584]{1,0:T(8,128)S(1)}, f32[32,3584]{1,0:T(8,128)S(1)}, f32[32,1024]{1,0:T(8,128)S(1)}, f32[32,128]{1,0:T(8,128)S(1)}, bf16[1024,3584]{1,0:T(8,128)(2,1)S(1)}) custom-call(s32[4]{0:T(128)S(1)} %pad_add_fusion.refs_0_.at, bf16[32,2048]{1,0:T(8,128)(2,1)S(1)} %get-tuple-element.33.refs_1_, bf16[16,128]{1,0:T(8,128)(2,1)S(1)} %bitcast.9, ...), custom_call_target="tpu_custom_call" | custom-call | flops 469762048 | bytes 14680064 | tf_op jit(solution)/shard_map/expand_first/pallas_call | solution.py:409
  50.7 0.0 collective-permute-done.9.refs_8_
  50.7 1.9 %expand_send.1 = (bf16[32,3968]{1,0:T(8,128)(2,1)S(1)}, f32[32,1024]{1,0:T(8,128)S(1)}, bf16[32,1024]{1,0:T(8,128)(2,1)S(1)}) custom-call(s32[4]{0:T(128)S(1)} %pad_add_fusion.refs_0_.at, bf16[32,2048]{1,0:T(8,128)(2,1)S(1)} %get-tuple-element.33.refs_1_, bf16[16,128]{1,0:T(8,128)(2,1)S(1)} %bitcast.10, bf16[1024,3584]{1,0:T(8,128)(2,1)S(1)} %get-tuple-element.41.refs_3_.wg, ...), custom_call_target="tpu_custom_call" | custom-call | flops 234881024 | bytes 7340032 | tf_op jit(solution)/shard_map/expand_send/pallas_call | solution.py:443
  52.6 0.1 collective-permute-start.10
  52.7 1.9 %expand_keep.1.keep = bf16[32,3584]{1,0:T(8,128)(2,1)S(1)} custom-call(s32[4]{0:T(128)S(1)} %pad_add_fusion.refs_0_.at, bf16[32,1024]{1,0:T(8,128)(2,1)S(1)} %get-tuple-element.49.x, bf16[1024,3584]{1,0:T(8,128)(2,1)S(1)} %get-tuple-element.41.refs_3_.wg, bf16[1024,3584]{1,0:T(8,128)(2,1)S(1)} %get-tuple-element.46.refs_4_.wu, ...), custom_call_target="tpu_custom_call" | custom-call | flops 234881024 | bytes 7340032 | tf_op jit(solution)/shard_map/expand_keep/pallas_call | solution.py:461
  54.6 0.0 collective-permute-done.10.received
  54.6 0.1 pair.1.refs_1_.refs_0_
  54.7 0.6 collective-permute-start.11
  55.2 6.0 %fetch.7 = (bf16[1792,2048]{1,0:T(8,128)(2,1)S(1)}, bf16[1792,2048]{1,0:T(8,128)(2,1)S(1)}, f32[8,128]{1,0:T(8,128)S(1)}) custom-call(s32[4]{0:T(128)S(1)} %pad_add_fusion.refs_0_.at, bf16[32,3968]{1,0:T(8,128)(2,1)S(1)} %pair.1.refs_1_.refs_0_, bf16[3584,2048]{1,0:T(8,128)(2,1)} %refs_3_.3, bf16[3584,2048]{1,0:T(8,128)(2,1)} %refs_3_.3), custom_call_target="tpu_custom_call" | custom-call | bytes 29360128 | tf_op jit(solution)/shard_map/fetch/pallas_call | solution.py:94
  61.3 2.0 %collective-permute-done.11.refs_1_ = bf16[32,3968]{1,0:T(8,128)(2,1)S(1)} collective-permute-done((bf16[32,3968]{1,0:T(8,128)(2,1)S(1)}, bf16[32,3968]{1,0:T(8,128)(2,1)S(1)}, u32[]{:S(2)}, u32[]{:S(2)}) %collective-permute-start.11) | collective-permute-done | bytes 253984 | tf_op jit(solution)/shard_map/ppermute | solution.py:592
  63.3 0.1 gated.1.hidden
  63.4 0.1 collective-permute-start.12
  63.5 1.4 %contract.1.refs_3_ = f32[32,2048]{1,0:T(8,128)S(1)} custom-call(bf16[32,1792]{1,0:T(8,128)(2,1)S(1)} %gated.1.hidden, bf16[1792,2048]{1,0:T(8,128)(2,1)S(1)} %get-tuple-element.54.w), custom_call_target="tpu_custom_call" | custom-call | flops 234881024 | bytes 7340032 | tf_op jit(solution)/shard_map/contract/pallas_call | solution.py:523
  64.8 0.0 collective-permute-done.12.refs_1_
  64.8 1.9 %contract_last.1 = (f32[8,2048]{1,0:T(8,128)S(1)}, bf16[8,2048]{1,0:T(8,128)(2,1)S(1)}, bf16[8,2048]{1,0:T(8,128)(2,1)S(1)}, bf16[8,2048]{1,0:T(8,128)(2,1)S(1)}) custom-call(s32[4]{0:T(128)S(1)} %pad_add_fusion.refs_0_.at, bf16[32,1792]{1,0:T(8,128)(2,1)S(1)} %collective-permute-done.12.refs_1_, bf16[1792,2048]{1,0:T(8,128)(2,1)S(1)} %get-tuple-element.53.refs_2_, ...), custom_call_target="tpu_custom_call" | custom-call | flops 234881024 | bytes 7340032 | tf_op jit(solution)/shard_map/contract_last/pallas_call | solution.py:560
  66.8 1.6 %collective-permute-start.15 = (bf16[8,2048]{1,0:T(8,128)(2,1)S(1)}, bf16[8,2048]{1,0:T(8,128)(2,1)S(1)}, u32[]{:S(2)}, u32[]{:S(2)}) collective-permute-start(bf16[8,2048]{1,0:T(8,128)(2,1)S(1)} %get-tuple-element.60), channel_id=1, source_target_pairs={{0,3},{1,2},{2,1},{3,0},{4,7},{5,6},{6,5},{7,4},{8,11},{9,10},{10,... | collective-permute-start | bytes 98312 | tf_op jit(solution)/shard_map/ppermute | solution.py:592
  68.4 0.0 collective-permute-start.14
  68.4 2.8 %collective-permute-start.13 = (bf16[8,2048]{1,0:T(8,128)(2,1)S(1)}, bf16[8,2048]{1,0:T(8,128)(2,1)S(1)}, u32[]{:S(2)}, u32[]{:S(2)}) collective-permute-start(bf16[8,2048]{1,0:T(8,128)(2,1)S(1)} %get-tuple-element.58), channel_id=1, source_target_pairs={{0,1},{1,0},{2,3},{3,2},{4,5},{5,4},{6,7},{7,6},{8,9},{9,8},{10,11... | collective-permute-start | bytes 98312 | tf_op jit(solution)/shard_map/ppermute | solution.py:592
  71.2 1.6 %collective-permute-done.15 = bf16[8,2048]{1,0:T(8,128)(2,1)S(1)} collective-permute-done((bf16[8,2048]{1,0:T(8,128)(2,1)S(1)}, bf16[8,2048]{1,0:T(8,128)(2,1)S(1)}, u32[]{:S(2)}, u32[]{:S(2)}) %collective-permute-start.15) | collective-permute-done | bytes 32800 | tf_op jit(solution)/shard_map/ppermute | solution.py:592
  72.9 1.0 %collective-permute-done.14 = bf16[8,2048]{1,0:T(8,128)(2,1)S(1)} collective-permute-done((bf16[8,2048]{1,0:T(8,128)(2,1)S(1)}, bf16[8,2048]{1,0:T(8,128)(2,1)S(1)}, u32[]{:S(2)}, u32[]{:S(2)}) %collective-permute-start.14) | collective-permute-done | bytes 32800 | tf_op jit(solution)/shard_map/ppermute | solution.py:592
  73.8 0.0 collective-permute-done.13
  73.8 0.6 add_convert_fusion
  (5 shorter events, 0.0 us)
Async XLA Ops:
  0.0 8.2 %copy-start.1 = (s32[8]{0:T(128)S(1)}, s32[8]{0:T(128)}, u32[]{:S(2)}) copy-start(s32[8]{0:T(128)} %param.24) | copy-start | bytes 100
  0.0 8.6 %copy-start.2 = (s32[8]{0:T(128)S(1)}, s32[8]{0:T(128)}, u32[]{:S(2)}) copy-start(s32[8]{0:T(128)} %param.25) | copy-start | bytes 100
  5.2 8.7 %collective-permute-start = (bf16[32,2560]{1,0:T(8,128)(2,1)S(1)}, bf16[32,2560]{1,0:T(8,128)(2,1)S(1)}, u32[]{:S(2)}, u32[]{:S(2)}) collective-permute-start(bf16[32,2560]{1,0:T(8,128)(2,1)S(1)} %get-tuple-element.34.refs_1_.refs_5_), channel_id=1, source_target_pairs={{0,8},{4,12},{8,0},{12,4},{1,9},{5,13},{9,1},{13,5},{2,10},{6,14},... | collective-permute-start | bytes 491528 | tf_op jit(solution)/shard_map/ppermute | solution.py:592
  8.2 6.2 %collective-permute-start.1 = (bf16[32,2560]{1,0:T(8,128)(2,1)S(1)}, bf16[32,2560]{1,0:T(8,128)(2,1)S(1)}, u32[]{:S(2)}, u32[]{:S(2)}) collective-permute-start(bf16[32,2560]{1,0:T(8,128)(2,1)S(1)} %get-tuple-element.34.refs_1_.refs_5_), channel_id=1, source_target_pairs={{0,4},{4,0},{8,12},{12,8},{1,5},{5,1},{9,13},{13,9},{2,6},{6,2},{1... | collective-permute-start | bytes 491528 | tf_op jit(solution)/shard_map/ppermute | solution.py:592
  13.9 1.6 %collective-permute-start.2 = (bf16[32,2560]{1,0:T(8,128)(2,1)S(1)}, bf16[32,2560]{1,0:T(8,128)(2,1)S(1)}, u32[]{:S(2)}, u32[]{:S(2)}) collective-permute-start(bf16[32,2560]{1,0:T(8,128)(2,1)S(1)} %hold.2.refs_6_), channel_id=1, source_target_pairs={{0,4},{4,0},{8,12},{12,8},{1,5},{5,1},{9,13},{13,9},{2,6},{6,2},{1... | collective-permute-start | bytes 491528 | tf_op jit(solution)/shard_map/ppermute | solution.py:592
  21.9 6.4 %collective-permute-start.3 = (bf16[32,2432]{1,0:T(8,128)(2,1)S(1)}, bf16[32,2432]{1,0:T(8,128)(2,1)S(1)}, u32[]{:S(2)}, u32[]{:S(2)}) collective-permute-start(bf16[32,2432]{1,0:T(8,128)(2,1)S(1)} %get-tuple-element.38.refs_1_), channel_id=1, source_target_pairs={{0,8},{4,12},{8,0},{12,4},{1,9},{5,13},{9,1},{13,5},{2,10},{6,14},... | collective-permute-start | bytes 466952 | tf_op jit(solution)/shard_map/ppermute | solution.py:592
  22.1 6.2 %collective-permute-start.4 = (bf16[32,2432]{1,0:T(8,128)(2,1)S(1)}, bf16[32,2432]{1,0:T(8,128)(2,1)S(1)}, u32[]{:S(2)}, u32[]{:S(2)}) collective-permute-start(bf16[32,2432]{1,0:T(8,128)(2,1)S(1)} %get-tuple-element.38.refs_1_), channel_id=1, source_target_pairs={{0,4},{4,0},{8,12},{12,8},{1,5},{5,1},{9,13},{13,9},{2,6},{6,2},{1... | collective-permute-start | bytes 466952 | tf_op jit(solution)/shard_map/ppermute | solution.py:592
  28.3 1.4 %collective-permute-start.5 = (bf16[32,2432]{1,0:T(8,128)(2,1)S(1)}, bf16[32,2432]{1,0:T(8,128)(2,1)S(1)}, u32[]{:S(2)}, u32[]{:S(2)}) collective-permute-start(bf16[32,2432]{1,0:T(8,128)(2,1)S(1)} %hold.3.refs_2_), channel_id=1, source_target_pairs={{0,4},{4,0},{8,12},{12,8},{1,5},{5,1},{9,13},{13,9},{2,6},{6,2},{1... | collective-permute-start | bytes 466952 | tf_op jit(solution)/shard_map/ppermute | solution.py:592
  30.7 4.3 %collective-permute-start.7 = (bf16[32,1024]{1,0:T(8,128)(2,1)S(1)}, bf16[32,1024]{1,0:T(8,128)(2,1)S(1)}, u32[]{:S(2)}, u32[]{:S(2)}) collective-permute-start(bf16[32,1024]{1,0:T(8,128)(2,1)S(1)} %get-tuple-element.45.one), channel_id=1, source_target_pairs={{0,1},{1,0},{2,3},{3,2},{4,5},{5,4},{6,7},{7,6},{8,9},{9,8},{10,11... | collective-permute-start | bytes 196616 | tf_op jit(solution)/shard_map/ppermute | solution.py:592
  33.1 4.5 %collective-permute-start.6 = (bf16[32,1024]{1,0:T(8,128)(2,1)S(1)}, bf16[32,1024]{1,0:T(8,128)(2,1)S(1)}, u32[]{:S(2)}, u32[]{:S(2)}) collective-permute-start(bf16[32,1024]{1,0:T(8,128)(2,1)S(1)} %output_second.1.one), channel_id=1, source_target_pairs={{0,1},{1,0},{2,3},{3,2},{4,5},{5,4},{6,7},{7,6},{8,9},{9,8},{10,11... | collective-permute-start | bytes 196616 | tf_op jit(solution)/shard_map/ppermute | solution.py:592
  35.0 9.4 %collective-permute-start.8 = (bf16[32,1024]{1,0:T(8,128)(2,1)S(1)}, bf16[32,1024]{1,0:T(8,128)(2,1)S(1)}, u32[]{:S(2)}, u32[]{:S(2)}) collective-permute-start(bf16[32,1024]{1,0:T(8,128)(2,1)S(1)} %add.42.refs_7_), channel_id=1, source_target_pairs={{0,2},{1,3},{2,0},{3,1},{4,6},{5,7},{6,4},{7,5},{8,10},{9,11},{10,... | collective-permute-start | bytes 196616 | tf_op jit(solution)/shard_map/ppermute | solution.py:592
  37.7 6.8 %copy-start = (bf16[2048]{0:T(1024)(128)(2,1)S(1)}, bf16[2048]{0:T(1024)(128)(2,1)}, u32[]{:S(2)}) copy-start(bf16[2048]{0:T(1024)(128)(2,1)} %param.15) | copy-start | bytes 12292
  37.7 13.0 %collective-permute-start.9 = (bf16[32,1024]{1,0:T(8,128)(2,1)S(1)}, bf16[32,1024]{1,0:T(8,128)(2,1)S(1)}, u32[]{:S(2)}, u32[]{:S(2)}) collective-permute-start(bf16[32,1024]{1,0:T(8,128)(2,1)S(1)} %add.41.refs_1_.refs_7_), channel_id=1, source_target_pairs={{0,2},{1,3},{2,0},{3,1},{4,6},{5,7},{6,4},{7,5},{8,10},{9,11},{10,... | collective-permute-start | bytes 196616 | tf_op jit(solution)/shard_map/ppermute | solution.py:592
  52.6 2.0 %collective-permute-start.10 = (bf16[32,3968]{1,0:T(8,128)(2,1)S(1)}, bf16[32,3968]{1,0:T(8,128)(2,1)S(1)}, u32[]{:S(2)}, u32[]{:S(2)}) collective-permute-start(bf16[32,3968]{1,0:T(8,128)(2,1)S(1)} %get-tuple-element.51.stats), channel_id=1, source_target_pairs={{0,4},{4,0},{8,12},{12,8},{1,5},{5,1},{9,13},{13,9},{2,6},{6,2},{1... | collective-permute-start | bytes 761864 | tf_op jit(solution)/shard_map/ppermute | solution.py:592
  54.7 8.6 %collective-permute-start.11 = (bf16[32,3968]{1,0:T(8,128)(2,1)S(1)}, bf16[32,3968]{1,0:T(8,128)(2,1)S(1)}, u32[]{:S(2)}, u32[]{:S(2)}) collective-permute-start(bf16[32,3968]{1,0:T(8,128)(2,1)S(1)} %pair.1.refs_1_.refs_0_), channel_id=1, source_target_pairs={{0,8},{4,12},{8,0},{12,4},{1,9},{5,13},{9,1},{13,5},{2,10},{6,14},... | collective-permute-start | bytes 761864 | tf_op jit(solution)/shard_map/ppermute | solution.py:592
  63.4 1.4 %collective-permute-start.12 = (bf16[32,1792]{1,0:T(8,128)(2,1)S(1)}, bf16[32,1792]{1,0:T(8,128)(2,1)S(1)}, u32[]{:S(2)}, u32[]{:S(2)}) collective-permute-start(bf16[32,1792]{1,0:T(8,128)(2,1)S(1)} %gated.1.hidden), channel_id=1, source_target_pairs={{0,4},{4,0},{8,12},{12,8},{1,5},{5,1},{9,13},{13,9},{2,6},{6,2},{1... | collective-permute-start | bytes 344072 | tf_op jit(solution)/shard_map/ppermute | solution.py:592
  66.8 6.1 %collective-permute-start.15 = (bf16[8,2048]{1,0:T(8,128)(2,1)S(1)}, bf16[8,2048]{1,0:T(8,128)(2,1)S(1)}, u32[]{:S(2)}, u32[]{:S(2)}) collective-permute-start(bf16[8,2048]{1,0:T(8,128)(2,1)S(1)} %get-tuple-element.60), channel_id=1, source_target_pairs={{0,3},{1,2},{2,1},{3,0},{4,7},{5,6},{6,5},{7,4},{8,11},{9,10},{10,... | collective-permute-start | bytes 98312 | tf_op jit(solution)/shard_map/ppermute | solution.py:592
  68.4 5.4 %collective-permute-start.14 = (bf16[8,2048]{1,0:T(8,128)(2,1)S(1)}, bf16[8,2048]{1,0:T(8,128)(2,1)S(1)}, u32[]{:S(2)}, u32[]{:S(2)}) collective-permute-start(bf16[8,2048]{1,0:T(8,128)(2,1)S(1)} %get-tuple-element.59), channel_id=1, source_target_pairs={{0,2},{1,3},{2,0},{3,1},{4,6},{5,7},{6,4},{7,5},{8,10},{9,11},{10,... | collective-permute-start | bytes 98312 | tf_op jit(solution)/shard_map/ppermute | solution.py:592
  68.4 5.4 %collective-permute-start.13 = (bf16[8,2048]{1,0:T(8,128)(2,1)S(1)}, bf16[8,2048]{1,0:T(8,128)(2,1)S(1)}, u32[]{:S(2)}, u32[]{:S(2)}) collective-permute-start(bf16[8,2048]{1,0:T(8,128)(2,1)S(1)} %get-tuple-element.58), channel_id=1, source_target_pairs={{0,1},{1,0},{2,3},{3,2},{4,5},{5,4},{6,7},{7,6},{8,9},{9,8},{10,11... | collective-permute-start | bytes 98312 | tf_op jit(solution)/shard_map/ppermute | solution.py:592

commit v4 on v3

--- a/solution.py
+++ b/solution.py
@@ -75,6 +75,14 @@
             )
             for p in range(self.count // step)
         ]
+
+
+def beside(copies, at, compute):
+    for copy in copies:
+        copy.start()
+    pl.when(at[2] >= 0)(compute)
+    for copy in copies:
+        copy.wait()
 
 
 def fetch_kernel(wanted, skip, at, *refs):
@@ -202,9 +210,14 @@
 
 def attend_kernel(n, part, at, cos, sin, cache, source, *rest):
     parts, (out, held, queries, total, stats_f, sems) = rest[:n], rest[n:]
-    copies = part.copies(at, source, held, sems)
-    for copy in copies:
-        copy.start()
+    beside(
+        part.copies(at, source, held, sems),
+        at,
+        lambda: attention(at, cos, sin, cache, parts, out, queries, total, stats_f),
+    )
+
+
+def attention(at, cos, sin, cache, parts, out, queries, total, stats_f):
     rows, q_cols = queries.shape
     context, kv_cols = cache.shape[2:]
     kv_heads = kv_cols // HEAD_WIDTH
@@ -284,8 +297,6 @@
     out[:, :q_cols] = total[...].astype(bf16)
     for p, term in enumerate(thirds(stats_f[...])):
         out[:, q_cols + p * LANES : q_cols + (p + 1) * LANES] = term
-    for copy in copies:
-        copy.wait()
 
 
 def attend(at, cos, sin, cache, parts, part):
@@ -319,8 +330,12 @@
         ).astype(out.dtype)
 
 
-def output_first_kernel(n, w, *rest):
-    values, (out, attended) = rest[:n], rest[n:]
+def output_first_kernel(n, part, at, w, source, *rest):
+    values, (out, attended, held, sems) = rest[:n], rest[n:]
+    beside(part.copies(at, source, held, sems), at, lambda: combine(w, values, out, attended))
+
+
+def combine(w, values, out, attended):
     heads = attended.shape[1] // HEAD_WIDTH
     stats = [joined(v, attended.shape[1]) for v in values]
     top = stats[0]
@@ -336,20 +351,22 @@
     product(attended, w, out, 0, out.shape[1])
 
 
-def output_first(values, w):
+def output_first(at, values, w, part):
     rows, half = values[0].shape[0], w.shape[1] // 2
     return pl.pallas_call(
-        lambda *refs: output_first_kernel(len(values), *refs),
-        in_specs=[VMEM] * (1 + len(values)),
-        out_specs=[VMEM, VMEM],
+        lambda *refs: output_first_kernel(len(values), part, *refs),
+        in_specs=[SMEM, VMEM, HBM] + [VMEM] * len(values),
+        out_specs=[VMEM] * 3,
         out_shape=[
             jax.ShapeDtypeStruct((rows, half), bf16),
             jax.ShapeDtypeStruct((rows, w.shape[0]), bf16),
+            part.out,
         ],
+        scratch_shapes=[pltpu.SemaphoreType.DMA((2 * PIECES,))],
         compiler_params=params(4),
         cost_estimate=cost(rows, w),
         name="output_first",
-    )(w, *values)
+    )(at, w, in_hbm(part.array), *values)
 
 
 def output_second(attended, w):
@@ -366,14 +383,17 @@
 
 
 def half_of(side, x, wg, wu, out, before=None):
-    half = wg.shape[1] // 2
-    for base, w in ((0, wg), (half, wu)):
+    half = wg[0].shape[1] // 2
+    for base, pieces in ((0, wg), (half, wu)):
         for start, size in blocks_of(half, 512):
             cols = pl.ds(pl.multiple_of(side * half + start, LANES), size)
             to = slice(base + start, base + start + size)
-            term = jnp.dot(x[...], w[:, cols], preferred_element_type=f32)
-            if before is not None:
-                term = before[:, to] + term
+            term = None if before is None else before[:, to]
+            row = 0
+            for w in pieces:
+                more = jnp.dot(x[:, row : row + w.shape[0]], w[:, cols], preferred_element_type=f32)
+                term = more if term is None else term + more
+                row += w.shape[0]
             out[:, to] = term.astype(out.dtype)
 
 
@@ -391,24 +411,23 @@
     return square
 
 
-def expand_first_kernel(n, part, at, own, gain, wg, wu, _, source, *rest):
+def expand_first_kernel(n, part, at, own, gain, wg, wu, source, *rest):
     parts, (send, keep, resid, squares, held, x, gain_f, sems) = rest[:n], rest[n:]
-    copies = part.copies(at, source, held, sems)
-    for copy in copies:
-        copy.start()
-    squares[...] = residual(0, own, gain, parts, resid, x, gain_f)
-    half_of(1 - at[2], x, wg, wu, send)
-    half_of(at[2], x, wg, wu, keep)
-    for copy in copies:
-        copy.wait()
-
-
-def expand_first(at, own, gain, parts, wg, wu, part, after):
+
+    def compute():
+        squares[...] = residual(0, own, gain, parts, resid, x, gain_f)
+        half_of(1 - at[2], x, [wg], [wu], send)
+        half_of(at[2], x, [wg], [wu], keep)
+
+    beside(part.copies(at, source, held, sems), at, compute)
+
+
+def expand_first(at, own, gain, parts, wg, wu, part):
     rows, depth = own.shape
     width = wg.shape[1]
     return pl.pallas_call(
         lambda *refs: expand_first_kernel(len(parts), part, *refs),
-        in_specs=[SMEM] + [VMEM] * 4 + [ANY, HBM] + [VMEM] * len(parts),
+        in_specs=[SMEM] + [VMEM] * 4 + [HBM] + [VMEM] * len(parts),
         out_specs=[VMEM] * 5,
         out_shape=[
             jax.ShapeDtypeStruct((rows, width), f32),
@@ -425,14 +444,14 @@
         compiler_params=params(4),
         cost_estimate=cost(rows, wg, wu),
         name="expand_first",
-    )(at, own, gain, wg, wu, after, in_hbm(part.array), *parts)
-
-
-def expand_send_kernel(n, at, own, gain, wg, wu, before, squares, *rest):
-    parts, (out, resid, x, gain_f) = rest[:n], rest[n:]
+    )(at, own, gain, wg, wu, in_hbm(part.array), *parts)
+
+
+def expand_send_kernel(n, g, at, own, gain, before, squares, *rest):
+    wg, wu, parts, (out, resid, x, gain_f) = rest[:g], rest[g : g + 1], rest[g + 1 : g + 1 + n], rest[g + 1 + n :]
     square = squares[...] + residual(1, own, gain, parts, resid, x, gain_f)
     square = jnp.broadcast_to(jnp.sum(square, axis=1, keepdims=True), square.shape)
-    width = wg.shape[1]
+    width = wu[0].shape[1]
     for p, term in enumerate(thirds(square)):
         out[:, width + p * LANES : width + (p + 1) * LANES] = term
     half_of(1 - at[2], x, wg, wu, out, before)
@@ -441,32 +460,32 @@
 def expand_send(at, own, gain, parts, wg, wu, before, squares):
     rows, depth = own.shape
     return pl.pallas_call(
-        lambda *refs: expand_send_kernel(len(parts), *refs),
-        in_specs=[SMEM] + [VMEM] * (6 + len(parts)),
+        lambda *refs: expand_send_kernel(len(parts), len(wg), *refs),
+        in_specs=[SMEM] + [VMEM] * (5 + len(wg) + len(parts)),
         out_specs=[VMEM] * 3,
         out_shape=[
-            jax.ShapeDtypeStruct((rows, wg.shape[1] + 3 * LANES), bf16),
+            jax.ShapeDtypeStruct((rows, wu.shape[1] + 3 * LANES), bf16),
             jax.ShapeDtypeStruct((rows, depth // 2), f32),
             jax.ShapeDtypeStruct((rows, depth // 2), bf16),
         ],
         scratch_shapes=[pltpu.VMEM((depth // LANES, LANES), f32)],
         compiler_params=params(4),
-        cost_estimate=cost(rows, wg),
+        cost_estimate=cost(rows, wu),
         name="expand_send",
-    )(at, own, gain, wg, wu, before, squares, *parts)
+    )(at, own, gain, before, squares, *wg, wu, *parts)
 
 
 def expand_keep(at, x, wg, wu, before):
     rows = x.shape[0]
     return pl.pallas_call(
-        lambda at, x, wg, wu, before, out: half_of(at[2], x, wg, wu, out, before),
-        in_specs=[SMEM] + [VMEM] * 4,
+        lambda at, x, before, *refs: half_of(at[2], x, refs[:-2], refs[-2:-1], refs[-1], before),
+        in_specs=[SMEM] + [VMEM] * (3 + len(wg)),
         out_specs=VMEM,
-        out_shape=jax.ShapeDtypeStruct((rows, wg.shape[1]), bf16),
-        compiler_params=params(4),
-        cost_estimate=cost(rows, wg),
+        out_shape=jax.ShapeDtypeStruct((rows, wu.shape[1]), bf16),
+        compiler_params=params(4),
+        cost_estimate=cost(rows, wu),
         name="expand_keep",
-    )(at, x, wg, wu, before)
+    )(at, x, before, *wg, wu)
 
 
 def pair_kernel(keep, received, stats, out):
@@ -642,14 +661,17 @@
     cache = cache.reshape(kv_cache.shape)
     value, w_out = attend(meta, cos, sin, cache, gathered(qkv, "wide", token), Part(w_out))
 
-    up_0, token = fetch(at, value, Part(w_up, 0, half))
-    out_0, attended = output_first(gathered(value, "wide", token), w_out)
+    quarter = half // 2
+    up_0, gate_1, token = fetch(at, value, Part(w_up, 0, half), Part(w_gate, half, quarter))
+    out_0, attended, gate_2 = output_first(
+        at, gathered(value, "wide", token), w_out, Part(w_gate, half + quarter, quarter)
+    )
     out_1 = output_second(attended, w_out)
     parts_0, parts_1 = summed(out_0, "head"), summed(out_1, "head")
-    gate_1, token = fetch(at, parts_1[0], Part(w_gate, half, half))
     send, keep, resid_0, squares, up_1 = expand_first(
-        at, own, gain, parts_0, gate_0, up_0, Part(w_up, half, half), token
+        at, own, gain, parts_0, gate_0, up_0, Part(w_up, half, half)
     )
+    gate_1 = (gate_1, gate_2)
     send, resid_1, x = expand_send(at, own, gain, parts_1, gate_1, up_1, send, squares)
     received = swap(send, "wide", 1)
     total = pair(expand_keep(at, x, gate_1, up_1, keep), received, send)

time: 74.6 us -> 72.1 us (0.966)
  Pallas kernels: 45.7 us -> 39.9 us
  starting transfers between devices: 16.9 us -> 19.4 us
  waiting for transfers between devices: 10.5 us -> 11.3 us
    pallas_call x4 -> x3, Pallas kernels: 18.7 us -> 16.1 us  [fetch(): pl.pallas_call(lambda *refs: fetch_kernel(wanted, len(after), *refs), in_...]
    pallas_call x1, Pallas kernels: 6.26 us -> 3.79 us  [expand_first(): pl.pallas_call(lambda *refs: expand_first_kernel(len(parts), part, *refs)...]
    ppermute x16, starting transfers between devices: 16.9 us -> 19.4 us  [swap(): return lax.ppermute(x, axis, [(i, i ^ bit) for i in range(n)])]
    pallas_call x1, Pallas kernels: 6.45 us -> 4.09 us  [attend(): pl.pallas_call(lambda *refs: attend_kernel(len(parts), part, *refs), in_s...]
    pallas_call x3, Pallas kernels: 4.78 us -> 6.49 us  [the longest x1 2.67 us: output_first(): pl.pallas_call(lambda *refs: output_first_kernel(len(values), part, *refs...]
    ppermute x16, waiting for transfers between devices: 10.5 us -> 11.3 us  [swap(): return lax.ppermute(x, axis, [(i, i ^ bit) for i in range(n)])]
  transfers between devices with their start and end apart: 16 -> 16, of which waited for: 7 -> 8; matrix products, arithmetic and copies ran while one was open for 1% -> 1% of each run, Pallas kernels for 39% -> 33%
where the time goes in v4:
time: 72.1 us; the launch traced here: 72 us
  Pallas kernels  39.9 us (55%)
  starting transfers between devices  19.4 us (27%)
  waiting for transfers between devices  11.3 us (16%)
  other arithmetic  1.02 us (1%)
    ppermute x16, starting transfers between devices, swap(): return lax.ppermute(x, axis, [(i, i ^ bit) for i in range(n)])  19.4 us
    pallas_call x3, Pallas kernels, fetch(): pl.pallas_call(lambda *refs: fetch_kernel(wanted, len(after), *refs), in_...  16.1 us
    ppermute x16, waiting for transfers between devices, swap(): return lax.ppermute(x, axis, [(i, i ^ bit) for i in range(n)])  11.3 us
    pallas_call x1, Pallas kernels, project(): pl.pallas_call(lambda *refs: project_kernel(chunks, *refs), in_specs=[SME...  5.11 us
    pallas_call x1, Pallas kernels, attend(): pl.pallas_call(lambda *refs: attend_kernel(len(parts), part, *refs), in_s...  4.09 us
    pallas_call x1, Pallas kernels, expand_first(): pl.pallas_call(lambda *refs: expand_first_kernel(len(parts), part, *refs)...  3.79 us
    pallas_call x1, Pallas kernels, output_first(): pl.pallas_call(lambda *refs: output_first_kernel(len(values), part, *refs...  2.67 us
    pallas_call x1, Pallas kernels, contract_last(): pl.pallas_call(lambda *refs: contract_last_kernel(n, *refs), in_specs=[SM...  1.94 us
  transfers between devices with their start and end apart: 16, of which 8 were waited for; matrix products, arithmetic and copies ran while one was open for 1% of the time, Pallas kernels for 33%

profile of v4, /device:TPU:0, one launch (start us, length us, event | category | flops | bytes accessed | tf_op | source)
XLA Modules:
  0.0 72.0 jit_solution(10204849704039229248)
XLA Ops:
  0.0 0.0 copy-start.1
  0.0 0.0 copy-start.2
  0.0 0.1 pad_add_fusion.refs_0_.at
  0.1 5.1 %project.1 = (bf16[32,2560]{1,0:T(8,128)(2,1)S(1)}, bf16[32,2048]{1,0:T(8,128)(2,1)S(1)}) custom-call(s32[4]{0:T(128)S(1)} %pad_add_fusion.refs_0_.at, bf16[32,8192]{1,0:T(8,128)(2,1)} %refs_1_.1, bf16[64,128]{1,0:T(8,128)(2,1)} %bitcast.12, bf16[2048,2048]{1,0:T(8,128)(2,1)} %refs_3_.3, bf16[2048,256]{1,0:T(8,128)(2,1)} %refs_4_.2, bf16[2048,256]{1,0:T(8,128)(2,1)} %refs_5_.2), custom_call_target="tpu_custom_call" | custom-call | flops 335544320 | bytes 10485760 | tf_op jit(solution)/shard_map/project/pallas_call | solution.py:186
  5.2 0.5 collective-permute-start.1
  5.7 2.6 %collective-permute-start = (bf16[32,2560]{1,0:T(8,128)(2,1)S(1)}, bf16[32,2560]{1,0:T(8,128)(2,1)S(1)}, u32[]{:S(2)}, u32[]{:S(2)}) collective-permute-start(bf16[32,2560]{1,0:T(8,128)(2,1)S(1)} %get-tuple-element.34.refs_1_.refs_5_), channel_id=1, source_target_pairs={{0,8},{4,12},{8,0},{12,4},{1,9},{5,13},{9,1},{13,5},{2,10},{6,14},... | collective-permute-start | bytes 491528 | tf_op jit(solution)/shard_map/ppermute | solution.py:611
  8.3 0.0 copy-done.1
  8.3 0.1 add_convert_fusion.1
  8.4 0.1 convert_element_type.24
  8.5 0.1 fusion
  8.6 0.0 copy-done.2
  8.6 0.1 concatenate.10.refs_2_.refs_0_
  8.7 0.1 pad_maximum_fusion
  8.8 5.1 %fetch.3 = (bf16[16,512,256]{2,1,0:T(8,128)(2,1)S(1)}, bf16[1024,3584]{1,0:T(8,128)(2,1)S(1)}, f32[8,128]{1,0:T(8,128)S(1)}) custom-call(s32[4]{0:T(128)S(1)} %pad_add_fusion.refs_0_.at, bf16[32,2560]{1,0:T(8,128)(2,1)S(1)} %get-tuple-element.34.refs_1_.refs_5_, s32[20]{0:T(128)S(1)} %concatenate.10.refs_2_.refs_0_, ...), custom_call_target="tpu_custom_call" | custom-call | bytes 23068672 | tf_op jit(solution)/shard_map/fetch/pallas_call | solution.py:102
  13.9 0.0 collective-permute-done.__0_
  14.0 0.2 collective-permute-start.2
  14.2 0.0 collective-permute-done.1.refs_7_
  14.2 1.2 %collective-permute-done.2.refs_8_ = bf16[32,2560]{1,0:T(8,128)(2,1)S(1)} collective-permute-done((bf16[32,2560]{1,0:T(8,128)(2,1)S(1)}, bf16[32,2560]{1,0:T(8,128)(2,1)S(1)}, u32[]{:S(2)}, u32[]{:S(2)}) %collective-permute-start.2) | collective-permute-done | bytes 163872 | tf_op jit(solution)/shard_map/ppermute | solution.py:611
  15.4 4.1 %attend.1 = (bf16[32,2432]{1,0:T(8,128)(2,1)S(1)}, bf16[2048,2048]{1,0:T(8,128)(2,1)S(1)}) custom-call(s32[20]{0:T(128)S(1)} %concatenate.10.refs_2_.refs_0_, f32[32,128]{1,0:T(8,128)S(1)} %get-tuple-element.64.refs_3_.refs_1_, f32[32,128]{1,0:T(8,128)S(1)} %get-tuple-element.65.refs_4_.refs_2_, bf16[2,8,512,256]{3,2,1,0:T(8,128)(2,1)S(1)} %bitcast.8, ...), custom_call_target="tpu_custom_call" | custom-call | flops 134217728 | bytes 4194304 | tf_op jit(solution)/shard_map/attend/pallas_call | solution.py:305
  19.5 0.9 %collective-permute-start.3 = (bf16[32,2432]{1,0:T(8,128)(2,1)S(1)}, bf16[32,2432]{1,0:T(8,128)(2,1)S(1)}, u32[]{:S(2)}, u32[]{:S(2)}) collective-permute-start(bf16[32,2432]{1,0:T(8,128)(2,1)S(1)} %get-tuple-element.38.refs_1_.refs_3_), channel_id=1, source_target_pairs={{0,8},{4,12},{8,0},{12,4},{1,9},{5,13},{9,1},{13,5},{2,10},{6,14},... | collective-permute-start | bytes 466952 | tf_op jit(solution)/shard_map/ppermute | solution.py:611
  20.4 0.0 collective-permute-start.4
  20.4 4.9 %fetch.4 = (bf16[1024,3584]{1,0:T(8,128)(2,1)S(1)}, bf16[512,3584]{1,0:T(8,128)(2,1)S(1)}, f32[8,128]{1,0:T(8,128)S(1)}) custom-call(s32[4]{0:T(128)S(1)} %pad_add_fusion.refs_0_.at, bf16[32,2432]{1,0:T(8,128)(2,1)S(1)} %get-tuple-element.38.refs_1_.refs_3_, bf16[2048,3584]{1,0:T(8,128)(2,1)} %refs_5_.3, bf16[2048,3584]{1,0:T(8,128)(2,1)} %refs_2_.4), custom_call_target="tpu_custom_call" | custom-call | bytes 22020096 | tf_op jit(solution)/shard_map/fetch/pallas_call | solution.py:102
  25.4 0.3 collective-permute-done.3.__0_
  25.7 0.3 collective-permute-start.5
  25.9 0.0 collective-permute-done.4.refs_5_
  26.0 1.1 %collective-permute-done.5.refs_6_ = bf16[32,2432]{1,0:T(8,128)(2,1)S(1)} collective-permute-done((bf16[32,2432]{1,0:T(8,128)(2,1)S(1)}, bf16[32,2432]{1,0:T(8,128)(2,1)S(1)}, u32[]{:S(2)}, u32[]{:S(2)}) %collective-permute-start.5) | collective-permute-done | bytes 155680 | tf_op jit(solution)/shard_map/ppermute | solution.py:611
  27.1 2.7 %output_first.1 = (bf16[32,1024]{1,0:T(8,128)(2,1)S(1)}, bf16[32,2048]{1,0:T(8,128)(2,1)S(1)}, bf16[512,3584]{1,0:T(8,128)(2,1)S(1)}) custom-call(s32[4]{0:T(128)S(1)} %pad_add_fusion.refs_0_.at, bf16[2048,2048]{1,0:T(8,128)(2,1)S(1)} %get-tuple-element.40.refs_1_.w, bf16[2048,3584]{1,0:T(8,128)(2,1)} %refs_2_.4, ...), custom_call_target="tpu_custom_call" | custom-call | flops 268435456 | bytes 8388608 | tf_op jit(solution)/shard_map/output_first/pallas_call | solution.py:356
  29.7 0.0 copy-start
  29.8 1.6 %collective-permute-start.6 = (bf16[32,1024]{1,0:T(8,128)(2,1)S(1)}, bf16[32,1024]{1,0:T(8,128)(2,1)S(1)}, u32[]{:S(2)}, u32[]{:S(2)}) collective-permute-start(bf16[32,1024]{1,0:T(8,128)(2,1)S(1)} %get-tuple-element.42.one), channel_id=1, source_target_pairs={{0,1},{1,0},{2,3},{3,2},{4,5},{5,4},{6,7},{7,6},{8,9},{9,8},{10,11... | collective-permute-start | bytes 196616 | tf_op jit(solution)/shard_map/ppermute | solution.py:611
  31.4 0.8 %output_second.1.one = bf16[32,1024]{1,0:T(8,128)(2,1)S(1)} custom-call(bf16[32,2048]{1,0:T(8,128)(2,1)S(1)} %get-tuple-element.48.x, bf16[2048,2048]{1,0:T(8,128)(2,1)S(1)} %get-tuple-element.40.refs_1_.w), custom_call_target="tpu_custom_call" | custom-call | flops 268435456 | bytes 8388608 | tf_op jit(solution)/shard_map/output_second/pallas_call | solution.py:374
  32.2 0.5 collective-permute-start.8
  32.7 1.4 %collective-permute-done.6.two = bf16[32,1024]{1,0:T(8,128)(2,1)S(1)} collective-permute-done((bf16[32,1024]{1,0:T(8,128)(2,1)S(1)}, bf16[32,1024]{1,0:T(8,128)(2,1)S(1)}, u32[]{:S(2)}, u32[]{:S(2)}) %collective-permute-start.6) | collective-permute-done | bytes 65568 | tf_op jit(solution)/shard_map/ppermute | solution.py:611
  34.1 2.7 %collective-permute-start.7 = (bf16[32,1024]{1,0:T(8,128)(2,1)S(1)}, bf16[32,1024]{1,0:T(8,128)(2,1)S(1)}, u32[]{:S(2)}, u32[]{:S(2)}) collective-permute-start(bf16[32,1024]{1,0:T(8,128)(2,1)S(1)} %add.41.refs_6_), channel_id=1, source_target_pairs={{0,2},{1,3},{2,0},{3,1},{4,6},{5,7},{6,4},{7,5},{8,10},{9,11},{10,... | collective-permute-start | bytes 196616 | tf_op jit(solution)/shard_map/ppermute | solution.py:611
  36.8 0.0 collective-permute-done.8.two
  36.8 3.1 %collective-permute-start.9 = (bf16[32,1024]{1,0:T(8,128)(2,1)S(1)}, bf16[32,1024]{1,0:T(8,128)(2,1)S(1)}, u32[]{:S(2)}, u32[]{:S(2)}) collective-permute-start(bf16[32,1024]{1,0:T(8,128)(2,1)S(1)} %add.42.refs_8_), channel_id=1, source_target_pairs={{0,2},{1,3},{2,0},{3,1},{4,6},{5,7},{6,4},{7,5},{8,10},{9,11},{10,... | collective-permute-start | bytes 196616 | tf_op jit(solution)/shard_map/ppermute | solution.py:611
  39.9 0.2 collective-permute-done.7.refs_7_
  40.0 0.0 copy-done
  40.0 3.8 %expand_first.1 = (f32[32,3584]{1,0:T(8,128)S(1)}, f32[32,3584]{1,0:T(8,128)S(1)}, f32[32,1024]{1,0:T(8,128)S(1)}, f32[32,128]{1,0:T(8,128)S(1)}, bf16[1024,3584]{1,0:T(8,128)(2,1)S(1)}) custom-call(s32[4]{0:T(128)S(1)} %pad_add_fusion.refs_0_.at, bf16[32,2048]{1,0:T(8,128)(2,1)S(1)} %get-tuple-element.33.refs_1_, bf16[16,128]{1,0:T(8,128)(2,1)S(1)} %bitcast.9, ...), custom_call_target="tpu_custom_call" | custom-call | flops 469762048 | bytes 14680064 | tf_op jit(solution)/shard_map/expand_first/pallas_call | solution.py:428
  43.8 0.0 collective-permute-done.9.refs_9_
  43.8 1.9 %expand_send.1 = (bf16[32,3968]{1,0:T(8,128)(2,1)S(1)}, f32[32,1024]{1,0:T(8,128)S(1)}, bf16[32,1024]{1,0:T(8,128)(2,1)S(1)}) custom-call(s32[4]{0:T(128)S(1)} %pad_add_fusion.refs_0_.at, bf16[32,2048]{1,0:T(8,128)(2,1)S(1)} %get-tuple-element.33.refs_1_, bf16[16,128]{1,0:T(8,128)(2,1)S(1)} %bitcast.10, f32[32,3584]{1,0:T(8,128)S(1)} %get-tuple-element.43.refs_3_, ...), custom_call_target="tpu_custom_call" | custom-call | flops 234881024 | bytes 7340032 | tf_op jit(solution)/shard_map/expand_send/pallas_call | solution.py:462
  45.7 0.1 collective-permute-start.10
  45.8 1.9 %expand_keep.1.keep = bf16[32,3584]{1,0:T(8,128)(2,1)S(1)} custom-call(s32[4]{0:T(128)S(1)} %pad_add_fusion.refs_0_.at, bf16[32,1024]{1,0:T(8,128)(2,1)S(1)} %get-tuple-element.49.x, f32[32,3584]{1,0:T(8,128)S(1)} %get-tuple-element.50.before, bf16[512,3584]{1,0:T(8,128)(2,1)S(1)} %get-tuple-element.45.refs_5_.refs_0_, ...), custom_call_target="tpu_custom_call" | custom-call | flops 234881024 | bytes 7340032 | tf_op jit(solution)/shard_map/expand_keep/pallas_call | solution.py:480
  47.7 0.0 collective-permute-done.10.received
  47.7 0.1 pair.1.refs_1_.refs_0_
  47.8 1.2 %collective-permute-start.11 = (bf16[32,3968]{1,0:T(8,128)(2,1)S(1)}, bf16[32,3968]{1,0:T(8,128)(2,1)S(1)}, u32[]{:S(2)}, u32[]{:S(2)}) collective-permute-start(bf16[32,3968]{1,0:T(8,128)(2,1)S(1)} %pair.1.refs_1_.refs_0_), channel_id=1, source_target_pairs={{0,8},{4,12},{8,0},{12,4},{1,9},{5,13},{9,1},{13,5},{2,10},{6,14},... | collective-permute-start | bytes 761864 | tf_op jit(solution)/shard_map/ppermute | solution.py:611
  49.0 6.0 %fetch.5 = (bf16[1792,2048]{1,0:T(8,128)(2,1)S(1)}, bf16[1792,2048]{1,0:T(8,128)(2,1)S(1)}, f32[8,128]{1,0:T(8,128)S(1)}) custom-call(s32[4]{0:T(128)S(1)} %pad_add_fusion.refs_0_.at, bf16[32,3968]{1,0:T(8,128)(2,1)S(1)} %pair.1.refs_1_.refs_0_, bf16[3584,2048]{1,0:T(8,128)(2,1)} %refs_3_.5, bf16[3584,2048]{1,0:T(8,128)(2,1)} %refs_3_.5), custom_call_target="tpu_custom_call" | custom-call | bytes 29360128 | tf_op jit(solution)/shard_map/fetch/pallas_call | solution.py:102
  55.1 1.4 %collective-permute-done.11.refs_1_ = bf16[32,3968]{1,0:T(8,128)(2,1)S(1)} collective-permute-done((bf16[32,3968]{1,0:T(8,128)(2,1)S(1)}, bf16[32,3968]{1,0:T(8,128)(2,1)S(1)}, u32[]{:S(2)}, u32[]{:S(2)}) %collective-permute-start.11) | collective-permute-done | bytes 253984 | tf_op jit(solution)/shard_map/ppermute | solution.py:611
  56.4 0.1 gated.1.hidden
  56.6 0.1 collective-permute-start.12
  56.6 1.4 %contract.1.refs_3_ = f32[32,2048]{1,0:T(8,128)S(1)} custom-call(bf16[32,1792]{1,0:T(8,128)(2,1)S(1)} %gated.1.hidden, bf16[1792,2048]{1,0:T(8,128)(2,1)S(1)} %get-tuple-element.54.w), custom_call_target="tpu_custom_call" | custom-call | flops 234881024 | bytes 7340032 | tf_op jit(solution)/shard_map/contract/pallas_call | solution.py:542
  58.0 0.0 collective-permute-done.12.refs_1_
  58.0 1.9 %contract_last.1 = (f32[8,2048]{1,0:T(8,128)S(1)}, bf16[8,2048]{1,0:T(8,128)(2,1)S(1)}, bf16[8,2048]{1,0:T(8,128)(2,1)S(1)}, bf16[8,2048]{1,0:T(8,128)(2,1)S(1)}) custom-call(s32[4]{0:T(128)S(1)} %pad_add_fusion.refs_0_.at, bf16[32,1792]{1,0:T(8,128)(2,1)S(1)} %collective-permute-done.12.refs_1_, bf16[1792,2048]{1,0:T(8,128)(2,1)S(1)} %get-tuple-element.53.refs_2_, ...), custom_call_target="tpu_custom_call" | custom-call | flops 234881024 | bytes 7340032 | tf_op jit(solution)/shard_map/contract_last/pallas_call | solution.py:579
  59.9 2.2 %collective-permute-start.13 = (bf16[8,2048]{1,0:T(8,128)(2,1)S(1)}, bf16[8,2048]{1,0:T(8,128)(2,1)S(1)}, u32[]{:S(2)}, u32[]{:S(2)}) collective-permute-start(bf16[8,2048]{1,0:T(8,128)(2,1)S(1)} %get-tuple-element.58), channel_id=1, source_target_pairs={{0,1},{1,0},{2,3},{3,2},{4,5},{5,4},{6,7},{7,6},{8,9},{9,8},{10,11... | collective-permute-start | bytes 98312 | tf_op jit(solution)/shard_map/ppermute | solution.py:611
  62.1 3.5 %collective-permute-start.14 = (bf16[8,2048]{1,0:T(8,128)(2,1)S(1)}, bf16[8,2048]{1,0:T(8,128)(2,1)S(1)}, u32[]{:S(2)}, u32[]{:S(2)}) collective-permute-start(bf16[8,2048]{1,0:T(8,128)(2,1)S(1)} %get-tuple-element.59), channel_id=1, source_target_pairs={{0,2},{1,3},{2,0},{3,1},{4,6},{5,7},{6,4},{7,5},{8,10},{9,11},{10,... | collective-permute-start | bytes 98312 | tf_op jit(solution)/shard_map/ppermute | solution.py:611
  65.6 0.0 collective-permute-start.15
  65.6 0.0 collective-permute-done.13
  65.6 2.6 %collective-permute-done.14 = bf16[8,2048]{1,0:T(8,128)(2,1)S(1)} collective-permute-done((bf16[8,2048]{1,0:T(8,128)(2,1)S(1)}, bf16[8,2048]{1,0:T(8,128)(2,1)S(1)}, u32[]{:S(2)}, u32[]{:S(2)}) %collective-permute-start.14) | collective-permute-done | bytes 32800 | tf_op jit(solution)/shard_map/ppermute | solution.py:611
  68.2 3.1 %collective-permute-done.15 = bf16[8,2048]{1,0:T(8,128)(2,1)S(1)} collective-permute-done((bf16[8,2048]{1,0:T(8,128)(2,1)S(1)}, bf16[8,2048]{1,0:T(8,128)(2,1)S(1)}, u32[]{:S(2)}, u32[]{:S(2)}) %collective-permute-start.15) | collective-permute-done | bytes 32800 | tf_op jit(solution)/shard_map/ppermute | solution.py:611
  71.3 0.6 add_convert_fusion
  (5 shorter events, 0.1 us)
Async XLA Ops:
  0.0 8.3 %copy-start.1 = (s32[8]{0:T(128)S(1)}, s32[8]{0:T(128)}, u32[]{:S(2)}) copy-start(s32[8]{0:T(128)} %param.24) | copy-start | bytes 100
  0.0 8.6 %copy-start.2 = (s32[8]{0:T(128)S(1)}, s32[8]{0:T(128)}, u32[]{:S(2)}) copy-start(s32[8]{0:T(128)} %param.25) | copy-start | bytes 100
  5.2 9.0 %collective-permute-start.1 = (bf16[32,2560]{1,0:T(8,128)(2,1)S(1)}, bf16[32,2560]{1,0:T(8,128)(2,1)S(1)}, u32[]{:S(2)}, u32[]{:S(2)}) collective-permute-start(bf16[32,2560]{1,0:T(8,128)(2,1)S(1)} %get-tuple-element.34.refs_1_.refs_5_), channel_id=1, source_target_pairs={{0,4},{4,0},{8,12},{12,8},{1,5},{5,1},{9,13},{13,9},{2,6},{6,2},{1... | collective-permute-start | bytes 491528 | tf_op jit(solution)/shard_map/ppermute | solution.py:611
  5.7 8.2 %collective-permute-start = (bf16[32,2560]{1,0:T(8,128)(2,1)S(1)}, bf16[32,2560]{1,0:T(8,128)(2,1)S(1)}, u32[]{:S(2)}, u32[]{:S(2)}) collective-permute-start(bf16[32,2560]{1,0:T(8,128)(2,1)S(1)} %get-tuple-element.34.refs_1_.refs_5_), channel_id=1, source_target_pairs={{0,8},{4,12},{8,0},{12,4},{1,9},{5,13},{9,1},{13,5},{2,10},{6,14},... | collective-permute-start | bytes 491528 | tf_op jit(solution)/shard_map/ppermute | solution.py:611
  14.0 1.5 %collective-permute-start.2 = (bf16[32,2560]{1,0:T(8,128)(2,1)S(1)}, bf16[32,2560]{1,0:T(8,128)(2,1)S(1)}, u32[]{:S(2)}, u32[]{:S(2)}) collective-permute-start(bf16[32,2560]{1,0:T(8,128)(2,1)S(1)} %hold.2.refs_6_), channel_id=1, source_target_pairs={{0,4},{4,0},{8,12},{12,8},{1,5},{5,1},{9,13},{13,9},{2,6},{6,2},{1... | collective-permute-start | bytes 491528 | tf_op jit(solution)/shard_map/ppermute | solution.py:611
  19.5 6.2 %collective-permute-start.3 = (bf16[32,2432]{1,0:T(8,128)(2,1)S(1)}, bf16[32,2432]{1,0:T(8,128)(2,1)S(1)}, u32[]{:S(2)}, u32[]{:S(2)}) collective-permute-start(bf16[32,2432]{1,0:T(8,128)(2,1)S(1)} %get-tuple-element.38.refs_1_.refs_3_), channel_id=1, source_target_pairs={{0,8},{4,12},{8,0},{12,4},{1,9},{5,13},{9,1},{13,5},{2,10},{6,14},... | collective-permute-start | bytes 466952 | tf_op jit(solution)/shard_map/ppermute | solution.py:611
  20.4 5.5 %collective-permute-start.4 = (bf16[32,2432]{1,0:T(8,128)(2,1)S(1)}, bf16[32,2432]{1,0:T(8,128)(2,1)S(1)}, u32[]{:S(2)}, u32[]{:S(2)}) collective-permute-start(bf16[32,2432]{1,0:T(8,128)(2,1)S(1)} %get-tuple-element.38.refs_1_.refs_3_), channel_id=1, source_target_pairs={{0,4},{4,0},{8,12},{12,8},{1,5},{5,1},{9,13},{13,9},{2,6},{6,2},{1... | collective-permute-start | bytes 466952 | tf_op jit(solution)/shard_map/ppermute | solution.py:611
  25.7 1.4 %collective-permute-start.5 = (bf16[32,2432]{1,0:T(8,128)(2,1)S(1)}, bf16[32,2432]{1,0:T(8,128)(2,1)S(1)}, u32[]{:S(2)}, u32[]{:S(2)}) collective-permute-start(bf16[32,2432]{1,0:T(8,128)(2,1)S(1)} %hold.3.refs_4_), channel_id=1, source_target_pairs={{0,4},{4,0},{8,12},{12,8},{1,5},{5,1},{9,13},{13,9},{2,6},{6,2},{1... | collective-permute-start | bytes 466952 | tf_op jit(solution)/shard_map/ppermute | solution.py:611
  29.7 10.3 %copy-start = (bf16[2048]{0:T(1024)(128)(2,1)S(1)}, bf16[2048]{0:T(1024)(128)(2,1)}, u32[]{:S(2)}) copy-start(bf16[2048]{0:T(1024)(128)(2,1)} %param.15) | copy-start | bytes 12292
  29.8 4.3 %collective-permute-start.6 = (bf16[32,1024]{1,0:T(8,128)(2,1)S(1)}, bf16[32,1024]{1,0:T(8,128)(2,1)S(1)}, u32[]{:S(2)}, u32[]{:S(2)}) collective-permute-start(bf16[32,1024]{1,0:T(8,128)(2,1)S(1)} %get-tuple-element.42.one), channel_id=1, source_target_pairs={{0,1},{1,0},{2,3},{3,2},{4,5},{5,4},{6,7},{7,6},{8,9},{9,8},{10,11... | collective-permute-start | bytes 196616 | tf_op jit(solution)/shard_map/ppermute | solution.py:611
  32.2 4.5 %collective-permute-start.8 = (bf16[32,1024]{1,0:T(8,128)(2,1)S(1)}, bf16[32,1024]{1,0:T(8,128)(2,1)S(1)}, u32[]{:S(2)}, u32[]{:S(2)}) collective-permute-start(bf16[32,1024]{1,0:T(8,128)(2,1)S(1)} %output_second.1.one), channel_id=1, source_target_pairs={{0,1},{1,0},{2,3},{3,2},{4,5},{5,4},{6,7},{7,6},{8,9},{9,8},{10,11... | collective-permute-start | bytes 196616 | tf_op jit(solution)/shard_map/ppermute | solution.py:611
  34.1 5.9 %collective-permute-start.7 = (bf16[32,1024]{1,0:T(8,128)(2,1)S(1)}, bf16[32,1024]{1,0:T(8,128)(2,1)S(1)}, u32[]{:S(2)}, u32[]{:S(2)}) collective-permute-start(bf16[32,1024]{1,0:T(8,128)(2,1)S(1)} %add.41.refs_6_), channel_id=1, source_target_pairs={{0,2},{1,3},{2,0},{3,1},{4,6},{5,7},{6,4},{7,5},{8,10},{9,11},{10,... | collective-permute-start | bytes 196616 | tf_op jit(solution)/shard_map/ppermute | solution.py:611
  36.8 7.0 %collective-permute-start.9 = (bf16[32,1024]{1,0:T(8,128)(2,1)S(1)}, bf16[32,1024]{1,0:T(8,128)(2,1)S(1)}, u32[]{:S(2)}, u32[]{:S(2)}) collective-permute-start(bf16[32,1024]{1,0:T(8,128)(2,1)S(1)} %add.42.refs_8_), channel_id=1, source_target_pairs={{0,2},{1,3},{2,0},{3,1},{4,6},{5,7},{6,4},{7,5},{8,10},{9,11},{10,... | collective-permute-start | bytes 196616 | tf_op jit(solution)/shard_map/ppermute | solution.py:611
  45.7 2.0 %collective-permute-start.10 = (bf16[32,3968]{1,0:T(8,128)(2,1)S(1)}, bf16[32,3968]{1,0:T(8,128)(2,1)S(1)}, u32[]{:S(2)}, u32[]{:S(2)}) collective-permute-start(bf16[32,3968]{1,0:T(8,128)(2,1)S(1)} %get-tuple-element.51.stats), channel_id=1, source_target_pairs={{0,4},{4,0},{8,12},{12,8},{1,5},{5,1},{9,13},{13,9},{2,6},{6,2},{1... | collective-permute-start | bytes 761864 | tf_op jit(solution)/shard_map/ppermute | solution.py:611
  47.8 8.6 %collective-permute-start.11 = (bf16[32,3968]{1,0:T(8,128)(2,1)S(1)}, bf16[32,3968]{1,0:T(8,128)(2,1)S(1)}, u32[]{:S(2)}, u32[]{:S(2)}) collective-permute-start(bf16[32,3968]{1,0:T(8,128)(2,1)S(1)} %pair.1.refs_1_.refs_0_), channel_id=1, source_target_pairs={{0,8},{4,12},{8,0},{12,4},{1,9},{5,13},{9,1},{13,5},{2,10},{6,14},... | collective-permute-start | bytes 761864 | tf_op jit(solution)/shard_map/ppermute | solution.py:611
  56.6 1.4 %collective-permute-start.12 = (bf16[32,1792]{1,0:T(8,128)(2,1)S(1)}, bf16[32,1792]{1,0:T(8,128)(2,1)S(1)}, u32[]{:S(2)}, u32[]{:S(2)}) collective-permute-start(bf16[32,1792]{1,0:T(8,128)(2,1)S(1)} %gated.1.hidden), channel_id=1, source_target_pairs={{0,4},{4,0},{8,12},{12,8},{1,5},{5,1},{9,13},{13,9},{2,6},{6,2},{1... | collective-permute-start | bytes 344072 | tf_op jit(solution)/shard_map/ppermute | solution.py:611
  59.9 5.7 %collective-permute-start.13 = (bf16[8,2048]{1,0:T(8,128)(2,1)S(1)}, bf16[8,2048]{1,0:T(8,128)(2,1)S(1)}, u32[]{:S(2)}, u32[]{:S(2)}) collective-permute-start(bf16[8,2048]{1,0:T(8,128)(2,1)S(1)} %get-tuple-element.58), channel_id=1, source_target_pairs={{0,1},{1,0},{2,3},{3,2},{4,5},{5,4},{6,7},{7,6},{8,9},{9,8},{10,11... | collective-permute-start | bytes 98312 | tf_op jit(solution)/shard_map/ppermute | solution.py:611
  62.1 6.1 %collective-permute-start.14 = (bf16[8,2048]{1,0:T(8,128)(2,1)S(1)}, bf16[8,2048]{1,0:T(8,128)(2,1)S(1)}, u32[]{:S(2)}, u32[]{:S(2)}) collective-permute-start(bf16[8,2048]{1,0:T(8,128)(2,1)S(1)} %get-tuple-element.59), channel_id=1, source_target_pairs={{0,2},{1,3},{2,0},{3,1},{4,6},{5,7},{6,4},{7,5},{8,10},{9,11},{10,... | collective-permute-start | bytes 98312 | tf_op jit(solution)/shard_map/ppermute | solution.py:611
  65.6 5.7 %collective-permute-start.15 = (bf16[8,2048]{1,0:T(8,128)(2,1)S(1)}, bf16[8,2048]{1,0:T(8,128)(2,1)S(1)}, u32[]{:S(2)}, u32[]{:S(2)}) collective-permute-start(bf16[8,2048]{1,0:T(8,128)(2,1)S(1)} %get-tuple-element.60), channel_id=1, source_target_pairs={{0,3},{1,2},{2,1},{3,0},{4,7},{5,6},{6,5},{7,4},{8,11},{9,10},{10,... | collective-permute-start | bytes 98312 | tf_op jit(solution)/shard_map/ppermute | solution.py:611

commit v5 on v4

--- a/solution.py
+++ b/solution.py
@@ -625,8 +625,8 @@
     return parts
 
 
-def summed(x, axis):
-    *bits, last = bits_of(axis)
+def summed(x, axis, order):
+    *bits, last = bits_of(axis)[::order]
     for bit in bits:
         x = add(x, swap(x, axis, bit))
     return x, swap(x, axis, last)
@@ -667,7 +667,7 @@
         at, gathered(value, "wide", token), w_out, Part(w_gate, half + quarter, quarter)
     )
     out_1 = output_second(attended, w_out)
-    parts_0, parts_1 = summed(out_0, "head"), summed(out_1, "head")
+    parts_0, parts_1 = summed(out_0, "head", 1), summed(out_1, "head", -1)
     send, keep, resid_0, squares, up_1 = expand_first(
         at, own, gain, parts_0, gate_0, up_0, Part(w_up, half, half)
     )

time: 72.1 us -> 71.2 us (0.988)
  starting transfers between devices: 19.4 us -> 17.1 us
  waiting for transfers between devices: 11.3 us -> 12.7 us
    ppermute x16, starting transfers between devices: 19.4 us -> 17.1 us  [swap(): return lax.ppermute(x, axis, [(i, i ^ bit) for i in range(n)])]
    ppermute x16, waiting for transfers between devices: 11.3 us -> 12.7 us  [swap(): return lax.ppermute(x, axis, [(i, i ^ bit) for i in range(n)])]
  transfers between devices with their start and end apart: 16 -> 16, of which waited for: 8 -> 8; matrix products, arithmetic and copies ran while one was open for 1% -> 1% of each run, Pallas kernels for 33% -> 34%
where the time goes in v5:
time: 71.2 us; the launch traced here: 71 us
  Pallas kernels  39.9 us (56%)
  starting transfers between devices  17.1 us (24%)
  waiting for transfers between devices  12.7 us (18%)
  other arithmetic  1.02 us (1%)
    ppermute x16, starting transfers between devices, swap(): return lax.ppermute(x, axis, [(i, i ^ bit) for i in range(n)])  17.1 us
    pallas_call x3, Pallas kernels, fetch(): pl.pallas_call(lambda *refs: fetch_kernel(wanted, len(after), *refs), in_...  16.1 us
    ppermute x16, waiting for transfers between devices, swap(): return lax.ppermute(x, axis, [(i, i ^ bit) for i in range(n)])  12.7 us
    pallas_call x1, Pallas kernels, project(): pl.pallas_call(lambda *refs: project_kernel(chunks, *refs), in_specs=[SME...  5.11 us
    pallas_call x1, Pallas kernels, attend(): pl.pallas_call(lambda *refs: attend_kernel(len(parts), part, *refs), in_s...  4.09 us
    pallas_call x1, Pallas kernels, expand_first(): pl.pallas_call(lambda *refs: expand_first_kernel(len(parts), part, *refs)...  3.79 us
    pallas_call x1, Pallas kernels, output_first(): pl.pallas_call(lambda *refs: output_first_kernel(len(values), part, *refs...  2.67 us
    pallas_call x1, Pallas kernels, contract_last(): pl.pallas_call(lambda *refs: contract_last_kernel(n, *refs), in_specs=[SM...  1.94 us
  transfers between devices with their start and end apart: 16, of which 8 were waited for; matrix products, arithmetic and copies ran while one was open for 1% of the time, Pallas kernels for 34%

profile of v5, /device:TPU:0, one launch (start us, length us, event | category | flops | bytes accessed | tf_op | source)
XLA Modules:
  0.0 71.0 jit_solution(9453552894886739422)
XLA Ops:
  0.0 0.0 copy-start.1
  0.0 0.0 copy-start.2
  0.0 0.1 pad_add_fusion.refs_0_.at
  0.1 5.1 %project.1 = (bf16[32,2560]{1,0:T(8,128)(2,1)S(1)}, bf16[32,2048]{1,0:T(8,128)(2,1)S(1)}) custom-call(s32[4]{0:T(128)S(1)} %pad_add_fusion.refs_0_.at, bf16[32,8192]{1,0:T(8,128)(2,1)} %refs_1_.1, bf16[64,128]{1,0:T(8,128)(2,1)} %bitcast.12, bf16[2048,2048]{1,0:T(8,128)(2,1)} %refs_3_.3, bf16[2048,256]{1,0:T(8,128)(2,1)} %refs_4_.2, bf16[2048,256]{1,0:T(8,128)(2,1)} %refs_5_.2), custom_call_target="tpu_custom_call" | custom-call | flops 335544320 | bytes 10485760 | tf_op jit(solution)/shard_map/project/pallas_call | solution.py:186
  5.2 0.5 collective-permute-start.1
  5.7 2.6 %collective-permute-start = (bf16[32,2560]{1,0:T(8,128)(2,1)S(1)}, bf16[32,2560]{1,0:T(8,128)(2,1)S(1)}, u32[]{:S(2)}, u32[]{:S(2)}) collective-permute-start(bf16[32,2560]{1,0:T(8,128)(2,1)S(1)} %get-tuple-element.34.refs_1_.refs_5_), channel_id=1, source_target_pairs={{0,8},{4,12},{8,0},{12,4},{1,9},{5,13},{9,1},{13,5},{2,10},{6,14},... | collective-permute-start | bytes 491528 | tf_op jit(solution)/shard_map/ppermute | solution.py:611
  8.3 0.0 copy-done.1
  8.3 0.1 add_convert_fusion.1
  8.4 0.1 convert_element_type.24
  8.5 0.1 fusion
  8.6 0.0 copy-done.2
  8.6 0.1 concatenate.10.refs_2_.refs_0_
  8.7 0.1 pad_maximum_fusion
  8.8 5.1 %fetch.3 = (bf16[16,512,256]{2,1,0:T(8,128)(2,1)S(1)}, bf16[1024,3584]{1,0:T(8,128)(2,1)S(1)}, f32[8,128]{1,0:T(8,128)S(1)}) custom-call(s32[4]{0:T(128)S(1)} %pad_add_fusion.refs_0_.at, bf16[32,2560]{1,0:T(8,128)(2,1)S(1)} %get-tuple-element.34.refs_1_.refs_5_, s32[20]{0:T(128)S(1)} %concatenate.10.refs_2_.refs_0_, ...), custom_call_target="tpu_custom_call" | custom-call | bytes 23068672 | tf_op jit(solution)/shard_map/fetch/pallas_call | solution.py:102
  13.9 0.0 collective-permute-done.__0_
  14.0 0.2 collective-permute-start.2
  14.2 0.0 collective-permute-done.1.refs_7_
  14.2 1.2 %collective-permute-done.2.refs_8_ = bf16[32,2560]{1,0:T(8,128)(2,1)S(1)} collective-permute-done((bf16[32,2560]{1,0:T(8,128)(2,1)S(1)}, bf16[32,2560]{1,0:T(8,128)(2,1)S(1)}, u32[]{:S(2)}, u32[]{:S(2)}) %collective-permute-start.2) | collective-permute-done | bytes 163872 | tf_op jit(solution)/shard_map/ppermute | solution.py:611
  15.4 4.1 %attend.1 = (bf16[32,2432]{1,0:T(8,128)(2,1)S(1)}, bf16[2048,2048]{1,0:T(8,128)(2,1)S(1)}) custom-call(s32[20]{0:T(128)S(1)} %concatenate.10.refs_2_.refs_0_, f32[32,128]{1,0:T(8,128)S(1)} %get-tuple-element.64.refs_3_.refs_1_, f32[32,128]{1,0:T(8,128)S(1)} %get-tuple-element.65.refs_4_.refs_2_, bf16[2,8,512,256]{3,2,1,0:T(8,128)(2,1)S(1)} %bitcast.8, ...), custom_call_target="tpu_custom_call" | custom-call | flops 134217728 | bytes 4194304 | tf_op jit(solution)/shard_map/attend/pallas_call | solution.py:305
  19.5 0.9 %collective-permute-start.3 = (bf16[32,2432]{1,0:T(8,128)(2,1)S(1)}, bf16[32,2432]{1,0:T(8,128)(2,1)S(1)}, u32[]{:S(2)}, u32[]{:S(2)}) collective-permute-start(bf16[32,2432]{1,0:T(8,128)(2,1)S(1)} %get-tuple-element.38.refs_1_.refs_3_), channel_id=1, source_target_pairs={{0,8},{4,12},{8,0},{12,4},{1,9},{5,13},{9,1},{13,5},{2,10},{6,14},... | collective-permute-start | bytes 466952 | tf_op jit(solution)/shard_map/ppermute | solution.py:611
  20.4 0.0 collective-permute-start.4
  20.4 4.9 %fetch.4 = (bf16[1024,3584]{1,0:T(8,128)(2,1)S(1)}, bf16[512,3584]{1,0:T(8,128)(2,1)S(1)}, f32[8,128]{1,0:T(8,128)S(1)}) custom-call(s32[4]{0:T(128)S(1)} %pad_add_fusion.refs_0_.at, bf16[32,2432]{1,0:T(8,128)(2,1)S(1)} %get-tuple-element.38.refs_1_.refs_3_, bf16[2048,3584]{1,0:T(8,128)(2,1)} %refs_5_.3, bf16[2048,3584]{1,0:T(8,128)(2,1)} %refs_2_.4), custom_call_target="tpu_custom_call" | custom-call | bytes 22020096 | tf_op jit(solution)/shard_map/fetch/pallas_call | solution.py:102
  25.4 0.3 collective-permute-done.3.__0_
  25.7 0.3 collective-permute-start.5
  25.9 0.0 collective-permute-done.4.refs_5_
  26.0 1.1 %collective-permute-done.5.refs_6_ = bf16[32,2432]{1,0:T(8,128)(2,1)S(1)} collective-permute-done((bf16[32,2432]{1,0:T(8,128)(2,1)S(1)}, bf16[32,2432]{1,0:T(8,128)(2,1)S(1)}, u32[]{:S(2)}, u32[]{:S(2)}) %collective-permute-start.5) | collective-permute-done | bytes 155680 | tf_op jit(solution)/shard_map/ppermute | solution.py:611
  27.1 2.7 %output_first.1 = (bf16[32,1024]{1,0:T(8,128)(2,1)S(1)}, bf16[32,2048]{1,0:T(8,128)(2,1)S(1)}, bf16[512,3584]{1,0:T(8,128)(2,1)S(1)}) custom-call(s32[4]{0:T(128)S(1)} %pad_add_fusion.refs_0_.at, bf16[2048,2048]{1,0:T(8,128)(2,1)S(1)} %get-tuple-element.40.refs_1_.w, bf16[2048,3584]{1,0:T(8,128)(2,1)} %refs_2_.4, ...), custom_call_target="tpu_custom_call" | custom-call | flops 268435456 | bytes 8388608 | tf_op jit(solution)/shard_map/output_first/pallas_call | solution.py:356
  29.7 0.0 copy-start
  29.8 1.6 %collective-permute-start.6 = (bf16[32,1024]{1,0:T(8,128)(2,1)S(1)}, bf16[32,1024]{1,0:T(8,128)(2,1)S(1)}, u32[]{:S(2)}, u32[]{:S(2)}) collective-permute-start(bf16[32,1024]{1,0:T(8,128)(2,1)S(1)} %get-tuple-element.42.one), channel_id=1, source_target_pairs={{0,1},{1,0},{2,3},{3,2},{4,5},{5,4},{6,7},{7,6},{8,9},{9,8},{10,11... | collective-permute-start | bytes 196616 | tf_op jit(solution)/shard_map/ppermute | solution.py:611
  31.4 0.8 %output_second.1.one = bf16[32,1024]{1,0:T(8,128)(2,1)S(1)} custom-call(bf16[32,2048]{1,0:T(8,128)(2,1)S(1)} %get-tuple-element.48.x, bf16[2048,2048]{1,0:T(8,128)(2,1)S(1)} %get-tuple-element.40.refs_1_.w), custom_call_target="tpu_custom_call" | custom-call | flops 268435456 | bytes 8388608 | tf_op jit(solution)/shard_map/output_second/pallas_call | solution.py:374
  32.2 2.6 %collective-permute-start.8 = (bf16[32,1024]{1,0:T(8,128)(2,1)S(1)}, bf16[32,1024]{1,0:T(8,128)(2,1)S(1)}, u32[]{:S(2)}, u32[]{:S(2)}) collective-permute-start(bf16[32,1024]{1,0:T(8,128)(2,1)S(1)} %output_second.1.one), channel_id=1, source_target_pairs={{0,2},{1,3},{2,0},{3,1},{4,6},{5,7},{6,4},{7,5},{8,10},{9,11},{10,... | collective-permute-start | bytes 196616 | tf_op jit(solution)/shard_map/ppermute | solution.py:611
  34.8 0.0 collective-permute-done.6.two
  34.9 2.4 %collective-permute-start.7 = (bf16[32,1024]{1,0:T(8,128)(2,1)S(1)}, bf16[32,1024]{1,0:T(8,128)(2,1)S(1)}, u32[]{:S(2)}, u32[]{:S(2)}) collective-permute-start(bf16[32,1024]{1,0:T(8,128)(2,1)S(1)} %add.41.refs_6_), channel_id=1, source_target_pairs={{0,2},{1,3},{2,0},{3,1},{4,6},{5,7},{6,4},{7,5},{8,10},{9,11},{10,... | collective-permute-start | bytes 196616 | tf_op jit(solution)/shard_map/ppermute | solution.py:611
  37.3 2.4 %collective-permute-done.8.two = bf16[32,1024]{1,0:T(8,128)(2,1)S(1)} collective-permute-done((bf16[32,1024]{1,0:T(8,128)(2,1)S(1)}, bf16[32,1024]{1,0:T(8,128)(2,1)S(1)}, u32[]{:S(2)}, u32[]{:S(2)}) %collective-permute-start.8) | collective-permute-done | bytes 65568 | tf_op jit(solution)/shard_map/ppermute | solution.py:611
  39.7 0.1 collective-permute-start.9
  39.7 1.6 %collective-permute-done.7.refs_7_ = bf16[32,1024]{1,0:T(8,128)(2,1)S(1)} collective-permute-done((bf16[32,1024]{1,0:T(8,128)(2,1)S(1)}, bf16[32,1024]{1,0:T(8,128)(2,1)S(1)}, u32[]{:S(2)}, u32[]{:S(2)}) %collective-permute-start.7) | collective-permute-done | bytes 65568 | tf_op jit(solution)/shard_map/ppermute | solution.py:611
  41.3 0.0 copy-done
  41.3 3.8 %expand_first.1 = (f32[32,3584]{1,0:T(8,128)S(1)}, f32[32,3584]{1,0:T(8,128)S(1)}, f32[32,1024]{1,0:T(8,128)S(1)}, f32[32,128]{1,0:T(8,128)S(1)}, bf16[1024,3584]{1,0:T(8,128)(2,1)S(1)}) custom-call(s32[4]{0:T(128)S(1)} %pad_add_fusion.refs_0_.at, bf16[32,2048]{1,0:T(8,128)(2,1)S(1)} %get-tuple-element.33.refs_1_, bf16[16,128]{1,0:T(8,128)(2,1)S(1)} %bitcast.9, ...), custom_call_target="tpu_custom_call" | custom-call | flops 469762048 | bytes 14680064 | tf_op jit(solution)/shard_map/expand_first/pallas_call | solution.py:428
  45.1 0.0 collective-permute-done.9.refs_9_
  45.1 1.9 %expand_send.1 = (bf16[32,3968]{1,0:T(8,128)(2,1)S(1)}, f32[32,1024]{1,0:T(8,128)S(1)}, bf16[32,1024]{1,0:T(8,128)(2,1)S(1)}) custom-call(s32[4]{0:T(128)S(1)} %pad_add_fusion.refs_0_.at, bf16[32,2048]{1,0:T(8,128)(2,1)S(1)} %get-tuple-element.33.refs_1_, bf16[16,128]{1,0:T(8,128)(2,1)S(1)} %bitcast.10, f32[32,3584]{1,0:T(8,128)S(1)} %get-tuple-element.43.refs_3_, ...), custom_call_target="tpu_custom_call" | custom-call | flops 234881024 | bytes 7340032 | tf_op jit(solution)/shard_map/expand_send/pallas_call | solution.py:462
  47.1 0.1 collective-permute-start.10
  47.1 1.9 %expand_keep.1.keep = bf16[32,3584]{1,0:T(8,128)(2,1)S(1)} custom-call(s32[4]{0:T(128)S(1)} %pad_add_fusion.refs_0_.at, bf16[32,1024]{1,0:T(8,128)(2,1)S(1)} %get-tuple-element.49.x, f32[32,3584]{1,0:T(8,128)S(1)} %get-tuple-element.50.before, bf16[512,3584]{1,0:T(8,128)(2,1)S(1)} %get-tuple-element.45.refs_5_.refs_0_, ...), custom_call_target="tpu_custom_call" | custom-call | flops 234881024 | bytes 7340032 | tf_op jit(solution)/shard_map/expand_keep/pallas_call | solution.py:480
  49.0 0.0 collective-permute-done.10.received
  49.0 0.1 pair.1.refs_1_.refs_0_
  49.1 1.2 %collective-permute-start.11 = (bf16[32,3968]{1,0:T(8,128)(2,1)S(1)}, bf16[32,3968]{1,0:T(8,128)(2,1)S(1)}, u32[]{:S(2)}, u32[]{:S(2)}) collective-permute-start(bf16[32,3968]{1,0:T(8,128)(2,1)S(1)} %pair.1.refs_1_.refs_0_), channel_id=1, source_target_pairs={{0,8},{4,12},{8,0},{12,4},{1,9},{5,13},{9,1},{13,5},{2,10},{6,14},... | collective-permute-start | bytes 761864 | tf_op jit(solution)/shard_map/ppermute | solution.py:611
  50.4 6.0 %fetch.5 = (bf16[1792,2048]{1,0:T(8,128)(2,1)S(1)}, bf16[1792,2048]{1,0:T(8,128)(2,1)S(1)}, f32[8,128]{1,0:T(8,128)S(1)}) custom-call(s32[4]{0:T(128)S(1)} %pad_add_fusion.refs_0_.at, bf16[32,3968]{1,0:T(8,128)(2,1)S(1)} %pair.1.refs_1_.refs_0_, bf16[3584,2048]{1,0:T(8,128)(2,1)} %refs_3_.5, bf16[3584,2048]{1,0:T(8,128)(2,1)} %refs_3_.5), custom_call_target="tpu_custom_call" | custom-call | bytes 29360128 | tf_op jit(solution)/shard_map/fetch/pallas_call | solution.py:102
  56.4 1.3 %collective-permute-done.11.refs_1_ = bf16[32,3968]{1,0:T(8,128)(2,1)S(1)} collective-permute-done((bf16[32,3968]{1,0:T(8,128)(2,1)S(1)}, bf16[32,3968]{1,0:T(8,128)(2,1)S(1)}, u32[]{:S(2)}, u32[]{:S(2)}) %collective-permute-start.11) | collective-permute-done | bytes 253984 | tf_op jit(solution)/shard_map/ppermute | solution.py:611
  57.7 0.1 gated.1.hidden
  57.9 0.1 collective-permute-start.12
  57.9 1.4 %contract.1.refs_3_ = f32[32,2048]{1,0:T(8,128)S(1)} custom-call(bf16[32,1792]{1,0:T(8,128)(2,1)S(1)} %gated.1.hidden, bf16[1792,2048]{1,0:T(8,128)(2,1)S(1)} %get-tuple-element.54.w), custom_call_target="tpu_custom_call" | custom-call | flops 234881024 | bytes 7340032 | tf_op jit(solution)/shard_map/contract/pallas_call | solution.py:542
  59.3 0.0 collective-permute-done.12.refs_1_
  59.3 1.9 %contract_last.1 = (f32[8,2048]{1,0:T(8,128)S(1)}, bf16[8,2048]{1,0:T(8,128)(2,1)S(1)}, bf16[8,2048]{1,0:T(8,128)(2,1)S(1)}, bf16[8,2048]{1,0:T(8,128)(2,1)S(1)}) custom-call(s32[4]{0:T(128)S(1)} %pad_add_fusion.refs_0_.at, bf16[32,1792]{1,0:T(8,128)(2,1)S(1)} %collective-permute-done.12.refs_1_, bf16[1792,2048]{1,0:T(8,128)(2,1)S(1)} %get-tuple-element.53.refs_2_, ...), custom_call_target="tpu_custom_call" | custom-call | flops 234881024 | bytes 7340032 | tf_op jit(solution)/shard_map/contract_last/pallas_call | solution.py:579
  61.2 0.5 collective-permute-start.13
  61.7 3.0 %collective-permute-start.14 = (bf16[8,2048]{1,0:T(8,128)(2,1)S(1)}, bf16[8,2048]{1,0:T(8,128)(2,1)S(1)}, u32[]{:S(2)}, u32[]{:S(2)}) collective-permute-start(bf16[8,2048]{1,0:T(8,128)(2,1)S(1)} %get-tuple-element.59), channel_id=1, source_target_pairs={{0,2},{1,3},{2,0},{3,1},{4,6},{5,7},{6,4},{7,5},{8,10},{9,11},{10,... | collective-permute-start | bytes 98312 | tf_op jit(solution)/shard_map/ppermute | solution.py:611
  64.7 1.0 %collective-permute-start.15 = (bf16[8,2048]{1,0:T(8,128)(2,1)S(1)}, bf16[8,2048]{1,0:T(8,128)(2,1)S(1)}, u32[]{:S(2)}, u32[]{:S(2)}) collective-permute-start(bf16[8,2048]{1,0:T(8,128)(2,1)S(1)} %get-tuple-element.60), channel_id=1, source_target_pairs={{0,3},{1,2},{2,1},{3,0},{4,7},{5,6},{6,5},{7,4},{8,11},{9,10},{10,... | collective-permute-start | bytes 98312 | tf_op jit(solution)/shard_map/ppermute | solution.py:611
  65.7 0.0 collective-permute-done.13
  65.7 0.9 %collective-permute-done.14 = bf16[8,2048]{1,0:T(8,128)(2,1)S(1)} collective-permute-done((bf16[8,2048]{1,0:T(8,128)(2,1)S(1)}, bf16[8,2048]{1,0:T(8,128)(2,1)S(1)}, u32[]{:S(2)}, u32[]{:S(2)}) %collective-permute-start.14) | collective-permute-done | bytes 32800 | tf_op jit(solution)/shard_map/ppermute | solution.py:611
  66.6 3.8 %collective-permute-done.15 = bf16[8,2048]{1,0:T(8,128)(2,1)S(1)} collective-permute-done((bf16[8,2048]{1,0:T(8,128)(2,1)S(1)}, bf16[8,2048]{1,0:T(8,128)(2,1)S(1)}, u32[]{:S(2)}, u32[]{:S(2)}) %collective-permute-start.15) | collective-permute-done | bytes 32800 | tf_op jit(solution)/shard_map/ppermute | solution.py:611
  70.4 0.6 add_convert_fusion
  (5 shorter events, 0.1 us)
Async XLA Ops:
  0.0 8.3 %copy-start.1 = (s32[8]{0:T(128)S(1)}, s32[8]{0:T(128)}, u32[]{:S(2)}) copy-start(s32[8]{0:T(128)} %param.24) | copy-start | bytes 100
  0.0 8.6 %copy-start.2 = (s32[8]{0:T(128)S(1)}, s32[8]{0:T(128)}, u32[]{:S(2)}) copy-start(s32[8]{0:T(128)} %param.25) | copy-start | bytes 100
  5.2 9.0 %collective-permute-start.1 = (bf16[32,2560]{1,0:T(8,128)(2,1)S(1)}, bf16[32,2560]{1,0:T(8,128)(2,1)S(1)}, u32[]{:S(2)}, u32[]{:S(2)}) collective-permute-start(bf16[32,2560]{1,0:T(8,128)(2,1)S(1)} %get-tuple-element.34.refs_1_.refs_5_), channel_id=1, source_target_pairs={{0,4},{4,0},{8,12},{12,8},{1,5},{5,1},{9,13},{13,9},{2,6},{6,2},{1... | collective-permute-start | bytes 491528 | tf_op jit(solution)/shard_map/ppermute | solution.py:611
  5.7 8.2 %collective-permute-start = (bf16[32,2560]{1,0:T(8,128)(2,1)S(1)}, bf16[32,2560]{1,0:T(8,128)(2,1)S(1)}, u32[]{:S(2)}, u32[]{:S(2)}) collective-permute-start(bf16[32,2560]{1,0:T(8,128)(2,1)S(1)} %get-tuple-element.34.refs_1_.refs_5_), channel_id=1, source_target_pairs={{0,8},{4,12},{8,0},{12,4},{1,9},{5,13},{9,1},{13,5},{2,10},{6,14},... | collective-permute-start | bytes 491528 | tf_op jit(solution)/shard_map/ppermute | solution.py:611
  14.0 1.5 %collective-permute-start.2 = (bf16[32,2560]{1,0:T(8,128)(2,1)S(1)}, bf16[32,2560]{1,0:T(8,128)(2,1)S(1)}, u32[]{:S(2)}, u32[]{:S(2)}) collective-permute-start(bf16[32,2560]{1,0:T(8,128)(2,1)S(1)} %hold.2.refs_6_), channel_id=1, source_target_pairs={{0,4},{4,0},{8,12},{12,8},{1,5},{5,1},{9,13},{13,9},{2,6},{6,2},{1... | collective-permute-start | bytes 491528 | tf_op jit(solution)/shard_map/ppermute | solution.py:611
  19.5 6.2 %collective-permute-start.3 = (bf16[32,2432]{1,0:T(8,128)(2,1)S(1)}, bf16[32,2432]{1,0:T(8,128)(2,1)S(1)}, u32[]{:S(2)}, u32[]{:S(2)}) collective-permute-start(bf16[32,2432]{1,0:T(8,128)(2,1)S(1)} %get-tuple-element.38.refs_1_.refs_3_), channel_id=1, source_target_pairs={{0,8},{4,12},{8,0},{12,4},{1,9},{5,13},{9,1},{13,5},{2,10},{6,14},... | collective-permute-start | bytes 466952 | tf_op jit(solution)/shard_map/ppermute | solution.py:611
  20.4 5.5 %collective-permute-start.4 = (bf16[32,2432]{1,0:T(8,128)(2,1)S(1)}, bf16[32,2432]{1,0:T(8,128)(2,1)S(1)}, u32[]{:S(2)}, u32[]{:S(2)}) collective-permute-start(bf16[32,2432]{1,0:T(8,128)(2,1)S(1)} %get-tuple-element.38.refs_1_.refs_3_), channel_id=1, source_target_pairs={{0,4},{4,0},{8,12},{12,8},{1,5},{5,1},{9,13},{13,9},{2,6},{6,2},{1... | collective-permute-start | bytes 466952 | tf_op jit(solution)/shard_map/ppermute | solution.py:611
  25.7 1.4 %collective-permute-start.5 = (bf16[32,2432]{1,0:T(8,128)(2,1)S(1)}, bf16[32,2432]{1,0:T(8,128)(2,1)S(1)}, u32[]{:S(2)}, u32[]{:S(2)}) collective-permute-start(bf16[32,2432]{1,0:T(8,128)(2,1)S(1)} %hold.3.refs_4_), channel_id=1, source_target_pairs={{0,4},{4,0},{8,12},{12,8},{1,5},{5,1},{9,13},{13,9},{2,6},{6,2},{1... | collective-permute-start | bytes 466952 | tf_op jit(solution)/shard_map/ppermute | solution.py:611
  29.7 11.6 %copy-start = (bf16[2048]{0:T(1024)(128)(2,1)S(1)}, bf16[2048]{0:T(1024)(128)(2,1)}, u32[]{:S(2)}) copy-start(bf16[2048]{0:T(1024)(128)(2,1)} %param.15) | copy-start | bytes 12292
  29.8 5.1 %collective-permute-start.6 = (bf16[32,1024]{1,0:T(8,128)(2,1)S(1)}, bf16[32,1024]{1,0:T(8,128)(2,1)S(1)}, u32[]{:S(2)}, u32[]{:S(2)}) collective-permute-start(bf16[32,1024]{1,0:T(8,128)(2,1)S(1)} %get-tuple-element.42.one), channel_id=1, source_target_pairs={{0,1},{1,0},{2,3},{3,2},{4,5},{5,4},{6,7},{7,6},{8,9},{9,8},{10,11... | collective-permute-start | bytes 196616 | tf_op jit(solution)/shard_map/ppermute | solution.py:611
  32.2 7.4 %collective-permute-start.8 = (bf16[32,1024]{1,0:T(8,128)(2,1)S(1)}, bf16[32,1024]{1,0:T(8,128)(2,1)S(1)}, u32[]{:S(2)}, u32[]{:S(2)}) collective-permute-start(bf16[32,1024]{1,0:T(8,128)(2,1)S(1)} %output_second.1.one), channel_id=1, source_target_pairs={{0,2},{1,3},{2,0},{3,1},{4,6},{5,7},{6,4},{7,5},{8,10},{9,11},{10,... | collective-permute-start | bytes 196616 | tf_op jit(solution)/shard_map/ppermute | solution.py:611
  34.9 6.5 %collective-permute-start.7 = (bf16[32,1024]{1,0:T(8,128)(2,1)S(1)}, bf16[32,1024]{1,0:T(8,128)(2,1)S(1)}, u32[]{:S(2)}, u32[]{:S(2)}) collective-permute-start(bf16[32,1024]{1,0:T(8,128)(2,1)S(1)} %add.41.refs_6_), channel_id=1, source_target_pairs={{0,2},{1,3},{2,0},{3,1},{4,6},{5,7},{6,4},{7,5},{8,10},{9,11},{10,... | collective-permute-start | bytes 196616 | tf_op jit(solution)/shard_map/ppermute | solution.py:611
  39.7 5.5 %collective-permute-start.9 = (bf16[32,1024]{1,0:T(8,128)(2,1)S(1)}, bf16[32,1024]{1,0:T(8,128)(2,1)S(1)}, u32[]{:S(2)}, u32[]{:S(2)}) collective-permute-start(bf16[32,1024]{1,0:T(8,128)(2,1)S(1)} %add.42.refs_8_), channel_id=1, source_target_pairs={{0,1},{1,0},{2,3},{3,2},{4,5},{5,4},{6,7},{7,6},{8,9},{9,8},{10,11... | collective-permute-start | bytes 196616 | tf_op jit(solution)/shard_map/ppermute | solution.py:611
  47.1 2.0 %collective-permute-start.10 = (bf16[32,3968]{1,0:T(8,128)(2,1)S(1)}, bf16[32,3968]{1,0:T(8,128)(2,1)S(1)}, u32[]{:S(2)}, u32[]{:S(2)}) collective-permute-start(bf16[32,3968]{1,0:T(8,128)(2,1)S(1)} %get-tuple-element.51.stats), channel_id=1, source_target_pairs={{0,4},{4,0},{8,12},{12,8},{1,5},{5,1},{9,13},{13,9},{2,6},{6,2},{1... | collective-permute-start | bytes 761864 | tf_op jit(solution)/shard_map/ppermute | solution.py:611
  49.1 8.6 %collective-permute-start.11 = (bf16[32,3968]{1,0:T(8,128)(2,1)S(1)}, bf16[32,3968]{1,0:T(8,128)(2,1)S(1)}, u32[]{:S(2)}, u32[]{:S(2)}) collective-permute-start(bf16[32,3968]{1,0:T(8,128)(2,1)S(1)} %pair.1.refs_1_.refs_0_), channel_id=1, source_target_pairs={{0,8},{4,12},{8,0},{12,4},{1,9},{5,13},{9,1},{13,5},{2,10},{6,14},... | collective-permute-start | bytes 761864 | tf_op jit(solution)/shard_map/ppermute | solution.py:611
  57.9 1.4 %collective-permute-start.12 = (bf16[32,1792]{1,0:T(8,128)(2,1)S(1)}, bf16[32,1792]{1,0:T(8,128)(2,1)S(1)}, u32[]{:S(2)}, u32[]{:S(2)}) collective-permute-start(bf16[32,1792]{1,0:T(8,128)(2,1)S(1)} %gated.1.hidden), channel_id=1, source_target_pairs={{0,4},{4,0},{8,12},{12,8},{1,5},{5,1},{9,13},{13,9},{2,6},{6,2},{1... | collective-permute-start | bytes 344072 | tf_op jit(solution)/shard_map/ppermute | solution.py:611
  61.2 4.5 %collective-permute-start.13 = (bf16[8,2048]{1,0:T(8,128)(2,1)S(1)}, bf16[8,2048]{1,0:T(8,128)(2,1)S(1)}, u32[]{:S(2)}, u32[]{:S(2)}) collective-permute-start(bf16[8,2048]{1,0:T(8,128)(2,1)S(1)} %get-tuple-element.58), channel_id=1, source_target_pairs={{0,1},{1,0},{2,3},{3,2},{4,5},{5,4},{6,7},{7,6},{8,9},{9,8},{10,11... | collective-permute-start | bytes 98312 | tf_op jit(solution)/shard_map/ppermute | solution.py:611
  61.7 4.9 %collective-permute-start.14 = (bf16[8,2048]{1,0:T(8,128)(2,1)S(1)}, bf16[8,2048]{1,0:T(8,128)(2,1)S(1)}, u32[]{:S(2)}, u32[]{:S(2)}) collective-permute-start(bf16[8,2048]{1,0:T(8,128)(2,1)S(1)} %get-tuple-element.59), channel_id=1, source_target_pairs={{0,2},{1,3},{2,0},{3,1},{4,6},{5,7},{6,4},{7,5},{8,10},{9,11},{10,... | collective-permute-start | bytes 98312 | tf_op jit(solution)/shard_map/ppermute | solution.py:611
  64.7 5.7 %collective-permute-start.15 = (bf16[8,2048]{1,0:T(8,128)(2,1)S(1)}, bf16[8,2048]{1,0:T(8,128)(2,1)S(1)}, u32[]{:S(2)}, u32[]{:S(2)}) collective-permute-start(bf16[8,2048]{1,0:T(8,128)(2,1)S(1)} %get-tuple-element.60), channel_id=1, source_target_pairs={{0,3},{1,2},{2,1},{3,0},{4,7},{5,6},{6,5},{7,4},{8,11},{9,10},{10,... | collective-permute-start | bytes 98312 | tf_op jit(solution)/shard_map/ppermute | solution.py:611

commit v6 on v3

--- a/solution.py
+++ b/solution.py
@@ -200,11 +200,8 @@
     )(at, in_hbm(tokens), in_hbm(gain.reshape(model // LANES, LANES)), in_hbm(wq), in_hbm(wk), in_hbm(wv))
 
 
-def attend_kernel(n, part, at, cos, sin, cache, source, *rest):
-    parts, (out, held, queries, total, stats_f, sems) = rest[:n], rest[n:]
-    copies = part.copies(at, source, held, sems)
-    for copy in copies:
-        copy.start()
+def attend_kernel(n, at, cos, sin, cache, *rest):
+    parts, (out, queries, total, stats_f) = rest[:n], rest[n:]
     rows, q_cols = queries.shape
     context, kv_cols = cache.shape[2:]
     kv_heads = kv_cols // HEAD_WIDTH
@@ -284,28 +281,25 @@
     out[:, :q_cols] = total[...].astype(bf16)
     for p, term in enumerate(thirds(stats_f[...])):
         out[:, q_cols + p * LANES : q_cols + (p + 1) * LANES] = term
-    for copy in copies:
-        copy.wait()
-
-
-def attend(at, cos, sin, cache, parts, part):
+
+
+def attend(at, cos, sin, cache, parts):
     rows, width = parts[0].shape
     q_cols = width - 2 * cache.shape[3]
     return pl.pallas_call(
-        lambda *refs: attend_kernel(len(parts), part, *refs),
-        in_specs=[SMEM] + [VMEM] * 3 + [HBM] + [VMEM] * len(parts),
-        out_specs=[VMEM, VMEM],
-        out_shape=[jax.ShapeDtypeStruct((rows, q_cols + 3 * LANES), bf16), part.out],
+        lambda *refs: attend_kernel(len(parts), *refs),
+        in_specs=[SMEM] + [VMEM] * (3 + len(parts)),
+        out_specs=VMEM,
+        out_shape=jax.ShapeDtypeStruct((rows, q_cols + 3 * LANES), bf16),
         scratch_shapes=[
             pltpu.VMEM((rows, q_cols), f32),
             pltpu.VMEM((rows, q_cols), f32),
             pltpu.VMEM((rows, LANES), f32),
-            pltpu.SemaphoreType.DMA((2 * PIECES,)),
         ],
         compiler_params=params(6),
         cost_estimate=cost(rows, cache),
         name="attend",
-    )(at, cos, sin, cache, in_hbm(part.array), *parts)
+    )(at, cos, sin, cache, *parts)
 
 
 def joined(ref, start):
@@ -341,7 +335,7 @@
     return pl.pallas_call(
         lambda *refs: output_first_kernel(len(values), *refs),
         in_specs=[VMEM] * (1 + len(values)),
-        out_specs=[VMEM, VMEM],
+        out_specs=[VMEM] * 2,
         out_shape=[
             jax.ShapeDtypeStruct((rows, half), bf16),
             jax.ShapeDtypeStruct((rows, w.shape[0]), bf16),
@@ -365,16 +359,38 @@
     )(attended, w)
 
 
-def half_of(side, x, wg, wu, out, before=None):
-    half = wg.shape[1] // 2
-    for base, w in ((0, wg), (half, wu)):
-        for start, size in blocks_of(half, 512):
-            cols = pl.ds(pl.multiple_of(side * half + start, LANES), size)
-            to = slice(base + start, base + start + size)
-            term = jnp.dot(x[...], w[:, cols], preferred_element_type=f32)
-            if before is not None:
-                term = before[:, to] + term
-            out[:, to] = term.astype(out.dtype)
+SLOTS = 3
+WIDE = 896
+
+
+def half_of(sides, x, row, wg, wu, held, sems):
+    count, half = x.shape[1], wg.shape[1] // 2
+    jobs = []
+    for side, out, before in sides:
+        for base, w in ((0, wg), (half, wu)):
+            for start, size in blocks_of(half, WIDE):
+                slot = len(jobs) % SLOTS
+                cols = pl.ds(pl.multiple_of(side * half + start, LANES), size)
+                copy = pltpu.make_async_copy(
+                    w.at[pl.ds(row, count), cols], held.at[slot, :, pl.ds(0, size)], sems.at[slot]
+                )
+                jobs.append((copy, slot, size, base + start, out, before))
+    for copy, *_ in jobs[: SLOTS - 1]:
+        copy.start()
+    for n, (copy, slot, size, to, out, before) in enumerate(jobs):
+        copy.wait()
+        if n + SLOTS - 1 < len(jobs):
+            jobs[n + SLOTS - 1][0].start()
+        term = jnp.dot(x[...], held[slot, :, :size], preferred_element_type=f32)
+        cols = slice(to, to + size)
+        if before is not None:
+            term = before[:, cols] + term
+        out[:, cols] = term.astype(out.dtype)
+
+
+def block_scratch(count, half):
+    width = max(size for _, size in blocks_of(half, WIDE))
+    return [pltpu.VMEM((SLOTS, count, width), bf16), pltpu.SemaphoreType.DMA((SLOTS,))]
 
 
 def residual(which, own, gain, parts, resid, x, gain_f):
@@ -391,82 +407,81 @@
     return square
 
 
-def expand_first_kernel(n, part, at, own, gain, wg, wu, _, source, *rest):
-    parts, (send, keep, resid, squares, held, x, gain_f, sems) = rest[:n], rest[n:]
-    copies = part.copies(at, source, held, sems)
-    for copy in copies:
-        copy.start()
+def expand_first_kernel(n, at, own, gain, wg, wu, *rest):
+    parts, (send, keep, resid, squares, x, gain_f, held, sems) = rest[:n], rest[n:]
     squares[...] = residual(0, own, gain, parts, resid, x, gain_f)
-    half_of(1 - at[2], x, wg, wu, send)
-    half_of(at[2], x, wg, wu, keep)
-    for copy in copies:
-        copy.wait()
-
-
-def expand_first(at, own, gain, parts, wg, wu, part, after):
+    half_of([(1 - at[2], send, None), (at[2], keep, None)], x, 0, wg, wu, held, sems)
+
+
+def expand_first(at, own, gain, parts, wg, wu):
     rows, depth = own.shape
     width = wg.shape[1]
     return pl.pallas_call(
-        lambda *refs: expand_first_kernel(len(parts), part, *refs),
-        in_specs=[SMEM] + [VMEM] * 4 + [ANY, HBM] + [VMEM] * len(parts),
-        out_specs=[VMEM] * 5,
+        lambda *refs: expand_first_kernel(len(parts), *refs),
+        in_specs=[SMEM] + [VMEM] * 2 + [ANY] * 2 + [VMEM] * len(parts),
+        out_specs=[VMEM] * 4,
         out_shape=[
             jax.ShapeDtypeStruct((rows, width), f32),
             jax.ShapeDtypeStruct((rows, width), f32),
             jax.ShapeDtypeStruct((rows, depth // 2), f32),
             jax.ShapeDtypeStruct((rows, LANES), f32),
-            part.out,
         ],
         scratch_shapes=[
             pltpu.VMEM((rows, depth // 2), bf16),
             pltpu.VMEM((depth // LANES, LANES), f32),
-            pltpu.SemaphoreType.DMA((2 * PIECES,)),
-        ],
-        compiler_params=params(4),
+        ]
+        + block_scratch(depth // 2, width // 2),
+        compiler_params=params(9),
         cost_estimate=cost(rows, wg, wu),
         name="expand_first",
-    )(at, own, gain, wg, wu, after, in_hbm(part.array), *parts)
-
-
-def expand_send_kernel(n, at, own, gain, wg, wu, before, squares, *rest):
-    parts, (out, resid, x, gain_f) = rest[:n], rest[n:]
+    )(at, own, gain, wg, wu, *parts)
+
+
+def expand_send_kernel(n, at, own, gain, before, squares, wg, wu, *rest):
+    parts, (out, resid, x, gain_f, held, sems) = rest[:n], rest[n:]
     square = squares[...] + residual(1, own, gain, parts, resid, x, gain_f)
     square = jnp.broadcast_to(jnp.sum(square, axis=1, keepdims=True), square.shape)
-    width = wg.shape[1]
+    width = wu.shape[1]
     for p, term in enumerate(thirds(square)):
         out[:, width + p * LANES : width + (p + 1) * LANES] = term
-    half_of(1 - at[2], x, wg, wu, out, before)
+    half_of([(1 - at[2], out, before)], x, x.shape[1], wg, wu, held, sems)
 
 
 def expand_send(at, own, gain, parts, wg, wu, before, squares):
     rows, depth = own.shape
     return pl.pallas_call(
         lambda *refs: expand_send_kernel(len(parts), *refs),
-        in_specs=[SMEM] + [VMEM] * (6 + len(parts)),
+        in_specs=[SMEM] + [VMEM] * 4 + [ANY] * 2 + [VMEM] * len(parts),
         out_specs=[VMEM] * 3,
         out_shape=[
-            jax.ShapeDtypeStruct((rows, wg.shape[1] + 3 * LANES), bf16),
+            jax.ShapeDtypeStruct((rows, wu.shape[1] + 3 * LANES), bf16),
             jax.ShapeDtypeStruct((rows, depth // 2), f32),
             jax.ShapeDtypeStruct((rows, depth // 2), bf16),
         ],
-        scratch_shapes=[pltpu.VMEM((depth // LANES, LANES), f32)],
-        compiler_params=params(4),
-        cost_estimate=cost(rows, wg),
+        scratch_shapes=[pltpu.VMEM((depth // LANES, LANES), f32)]
+        + block_scratch(depth // 2, wu.shape[1] // 2),
+        compiler_params=params(9),
+        cost_estimate=cost(rows, wu),
         name="expand_send",
-    )(at, own, gain, wg, wu, before, squares, *parts)
+    )(at, own, gain, before, squares, wg, wu, *parts)
+
+
+def expand_keep_kernel(at, x, before, wg, wu, out, held, sems):
+    half_of([(at[2], out, before)], x, x.shape[1], wg, wu, held, sems)
 
 
 def expand_keep(at, x, wg, wu, before):
     rows = x.shape[0]
     return pl.pallas_call(
-        lambda at, x, wg, wu, before, out: half_of(at[2], x, wg, wu, out, before),
-        in_specs=[SMEM] + [VMEM] * 4,
-        out_specs=VMEM,
-        out_shape=jax.ShapeDtypeStruct((rows, wg.shape[1]), bf16),
-        compiler_params=params(4),
-        cost_estimate=cost(rows, wg),
+        expand_keep_kernel,
+        in_specs=[SMEM] + [VMEM] * 2 + [ANY] * 2,
+        out_specs=VMEM,
+        out_shape=jax.ShapeDtypeStruct((rows, wu.shape[1]), bf16),
+        scratch_shapes=block_scratch(x.shape[1], wu.shape[1] // 2),
+        compiler_params=params(9),
+        cost_estimate=cost(rows, wu),
         name="expand_keep",
-    )(at, x, wg, wu, before)
+    )(at, x, before, wg, wu)
 
 
 def pair_kernel(keep, received, stats, out):
@@ -597,17 +612,17 @@
     return [1 << b for b in range(n.bit_length() - 1)]
 
 
-def gathered(x, axis, token):
+def gathered(x, axis, token=None):
     parts = [x]
     for bit in reversed(bits_of(axis)):
         parts = parts + [swap(p, axis, bit) for p in parts]
-        if bit > 1:
+        if bit > 1 and token is not None:
             parts = parts[:-1] + [hold(parts[-1], token)]
     return parts
 
 
-def summed(x, axis):
-    *bits, last = bits_of(axis)
+def summed(x, axis, order):
+    *bits, last = bits_of(axis)[::order]
     for bit in bits:
         x = add(x, swap(x, axis, bit))
     return x, swap(x, axis, last)
@@ -638,21 +653,16 @@
 
     flat_cache = kv_cache.reshape((-1,) + kv_cache.shape[2:])
     meta = jnp.concatenate([at, lengths, slots])
-    cache, gate_0, token = fetch(at, (qkv, meta, cos, sin), Part(flat_cache), Part(w_gate, 0, half))
+    cache, w_out, token = fetch(at, (qkv, meta, cos, sin), Part(flat_cache), Part(w_out))
     cache = cache.reshape(kv_cache.shape)
-    value, w_out = attend(meta, cos, sin, cache, gathered(qkv, "wide", token), Part(w_out))
-
-    up_0, token = fetch(at, value, Part(w_up, 0, half))
-    out_0, attended = output_first(gathered(value, "wide", token), w_out)
+    value = attend(meta, cos, sin, cache, gathered(qkv, "wide", token))
+    out_0, attended = output_first(gathered(value, "wide"), w_out)
     out_1 = output_second(attended, w_out)
-    parts_0, parts_1 = summed(out_0, "head"), summed(out_1, "head")
-    gate_1, token = fetch(at, parts_1[0], Part(w_gate, half, half))
-    send, keep, resid_0, squares, up_1 = expand_first(
-        at, own, gain, parts_0, gate_0, up_0, Part(w_up, half, half), token
-    )
-    send, resid_1, x = expand_send(at, own, gain, parts_1, gate_1, up_1, send, squares)
+    parts_0, parts_1 = summed(out_0, "head", 1), summed(out_1, "head", -1)
+    send, keep, resid_0, squares = expand_first(at, own, gain, parts_0, w_gate, w_up)
+    send, resid_1, x = expand_send(at, own, gain, parts_1, w_gate, w_up, send, squares)
     received = swap(send, "wide", 1)
-    total = pair(expand_keep(at, x, gate_1, up_1, keep), received, send)
+    total = pair(expand_keep(at, x, w_gate, w_up, keep), received, send)
     down_own, down_other, token = fetch(at, total, Part(w_down, side=0), Part(w_down, side=1))
     for bit in bits_of("wide")[1:-1]:
         there = swap(total, "wide", bit)

time: 74.6 us -> 73.1 us (0.980)
  Pallas kernels: 45.7 us -> 37.1 us
  waiting for transfers between devices: 10.5 us -> 18.8 us
  starting transfers between devices: 16.9 us -> 15.6 us
    ppermute x16, waiting for transfers between devices: 10.5 us -> 18.8 us  [swap(): return lax.ppermute(x, axis, [(i, i ^ bit) for i in range(n)])]
    pallas_call x4 -> x2, Pallas kernels: 18.7 us -> 11.7 us  [fetch(): pl.pallas_call(lambda *refs: fetch_kernel(wanted, len(after), *refs), in_...]
    pallas_call x3, Pallas kernels: 14.6 us -> 11.9 us  [the longest x1 5.48 us: expand_first(): pl.pallas_call(lambda *refs: expand_first_kernel(len(parts), *refs), in_s...]
    ppermute x16, starting transfers between devices: 16.9 us -> 15.6 us  [swap(): return lax.ppermute(x, axis, [(i, i ^ bit) for i in range(n)])]
    pallas_call x1, Pallas kernels: 1.91 us -> 3.06 us  [expand_send(): pl.pallas_call(lambda *refs: expand_send_kernel(len(parts), *refs), in_sp...]
  transfers between devices with their start and end apart: 16 -> 16, of which waited for: 7 -> 8; matrix products, arithmetic and copies ran while one was open for 1% -> 1% of each run, Pallas kernels for 39% -> 31%
where the time goes in v6:
time: 73.1 us; the launch traced here: 72.9 us
  Pallas kernels  37.1 us (51%)
  waiting for transfers between devices  18.8 us (26%)
  starting transfers between devices  15.6 us (21%)
  other arithmetic  1.02 us (1%)
    ppermute x16, waiting for transfers between devices, swap(): return lax.ppermute(x, axis, [(i, i ^ bit) for i in range(n)])  18.8 us
    ppermute x16, starting transfers between devices, swap(): return lax.ppermute(x, axis, [(i, i ^ bit) for i in range(n)])  15.6 us
    pallas_call x2, Pallas kernels, fetch(): pl.pallas_call(lambda *refs: fetch_kernel(wanted, len(after), *refs), in_...  11.7 us
    pallas_call x1, Pallas kernels, expand_first(): pl.pallas_call(lambda *refs: expand_first_kernel(len(parts), *refs), in_s...  5.48 us
    pallas_call x1, Pallas kernels, project(): pl.pallas_call(lambda *refs: project_kernel(chunks, *refs), in_specs=[SME...  5.11 us
    pallas_call x1, Pallas kernels, attend(): pl.pallas_call(lambda *refs: attend_kernel(len(parts), *refs), in_specs=[...  3.46 us
    pallas_call x1, Pallas kernels, expand_send(): pl.pallas_call(lambda *refs: expand_send_kernel(len(parts), *refs), in_sp...  3.06 us
    pallas_call x1, Pallas kernels, expand_keep(): pl.pallas_call(expand_keep_kernel, in_specs=[SMEM] + [VMEM] * 2 + [ANY] *...  2.93 us
  transfers between devices with their start and end apart: 16, of which 8 were waited for; matrix products, arithmetic and copies ran while one was open for 1% of the time, Pallas kernels for 31%

profile of v6, /device:TPU:0, one launch (start us, length us, event | category | flops | bytes accessed | tf_op | source)
XLA Modules:
  0.0 72.9 jit_solution(12865385900320163009)
XLA Ops:
  0.0 0.0 copy-start.2
  0.0 0.0 copy-start.3
  0.0 0.1 pad_add_fusion.refs_0_.at
  0.1 5.1 %project.1 = (bf16[32,2560]{1,0:T(8,128)(2,1)S(1)}, bf16[32,2048]{1,0:T(8,128)(2,1)S(1)}) custom-call(s32[4]{0:T(128)S(1)} %pad_add_fusion.refs_0_.at, bf16[32,8192]{1,0:T(8,128)(2,1)} %refs_1_.1, bf16[64,128]{1,0:T(8,128)(2,1)} %bitcast.14, bf16[2048,2048]{1,0:T(8,128)(2,1)} %refs_3_.3, bf16[2048,256]{1,0:T(8,128)(2,1)} %refs_4_.2, bf16[2048,256]{1,0:T(8,128)(2,1)} %refs_5_.2), custom_call_target="tpu_custom_call" | custom-call | flops 335544320 | bytes 10485760 | tf_op jit(solution)/shard_map/project/pallas_call | solution.py:178
  5.2 0.5 collective-permute-start.1
  5.7 2.6 %collective-permute-start = (bf16[32,2560]{1,0:T(8,128)(2,1)S(1)}, bf16[32,2560]{1,0:T(8,128)(2,1)S(1)}, u32[]{:S(2)}, u32[]{:S(2)}) collective-permute-start(bf16[32,2560]{1,0:T(8,128)(2,1)S(1)} %get-tuple-element.27.refs_1_.refs_4_), channel_id=1, source_target_pairs={{0,8},{4,12},{8,0},{12,4},{1,9},{5,13},{9,1},{13,5},{2,10},{6,14},... | collective-permute-start | bytes 491528 | tf_op jit(solution)/shard_map/ppermute | solution.py:607
  8.3 0.0 copy-done.2
  8.3 0.1 add_convert_fusion.1
  8.4 0.1 convert_element_type.24
  8.5 0.1 fusion
  8.6 0.0 copy-done.3
  8.6 0.1 concatenate.10.refs_2_.refs_0_
  8.7 0.1 pad_maximum_fusion
  8.8 0.0 slice-start
  8.8 0.0 slice-start.1
  8.8 5.7 %fetch.2 = (bf16[16,512,256]{2,1,0:T(8,128)(2,1)S(1)}, bf16[2048,2048]{1,0:T(8,128)(2,1)S(1)}, f32[8,128]{1,0:T(8,128)S(1)}) custom-call(s32[4]{0:T(128)S(1)} %pad_add_fusion.refs_0_.at, bf16[32,2560]{1,0:T(8,128)(2,1)S(1)} %get-tuple-element.27.refs_1_.refs_4_, s32[20]{0:T(128)S(1)} %concatenate.10.refs_2_.refs_0_, ...), custom_call_target="tpu_custom_call" | custom-call | bytes 25165824 | tf_op jit(solution)/shard_map/fetch/pallas_call | solution.py:94
  14.5 0.0 collective-permute-done.__0_
  14.5 0.2 collective-permute-start.2
  14.8 0.0 collective-permute-done.1.refs_6_
  14.8 1.2 %collective-permute-done.2.refs_7_ = bf16[32,2560]{1,0:T(8,128)(2,1)S(1)} collective-permute-done((bf16[32,2560]{1,0:T(8,128)(2,1)S(1)}, bf16[32,2560]{1,0:T(8,128)(2,1)S(1)}, u32[]{:S(2)}, u32[]{:S(2)}) %collective-permute-start.2) | collective-permute-done | bytes 163872 | tf_op jit(solution)/shard_map/ppermute | solution.py:607
  16.0 3.5 %attend.1.refs_1_ = bf16[32,2432]{1,0:T(8,128)(2,1)S(1)} custom-call(s32[20]{0:T(128)S(1)} %concatenate.10.refs_2_.refs_0_, f32[32,128]{1,0:T(8,128)S(1)} %get-tuple-element.50.refs_3_.refs_1_, f32[32,128]{1,0:T(8,128)S(1)} %get-tuple-element.51.refs_4_.refs_2_, bf16[2,8,512,256]{3,2,1,0:T(8,128)(2,1)S(1)} %bitcast.10, ...), custom_call_target="tpu_custom_call" | custom-call | flops 134217728 | bytes 4194304 | tf_op jit(solution)/shard_map/attend/pallas_call | solution.py:289
  19.5 0.3 collective-permute-start.3
  19.8 0.0 collective-permute-start.4
  19.8 5.8 %collective-permute-done.3.refs_2_ = bf16[32,2432]{1,0:T(8,128)(2,1)S(1)} collective-permute-done((bf16[32,2432]{1,0:T(8,128)(2,1)S(1)}, bf16[32,2432]{1,0:T(8,128)(2,1)S(1)}, u32[]{:S(2)}, u32[]{:S(2)}) %collective-permute-start.3) | collective-permute-done | bytes 155680 | tf_op jit(solution)/shard_map/ppermute | solution.py:607
  25.6 0.0 collective-permute-start.5
  25.6 0.0 collective-permute-done.4.refs_3_
  25.6 1.4 %collective-permute-done.5.refs_4_ = bf16[32,2432]{1,0:T(8,128)(2,1)S(1)} collective-permute-done((bf16[32,2432]{1,0:T(8,128)(2,1)S(1)}, bf16[32,2432]{1,0:T(8,128)(2,1)S(1)}, u32[]{:S(2)}, u32[]{:S(2)}) %collective-permute-start.5) | collective-permute-done | bytes 155680 | tf_op jit(solution)/shard_map/ppermute | solution.py:607
  27.0 1.0 %output_first.1 = (bf16[32,1024]{1,0:T(8,128)(2,1)S(1)}, bf16[32,2048]{1,0:T(8,128)(2,1)S(1)}) custom-call(bf16[2048,2048]{1,0:T(8,128)(2,1)S(1)} %get-tuple-element.28.refs_0_.w, bf16[32,2432]{1,0:T(8,128)(2,1)S(1)} %attend.1.refs_1_, bf16[32,2432]{1,0:T(8,128)(2,1)S(1)} %collective-permute-done.3.refs_2_, ...), custom_call_target="tpu_custom_call" | custom-call | flops 268435456 | bytes 8388608 | tf_op jit(solution)/shard_map/output_first/pallas_call | solution.py:335
  28.0 1.6 %collective-permute-start.6 = (bf16[32,1024]{1,0:T(8,128)(2,1)S(1)}, bf16[32,1024]{1,0:T(8,128)(2,1)S(1)}, u32[]{:S(2)}, u32[]{:S(2)}) collective-permute-start(bf16[32,1024]{1,0:T(8,128)(2,1)S(1)} %get-tuple-element.31.one), channel_id=1, source_target_pairs={{0,1},{1,0},{2,3},{3,2},{4,5},{5,4},{6,7},{7,6},{8,9},{9,8},{10,11... | collective-permute-start | bytes 196616 | tf_op jit(solution)/shard_map/ppermute | solution.py:607
  29.6 0.8 %output_second.1.one = bf16[32,1024]{1,0:T(8,128)(2,1)S(1)} custom-call(bf16[32,2048]{1,0:T(8,128)(2,1)S(1)} %get-tuple-element.34.x, bf16[2048,2048]{1,0:T(8,128)(2,1)S(1)} %get-tuple-element.28.refs_0_.w), custom_call_target="tpu_custom_call" | custom-call | flops 268435456 | bytes 8388608 | tf_op jit(solution)/shard_map/output_second/pallas_call | solution.py:351
  30.4 2.6 %collective-permute-start.8 = (bf16[32,1024]{1,0:T(8,128)(2,1)S(1)}, bf16[32,1024]{1,0:T(8,128)(2,1)S(1)}, u32[]{:S(2)}, u32[]{:S(2)}) collective-permute-start(bf16[32,1024]{1,0:T(8,128)(2,1)S(1)} %output_second.1.one), channel_id=1, source_target_pairs={{0,2},{1,3},{2,0},{3,1},{4,6},{5,7},{6,4},{7,5},{8,10},{9,11},{10,... | collective-permute-start | bytes 196616 | tf_op jit(solution)/shard_map/ppermute | solution.py:607
  33.0 0.0 collective-permute-done.6.two
  33.0 2.5 %collective-permute-start.7 = (bf16[32,1024]{1,0:T(8,128)(2,1)S(1)}, bf16[32,1024]{1,0:T(8,128)(2,1)S(1)}, u32[]{:S(2)}, u32[]{:S(2)}) collective-permute-start(bf16[32,1024]{1,0:T(8,128)(2,1)S(1)} %add.41.refs_5_), channel_id=1, source_target_pairs={{0,2},{1,3},{2,0},{3,1},{4,6},{5,7},{6,4},{7,5},{8,10},{9,11},{10,... | collective-permute-start | bytes 196616 | tf_op jit(solution)/shard_map/ppermute | solution.py:607
  35.6 2.1 %collective-permute-done.8.two = bf16[32,1024]{1,0:T(8,128)(2,1)S(1)} collective-permute-done((bf16[32,1024]{1,0:T(8,128)(2,1)S(1)}, bf16[32,1024]{1,0:T(8,128)(2,1)S(1)}, u32[]{:S(2)}, u32[]{:S(2)}) %collective-permute-start.8) | collective-permute-done | bytes 65568 | tf_op jit(solution)/shard_map/ppermute | solution.py:607
  37.7 0.1 collective-permute-start.9
  37.8 1.6 %collective-permute-done.7.refs_6_ = bf16[32,1024]{1,0:T(8,128)(2,1)S(1)} collective-permute-done((bf16[32,1024]{1,0:T(8,128)(2,1)S(1)}, bf16[32,1024]{1,0:T(8,128)(2,1)S(1)}, u32[]{:S(2)}, u32[]{:S(2)}) %collective-permute-start.7) | collective-permute-done | bytes 65568 | tf_op jit(solution)/shard_map/ppermute | solution.py:607
  39.4 0.0 slice-done
  39.4 0.0 slice-done.1
  39.4 0.0 slice-done.2
  39.4 0.0 slice-done.3
  39.4 0.0 copy-done
  39.4 0.0 copy-done.1
  39.4 5.5 %expand_first.1 = (f32[32,3584]{1,0:T(8,128)S(1)}, f32[32,3584]{1,0:T(8,128)S(1)}, f32[32,1024]{1,0:T(8,128)S(1)}, f32[32,128]{1,0:T(8,128)S(1)}) custom-call(s32[4]{0:T(128)S(1)} %pad_add_fusion.refs_0_.at, bf16[32,2048]{1,0:T(8,128)(2,1)S(1)} %get-tuple-element.26.refs_1_, bf16[16,128]{1,0:T(8,128)(2,1)S(1)} %bitcast.11, bf16[2048,3584]{1,0:T(8,128)(2,1)S(1)} %bitcast.9, ...), custom_call_target="tpu_custom_call" | custom-call | flops 939524096 | bytes 29360128 | tf_op jit(solution)/shard_map/expand_first/pallas_call | solution.py:419
  44.9 0.0 collective-permute-done.9.refs_8_
  44.9 3.1 %expand_send.1 = (bf16[32,3968]{1,0:T(8,128)(2,1)S(1)}, f32[32,1024]{1,0:T(8,128)S(1)}, bf16[32,1024]{1,0:T(8,128)(2,1)S(1)}) custom-call(s32[4]{0:T(128)S(1)} %pad_add_fusion.refs_0_.at, bf16[32,2048]{1,0:T(8,128)(2,1)S(1)} %get-tuple-element.26.refs_1_, bf16[16,128]{1,0:T(8,128)(2,1)S(1)} %bitcast.12, f32[32,3584]{1,0:T(8,128)S(1)} %get-tuple-element.32.refs_3_, ...), custom_call_target="tpu_custom_call" | custom-call | flops 469762048 | bytes 14680064 | tf_op jit(solution)/shard_map/expand_send/pallas_call | solution.py:452
  48.0 0.1 collective-permute-start.10
  48.1 2.9 %expand_keep.1.keep = bf16[32,3584]{1,0:T(8,128)(2,1)S(1)} custom-call(s32[4]{0:T(128)S(1)} %pad_add_fusion.refs_0_.at, bf16[32,1024]{1,0:T(8,128)(2,1)S(1)} %get-tuple-element.35.x, f32[32,3584]{1,0:T(8,128)S(1)} %get-tuple-element.36.before, bf16[2048,3584]{1,0:T(8,128)(2,1)S(1)} %bitcast.9, bf16[2048,3584]{1,0:T(8,128)(2,1)S(1)} %copy-done), custom_call_target="tpu_custom_call" | custom-call | flops 469762048 | bytes 14680064 | tf_op jit(solution)/shard_map/expand_keep/pallas_call | solution.py:475
  51.0 0.0 collective-permute-done.10.received
  51.0 0.1 pair.1.refs_1_.refs_0_
  51.1 0.5 collective-permute-start.11
  51.7 6.0 %fetch.3 = (bf16[1792,2048]{1,0:T(8,128)(2,1)S(1)}, bf16[1792,2048]{1,0:T(8,128)(2,1)S(1)}, f32[8,128]{1,0:T(8,128)S(1)}) custom-call(s32[4]{0:T(128)S(1)} %pad_add_fusion.refs_0_.at, bf16[32,3968]{1,0:T(8,128)(2,1)S(1)} %pair.1.refs_1_.refs_0_, bf16[3584,2048]{1,0:T(8,128)(2,1)} %refs_3_.5, bf16[3584,2048]{1,0:T(8,128)(2,1)} %refs_3_.5), custom_call_target="tpu_custom_call" | custom-call | bytes 29360128 | tf_op jit(solution)/shard_map/fetch/pallas_call | solution.py:94
  57.7 2.0 %collective-permute-done.11.refs_1_ = bf16[32,3968]{1,0:T(8,128)(2,1)S(1)} collective-permute-done((bf16[32,3968]{1,0:T(8,128)(2,1)S(1)}, bf16[32,3968]{1,0:T(8,128)(2,1)S(1)}, u32[]{:S(2)}, u32[]{:S(2)}) %collective-permute-start.11) | collective-permute-done | bytes 253984 | tf_op jit(solution)/shard_map/ppermute | solution.py:607
  59.7 0.1 gated.1.hidden
  59.9 0.1 collective-permute-start.12
  59.9 1.4 %contract.1.refs_3_ = f32[32,2048]{1,0:T(8,128)S(1)} custom-call(bf16[32,1792]{1,0:T(8,128)(2,1)S(1)} %gated.1.hidden, bf16[1792,2048]{1,0:T(8,128)(2,1)S(1)} %get-tuple-element.40.w), custom_call_target="tpu_custom_call" | custom-call | flops 234881024 | bytes 7340032 | tf_op jit(solution)/shard_map/contract/pallas_call | solution.py:538
  61.3 0.0 collective-permute-done.12.refs_1_
  61.3 1.9 %contract_last.1 = (f32[8,2048]{1,0:T(8,128)S(1)}, bf16[8,2048]{1,0:T(8,128)(2,1)S(1)}, bf16[8,2048]{1,0:T(8,128)(2,1)S(1)}, bf16[8,2048]{1,0:T(8,128)(2,1)S(1)}) custom-call(s32[4]{0:T(128)S(1)} %pad_add_fusion.refs_0_.at, bf16[32,1792]{1,0:T(8,128)(2,1)S(1)} %collective-permute-done.12.refs_1_, bf16[1792,2048]{1,0:T(8,128)(2,1)S(1)} %get-tuple-element.39.refs_2_, ...), custom_call_target="tpu_custom_call" | custom-call | flops 234881024 | bytes 7340032 | tf_op jit(solution)/shard_map/contract_last/pallas_call | solution.py:575
  63.2 0.5 collective-permute-start.13
  63.7 2.8 %collective-permute-start.14 = (bf16[8,2048]{1,0:T(8,128)(2,1)S(1)}, bf16[8,2048]{1,0:T(8,128)(2,1)S(1)}, u32[]{:S(2)}, u32[]{:S(2)}) collective-permute-start(bf16[8,2048]{1,0:T(8,128)(2,1)S(1)} %get-tuple-element.45), channel_id=1, source_target_pairs={{0,2},{1,3},{2,0},{3,1},{4,6},{5,7},{6,4},{7,5},{8,10},{9,11},{10,... | collective-permute-start | bytes 98312 | tf_op jit(solution)/shard_map/ppermute | solution.py:607
  66.6 1.1 %collective-permute-start.15 = (bf16[8,2048]{1,0:T(8,128)(2,1)S(1)}, bf16[8,2048]{1,0:T(8,128)(2,1)S(1)}, u32[]{:S(2)}, u32[]{:S(2)}) collective-permute-start(bf16[8,2048]{1,0:T(8,128)(2,1)S(1)} %get-tuple-element.46), channel_id=1, source_target_pairs={{0,3},{1,2},{2,1},{3,0},{4,7},{5,6},{6,5},{7,4},{8,11},{9,10},{10,... | collective-permute-start | bytes 98312 | tf_op jit(solution)/shard_map/ppermute | solution.py:607
  67.7 0.0 collective-permute-done.13
  67.7 0.9 %collective-permute-done.14 = bf16[8,2048]{1,0:T(8,128)(2,1)S(1)} collective-permute-done((bf16[8,2048]{1,0:T(8,128)(2,1)S(1)}, bf16[8,2048]{1,0:T(8,128)(2,1)S(1)}, u32[]{:S(2)}, u32[]{:S(2)}) %collective-permute-start.14) | collective-permute-done | bytes 32800 | tf_op jit(solution)/shard_map/ppermute | solution.py:607
  68.6 3.7 %collective-permute-done.15 = bf16[8,2048]{1,0:T(8,128)(2,1)S(1)} collective-permute-done((bf16[8,2048]{1,0:T(8,128)(2,1)S(1)}, bf16[8,2048]{1,0:T(8,128)(2,1)S(1)}, u32[]{:S(2)}, u32[]{:S(2)}) %collective-permute-start.15) | collective-permute-done | bytes 32800 | tf_op jit(solution)/shard_map/ppermute | solution.py:607
  72.3 0.6 add_convert_fusion
  (9 shorter events, 0.1 us)
Async XLA Ops:
  0.0 8.3 %copy-start.2 = (s32[8]{0:T(128)S(1)}, s32[8]{0:T(128)}, u32[]{:S(2)}) copy-start(s32[8]{0:T(128)} %param.24) | copy-start | bytes 100
  0.0 8.6 %copy-start.3 = (s32[8]{0:T(128)S(1)}, s32[8]{0:T(128)}, u32[]{:S(2)}) copy-start(s32[8]{0:T(128)} %param.25) | copy-start | bytes 100
  5.2 9.6 %collective-permute-start.1 = (bf16[32,2560]{1,0:T(8,128)(2,1)S(1)}, bf16[32,2560]{1,0:T(8,128)(2,1)S(1)}, u32[]{:S(2)}, u32[]{:S(2)}) collective-permute-start(bf16[32,2560]{1,0:T(8,128)(2,1)S(1)} %get-tuple-element.27.refs_1_.refs_4_), channel_id=1, source_target_pairs={{0,4},{4,0},{8,12},{12,8},{1,5},{5,1},{9,13},{13,9},{2,6},{6,2},{1... | collective-permute-start | bytes 491528 | tf_op jit(solution)/shard_map/ppermute | solution.py:607
  5.7 8.8 %collective-permute-start = (bf16[32,2560]{1,0:T(8,128)(2,1)S(1)}, bf16[32,2560]{1,0:T(8,128)(2,1)S(1)}, u32[]{:S(2)}, u32[]{:S(2)}) collective-permute-start(bf16[32,2560]{1,0:T(8,128)(2,1)S(1)} %get-tuple-element.27.refs_1_.refs_4_), channel_id=1, source_target_pairs={{0,8},{4,12},{8,0},{12,4},{1,9},{5,13},{9,1},{13,5},{2,10},{6,14},... | collective-permute-start | bytes 491528 | tf_op jit(solution)/shard_map/ppermute | solution.py:607
  8.8 30.6 %slice-start = ((s8[14680064]{0:T(1024)(128)(4,1)}), s8[4194304]{0:T(1024)(128)(4,1)S(1)}, s32[]{:S(2)}) async-start(s8[14680064]{0:T(1024)(128)(4,1)} %bitcast.8), calls=%async_computation | async-start | bytes 8388608
  8.8 30.6 %slice-start.1 = ((s8[14680064]{0:T(1024)(128)(4,1)}), s8[4194304]{0:T(1024)(128)(4,1)S(1)}, s32[]{:S(2)}) async-start(s8[14680064]{0:T(1024)(128)(4,1)} %bitcast.8), calls=%async_computation.1 | async-start | bytes 8388608
  14.5 1.5 %collective-permute-start.2 = (bf16[32,2560]{1,0:T(8,128)(2,1)S(1)}, bf16[32,2560]{1,0:T(8,128)(2,1)S(1)}, u32[]{:S(2)}, u32[]{:S(2)}) collective-permute-start(bf16[32,2560]{1,0:T(8,128)(2,1)S(1)} %hold.1.refs_5_), channel_id=1, source_target_pairs={{0,4},{4,0},{8,12},{12,8},{1,5},{5,1},{9,13},{13,9},{2,6},{6,2},{1... | collective-permute-start | bytes 491528 | tf_op jit(solution)/shard_map/ppermute | solution.py:607
  16.0 23.4 %slice-start.2 = ((s8[14680064]{0:T(1024)(128)(4,1)}), s8[4194304]{0:T(1024)(128)(4,1)S(1)}, s32[]{:S(2)}) async-start(s8[14680064]{0:T(1024)(128)(4,1)} %bitcast.8), calls=%async_computation.2 | async-start | bytes 8388608
  19.5 6.2 %collective-permute-start.3 = (bf16[32,2432]{1,0:T(8,128)(2,1)S(1)}, bf16[32,2432]{1,0:T(8,128)(2,1)S(1)}, u32[]{:S(2)}, u32[]{:S(2)}) collective-permute-start(bf16[32,2432]{1,0:T(8,128)(2,1)S(1)} %attend.1.refs_1_), channel_id=1, source_target_pairs={{0,8},{4,12},{8,0},{12,4},{1,9},{5,13},{9,1},{13,5},{2,10},{6,14},... | collective-permute-start | bytes 466952 | tf_op jit(solution)/shard_map/ppermute | solution.py:607
  19.8 5.8 %collective-permute-start.4 = (bf16[32,2432]{1,0:T(8,128)(2,1)S(1)}, bf16[32,2432]{1,0:T(8,128)(2,1)S(1)}, u32[]{:S(2)}, u32[]{:S(2)}) collective-permute-start(bf16[32,2432]{1,0:T(8,128)(2,1)S(1)} %attend.1.refs_1_), channel_id=1, source_target_pairs={{0,4},{4,0},{8,12},{12,8},{1,5},{5,1},{9,13},{13,9},{2,6},{6,2},{1... | collective-permute-start | bytes 466952 | tf_op jit(solution)/shard_map/ppermute | solution.py:607
  25.6 1.4 %collective-permute-start.5 = (bf16[32,2432]{1,0:T(8,128)(2,1)S(1)}, bf16[32,2432]{1,0:T(8,128)(2,1)S(1)}, u32[]{:S(2)}, u32[]{:S(2)}) collective-permute-start(bf16[32,2432]{1,0:T(8,128)(2,1)S(1)} %collective-permute-done.3.refs_2_), channel_id=1, source_target_pairs={{0,4},{4,0},{8,12},{12,8},{1,5},{5,1},{9,13},{13,9},{2,6},{6,2},{1... | collective-permute-start | bytes 466952 | tf_op jit(solution)/shard_map/ppermute | solution.py:607
  27.0 12.4 %slice-start.3 = ((s8[14680064]{0:T(1024)(128)(4,1)}), s8[2097152]{0:T(1024)(128)(4,1)S(1)}, s32[]{:S(2)}) async-start(s8[14680064]{0:T(1024)(128)(4,1)} %bitcast.8), calls=%async_computation.3 | async-start | bytes 4194304
  27.0 12.4 %copy-start = (bf16[2048,3584]{1,0:T(8,128)(2,1)S(1)}, bf16[2048,3584]{1,0:T(8,128)(2,1)}, u32[]{:S(2)}) copy-start(bf16[2048,3584]{1,0:T(8,128)(2,1)} %wu.1) | copy-start | bytes 44040196
  27.0 12.4 %copy-start.1 = (bf16[2048]{0:T(1024)(128)(2,1)S(1)}, bf16[2048]{0:T(1024)(128)(2,1)}, u32[]{:S(2)}) copy-start(bf16[2048]{0:T(1024)(128)(2,1)} %param.15) | copy-start | bytes 12292
  28.0 5.0 %collective-permute-start.6 = (bf16[32,1024]{1,0:T(8,128)(2,1)S(1)}, bf16[32,1024]{1,0:T(8,128)(2,1)S(1)}, u32[]{:S(2)}, u32[]{:S(2)}) collective-permute-start(bf16[32,1024]{1,0:T(8,128)(2,1)S(1)} %get-tuple-element.31.one), channel_id=1, source_target_pairs={{0,1},{1,0},{2,3},{3,2},{4,5},{5,4},{6,7},{7,6},{8,9},{9,8},{10,11... | collective-permute-start | bytes 196616 | tf_op jit(solution)/shard_map/ppermute | solution.py:607
  30.4 7.3 %collective-permute-start.8 = (bf16[32,1024]{1,0:T(8,128)(2,1)S(1)}, bf16[32,1024]{1,0:T(8,128)(2,1)S(1)}, u32[]{:S(2)}, u32[]{:S(2)}) collective-permute-start(bf16[32,1024]{1,0:T(8,128)(2,1)S(1)} %output_second.1.one), channel_id=1, source_target_pairs={{0,2},{1,3},{2,0},{3,1},{4,6},{5,7},{6,4},{7,5},{8,10},{9,11},{10,... | collective-permute-start | bytes 196616 | tf_op jit(solution)/shard_map/ppermute | solution.py:607
  33.0 6.4 %collective-permute-start.7 = (bf16[32,1024]{1,0:T(8,128)(2,1)S(1)}, bf16[32,1024]{1,0:T(8,128)(2,1)S(1)}, u32[]{:S(2)}, u32[]{:S(2)}) collective-permute-start(bf16[32,1024]{1,0:T(8,128)(2,1)S(1)} %add.41.refs_5_), channel_id=1, source_target_pairs={{0,2},{1,3},{2,0},{3,1},{4,6},{5,7},{6,4},{7,5},{8,10},{9,11},{10,... | collective-permute-start | bytes 196616 | tf_op jit(solution)/shard_map/ppermute | solution.py:607
  37.7 7.2 %collective-permute-start.9 = (bf16[32,1024]{1,0:T(8,128)(2,1)S(1)}, bf16[32,1024]{1,0:T(8,128)(2,1)S(1)}, u32[]{:S(2)}, u32[]{:S(2)}) collective-permute-start(bf16[32,1024]{1,0:T(8,128)(2,1)S(1)} %add.42.refs_7_), channel_id=1, source_target_pairs={{0,1},{1,0},{2,3},{3,2},{4,5},{5,4},{6,7},{7,6},{8,9},{9,8},{10,11... | collective-permute-start | bytes 196616 | tf_op jit(solution)/shard_map/ppermute | solution.py:607
  48.0 3.0 %collective-permute-start.10 = (bf16[32,3968]{1,0:T(8,128)(2,1)S(1)}, bf16[32,3968]{1,0:T(8,128)(2,1)S(1)}, u32[]{:S(2)}, u32[]{:S(2)}) collective-permute-start(bf16[32,3968]{1,0:T(8,128)(2,1)S(1)} %get-tuple-element.37.stats), channel_id=1, source_target_pairs={{0,4},{4,0},{8,12},{12,8},{1,5},{5,1},{9,13},{13,9},{2,6},{6,2},{1... | collective-permute-start | bytes 761864 | tf_op jit(solution)/shard_map/ppermute | solution.py:607
  51.1 8.6 %collective-permute-start.11 = (bf16[32,3968]{1,0:T(8,128)(2,1)S(1)}, bf16[32,3968]{1,0:T(8,128)(2,1)S(1)}, u32[]{:S(2)}, u32[]{:S(2)}) collective-permute-start(bf16[32,3968]{1,0:T(8,128)(2,1)S(1)} %pair.1.refs_1_.refs_0_), channel_id=1, source_target_pairs={{0,8},{4,12},{8,0},{12,4},{1,9},{5,13},{9,1},{13,5},{2,10},{6,14},... | collective-permute-start | bytes 761864 | tf_op jit(solution)/shard_map/ppermute | solution.py:607
  59.9 1.4 %collective-permute-start.12 = (bf16[32,1792]{1,0:T(8,128)(2,1)S(1)}, bf16[32,1792]{1,0:T(8,128)(2,1)S(1)}, u32[]{:S(2)}, u32[]{:S(2)}) collective-permute-start(bf16[32,1792]{1,0:T(8,128)(2,1)S(1)} %gated.1.hidden), channel_id=1, source_target_pairs={{0,4},{4,0},{8,12},{12,8},{1,5},{5,1},{9,13},{13,9},{2,6},{6,2},{1... | collective-permute-start | bytes 344072 | tf_op jit(solution)/shard_map/ppermute | solution.py:607
  63.2 4.5 %collective-permute-start.13 = (bf16[8,2048]{1,0:T(8,128)(2,1)S(1)}, bf16[8,2048]{1,0:T(8,128)(2,1)S(1)}, u32[]{:S(2)}, u32[]{:S(2)}) collective-permute-start(bf16[8,2048]{1,0:T(8,128)(2,1)S(1)} %get-tuple-element.44), channel_id=1, source_target_pairs={{0,1},{1,0},{2,3},{3,2},{4,5},{5,4},{6,7},{7,6},{8,9},{9,8},{10,11... | collective-permute-start | bytes 98312 | tf_op jit(solution)/shard_map/ppermute | solution.py:607
  63.7 4.9 %collective-permute-start.14 = (bf16[8,2048]{1,0:T(8,128)(2,1)S(1)}, bf16[8,2048]{1,0:T(8,128)(2,1)S(1)}, u32[]{:S(2)}, u32[]{:S(2)}) collective-permute-start(bf16[8,2048]{1,0:T(8,128)(2,1)S(1)} %get-tuple-element.45), channel_id=1, source_target_pairs={{0,2},{1,3},{2,0},{3,1},{4,6},{5,7},{6,4},{7,5},{8,10},{9,11},{10,... | collective-permute-start | bytes 98312 | tf_op jit(solution)/shard_map/ppermute | solution.py:607
  66.6 5.7 %collective-permute-start.15 = (bf16[8,2048]{1,0:T(8,128)(2,1)S(1)}, bf16[8,2048]{1,0:T(8,128)(2,1)S(1)}, u32[]{:S(2)}, u32[]{:S(2)}) collective-permute-start(bf16[8,2048]{1,0:T(8,128)(2,1)S(1)} %get-tuple-element.46), channel_id=1, source_target_pairs={{0,3},{1,2},{2,1},{3,0},{4,7},{5,6},{6,5},{7,4},{8,11},{9,10},{10,... | collective-permute-start | bytes 98312 | tf_op jit(solution)/shard_map/ppermute | solution.py:607

commit v7 on v6

--- a/solution.py
+++ b/solution.py
@@ -359,38 +359,49 @@
     )(attended, w)
 
 
-SLOTS = 3
 WIDE = 896
-
-
-def half_of(sides, x, row, wg, wu, held, sems):
+SPLIT = 4
+
+
+def half_of(at, sides, x, row, wg, wu, held, sems, prepare=None):
     count, half = x.shape[1], wg.shape[1] // 2
+    step = count // SPLIT
     jobs = []
     for side, out, before in sides:
         for base, w in ((0, wg), (half, wu)):
             for start, size in blocks_of(half, WIDE):
-                slot = len(jobs) % SLOTS
+                n = len(jobs)
                 cols = pl.ds(pl.multiple_of(side * half + start, LANES), size)
-                copy = pltpu.make_async_copy(
-                    w.at[pl.ds(row, count), cols], held.at[slot, :, pl.ds(0, size)], sems.at[slot]
-                )
-                jobs.append((copy, slot, size, base + start, out, before))
-    for copy, *_ in jobs[: SLOTS - 1]:
-        copy.start()
-    for n, (copy, slot, size, to, out, before) in enumerate(jobs):
-        copy.wait()
-        if n + SLOTS - 1 < len(jobs):
-            jobs[n + SLOTS - 1][0].start()
-        term = jnp.dot(x[...], held[slot, :, :size], preferred_element_type=f32)
-        cols = slice(to, to + size)
+                copies = [
+                    pltpu.make_async_copy(
+                        w.at[pl.ds(row + p * step, step), cols],
+                        held.at[n, pl.ds(p * step, step)],
+                        sems.at[n * SPLIT + p],
+                    )
+                    for p in range(SPLIT)
+                ]
+                jobs.append((copies, slice(base + start, base + start + size), out, before))
+    for copies, *_ in jobs:
+        for copy in copies:
+            copy.start()
+    if prepare is not None:
+        pl.when(at[2] >= 0)(prepare)
+    for n, (copies, cols, out, before) in enumerate(jobs):
+        for copy in copies:
+            copy.wait()
+        term = jnp.dot(x[...], held[n], preferred_element_type=f32)
         if before is not None:
             term = before[:, cols] + term
         out[:, cols] = term.astype(out.dtype)
 
 
-def block_scratch(count, half):
-    width = max(size for _, size in blocks_of(half, WIDE))
-    return [pltpu.VMEM((SLOTS, count, width), bf16), pltpu.SemaphoreType.DMA((SLOTS,))]
+def block_scratch(sides, count, half):
+    blocks = blocks_of(half, WIDE)
+    number = sides * 2 * len(blocks)
+    return [
+        pltpu.VMEM((number, count, blocks[0][1]), bf16),
+        pltpu.SemaphoreType.DMA((number * SPLIT,)),
+    ]
 
 
 def residual(which, own, gain, parts, resid, x, gain_f):
@@ -409,8 +420,13 @@
 
 def expand_first_kernel(n, at, own, gain, wg, wu, *rest):
     parts, (send, keep, resid, squares, x, gain_f, held, sems) = rest[:n], rest[n:]
-    squares[...] = residual(0, own, gain, parts, resid, x, gain_f)
-    half_of([(1 - at[2], send, None), (at[2], keep, None)], x, 0, wg, wu, held, sems)
+
+    def prepare():
+        squares[...] = residual(0, own, gain, parts, resid, x, gain_f)
+
+    half_of(
+        at, [(1 - at[2], send, None), (at[2], keep, None)], x, 0, wg, wu, held, sems, prepare
+    )
 
 
 def expand_first(at, own, gain, parts, wg, wu):
@@ -430,8 +446,8 @@
             pltpu.VMEM((rows, depth // 2), bf16),
             pltpu.VMEM((depth // LANES, LANES), f32),
         ]
-        + block_scratch(depth // 2, width // 2),
-        compiler_params=params(9),
+        + block_scratch(2, depth // 2, width // 2),
+        compiler_params=params(18),
         cost_estimate=cost(rows, wg, wu),
         name="expand_first",
     )(at, own, gain, wg, wu, *parts)
@@ -439,12 +455,15 @@
 
 def expand_send_kernel(n, at, own, gain, before, squares, wg, wu, *rest):
     parts, (out, resid, x, gain_f, held, sems) = rest[:n], rest[n:]
-    square = squares[...] + residual(1, own, gain, parts, resid, x, gain_f)
-    square = jnp.broadcast_to(jnp.sum(square, axis=1, keepdims=True), square.shape)
     width = wu.shape[1]
-    for p, term in enumerate(thirds(square)):
-        out[:, width + p * LANES : width + (p + 1) * LANES] = term
-    half_of([(1 - at[2], out, before)], x, x.shape[1], wg, wu, held, sems)
+
+    def prepare():
+        square = squares[...] + residual(1, own, gain, parts, resid, x, gain_f)
+        square = jnp.broadcast_to(jnp.sum(square, axis=1, keepdims=True), square.shape)
+        for p, term in enumerate(thirds(square)):
+            out[:, width + p * LANES : width + (p + 1) * LANES] = term
+
+    half_of(at, [(1 - at[2], out, before)], x, x.shape[1], wg, wu, held, sems, prepare)
 
 
 def expand_send(at, own, gain, parts, wg, wu, before, squares):
@@ -459,15 +478,15 @@
             jax.ShapeDtypeStruct((rows, depth // 2), bf16),
         ],
         scratch_shapes=[pltpu.VMEM((depth // LANES, LANES), f32)]
-        + block_scratch(depth // 2, wu.shape[1] // 2),
-        compiler_params=params(9),
+        + block_scratch(1, depth // 2, wu.shape[1] // 2),
+        compiler_params=params(10),
         cost_estimate=cost(rows, wu),
         name="expand_send",
     )(at, own, gain, before, squares, wg, wu, *parts)
 
 
 def expand_keep_kernel(at, x, before, wg, wu, out, held, sems):
-    half_of([(at[2], out, before)], x, x.shape[1], wg, wu, held, sems)
+    half_of(at, [(at[2], out, before)], x, x.shape[1], wg, wu, held, sems)
 
 
 def expand_keep(at, x, wg, wu, before):
@@ -477,8 +496,8 @@
         in_specs=[SMEM] + [VMEM] * 2 + [ANY] * 2,
         out_specs=VMEM,
         out_shape=jax.ShapeDtypeStruct((rows, wu.shape[1]), bf16),
-        scratch_shapes=block_scratch(x.shape[1], wu.shape[1] // 2),
-        compiler_params=params(9),
+        scratch_shapes=block_scratch(1, x.shape[1], wu.shape[1] // 2),
+        compiler_params=params(10),
         cost_estimate=cost(rows, wu),
         name="expand_keep",
     )(at, x, before, wg, wu)

time: 73.1 us -> 73.8 us (level)
  no operation moved by 1% of the time
where the time goes in v7:
time: 73.8 us; the launch traced here: 73.6 us
  Pallas kernels  37.8 us (51%)
  waiting for transfers between devices  18.8 us (25%)
  starting transfers between devices  15.6 us (21%)
  other arithmetic  1.02 us (1%)
    ppermute x16, waiting for transfers between devices, swap(): return lax.ppermute(x, axis, [(i, i ^ bit) for i in range(n)])  18.8 us
    ppermute x16, starting transfers between devices, swap(): return lax.ppermute(x, axis, [(i, i ^ bit) for i in range(n)])  15.6 us
    pallas_call x2, Pallas kernels, fetch(): pl.pallas_call(lambda *refs: fetch_kernel(wanted, len(after), *refs), in_...  11.7 us
    pallas_call x1, Pallas kernels, expand_first(): pl.pallas_call(lambda *refs: expand_first_kernel(len(parts), *refs), in_s...  5.68 us
    pallas_call x1, Pallas kernels, project(): pl.pallas_call(lambda *refs: project_kernel(chunks, *refs), in_specs=[SME...  5.11 us
    pallas_call x1, Pallas kernels, attend(): pl.pallas_call(lambda *refs: attend_kernel(len(parts), *refs), in_specs=[...  3.46 us
    pallas_call x1, Pallas kernels, expand_send(): pl.pallas_call(lambda *refs: expand_send_kernel(len(parts), *refs), in_sp...  3.42 us
    pallas_call x1, Pallas kernels, expand_keep(): pl.pallas_call(expand_keep_kernel, in_specs=[SMEM] + [VMEM] * 2 + [ANY] *...  3.1 us
  transfers between devices with their start and end apart: 16, of which 8 were waited for; matrix products, arithmetic and copies ran while one was open for 1% of the time, Pallas kernels for 31%

profile of v7, /device:TPU:0, one launch (start us, length us, event | category | flops | bytes accessed | tf_op | source)
XLA Modules:
  0.0 73.6 jit_solution(2818986786635334287)
XLA Ops:
  0.0 0.0 copy-start.2
  0.0 0.0 copy-start.3
  0.0 0.1 pad_add_fusion.refs_0_.at
  0.1 5.1 %project.1 = (bf16[32,2560]{1,0:T(8,128)(2,1)S(1)}, bf16[32,2048]{1,0:T(8,128)(2,1)S(1)}) custom-call(s32[4]{0:T(128)S(1)} %pad_add_fusion.refs_0_.at, bf16[32,8192]{1,0:T(8,128)(2,1)} %refs_1_.1, bf16[64,128]{1,0:T(8,128)(2,1)} %bitcast.14, bf16[2048,2048]{1,0:T(8,128)(2,1)} %refs_3_.3, bf16[2048,256]{1,0:T(8,128)(2,1)} %refs_4_.2, bf16[2048,256]{1,0:T(8,128)(2,1)} %refs_5_.2), custom_call_target="tpu_custom_call" | custom-call | flops 335544320 | bytes 10485760 | tf_op jit(solution)/shard_map/project/pallas_call | solution.py:178
  5.2 0.5 collective-permute-start.1
  5.7 2.6 %collective-permute-start = (bf16[32,2560]{1,0:T(8,128)(2,1)S(1)}, bf16[32,2560]{1,0:T(8,128)(2,1)S(1)}, u32[]{:S(2)}, u32[]{:S(2)}) collective-permute-start(bf16[32,2560]{1,0:T(8,128)(2,1)S(1)} %get-tuple-element.27.refs_1_.refs_4_), channel_id=1, source_target_pairs={{0,8},{4,12},{8,0},{12,4},{1,9},{5,13},{9,1},{13,5},{2,10},{6,14},... | collective-permute-start | bytes 491528 | tf_op jit(solution)/shard_map/ppermute | solution.py:626
  8.3 0.0 copy-done.2
  8.3 0.1 add_convert_fusion.1
  8.4 0.1 convert_element_type.24
  8.5 0.1 fusion
  8.6 0.0 copy-done.3
  8.6 0.1 concatenate.10.refs_2_.refs_0_
  8.7 0.1 pad_maximum_fusion
  8.8 0.0 slice-start
  8.8 5.7 %fetch.2 = (bf16[16,512,256]{2,1,0:T(8,128)(2,1)S(1)}, bf16[2048,2048]{1,0:T(8,128)(2,1)S(1)}, f32[8,128]{1,0:T(8,128)S(1)}) custom-call(s32[4]{0:T(128)S(1)} %pad_add_fusion.refs_0_.at, bf16[32,2560]{1,0:T(8,128)(2,1)S(1)} %get-tuple-element.27.refs_1_.refs_4_, s32[20]{0:T(128)S(1)} %concatenate.10.refs_2_.refs_0_, ...), custom_call_target="tpu_custom_call" | custom-call | bytes 25165824 | tf_op jit(solution)/shard_map/fetch/pallas_call | solution.py:94
  14.5 0.0 collective-permute-done.__0_
  14.5 0.2 collective-permute-start.2
  14.8 0.0 collective-permute-done.1.refs_6_
  14.8 1.2 %collective-permute-done.2.refs_7_ = bf16[32,2560]{1,0:T(8,128)(2,1)S(1)} collective-permute-done((bf16[32,2560]{1,0:T(8,128)(2,1)S(1)}, bf16[32,2560]{1,0:T(8,128)(2,1)S(1)}, u32[]{:S(2)}, u32[]{:S(2)}) %collective-permute-start.2) | collective-permute-done | bytes 163872 | tf_op jit(solution)/shard_map/ppermute | solution.py:626
  16.0 0.0 slice-start.2
  16.0 3.5 %attend.1.refs_1_ = bf16[32,2432]{1,0:T(8,128)(2,1)S(1)} custom-call(s32[20]{0:T(128)S(1)} %concatenate.10.refs_2_.refs_0_, f32[32,128]{1,0:T(8,128)S(1)} %get-tuple-element.50.refs_3_.refs_1_, f32[32,128]{1,0:T(8,128)S(1)} %get-tuple-element.51.refs_4_.refs_2_, bf16[2,8,512,256]{3,2,1,0:T(8,128)(2,1)S(1)} %bitcast.10, ...), custom_call_target="tpu_custom_call" | custom-call | flops 134217728 | bytes 4194304 | tf_op jit(solution)/shard_map/attend/pallas_call | solution.py:289
  19.5 0.3 collective-permute-start.3
  19.8 0.0 collective-permute-start.4
  19.8 5.8 %collective-permute-done.3.refs_2_ = bf16[32,2432]{1,0:T(8,128)(2,1)S(1)} collective-permute-done((bf16[32,2432]{1,0:T(8,128)(2,1)S(1)}, bf16[32,2432]{1,0:T(8,128)(2,1)S(1)}, u32[]{:S(2)}, u32[]{:S(2)}) %collective-permute-start.3) | collective-permute-done | bytes 155680 | tf_op jit(solution)/shard_map/ppermute | solution.py:626
  25.6 0.0 collective-permute-start.5
  25.6 0.0 collective-permute-done.4.refs_3_
  25.6 1.4 %collective-permute-done.5.refs_4_ = bf16[32,2432]{1,0:T(8,128)(2,1)S(1)} collective-permute-done((bf16[32,2432]{1,0:T(8,128)(2,1)S(1)}, bf16[32,2432]{1,0:T(8,128)(2,1)S(1)}, u32[]{:S(2)}, u32[]{:S(2)}) %collective-permute-start.5) | collective-permute-done | bytes 155680 | tf_op jit(solution)/shard_map/ppermute | solution.py:626
  27.0 1.0 %output_first.1 = (bf16[32,1024]{1,0:T(8,128)(2,1)S(1)}, bf16[32,2048]{1,0:T(8,128)(2,1)S(1)}) custom-call(bf16[2048,2048]{1,0:T(8,128)(2,1)S(1)} %get-tuple-element.28.refs_0_.w, bf16[32,2432]{1,0:T(8,128)(2,1)S(1)} %attend.1.refs_1_, bf16[32,2432]{1,0:T(8,128)(2,1)S(1)} %collective-permute-done.3.refs_2_, ...), custom_call_target="tpu_custom_call" | custom-call | flops 268435456 | bytes 8388608 | tf_op jit(solution)/shard_map/output_first/pallas_call | solution.py:335
  28.0 1.6 %collective-permute-start.6 = (bf16[32,1024]{1,0:T(8,128)(2,1)S(1)}, bf16[32,1024]{1,0:T(8,128)(2,1)S(1)}, u32[]{:S(2)}, u32[]{:S(2)}) collective-permute-start(bf16[32,1024]{1,0:T(8,128)(2,1)S(1)} %get-tuple-element.31.one), channel_id=1, source_target_pairs={{0,1},{1,0},{2,3},{3,2},{4,5},{5,4},{6,7},{7,6},{8,9},{9,8},{10,11... | collective-permute-start | bytes 196616 | tf_op jit(solution)/shard_map/ppermute | solution.py:626
  29.6 0.8 %output_second.1.one = bf16[32,1024]{1,0:T(8,128)(2,1)S(1)} custom-call(bf16[32,2048]{1,0:T(8,128)(2,1)S(1)} %get-tuple-element.34.x, bf16[2048,2048]{1,0:T(8,128)(2,1)S(1)} %get-tuple-element.28.refs_0_.w), custom_call_target="tpu_custom_call" | custom-call | flops 268435456 | bytes 8388608 | tf_op jit(solution)/shard_map/output_second/pallas_call | solution.py:351
  30.4 2.6 %collective-permute-start.8 = (bf16[32,1024]{1,0:T(8,128)(2,1)S(1)}, bf16[32,1024]{1,0:T(8,128)(2,1)S(1)}, u32[]{:S(2)}, u32[]{:S(2)}) collective-permute-start(bf16[32,1024]{1,0:T(8,128)(2,1)S(1)} %output_second.1.one), channel_id=1, source_target_pairs={{0,2},{1,3},{2,0},{3,1},{4,6},{5,7},{6,4},{7,5},{8,10},{9,11},{10,... | collective-permute-start | bytes 196616 | tf_op jit(solution)/shard_map/ppermute | solution.py:626
  33.0 0.0 collective-permute-done.6.two
  33.0 2.5 %collective-permute-start.7 = (bf16[32,1024]{1,0:T(8,128)(2,1)S(1)}, bf16[32,1024]{1,0:T(8,128)(2,1)S(1)}, u32[]{:S(2)}, u32[]{:S(2)}) collective-permute-start(bf16[32,1024]{1,0:T(8,128)(2,1)S(1)} %add.41.refs_5_), channel_id=1, source_target_pairs={{0,2},{1,3},{2,0},{3,1},{4,6},{5,7},{6,4},{7,5},{8,10},{9,11},{10,... | collective-permute-start | bytes 196616 | tf_op jit(solution)/shard_map/ppermute | solution.py:626
  35.5 2.2 %collective-permute-done.8.two = bf16[32,1024]{1,0:T(8,128)(2,1)S(1)} collective-permute-done((bf16[32,1024]{1,0:T(8,128)(2,1)S(1)}, bf16[32,1024]{1,0:T(8,128)(2,1)S(1)}, u32[]{:S(2)}, u32[]{:S(2)}) %collective-permute-start.8) | collective-permute-done | bytes 65568 | tf_op jit(solution)/shard_map/ppermute | solution.py:626
  37.7 0.1 collective-permute-start.9
  37.8 1.6 %collective-permute-done.7.refs_6_ = bf16[32,1024]{1,0:T(8,128)(2,1)S(1)} collective-permute-done((bf16[32,1024]{1,0:T(8,128)(2,1)S(1)}, bf16[32,1024]{1,0:T(8,128)(2,1)S(1)}, u32[]{:S(2)}, u32[]{:S(2)}) %collective-permute-start.7) | collective-permute-done | bytes 65568 | tf_op jit(solution)/shard_map/ppermute | solution.py:626
  39.4 0.0 slice-done
  39.4 0.0 slice-done.1
  39.4 0.0 slice-done.2
  39.4 0.0 slice-done.3
  39.4 0.0 copy-done
  39.4 0.0 copy-done.1
  39.4 5.7 %expand_first.1 = (f32[32,3584]{1,0:T(8,128)S(1)}, f32[32,3584]{1,0:T(8,128)S(1)}, f32[32,1024]{1,0:T(8,128)S(1)}, f32[32,128]{1,0:T(8,128)S(1)}) custom-call(s32[4]{0:T(128)S(1)} %pad_add_fusion.refs_0_.at, bf16[32,2048]{1,0:T(8,128)(2,1)S(1)} %get-tuple-element.26.refs_1_, bf16[16,128]{1,0:T(8,128)(2,1)S(1)} %bitcast.11, bf16[2048,3584]{1,0:T(8,128)(2,1)S(1)} %bitcast.9, ...), custom_call_target="tpu_custom_call" | custom-call | flops 939524096 | bytes 29360128 | tf_op jit(solution)/shard_map/expand_first/pallas_call | solution.py:435
  45.1 0.0 collective-permute-done.9.refs_8_
  45.1 3.4 %expand_send.1 = (bf16[32,3968]{1,0:T(8,128)(2,1)S(1)}, f32[32,1024]{1,0:T(8,128)S(1)}, bf16[32,1024]{1,0:T(8,128)(2,1)S(1)}) custom-call(s32[4]{0:T(128)S(1)} %pad_add_fusion.refs_0_.at, bf16[32,2048]{1,0:T(8,128)(2,1)S(1)} %get-tuple-element.26.refs_1_, bf16[16,128]{1,0:T(8,128)(2,1)S(1)} %bitcast.12, f32[32,3584]{1,0:T(8,128)S(1)} %get-tuple-element.32.refs_3_, ...), custom_call_target="tpu_custom_call" | custom-call | flops 469762048 | bytes 14680064 | tf_op jit(solution)/shard_map/expand_send/pallas_call | solution.py:471
  48.6 0.1 collective-permute-start.10
  48.6 3.1 %expand_keep.1.keep = bf16[32,3584]{1,0:T(8,128)(2,1)S(1)} custom-call(s32[4]{0:T(128)S(1)} %pad_add_fusion.refs_0_.at, bf16[32,1024]{1,0:T(8,128)(2,1)S(1)} %get-tuple-element.35.x, f32[32,3584]{1,0:T(8,128)S(1)} %get-tuple-element.36.before, bf16[2048,3584]{1,0:T(8,128)(2,1)S(1)} %bitcast.9, bf16[2048,3584]{1,0:T(8,128)(2,1)S(1)} %copy-done), custom_call_target="tpu_custom_call" | custom-call | flops 469762048 | bytes 14680064 | tf_op jit(solution)/shard_map/expand_keep/pallas_call | solution.py:494
  51.8 0.0 collective-permute-done.10.received
  51.8 0.1 pair.1.refs_1_.refs_0_
  51.8 0.5 collective-permute-start.11
  52.4 6.0 %fetch.3 = (bf16[1792,2048]{1,0:T(8,128)(2,1)S(1)}, bf16[1792,2048]{1,0:T(8,128)(2,1)S(1)}, f32[8,128]{1,0:T(8,128)S(1)}) custom-call(s32[4]{0:T(128)S(1)} %pad_add_fusion.refs_0_.at, bf16[32,3968]{1,0:T(8,128)(2,1)S(1)} %pair.1.refs_1_.refs_0_, bf16[3584,2048]{1,0:T(8,128)(2,1)} %refs_3_.5, bf16[3584,2048]{1,0:T(8,128)(2,1)} %refs_3_.5), custom_call_target="tpu_custom_call" | custom-call | bytes 29360128 | tf_op jit(solution)/shard_map/fetch/pallas_call | solution.py:94
  58.4 2.0 %collective-permute-done.11.refs_1_ = bf16[32,3968]{1,0:T(8,128)(2,1)S(1)} collective-permute-done((bf16[32,3968]{1,0:T(8,128)(2,1)S(1)}, bf16[32,3968]{1,0:T(8,128)(2,1)S(1)}, u32[]{:S(2)}, u32[]{:S(2)}) %collective-permute-start.11) | collective-permute-done | bytes 253984 | tf_op jit(solution)/shard_map/ppermute | solution.py:626
  60.4 0.1 gated.1.hidden
  60.6 0.1 collective-permute-start.12
  60.7 1.4 %contract.1.refs_3_ = f32[32,2048]{1,0:T(8,128)S(1)} custom-call(bf16[32,1792]{1,0:T(8,128)(2,1)S(1)} %gated.1.hidden, bf16[1792,2048]{1,0:T(8,128)(2,1)S(1)} %get-tuple-element.40.w), custom_call_target="tpu_custom_call" | custom-call | flops 234881024 | bytes 7340032 | tf_op jit(solution)/shard_map/contract/pallas_call | solution.py:557
  62.0 0.0 collective-permute-done.12.refs_1_
  62.0 1.9 %contract_last.1 = (f32[8,2048]{1,0:T(8,128)S(1)}, bf16[8,2048]{1,0:T(8,128)(2,1)S(1)}, bf16[8,2048]{1,0:T(8,128)(2,1)S(1)}, bf16[8,2048]{1,0:T(8,128)(2,1)S(1)}) custom-call(s32[4]{0:T(128)S(1)} %pad_add_fusion.refs_0_.at, bf16[32,1792]{1,0:T(8,128)(2,1)S(1)} %collective-permute-done.12.refs_1_, bf16[1792,2048]{1,0:T(8,128)(2,1)S(1)} %get-tuple-element.39.refs_2_, ...), custom_call_target="tpu_custom_call" | custom-call | flops 234881024 | bytes 7340032 | tf_op jit(solution)/shard_map/contract_last/pallas_call | solution.py:594
  64.0 0.5 collective-permute-start.13
  64.4 2.9 %collective-permute-start.14 = (bf16[8,2048]{1,0:T(8,128)(2,1)S(1)}, bf16[8,2048]{1,0:T(8,128)(2,1)S(1)}, u32[]{:S(2)}, u32[]{:S(2)}) collective-permute-start(bf16[8,2048]{1,0:T(8,128)(2,1)S(1)} %get-tuple-element.45), channel_id=1, source_target_pairs={{0,2},{1,3},{2,0},{3,1},{4,6},{5,7},{6,4},{7,5},{8,10},{9,11},{10,... | collective-permute-start | bytes 98312 | tf_op jit(solution)/shard_map/ppermute | solution.py:626
  67.3 1.1 %collective-permute-start.15 = (bf16[8,2048]{1,0:T(8,128)(2,1)S(1)}, bf16[8,2048]{1,0:T(8,128)(2,1)S(1)}, u32[]{:S(2)}, u32[]{:S(2)}) collective-permute-start(bf16[8,2048]{1,0:T(8,128)(2,1)S(1)} %get-tuple-element.46), channel_id=1, source_target_pairs={{0,3},{1,2},{2,1},{3,0},{4,7},{5,6},{6,5},{7,4},{8,11},{9,10},{10,... | collective-permute-start | bytes 98312 | tf_op jit(solution)/shard_map/ppermute | solution.py:626
  68.4 0.0 collective-permute-done.13
  68.4 0.9 %collective-permute-done.14 = bf16[8,2048]{1,0:T(8,128)(2,1)S(1)} collective-permute-done((bf16[8,2048]{1,0:T(8,128)(2,1)S(1)}, bf16[8,2048]{1,0:T(8,128)(2,1)S(1)}, u32[]{:S(2)}, u32[]{:S(2)}) %collective-permute-start.14) | collective-permute-done | bytes 32800 | tf_op jit(solution)/shard_map/ppermute | solution.py:626
  69.3 3.7 %collective-permute-done.15 = bf16[8,2048]{1,0:T(8,128)(2,1)S(1)} collective-permute-done((bf16[8,2048]{1,0:T(8,128)(2,1)S(1)}, bf16[8,2048]{1,0:T(8,128)(2,1)S(1)}, u32[]{:S(2)}, u32[]{:S(2)}) %collective-permute-start.15) | collective-permute-done | bytes 32800 | tf_op jit(solution)/shard_map/ppermute | solution.py:626
  73.0 0.6 add_convert_fusion
  (9 shorter events, 0.1 us)
Async XLA Ops:
  0.0 8.3 %copy-start.2 = (s32[8]{0:T(128)S(1)}, s32[8]{0:T(128)}, u32[]{:S(2)}) copy-start(s32[8]{0:T(128)} %param.24) | copy-start | bytes 100
  0.0 8.6 %copy-start.3 = (s32[8]{0:T(128)S(1)}, s32[8]{0:T(128)}, u32[]{:S(2)}) copy-start(s32[8]{0:T(128)} %param.25) | copy-start | bytes 100
  5.2 9.6 %collective-permute-start.1 = (bf16[32,2560]{1,0:T(8,128)(2,1)S(1)}, bf16[32,2560]{1,0:T(8,128)(2,1)S(1)}, u32[]{:S(2)}, u32[]{:S(2)}) collective-permute-start(bf16[32,2560]{1,0:T(8,128)(2,1)S(1)} %get-tuple-element.27.refs_1_.refs_4_), channel_id=1, source_target_pairs={{0,4},{4,0},{8,12},{12,8},{1,5},{5,1},{9,13},{13,9},{2,6},{6,2},{1... | collective-permute-start | bytes 491528 | tf_op jit(solution)/shard_map/ppermute | solution.py:626
  5.7 8.8 %collective-permute-start = (bf16[32,2560]{1,0:T(8,128)(2,1)S(1)}, bf16[32,2560]{1,0:T(8,128)(2,1)S(1)}, u32[]{:S(2)}, u32[]{:S(2)}) collective-permute-start(bf16[32,2560]{1,0:T(8,128)(2,1)S(1)} %get-tuple-element.27.refs_1_.refs_4_), channel_id=1, source_target_pairs={{0,8},{4,12},{8,0},{12,4},{1,9},{5,13},{9,1},{13,5},{2,10},{6,14},... | collective-permute-start | bytes 491528 | tf_op jit(solution)/shard_map/ppermute | solution.py:626
  8.8 30.6 %slice-start = ((s8[14680064]{0:T(1024)(128)(4,1)}), s8[4194304]{0:T(1024)(128)(4,1)S(1)}, s32[]{:S(2)}) async-start(s8[14680064]{0:T(1024)(128)(4,1)} %bitcast.8), calls=%async_computation | async-start | bytes 8388608
  8.8 30.6 %slice-start.1 = ((s8[14680064]{0:T(1024)(128)(4,1)}), s8[4194304]{0:T(1024)(128)(4,1)S(1)}, s32[]{:S(2)}) async-start(s8[14680064]{0:T(1024)(128)(4,1)} %bitcast.8), calls=%async_computation.1 | async-start | bytes 8388608
  14.5 1.5 %collective-permute-start.2 = (bf16[32,2560]{1,0:T(8,128)(2,1)S(1)}, bf16[32,2560]{1,0:T(8,128)(2,1)S(1)}, u32[]{:S(2)}, u32[]{:S(2)}) collective-permute-start(bf16[32,2560]{1,0:T(8,128)(2,1)S(1)} %hold.1.refs_5_), channel_id=1, source_target_pairs={{0,4},{4,0},{8,12},{12,8},{1,5},{5,1},{9,13},{13,9},{2,6},{6,2},{1... | collective-permute-start | bytes 491528 | tf_op jit(solution)/shard_map/ppermute | solution.py:626
  16.0 23.4 %slice-start.2 = ((s8[14680064]{0:T(1024)(128)(4,1)}), s8[4194304]{0:T(1024)(128)(4,1)S(1)}, s32[]{:S(2)}) async-start(s8[14680064]{0:T(1024)(128)(4,1)} %bitcast.8), calls=%async_computation.2 | async-start | bytes 8388608
  19.5 6.2 %collective-permute-start.3 = (bf16[32,2432]{1,0:T(8,128)(2,1)S(1)}, bf16[32,2432]{1,0:T(8,128)(2,1)S(1)}, u32[]{:S(2)}, u32[]{:S(2)}) collective-permute-start(bf16[32,2432]{1,0:T(8,128)(2,1)S(1)} %attend.1.refs_1_), channel_id=1, source_target_pairs={{0,8},{4,12},{8,0},{12,4},{1,9},{5,13},{9,1},{13,5},{2,10},{6,14},... | collective-permute-start | bytes 466952 | tf_op jit(solution)/shard_map/ppermute | solution.py:626
  19.8 5.8 %collective-permute-start.4 = (bf16[32,2432]{1,0:T(8,128)(2,1)S(1)}, bf16[32,2432]{1,0:T(8,128)(2,1)S(1)}, u32[]{:S(2)}, u32[]{:S(2)}) collective-permute-start(bf16[32,2432]{1,0:T(8,128)(2,1)S(1)} %attend.1.refs_1_), channel_id=1, source_target_pairs={{0,4},{4,0},{8,12},{12,8},{1,5},{5,1},{9,13},{13,9},{2,6},{6,2},{1... | collective-permute-start | bytes 466952 | tf_op jit(solution)/shard_map/ppermute | solution.py:626
  25.6 1.4 %collective-permute-start.5 = (bf16[32,2432]{1,0:T(8,128)(2,1)S(1)}, bf16[32,2432]{1,0:T(8,128)(2,1)S(1)}, u32[]{:S(2)}, u32[]{:S(2)}) collective-permute-start(bf16[32,2432]{1,0:T(8,128)(2,1)S(1)} %collective-permute-done.3.refs_2_), channel_id=1, source_target_pairs={{0,4},{4,0},{8,12},{12,8},{1,5},{5,1},{9,13},{13,9},{2,6},{6,2},{1... | collective-permute-start | bytes 466952 | tf_op jit(solution)/shard_map/ppermute | solution.py:626
  27.0 12.4 %slice-start.3 = ((s8[14680064]{0:T(1024)(128)(4,1)}), s8[2097152]{0:T(1024)(128)(4,1)S(1)}, s32[]{:S(2)}) async-start(s8[14680064]{0:T(1024)(128)(4,1)} %bitcast.8), calls=%async_computation.3 | async-start | bytes 4194304
  27.0 12.4 %copy-start = (bf16[2048,3584]{1,0:T(8,128)(2,1)S(1)}, bf16[2048,3584]{1,0:T(8,128)(2,1)}, u32[]{:S(2)}) copy-start(bf16[2048,3584]{1,0:T(8,128)(2,1)} %wu.1) | copy-start | bytes 44040196
  27.0 12.4 %copy-start.1 = (bf16[2048]{0:T(1024)(128)(2,1)S(1)}, bf16[2048]{0:T(1024)(128)(2,1)}, u32[]{:S(2)}) copy-start(bf16[2048]{0:T(1024)(128)(2,1)} %param.15) | copy-start | bytes 12292
  28.0 5.0 %collective-permute-start.6 = (bf16[32,1024]{1,0:T(8,128)(2,1)S(1)}, bf16[32,1024]{1,0:T(8,128)(2,1)S(1)}, u32[]{:S(2)}, u32[]{:S(2)}) collective-permute-start(bf16[32,1024]{1,0:T(8,128)(2,1)S(1)} %get-tuple-element.31.one), channel_id=1, source_target_pairs={{0,1},{1,0},{2,3},{3,2},{4,5},{5,4},{6,7},{7,6},{8,9},{9,8},{10,11... | collective-permute-start | bytes 196616 | tf_op jit(solution)/shard_map/ppermute | solution.py:626
  30.4 7.3 %collective-permute-start.8 = (bf16[32,1024]{1,0:T(8,128)(2,1)S(1)}, bf16[32,1024]{1,0:T(8,128)(2,1)S(1)}, u32[]{:S(2)}, u32[]{:S(2)}) collective-permute-start(bf16[32,1024]{1,0:T(8,128)(2,1)S(1)} %output_second.1.one), channel_id=1, source_target_pairs={{0,2},{1,3},{2,0},{3,1},{4,6},{5,7},{6,4},{7,5},{8,10},{9,11},{10,... | collective-permute-start | bytes 196616 | tf_op jit(solution)/shard_map/ppermute | solution.py:626
  33.0 6.4 %collective-permute-start.7 = (bf16[32,1024]{1,0:T(8,128)(2,1)S(1)}, bf16[32,1024]{1,0:T(8,128)(2,1)S(1)}, u32[]{:S(2)}, u32[]{:S(2)}) collective-permute-start(bf16[32,1024]{1,0:T(8,128)(2,1)S(1)} %add.41.refs_5_), channel_id=1, source_target_pairs={{0,2},{1,3},{2,0},{3,1},{4,6},{5,7},{6,4},{7,5},{8,10},{9,11},{10,... | collective-permute-start | bytes 196616 | tf_op jit(solution)/shard_map/ppermute | solution.py:626
  37.7 7.4 %collective-permute-start.9 = (bf16[32,1024]{1,0:T(8,128)(2,1)S(1)}, bf16[32,1024]{1,0:T(8,128)(2,1)S(1)}, u32[]{:S(2)}, u32[]{:S(2)}) collective-permute-start(bf16[32,1024]{1,0:T(8,128)(2,1)S(1)} %add.42.refs_7_), channel_id=1, source_target_pairs={{0,1},{1,0},{2,3},{3,2},{4,5},{5,4},{6,7},{7,6},{8,9},{9,8},{10,11... | collective-permute-start | bytes 196616 | tf_op jit(solution)/shard_map/ppermute | solution.py:626
  48.6 3.2 %collective-permute-start.10 = (bf16[32,3968]{1,0:T(8,128)(2,1)S(1)}, bf16[32,3968]{1,0:T(8,128)(2,1)S(1)}, u32[]{:S(2)}, u32[]{:S(2)}) collective-permute-start(bf16[32,3968]{1,0:T(8,128)(2,1)S(1)} %get-tuple-element.37.stats), channel_id=1, source_target_pairs={{0,4},{4,0},{8,12},{12,8},{1,5},{5,1},{9,13},{13,9},{2,6},{6,2},{1... | collective-permute-start | bytes 761864 | tf_op jit(solution)/shard_map/ppermute | solution.py:626
  51.8 8.6 %collective-permute-start.11 = (bf16[32,3968]{1,0:T(8,128)(2,1)S(1)}, bf16[32,3968]{1,0:T(8,128)(2,1)S(1)}, u32[]{:S(2)}, u32[]{:S(2)}) collective-permute-start(bf16[32,3968]{1,0:T(8,128)(2,1)S(1)} %pair.1.refs_1_.refs_0_), channel_id=1, source_target_pairs={{0,8},{4,12},{8,0},{12,4},{1,9},{5,13},{9,1},{13,5},{2,10},{6,14},... | collective-permute-start | bytes 761864 | tf_op jit(solution)/shard_map/ppermute | solution.py:626
  60.6 1.4 %collective-permute-start.12 = (bf16[32,1792]{1,0:T(8,128)(2,1)S(1)}, bf16[32,1792]{1,0:T(8,128)(2,1)S(1)}, u32[]{:S(2)}, u32[]{:S(2)}) collective-permute-start(bf16[32,1792]{1,0:T(8,128)(2,1)S(1)} %gated.1.hidden), channel_id=1, source_target_pairs={{0,4},{4,0},{8,12},{12,8},{1,5},{5,1},{9,13},{13,9},{2,6},{6,2},{1... | collective-permute-start | bytes 344072 | tf_op jit(solution)/shard_map/ppermute | solution.py:626
  64.0 4.5 %collective-permute-start.13 = (bf16[8,2048]{1,0:T(8,128)(2,1)S(1)}, bf16[8,2048]{1,0:T(8,128)(2,1)S(1)}, u32[]{:S(2)}, u32[]{:S(2)}) collective-permute-start(bf16[8,2048]{1,0:T(8,128)(2,1)S(1)} %get-tuple-element.44), channel_id=1, source_target_pairs={{0,1},{1,0},{2,3},{3,2},{4,5},{5,4},{6,7},{7,6},{8,9},{9,8},{10,11... | collective-permute-start | bytes 98312 | tf_op jit(solution)/shard_map/ppermute | solution.py:626
  64.4 4.9 %collective-permute-start.14 = (bf16[8,2048]{1,0:T(8,128)(2,1)S(1)}, bf16[8,2048]{1,0:T(8,128)(2,1)S(1)}, u32[]{:S(2)}, u32[]{:S(2)}) collective-permute-start(bf16[8,2048]{1,0:T(8,128)(2,1)S(1)} %get-tuple-element.45), channel_id=1, source_target_pairs={{0,2},{1,3},{2,0},{3,1},{4,6},{5,7},{6,4},{7,5},{8,10},{9,11},{10,... | collective-permute-start | bytes 98312 | tf_op jit(solution)/shard_map/ppermute | solution.py:626
  67.3 5.7 %collective-permute-start.15 = (bf16[8,2048]{1,0:T(8,128)(2,1)S(1)}, bf16[8,2048]{1,0:T(8,128)(2,1)S(1)}, u32[]{:S(2)}, u32[]{:S(2)}) collective-permute-start(bf16[8,2048]{1,0:T(8,128)(2,1)S(1)} %get-tuple-element.46), channel_id=1, source_target_pairs={{0,3},{1,2},{2,1},{3,0},{4,7},{5,6},{6,5},{7,4},{8,11},{9,10},{10,... | collective-permute-start | bytes 98312 | tf_op jit(solution)/shard_map/ppermute | solution.py:626

commit v8 on v7

--- a/solution.py
+++ b/solution.py
@@ -359,7 +359,7 @@
     )(attended, w)
 
 
-WIDE = 896
+WIDE = 1792
 SPLIT = 4
 
 

time: 73.8 us -> 72.1 us (0.977)
  Pallas kernels: 37.8 us -> 36.1 us
    pallas_call x1, Pallas kernels: 5.68 us -> 4.83 us  [expand_first(): pl.pallas_call(lambda *refs: expand_first_kernel(len(parts), *refs), in_s...]
  transfers between devices with their start and end apart: 16 -> 16, of which waited for: 8 -> 8; matrix products, arithmetic and copies ran while one was open for 1% -> 1% of each run, Pallas kernels for 31% -> 30%
where the time goes in v8:
time: 72.1 us; the launch traced here: 72 us
  Pallas kernels  36.1 us (50%)
  waiting for transfers between devices  18.8 us (26%)
  starting transfers between devices  15.6 us (22%)
  other arithmetic  1.02 us (1%)
    ppermute x16, waiting for transfers between devices, swap(): return lax.ppermute(x, axis, [(i, i ^ bit) for i in range(n)])  18.8 us
    ppermute x16, starting transfers between devices, swap(): return lax.ppermute(x, axis, [(i, i ^ bit) for i in range(n)])  15.6 us
    pallas_call x2, Pallas kernels, fetch(): pl.pallas_call(lambda *refs: fetch_kernel(wanted, len(after), *refs), in_...  11.7 us
    pallas_call x1, Pallas kernels, project(): pl.pallas_call(lambda *refs: project_kernel(chunks, *refs), in_specs=[SME...  5.11 us
    pallas_call x1, Pallas kernels, expand_first(): pl.pallas_call(lambda *refs: expand_first_kernel(len(parts), *refs), in_s...  4.83 us
    pallas_call x1, Pallas kernels, attend(): pl.pallas_call(lambda *refs: attend_kernel(len(parts), *refs), in_specs=[...  3.46 us
    pallas_call x1, Pallas kernels, expand_send(): pl.pallas_call(lambda *refs: expand_send_kernel(len(parts), *refs), in_sp...  3.01 us
    pallas_call x1, Pallas kernels, expand_keep(): pl.pallas_call(expand_keep_kernel, in_specs=[SMEM] + [VMEM] * 2 + [ANY] *...  2.69 us
  transfers between devices with their start and end apart: 16, of which 8 were waited for; matrix products, arithmetic and copies ran while one was open for 1% of the time, Pallas kernels for 30%

profile of v8, /device:TPU:0, one launch (start us, length us, event | category | flops | bytes accessed | tf_op | source)
XLA Modules:
  0.0 72.0 jit_solution(11028520925713661755)
XLA Ops:
  0.0 0.0 copy-start.2
  0.0 0.0 copy-start.3
  0.0 0.1 pad_add_fusion.refs_0_.at
  0.1 5.1 %project.1 = (bf16[32,2560]{1,0:T(8,128)(2,1)S(1)}, bf16[32,2048]{1,0:T(8,128)(2,1)S(1)}) custom-call(s32[4]{0:T(128)S(1)} %pad_add_fusion.refs_0_.at, bf16[32,8192]{1,0:T(8,128)(2,1)} %refs_1_.1, bf16[64,128]{1,0:T(8,128)(2,1)} %bitcast.14, bf16[2048,2048]{1,0:T(8,128)(2,1)} %refs_3_.3, bf16[2048,256]{1,0:T(8,128)(2,1)} %refs_4_.2, bf16[2048,256]{1,0:T(8,128)(2,1)} %refs_5_.2), custom_call_target="tpu_custom_call" | custom-call | flops 335544320 | bytes 10485760 | tf_op jit(solution)/shard_map/project/pallas_call | solution.py:178
  5.2 0.5 collective-permute-start.1
  5.7 2.6 %collective-permute-start = (bf16[32,2560]{1,0:T(8,128)(2,1)S(1)}, bf16[32,2560]{1,0:T(8,128)(2,1)S(1)}, u32[]{:S(2)}, u32[]{:S(2)}) collective-permute-start(bf16[32,2560]{1,0:T(8,128)(2,1)S(1)} %get-tuple-element.27.refs_1_.refs_4_), channel_id=1, source_target_pairs={{0,8},{4,12},{8,0},{12,4},{1,9},{5,13},{9,1},{13,5},{2,10},{6,14},... | collective-permute-start | bytes 491528 | tf_op jit(solution)/shard_map/ppermute | solution.py:626
  8.3 0.0 copy-done.2
  8.3 0.1 add_convert_fusion.1
  8.4 0.1 convert_element_type.24
  8.5 0.1 fusion
  8.6 0.0 copy-done.3
  8.6 0.1 concatenate.10.refs_2_.refs_0_
  8.7 0.1 pad_maximum_fusion
  8.8 0.0 slice-start
  8.8 5.7 %fetch.2 = (bf16[16,512,256]{2,1,0:T(8,128)(2,1)S(1)}, bf16[2048,2048]{1,0:T(8,128)(2,1)S(1)}, f32[8,128]{1,0:T(8,128)S(1)}) custom-call(s32[4]{0:T(128)S(1)} %pad_add_fusion.refs_0_.at, bf16[32,2560]{1,0:T(8,128)(2,1)S(1)} %get-tuple-element.27.refs_1_.refs_4_, s32[20]{0:T(128)S(1)} %concatenate.10.refs_2_.refs_0_, ...), custom_call_target="tpu_custom_call" | custom-call | bytes 25165824 | tf_op jit(solution)/shard_map/fetch/pallas_call | solution.py:94
  14.5 0.0 collective-permute-done.__0_
  14.5 0.2 collective-permute-start.2
  14.8 0.0 collective-permute-done.1.refs_6_
  14.8 1.2 %collective-permute-done.2.refs_7_ = bf16[32,2560]{1,0:T(8,128)(2,1)S(1)} collective-permute-done((bf16[32,2560]{1,0:T(8,128)(2,1)S(1)}, bf16[32,2560]{1,0:T(8,128)(2,1)S(1)}, u32[]{:S(2)}, u32[]{:S(2)}) %collective-permute-start.2) | collective-permute-done | bytes 163872 | tf_op jit(solution)/shard_map/ppermute | solution.py:626
  16.0 0.0 slice-start.2
  16.0 3.5 %attend.1.refs_1_ = bf16[32,2432]{1,0:T(8,128)(2,1)S(1)} custom-call(s32[20]{0:T(128)S(1)} %concatenate.10.refs_2_.refs_0_, f32[32,128]{1,0:T(8,128)S(1)} %get-tuple-element.50.refs_3_.refs_1_, f32[32,128]{1,0:T(8,128)S(1)} %get-tuple-element.51.refs_4_.refs_2_, bf16[2,8,512,256]{3,2,1,0:T(8,128)(2,1)S(1)} %bitcast.10, ...), custom_call_target="tpu_custom_call" | custom-call | flops 134217728 | bytes 4194304 | tf_op jit(solution)/shard_map/attend/pallas_call | solution.py:289
  19.5 0.3 collective-permute-start.3
  19.8 0.0 collective-permute-start.4
  19.8 5.8 %collective-permute-done.3.refs_2_ = bf16[32,2432]{1,0:T(8,128)(2,1)S(1)} collective-permute-done((bf16[32,2432]{1,0:T(8,128)(2,1)S(1)}, bf16[32,2432]{1,0:T(8,128)(2,1)S(1)}, u32[]{:S(2)}, u32[]{:S(2)}) %collective-permute-start.3) | collective-permute-done | bytes 155680 | tf_op jit(solution)/shard_map/ppermute | solution.py:626
  25.6 0.0 collective-permute-start.5
  25.6 0.0 collective-permute-done.4.refs_3_
  25.6 1.4 %collective-permute-done.5.refs_4_ = bf16[32,2432]{1,0:T(8,128)(2,1)S(1)} collective-permute-done((bf16[32,2432]{1,0:T(8,128)(2,1)S(1)}, bf16[32,2432]{1,0:T(8,128)(2,1)S(1)}, u32[]{:S(2)}, u32[]{:S(2)}) %collective-permute-start.5) | collective-permute-done | bytes 155680 | tf_op jit(solution)/shard_map/ppermute | solution.py:626
  27.0 1.0 %output_first.1 = (bf16[32,1024]{1,0:T(8,128)(2,1)S(1)}, bf16[32,2048]{1,0:T(8,128)(2,1)S(1)}) custom-call(bf16[2048,2048]{1,0:T(8,128)(2,1)S(1)} %get-tuple-element.28.refs_0_.w, bf16[32,2432]{1,0:T(8,128)(2,1)S(1)} %attend.1.refs_1_, bf16[32,2432]{1,0:T(8,128)(2,1)S(1)} %collective-permute-done.3.refs_2_, ...), custom_call_target="tpu_custom_call" | custom-call | flops 268435456 | bytes 8388608 | tf_op jit(solution)/shard_map/output_first/pallas_call | solution.py:335
  28.0 1.6 %collective-permute-start.6 = (bf16[32,1024]{1,0:T(8,128)(2,1)S(1)}, bf16[32,1024]{1,0:T(8,128)(2,1)S(1)}, u32[]{:S(2)}, u32[]{:S(2)}) collective-permute-start(bf16[32,1024]{1,0:T(8,128)(2,1)S(1)} %get-tuple-element.31.one), channel_id=1, source_target_pairs={{0,1},{1,0},{2,3},{3,2},{4,5},{5,4},{6,7},{7,6},{8,9},{9,8},{10,11... | collective-permute-start | bytes 196616 | tf_op jit(solution)/shard_map/ppermute | solution.py:626
  29.6 0.8 %output_second.1.one = bf16[32,1024]{1,0:T(8,128)(2,1)S(1)} custom-call(bf16[32,2048]{1,0:T(8,128)(2,1)S(1)} %get-tuple-element.34.x, bf16[2048,2048]{1,0:T(8,128)(2,1)S(1)} %get-tuple-element.28.refs_0_.w), custom_call_target="tpu_custom_call" | custom-call | flops 268435456 | bytes 8388608 | tf_op jit(solution)/shard_map/output_second/pallas_call | solution.py:351
  30.4 2.6 %collective-permute-start.8 = (bf16[32,1024]{1,0:T(8,128)(2,1)S(1)}, bf16[32,1024]{1,0:T(8,128)(2,1)S(1)}, u32[]{:S(2)}, u32[]{:S(2)}) collective-permute-start(bf16[32,1024]{1,0:T(8,128)(2,1)S(1)} %output_second.1.one), channel_id=1, source_target_pairs={{0,2},{1,3},{2,0},{3,1},{4,6},{5,7},{6,4},{7,5},{8,10},{9,11},{10,... | collective-permute-start | bytes 196616 | tf_op jit(solution)/shard_map/ppermute | solution.py:626
  33.0 0.0 collective-permute-done.6.two
  33.0 2.5 %collective-permute-start.7 = (bf16[32,1024]{1,0:T(8,128)(2,1)S(1)}, bf16[32,1024]{1,0:T(8,128)(2,1)S(1)}, u32[]{:S(2)}, u32[]{:S(2)}) collective-permute-start(bf16[32,1024]{1,0:T(8,128)(2,1)S(1)} %add.41.refs_5_), channel_id=1, source_target_pairs={{0,2},{1,3},{2,0},{3,1},{4,6},{5,7},{6,4},{7,5},{8,10},{9,11},{10,... | collective-permute-start | bytes 196616 | tf_op jit(solution)/shard_map/ppermute | solution.py:626
  35.5 2.2 %collective-permute-done.8.two = bf16[32,1024]{1,0:T(8,128)(2,1)S(1)} collective-permute-done((bf16[32,1024]{1,0:T(8,128)(2,1)S(1)}, bf16[32,1024]{1,0:T(8,128)(2,1)S(1)}, u32[]{:S(2)}, u32[]{:S(2)}) %collective-permute-start.8) | collective-permute-done | bytes 65568 | tf_op jit(solution)/shard_map/ppermute | solution.py:626
  37.7 0.1 collective-permute-start.9
  37.8 1.6 %collective-permute-done.7.refs_6_ = bf16[32,1024]{1,0:T(8,128)(2,1)S(1)} collective-permute-done((bf16[32,1024]{1,0:T(8,128)(2,1)S(1)}, bf16[32,1024]{1,0:T(8,128)(2,1)S(1)}, u32[]{:S(2)}, u32[]{:S(2)}) %collective-permute-start.7) | collective-permute-done | bytes 65568 | tf_op jit(solution)/shard_map/ppermute | solution.py:626
  39.4 0.0 slice-done
  39.4 0.0 slice-done.1
  39.4 0.0 slice-done.2
  39.4 0.0 slice-done.3
  39.4 0.0 copy-done
  39.4 0.0 copy-done.1
  39.4 4.8 %expand_first.1 = (f32[32,3584]{1,0:T(8,128)S(1)}, f32[32,3584]{1,0:T(8,128)S(1)}, f32[32,1024]{1,0:T(8,128)S(1)}, f32[32,128]{1,0:T(8,128)S(1)}) custom-call(s32[4]{0:T(128)S(1)} %pad_add_fusion.refs_0_.at, bf16[32,2048]{1,0:T(8,128)(2,1)S(1)} %get-tuple-element.26.refs_1_, bf16[16,128]{1,0:T(8,128)(2,1)S(1)} %bitcast.11, bf16[2048,3584]{1,0:T(8,128)(2,1)S(1)} %bitcast.9, ...), custom_call_target="tpu_custom_call" | custom-call | flops 939524096 | bytes 29360128 | tf_op jit(solution)/shard_map/expand_first/pallas_call | solution.py:435
  44.3 0.0 collective-permute-done.9.refs_8_
  44.3 3.0 %expand_send.1 = (bf16[32,3968]{1,0:T(8,128)(2,1)S(1)}, f32[32,1024]{1,0:T(8,128)S(1)}, bf16[32,1024]{1,0:T(8,128)(2,1)S(1)}) custom-call(s32[4]{0:T(128)S(1)} %pad_add_fusion.refs_0_.at, bf16[32,2048]{1,0:T(8,128)(2,1)S(1)} %get-tuple-element.26.refs_1_, bf16[16,128]{1,0:T(8,128)(2,1)S(1)} %bitcast.12, f32[32,3584]{1,0:T(8,128)S(1)} %get-tuple-element.32.refs_3_, ...), custom_call_target="tpu_custom_call" | custom-call | flops 469762048 | bytes 14680064 | tf_op jit(solution)/shard_map/expand_send/pallas_call | solution.py:471
  47.3 0.1 collective-permute-start.10
  47.4 2.7 %expand_keep.1.keep = bf16[32,3584]{1,0:T(8,128)(2,1)S(1)} custom-call(s32[4]{0:T(128)S(1)} %pad_add_fusion.refs_0_.at, bf16[32,1024]{1,0:T(8,128)(2,1)S(1)} %get-tuple-element.35.x, f32[32,3584]{1,0:T(8,128)S(1)} %get-tuple-element.36.before, bf16[2048,3584]{1,0:T(8,128)(2,1)S(1)} %bitcast.9, bf16[2048,3584]{1,0:T(8,128)(2,1)S(1)} %copy-done), custom_call_target="tpu_custom_call" | custom-call | flops 469762048 | bytes 14680064 | tf_op jit(solution)/shard_map/expand_keep/pallas_call | solution.py:494
  50.1 0.0 collective-permute-done.10.received
  50.1 0.1 pair.1.refs_1_.refs_0_
  50.2 0.5 collective-permute-start.11
  50.7 6.0 %fetch.3 = (bf16[1792,2048]{1,0:T(8,128)(2,1)S(1)}, bf16[1792,2048]{1,0:T(8,128)(2,1)S(1)}, f32[8,128]{1,0:T(8,128)S(1)}) custom-call(s32[4]{0:T(128)S(1)} %pad_add_fusion.refs_0_.at, bf16[32,3968]{1,0:T(8,128)(2,1)S(1)} %pair.1.refs_1_.refs_0_, bf16[3584,2048]{1,0:T(8,128)(2,1)} %refs_3_.5, bf16[3584,2048]{1,0:T(8,128)(2,1)} %refs_3_.5), custom_call_target="tpu_custom_call" | custom-call | bytes 29360128 | tf_op jit(solution)/shard_map/fetch/pallas_call | solution.py:94
  56.7 2.0 %collective-permute-done.11.refs_1_ = bf16[32,3968]{1,0:T(8,128)(2,1)S(1)} collective-permute-done((bf16[32,3968]{1,0:T(8,128)(2,1)S(1)}, bf16[32,3968]{1,0:T(8,128)(2,1)S(1)}, u32[]{:S(2)}, u32[]{:S(2)}) %collective-permute-start.11) | collective-permute-done | bytes 253984 | tf_op jit(solution)/shard_map/ppermute | solution.py:626
  58.8 0.1 gated.1.hidden
  58.9 0.1 collective-permute-start.12
  59.0 1.4 %contract.1.refs_3_ = f32[32,2048]{1,0:T(8,128)S(1)} custom-call(bf16[32,1792]{1,0:T(8,128)(2,1)S(1)} %gated.1.hidden, bf16[1792,2048]{1,0:T(8,128)(2,1)S(1)} %get-tuple-element.40.w), custom_call_target="tpu_custom_call" | custom-call | flops 234881024 | bytes 7340032 | tf_op jit(solution)/shard_map/contract/pallas_call | solution.py:557
  60.3 0.0 collective-permute-done.12.refs_1_
  60.3 1.9 %contract_last.1 = (f32[8,2048]{1,0:T(8,128)S(1)}, bf16[8,2048]{1,0:T(8,128)(2,1)S(1)}, bf16[8,2048]{1,0:T(8,128)(2,1)S(1)}, bf16[8,2048]{1,0:T(8,128)(2,1)S(1)}) custom-call(s32[4]{0:T(128)S(1)} %pad_add_fusion.refs_0_.at, bf16[32,1792]{1,0:T(8,128)(2,1)S(1)} %collective-permute-done.12.refs_1_, bf16[1792,2048]{1,0:T(8,128)(2,1)S(1)} %get-tuple-element.39.refs_2_, ...), custom_call_target="tpu_custom_call" | custom-call | flops 234881024 | bytes 7340032 | tf_op jit(solution)/shard_map/contract_last/pallas_call | solution.py:594
  62.3 0.5 collective-permute-start.13
  62.8 2.8 %collective-permute-start.14 = (bf16[8,2048]{1,0:T(8,128)(2,1)S(1)}, bf16[8,2048]{1,0:T(8,128)(2,1)S(1)}, u32[]{:S(2)}, u32[]{:S(2)}) collective-permute-start(bf16[8,2048]{1,0:T(8,128)(2,1)S(1)} %get-tuple-element.45), channel_id=1, source_target_pairs={{0,2},{1,3},{2,0},{3,1},{4,6},{5,7},{6,4},{7,5},{8,10},{9,11},{10,... | collective-permute-start | bytes 98312 | tf_op jit(solution)/shard_map/ppermute | solution.py:626
  65.6 1.1 %collective-permute-start.15 = (bf16[8,2048]{1,0:T(8,128)(2,1)S(1)}, bf16[8,2048]{1,0:T(8,128)(2,1)S(1)}, u32[]{:S(2)}, u32[]{:S(2)}) collective-permute-start(bf16[8,2048]{1,0:T(8,128)(2,1)S(1)} %get-tuple-element.46), channel_id=1, source_target_pairs={{0,3},{1,2},{2,1},{3,0},{4,7},{5,6},{6,5},{7,4},{8,11},{9,10},{10,... | collective-permute-start | bytes 98312 | tf_op jit(solution)/shard_map/ppermute | solution.py:626
  66.7 0.0 collective-permute-done.13
  66.7 0.9 %collective-permute-done.14 = bf16[8,2048]{1,0:T(8,128)(2,1)S(1)} collective-permute-done((bf16[8,2048]{1,0:T(8,128)(2,1)S(1)}, bf16[8,2048]{1,0:T(8,128)(2,1)S(1)}, u32[]{:S(2)}, u32[]{:S(2)}) %collective-permute-start.14) | collective-permute-done | bytes 32800 | tf_op jit(solution)/shard_map/ppermute | solution.py:626
  67.7 3.7 %collective-permute-done.15 = bf16[8,2048]{1,0:T(8,128)(2,1)S(1)} collective-permute-done((bf16[8,2048]{1,0:T(8,128)(2,1)S(1)}, bf16[8,2048]{1,0:T(8,128)(2,1)S(1)}, u32[]{:S(2)}, u32[]{:S(2)}) %collective-permute-start.15) | collective-permute-done | bytes 32800 | tf_op jit(solution)/shard_map/ppermute | solution.py:626
  71.3 0.6 add_convert_fusion
  (9 shorter events, 0.1 us)
Async XLA Ops:
  0.0 8.3 %copy-start.2 = (s32[8]{0:T(128)S(1)}, s32[8]{0:T(128)}, u32[]{:S(2)}) copy-start(s32[8]{0:T(128)} %param.24) | copy-start | bytes 100
  0.0 8.6 %copy-start.3 = (s32[8]{0:T(128)S(1)}, s32[8]{0:T(128)}, u32[]{:S(2)}) copy-start(s32[8]{0:T(128)} %param.25) | copy-start | bytes 100
  5.2 9.6 %collective-permute-start.1 = (bf16[32,2560]{1,0:T(8,128)(2,1)S(1)}, bf16[32,2560]{1,0:T(8,128)(2,1)S(1)}, u32[]{:S(2)}, u32[]{:S(2)}) collective-permute-start(bf16[32,2560]{1,0:T(8,128)(2,1)S(1)} %get-tuple-element.27.refs_1_.refs_4_), channel_id=1, source_target_pairs={{0,4},{4,0},{8,12},{12,8},{1,5},{5,1},{9,13},{13,9},{2,6},{6,2},{1... | collective-permute-start | bytes 491528 | tf_op jit(solution)/shard_map/ppermute | solution.py:626
  5.7 8.8 %collective-permute-start = (bf16[32,2560]{1,0:T(8,128)(2,1)S(1)}, bf16[32,2560]{1,0:T(8,128)(2,1)S(1)}, u32[]{:S(2)}, u32[]{:S(2)}) collective-permute-start(bf16[32,2560]{1,0:T(8,128)(2,1)S(1)} %get-tuple-element.27.refs_1_.refs_4_), channel_id=1, source_target_pairs={{0,8},{4,12},{8,0},{12,4},{1,9},{5,13},{9,1},{13,5},{2,10},{6,14},... | collective-permute-start | bytes 491528 | tf_op jit(solution)/shard_map/ppermute | solution.py:626
  8.8 30.6 %slice-start = ((s8[14680064]{0:T(1024)(128)(4,1)}), s8[4194304]{0:T(1024)(128)(4,1)S(1)}, s32[]{:S(2)}) async-start(s8[14680064]{0:T(1024)(128)(4,1)} %bitcast.8), calls=%async_computation | async-start | bytes 8388608
  8.8 30.6 %slice-start.1 = ((s8[14680064]{0:T(1024)(128)(4,1)}), s8[4194304]{0:T(1024)(128)(4,1)S(1)}, s32[]{:S(2)}) async-start(s8[14680064]{0:T(1024)(128)(4,1)} %bitcast.8), calls=%async_computation.1 | async-start | bytes 8388608
  14.5 1.5 %collective-permute-start.2 = (bf16[32,2560]{1,0:T(8,128)(2,1)S(1)}, bf16[32,2560]{1,0:T(8,128)(2,1)S(1)}, u32[]{:S(2)}, u32[]{:S(2)}) collective-permute-start(bf16[32,2560]{1,0:T(8,128)(2,1)S(1)} %hold.1.refs_5_), channel_id=1, source_target_pairs={{0,4},{4,0},{8,12},{12,8},{1,5},{5,1},{9,13},{13,9},{2,6},{6,2},{1... | collective-permute-start | bytes 491528 | tf_op jit(solution)/shard_map/ppermute | solution.py:626
  16.0 23.4 %slice-start.2 = ((s8[14680064]{0:T(1024)(128)(4,1)}), s8[4194304]{0:T(1024)(128)(4,1)S(1)}, s32[]{:S(2)}) async-start(s8[14680064]{0:T(1024)(128)(4,1)} %bitcast.8), calls=%async_computation.2 | async-start | bytes 8388608
  19.5 6.2 %collective-permute-start.3 = (bf16[32,2432]{1,0:T(8,128)(2,1)S(1)}, bf16[32,2432]{1,0:T(8,128)(2,1)S(1)}, u32[]{:S(2)}, u32[]{:S(2)}) collective-permute-start(bf16[32,2432]{1,0:T(8,128)(2,1)S(1)} %attend.1.refs_1_), channel_id=1, source_target_pairs={{0,8},{4,12},{8,0},{12,4},{1,9},{5,13},{9,1},{13,5},{2,10},{6,14},... | collective-permute-start | bytes 466952 | tf_op jit(solution)/shard_map/ppermute | solution.py:626
  19.8 5.8 %collective-permute-start.4 = (bf16[32,2432]{1,0:T(8,128)(2,1)S(1)}, bf16[32,2432]{1,0:T(8,128)(2,1)S(1)}, u32[]{:S(2)}, u32[]{:S(2)}) collective-permute-start(bf16[32,2432]{1,0:T(8,128)(2,1)S(1)} %attend.1.refs_1_), channel_id=1, source_target_pairs={{0,4},{4,0},{8,12},{12,8},{1,5},{5,1},{9,13},{13,9},{2,6},{6,2},{1... | collective-permute-start | bytes 466952 | tf_op jit(solution)/shard_map/ppermute | solution.py:626
  25.6 1.4 %collective-permute-start.5 = (bf16[32,2432]{1,0:T(8,128)(2,1)S(1)}, bf16[32,2432]{1,0:T(8,128)(2,1)S(1)}, u32[]{:S(2)}, u32[]{:S(2)}) collective-permute-start(bf16[32,2432]{1,0:T(8,128)(2,1)S(1)} %collective-permute-done.3.refs_2_), channel_id=1, source_target_pairs={{0,4},{4,0},{8,12},{12,8},{1,5},{5,1},{9,13},{13,9},{2,6},{6,2},{1... | collective-permute-start | bytes 466952 | tf_op jit(solution)/shard_map/ppermute | solution.py:626
  27.0 12.4 %slice-start.3 = ((s8[14680064]{0:T(1024)(128)(4,1)}), s8[2097152]{0:T(1024)(128)(4,1)S(1)}, s32[]{:S(2)}) async-start(s8[14680064]{0:T(1024)(128)(4,1)} %bitcast.8), calls=%async_computation.3 | async-start | bytes 4194304
  27.0 12.4 %copy-start = (bf16[2048,3584]{1,0:T(8,128)(2,1)S(1)}, bf16[2048,3584]{1,0:T(8,128)(2,1)}, u32[]{:S(2)}) copy-start(bf16[2048,3584]{1,0:T(8,128)(2,1)} %wu.1) | copy-start | bytes 44040196
  27.0 12.4 %copy-start.1 = (bf16[2048]{0:T(1024)(128)(2,1)S(1)}, bf16[2048]{0:T(1024)(128)(2,1)}, u32[]{:S(2)}) copy-start(bf16[2048]{0:T(1024)(128)(2,1)} %param.15) | copy-start | bytes 12292
  28.0 5.0 %collective-permute-start.6 = (bf16[32,1024]{1,0:T(8,128)(2,1)S(1)}, bf16[32,1024]{1,0:T(8,128)(2,1)S(1)}, u32[]{:S(2)}, u32[]{:S(2)}) collective-permute-start(bf16[32,1024]{1,0:T(8,128)(2,1)S(1)} %get-tuple-element.31.one), channel_id=1, source_target_pairs={{0,1},{1,0},{2,3},{3,2},{4,5},{5,4},{6,7},{7,6},{8,9},{9,8},{10,11... | collective-permute-start | bytes 196616 | tf_op jit(solution)/shard_map/ppermute | solution.py:626
  30.4 7.3 %collective-permute-start.8 = (bf16[32,1024]{1,0:T(8,128)(2,1)S(1)}, bf16[32,1024]{1,0:T(8,128)(2,1)S(1)}, u32[]{:S(2)}, u32[]{:S(2)}) collective-permute-start(bf16[32,1024]{1,0:T(8,128)(2,1)S(1)} %output_second.1.one), channel_id=1, source_target_pairs={{0,2},{1,3},{2,0},{3,1},{4,6},{5,7},{6,4},{7,5},{8,10},{9,11},{10,... | collective-permute-start | bytes 196616 | tf_op jit(solution)/shard_map/ppermute | solution.py:626
  33.0 6.4 %collective-permute-start.7 = (bf16[32,1024]{1,0:T(8,128)(2,1)S(1)}, bf16[32,1024]{1,0:T(8,128)(2,1)S(1)}, u32[]{:S(2)}, u32[]{:S(2)}) collective-permute-start(bf16[32,1024]{1,0:T(8,128)(2,1)S(1)} %add.41.refs_5_), channel_id=1, source_target_pairs={{0,2},{1,3},{2,0},{3,1},{4,6},{5,7},{6,4},{7,5},{8,10},{9,11},{10,... | collective-permute-start | bytes 196616 | tf_op jit(solution)/shard_map/ppermute | solution.py:626
  37.7 6.6 %collective-permute-start.9 = (bf16[32,1024]{1,0:T(8,128)(2,1)S(1)}, bf16[32,1024]{1,0:T(8,128)(2,1)S(1)}, u32[]{:S(2)}, u32[]{:S(2)}) collective-permute-start(bf16[32,1024]{1,0:T(8,128)(2,1)S(1)} %add.42.refs_7_), channel_id=1, source_target_pairs={{0,1},{1,0},{2,3},{3,2},{4,5},{5,4},{6,7},{7,6},{8,9},{9,8},{10,11... | collective-permute-start | bytes 196616 | tf_op jit(solution)/shard_map/ppermute | solution.py:626
  47.3 2.8 %collective-permute-start.10 = (bf16[32,3968]{1,0:T(8,128)(2,1)S(1)}, bf16[32,3968]{1,0:T(8,128)(2,1)S(1)}, u32[]{:S(2)}, u32[]{:S(2)}) collective-permute-start(bf16[32,3968]{1,0:T(8,128)(2,1)S(1)} %get-tuple-element.37.stats), channel_id=1, source_target_pairs={{0,4},{4,0},{8,12},{12,8},{1,5},{5,1},{9,13},{13,9},{2,6},{6,2},{1... | collective-permute-start | bytes 761864 | tf_op jit(solution)/shard_map/ppermute | solution.py:626
  50.2 8.6 %collective-permute-start.11 = (bf16[32,3968]{1,0:T(8,128)(2,1)S(1)}, bf16[32,3968]{1,0:T(8,128)(2,1)S(1)}, u32[]{:S(2)}, u32[]{:S(2)}) collective-permute-start(bf16[32,3968]{1,0:T(8,128)(2,1)S(1)} %pair.1.refs_1_.refs_0_), channel_id=1, source_target_pairs={{0,8},{4,12},{8,0},{12,4},{1,9},{5,13},{9,1},{13,5},{2,10},{6,14},... | collective-permute-start | bytes 761864 | tf_op jit(solution)/shard_map/ppermute | solution.py:626
  58.9 1.4 %collective-permute-start.12 = (bf16[32,1792]{1,0:T(8,128)(2,1)S(1)}, bf16[32,1792]{1,0:T(8,128)(2,1)S(1)}, u32[]{:S(2)}, u32[]{:S(2)}) collective-permute-start(bf16[32,1792]{1,0:T(8,128)(2,1)S(1)} %gated.1.hidden), channel_id=1, source_target_pairs={{0,4},{4,0},{8,12},{12,8},{1,5},{5,1},{9,13},{13,9},{2,6},{6,2},{1... | collective-permute-start | bytes 344072 | tf_op jit(solution)/shard_map/ppermute | solution.py:626
  62.3 4.5 %collective-permute-start.13 = (bf16[8,2048]{1,0:T(8,128)(2,1)S(1)}, bf16[8,2048]{1,0:T(8,128)(2,1)S(1)}, u32[]{:S(2)}, u32[]{:S(2)}) collective-permute-start(bf16[8,2048]{1,0:T(8,128)(2,1)S(1)} %get-tuple-element.44), channel_id=1, source_target_pairs={{0,1},{1,0},{2,3},{3,2},{4,5},{5,4},{6,7},{7,6},{8,9},{9,8},{10,11... | collective-permute-start | bytes 98312 | tf_op jit(solution)/shard_map/ppermute | solution.py:626
  62.8 4.9 %collective-permute-start.14 = (bf16[8,2048]{1,0:T(8,128)(2,1)S(1)}, bf16[8,2048]{1,0:T(8,128)(2,1)S(1)}, u32[]{:S(2)}, u32[]{:S(2)}) collective-permute-start(bf16[8,2048]{1,0:T(8,128)(2,1)S(1)} %get-tuple-element.45), channel_id=1, source_target_pairs={{0,2},{1,3},{2,0},{3,1},{4,6},{5,7},{6,4},{7,5},{8,10},{9,11},{10,... | collective-permute-start | bytes 98312 | tf_op jit(solution)/shard_map/ppermute | solution.py:626
  65.6 5.7 %collective-permute-start.15 = (bf16[8,2048]{1,0:T(8,128)(2,1)S(1)}, bf16[8,2048]{1,0:T(8,128)(2,1)S(1)}, u32[]{:S(2)}, u32[]{:S(2)}) collective-permute-start(bf16[8,2048]{1,0:T(8,128)(2,1)S(1)} %get-tuple-element.46), channel_id=1, source_target_pairs={{0,3},{1,2},{2,1},{3,0},{4,7},{5,6},{6,5},{7,4},{8,11},{9,10},{10,... | collective-permute-start | bytes 98312 | tf_op jit(solution)/shard_map/ppermute | solution.py:626

commit v9 on v8

--- a/solution.py
+++ b/solution.py
@@ -359,36 +359,30 @@
     )(attended, w)
 
 
-WIDE = 1792
-SPLIT = 4
+WIDE = 256
+AHEAD = 8
 
 
 def half_of(at, sides, x, row, wg, wu, held, sems, prepare=None):
-    count, half = x.shape[1], wg.shape[1] // 2
-    step = count // SPLIT
+    half = wg.shape[1] // 2
     jobs = []
     for side, out, before in sides:
         for base, w in ((0, wg), (half, wu)):
             for start, size in blocks_of(half, WIDE):
                 n = len(jobs)
                 cols = pl.ds(pl.multiple_of(side * half + start, LANES), size)
-                copies = [
-                    pltpu.make_async_copy(
-                        w.at[pl.ds(row + p * step, step), cols],
-                        held.at[n, pl.ds(p * step, step)],
-                        sems.at[n * SPLIT + p],
-                    )
-                    for p in range(SPLIT)
-                ]
-                jobs.append((copies, slice(base + start, base + start + size), out, before))
-    for copies, *_ in jobs:
-        for copy in copies:
-            copy.start()
+                copy = pltpu.make_async_copy(
+                    w.at[pl.ds(row, x.shape[1]), cols], held.at[n], sems.at[n]
+                )
+                jobs.append((copy, slice(base + start, base + start + size), out, before))
+    for copy, *_ in jobs[:AHEAD]:
+        copy.start()
     if prepare is not None:
         pl.when(at[2] >= 0)(prepare)
-    for n, (copies, cols, out, before) in enumerate(jobs):
-        for copy in copies:
-            copy.wait()
+    for n, (copy, cols, out, before) in enumerate(jobs):
+        copy.wait()
+        if n + AHEAD < len(jobs):
+            jobs[n + AHEAD][0].start()
         term = jnp.dot(x[...], held[n], preferred_element_type=f32)
         if before is not None:
             term = before[:, cols] + term
@@ -398,10 +392,7 @@
 def block_scratch(sides, count, half):
     blocks = blocks_of(half, WIDE)
     number = sides * 2 * len(blocks)
-    return [
-        pltpu.VMEM((number, count, blocks[0][1]), bf16),
-        pltpu.SemaphoreType.DMA((number * SPLIT,)),
-    ]
+    return [pltpu.VMEM((number, count, blocks[0][1]), bf16), pltpu.SemaphoreType.DMA((number,))]
 
 
 def residual(which, own, gain, parts, resid, x, gain_f):

time: 72.1 us -> 80.6 us (1.12)
  Pallas kernels: 36.1 us -> 44.6 us
    pallas_call x1, Pallas kernels: 4.83 us -> 9.05 us  [expand_first(): pl.pallas_call(lambda *refs: expand_first_kernel(len(parts), *refs), in_s...]
    pallas_call x1, Pallas kernels: 2.69 us -> 4.83 us  [expand_keep(): pl.pallas_call(expand_keep_kernel, in_specs=[SMEM] + [VMEM] * 2 + [ANY] *...]
    pallas_call x1, Pallas kernels: 3.01 us -> 5.15 us  [expand_send(): pl.pallas_call(lambda *refs: expand_send_kernel(len(parts), *refs), in_sp...]
  transfers between devices with their start and end apart: 16 -> 16, of which waited for: 8 -> 8; matrix products, arithmetic and copies ran while one was open for 1% -> 1% of each run, Pallas kernels for 30% -> 35%
where the time goes in v9:
time: 80.6 us; the launch traced here: 80.5 us
  Pallas kernels  44.6 us (55%)
  waiting for transfers between devices  18.8 us (23%)
  starting transfers between devices  15.6 us (19%)
  other arithmetic  1.02 us (1%)
    ppermute x16, waiting for transfers between devices, swap(): return lax.ppermute(x, axis, [(i, i ^ bit) for i in range(n)])  18.8 us
    ppermute x16, starting transfers between devices, swap(): return lax.ppermute(x, axis, [(i, i ^ bit) for i in range(n)])  15.6 us
    pallas_call x2, Pallas kernels, fetch(): pl.pallas_call(lambda *refs: fetch_kernel(wanted, len(after), *refs), in_...  11.7 us
    pallas_call x1, Pallas kernels, expand_first(): pl.pallas_call(lambda *refs: expand_first_kernel(len(parts), *refs), in_s...  9.05 us
    pallas_call x1, Pallas kernels, expand_send(): pl.pallas_call(lambda *refs: expand_send_kernel(len(parts), *refs), in_sp...  5.15 us
    pallas_call x1, Pallas kernels, project(): pl.pallas_call(lambda *refs: project_kernel(chunks, *refs), in_specs=[SME...  5.11 us
    pallas_call x1, Pallas kernels, expand_keep(): pl.pallas_call(expand_keep_kernel, in_specs=[SMEM] + [VMEM] * 2 + [ANY] *...  4.83 us
    pallas_call x1, Pallas kernels, attend(): pl.pallas_call(lambda *refs: attend_kernel(len(parts), *refs), in_specs=[...  3.46 us
  transfers between devices with their start and end apart: 16, of which 8 were waited for; matrix products, arithmetic and copies ran while one was open for 1% of the time, Pallas kernels for 35%

profile of v9, /device:TPU:0, one launch (start us, length us, event | category | flops | bytes accessed | tf_op | source)
XLA Modules:
  0.0 80.5 jit_solution(5717213097986477884)
XLA Ops:
  0.0 0.0 copy-start.2
  0.0 0.0 copy-start.3
  0.0 0.1 pad_add_fusion.refs_0_.at
  0.1 5.1 %project.1 = (bf16[32,2560]{1,0:T(8,128)(2,1)S(1)}, bf16[32,2048]{1,0:T(8,128)(2,1)S(1)}) custom-call(s32[4]{0:T(128)S(1)} %pad_add_fusion.refs_0_.at, bf16[32,8192]{1,0:T(8,128)(2,1)} %refs_1_.1, bf16[64,128]{1,0:T(8,128)(2,1)} %bitcast.14, bf16[2048,2048]{1,0:T(8,128)(2,1)} %refs_3_.3, bf16[2048,256]{1,0:T(8,128)(2,1)} %refs_4_.2, bf16[2048,256]{1,0:T(8,128)(2,1)} %refs_5_.2), custom_call_target="tpu_custom_call" | custom-call | flops 335544320 | bytes 10485760 | tf_op jit(solution)/shard_map/project/pallas_call | solution.py:178
  5.2 0.5 collective-permute-start.1
  5.7 2.6 %collective-permute-start = (bf16[32,2560]{1,0:T(8,128)(2,1)S(1)}, bf16[32,2560]{1,0:T(8,128)(2,1)S(1)}, u32[]{:S(2)}, u32[]{:S(2)}) collective-permute-start(bf16[32,2560]{1,0:T(8,128)(2,1)S(1)} %get-tuple-element.27.refs_1_.refs_4_), channel_id=1, source_target_pairs={{0,8},{4,12},{8,0},{12,4},{1,9},{5,13},{9,1},{13,5},{2,10},{6,14},... | collective-permute-start | bytes 491528 | tf_op jit(solution)/shard_map/ppermute | solution.py:617
  8.3 0.0 copy-done.2
  8.3 0.1 add_convert_fusion.1
  8.4 0.1 convert_element_type.24
  8.5 0.1 fusion
  8.6 0.0 copy-done.3
  8.6 0.1 concatenate.10.refs_2_.refs_0_
  8.7 0.1 pad_maximum_fusion
  8.8 0.0 slice-start
  8.8 0.0 slice-start.1
  8.8 5.7 %fetch.2 = (bf16[16,512,256]{2,1,0:T(8,128)(2,1)S(1)}, bf16[2048,2048]{1,0:T(8,128)(2,1)S(1)}, f32[8,128]{1,0:T(8,128)S(1)}) custom-call(s32[4]{0:T(128)S(1)} %pad_add_fusion.refs_0_.at, bf16[32,2560]{1,0:T(8,128)(2,1)S(1)} %get-tuple-element.27.refs_1_.refs_4_, s32[20]{0:T(128)S(1)} %concatenate.10.refs_2_.refs_0_, ...), custom_call_target="tpu_custom_call" | custom-call | bytes 25165824 | tf_op jit(solution)/shard_map/fetch/pallas_call | solution.py:94
  14.5 0.0 collective-permute-done.__0_
  14.5 0.2 collective-permute-start.2
  14.8 0.0 collective-permute-done.1.refs_6_
  14.8 1.2 %collective-permute-done.2.refs_7_ = bf16[32,2560]{1,0:T(8,128)(2,1)S(1)} collective-permute-done((bf16[32,2560]{1,0:T(8,128)(2,1)S(1)}, bf16[32,2560]{1,0:T(8,128)(2,1)S(1)}, u32[]{:S(2)}, u32[]{:S(2)}) %collective-permute-start.2) | collective-permute-done | bytes 163872 | tf_op jit(solution)/shard_map/ppermute | solution.py:617
  16.0 3.5 %attend.1.refs_1_ = bf16[32,2432]{1,0:T(8,128)(2,1)S(1)} custom-call(s32[20]{0:T(128)S(1)} %concatenate.10.refs_2_.refs_0_, f32[32,128]{1,0:T(8,128)S(1)} %get-tuple-element.50.refs_3_.refs_1_, f32[32,128]{1,0:T(8,128)S(1)} %get-tuple-element.51.refs_4_.refs_2_, bf16[2,8,512,256]{3,2,1,0:T(8,128)(2,1)S(1)} %bitcast.10, ...), custom_call_target="tpu_custom_call" | custom-call | flops 134217728 | bytes 4194304 | tf_op jit(solution)/shard_map/attend/pallas_call | solution.py:289
  19.5 0.3 collective-permute-start.3
  19.8 0.0 collective-permute-start.4
  19.8 5.8 %collective-permute-done.3.refs_2_ = bf16[32,2432]{1,0:T(8,128)(2,1)S(1)} collective-permute-done((bf16[32,2432]{1,0:T(8,128)(2,1)S(1)}, bf16[32,2432]{1,0:T(8,128)(2,1)S(1)}, u32[]{:S(2)}, u32[]{:S(2)}) %collective-permute-start.3) | collective-permute-done | bytes 155680 | tf_op jit(solution)/shard_map/ppermute | solution.py:617
  25.6 0.0 collective-permute-start.5
  25.6 0.0 collective-permute-done.4.refs_3_
  25.6 1.4 %collective-permute-done.5.refs_4_ = bf16[32,2432]{1,0:T(8,128)(2,1)S(1)} collective-permute-done((bf16[32,2432]{1,0:T(8,128)(2,1)S(1)}, bf16[32,2432]{1,0:T(8,128)(2,1)S(1)}, u32[]{:S(2)}, u32[]{:S(2)}) %collective-permute-start.5) | collective-permute-done | bytes 155680 | tf_op jit(solution)/shard_map/ppermute | solution.py:617
  27.0 1.0 %output_first.1 = (bf16[32,1024]{1,0:T(8,128)(2,1)S(1)}, bf16[32,2048]{1,0:T(8,128)(2,1)S(1)}) custom-call(bf16[2048,2048]{1,0:T(8,128)(2,1)S(1)} %get-tuple-element.28.refs_0_.w, bf16[32,2432]{1,0:T(8,128)(2,1)S(1)} %attend.1.refs_1_, bf16[32,2432]{1,0:T(8,128)(2,1)S(1)} %collective-permute-done.3.refs_2_, ...), custom_call_target="tpu_custom_call" | custom-call | flops 268435456 | bytes 8388608 | tf_op jit(solution)/shard_map/output_first/pallas_call | solution.py:335
  28.0 1.6 %collective-permute-start.6 = (bf16[32,1024]{1,0:T(8,128)(2,1)S(1)}, bf16[32,1024]{1,0:T(8,128)(2,1)S(1)}, u32[]{:S(2)}, u32[]{:S(2)}) collective-permute-start(bf16[32,1024]{1,0:T(8,128)(2,1)S(1)} %get-tuple-element.31.one), channel_id=1, source_target_pairs={{0,1},{1,0},{2,3},{3,2},{4,5},{5,4},{6,7},{7,6},{8,9},{9,8},{10,11... | collective-permute-start | bytes 196616 | tf_op jit(solution)/shard_map/ppermute | solution.py:617
  29.6 0.8 %output_second.1.one = bf16[32,1024]{1,0:T(8,128)(2,1)S(1)} custom-call(bf16[32,2048]{1,0:T(8,128)(2,1)S(1)} %get-tuple-element.34.x, bf16[2048,2048]{1,0:T(8,128)(2,1)S(1)} %get-tuple-element.28.refs_0_.w), custom_call_target="tpu_custom_call" | custom-call | flops 268435456 | bytes 8388608 | tf_op jit(solution)/shard_map/output_second/pallas_call | solution.py:351
  30.4 2.6 %collective-permute-start.8 = (bf16[32,1024]{1,0:T(8,128)(2,1)S(1)}, bf16[32,1024]{1,0:T(8,128)(2,1)S(1)}, u32[]{:S(2)}, u32[]{:S(2)}) collective-permute-start(bf16[32,1024]{1,0:T(8,128)(2,1)S(1)} %output_second.1.one), channel_id=1, source_target_pairs={{0,2},{1,3},{2,0},{3,1},{4,6},{5,7},{6,4},{7,5},{8,10},{9,11},{10,... | collective-permute-start | bytes 196616 | tf_op jit(solution)/shard_map/ppermute | solution.py:617
  33.0 0.0 collective-permute-done.6.two
  33.0 2.5 %collective-permute-start.7 = (bf16[32,1024]{1,0:T(8,128)(2,1)S(1)}, bf16[32,1024]{1,0:T(8,128)(2,1)S(1)}, u32[]{:S(2)}, u32[]{:S(2)}) collective-permute-start(bf16[32,1024]{1,0:T(8,128)(2,1)S(1)} %add.41.refs_5_), channel_id=1, source_target_pairs={{0,2},{1,3},{2,0},{3,1},{4,6},{5,7},{6,4},{7,5},{8,10},{9,11},{10,... | collective-permute-start | bytes 196616 | tf_op jit(solution)/shard_map/ppermute | solution.py:617
  35.5 2.2 %collective-permute-done.8.two = bf16[32,1024]{1,0:T(8,128)(2,1)S(1)} collective-permute-done((bf16[32,1024]{1,0:T(8,128)(2,1)S(1)}, bf16[32,1024]{1,0:T(8,128)(2,1)S(1)}, u32[]{:S(2)}, u32[]{:S(2)}) %collective-permute-start.8) | collective-permute-done | bytes 65568 | tf_op jit(solution)/shard_map/ppermute | solution.py:617
  37.7 0.1 collective-permute-start.9
  37.8 1.6 %collective-permute-done.7.refs_6_ = bf16[32,1024]{1,0:T(8,128)(2,1)S(1)} collective-permute-done((bf16[32,1024]{1,0:T(8,128)(2,1)S(1)}, bf16[32,1024]{1,0:T(8,128)(2,1)S(1)}, u32[]{:S(2)}, u32[]{:S(2)}) %collective-permute-start.7) | collective-permute-done | bytes 65568 | tf_op jit(solution)/shard_map/ppermute | solution.py:617
  39.4 0.0 slice-done
  39.4 0.0 slice-done.1
  39.4 0.0 slice-done.2
  39.4 0.0 slice-done.3
  39.4 0.0 copy-done
  39.4 0.0 copy-done.1
  39.4 9.1 %expand_first.1 = (f32[32,3584]{1,0:T(8,128)S(1)}, f32[32,3584]{1,0:T(8,128)S(1)}, f32[32,1024]{1,0:T(8,128)S(1)}, f32[32,128]{1,0:T(8,128)S(1)}) custom-call(s32[4]{0:T(128)S(1)} %pad_add_fusion.refs_0_.at, bf16[32,2048]{1,0:T(8,128)(2,1)S(1)} %get-tuple-element.26.refs_1_, bf16[16,128]{1,0:T(8,128)(2,1)S(1)} %bitcast.11, bf16[2048,3584]{1,0:T(8,128)(2,1)S(1)} %bitcast.9, ...), custom_call_target="tpu_custom_call" | custom-call | flops 939524096 | bytes 29360128 | tf_op jit(solution)/shard_map/expand_first/pallas_call | solution.py:426
  48.5 0.0 collective-permute-done.9.refs_8_
  48.5 5.1 %expand_send.1 = (bf16[32,3968]{1,0:T(8,128)(2,1)S(1)}, f32[32,1024]{1,0:T(8,128)S(1)}, bf16[32,1024]{1,0:T(8,128)(2,1)S(1)}) custom-call(s32[4]{0:T(128)S(1)} %pad_add_fusion.refs_0_.at, bf16[32,2048]{1,0:T(8,128)(2,1)S(1)} %get-tuple-element.26.refs_1_, bf16[16,128]{1,0:T(8,128)(2,1)S(1)} %bitcast.12, f32[32,3584]{1,0:T(8,128)S(1)} %get-tuple-element.32.refs_3_, ...), custom_call_target="tpu_custom_call" | custom-call | flops 469762048 | bytes 14680064 | tf_op jit(solution)/shard_map/expand_send/pallas_call | solution.py:462
  53.7 0.1 collective-permute-start.10
  53.7 4.8 %expand_keep.1.keep = bf16[32,3584]{1,0:T(8,128)(2,1)S(1)} custom-call(s32[4]{0:T(128)S(1)} %pad_add_fusion.refs_0_.at, bf16[32,1024]{1,0:T(8,128)(2,1)S(1)} %get-tuple-element.35.x, f32[32,3584]{1,0:T(8,128)S(1)} %get-tuple-element.36.before, bf16[2048,3584]{1,0:T(8,128)(2,1)S(1)} %bitcast.9, bf16[2048,3584]{1,0:T(8,128)(2,1)S(1)} %copy-done), custom_call_target="tpu_custom_call" | custom-call | flops 469762048 | bytes 14680064 | tf_op jit(solution)/shard_map/expand_keep/pallas_call | solution.py:485
  58.6 0.0 collective-permute-done.10.received
  58.6 0.1 pair.1.refs_1_.refs_0_
  58.7 0.5 collective-permute-start.11
  59.2 6.0 %fetch.3 = (bf16[1792,2048]{1,0:T(8,128)(2,1)S(1)}, bf16[1792,2048]{1,0:T(8,128)(2,1)S(1)}, f32[8,128]{1,0:T(8,128)S(1)}) custom-call(s32[4]{0:T(128)S(1)} %pad_add_fusion.refs_0_.at, bf16[32,3968]{1,0:T(8,128)(2,1)S(1)} %pair.1.refs_1_.refs_0_, bf16[3584,2048]{1,0:T(8,128)(2,1)} %refs_3_.5, bf16[3584,2048]{1,0:T(8,128)(2,1)} %refs_3_.5), custom_call_target="tpu_custom_call" | custom-call | bytes 29360128 | tf_op jit(solution)/shard_map/fetch/pallas_call | solution.py:94
  65.2 2.0 %collective-permute-done.11.refs_1_ = bf16[32,3968]{1,0:T(8,128)(2,1)S(1)} collective-permute-done((bf16[32,3968]{1,0:T(8,128)(2,1)S(1)}, bf16[32,3968]{1,0:T(8,128)(2,1)S(1)}, u32[]{:S(2)}, u32[]{:S(2)}) %collective-permute-start.11) | collective-permute-done | bytes 253984 | tf_op jit(solution)/shard_map/ppermute | solution.py:617
  67.3 0.1 gated.1.hidden
  67.4 0.1 collective-permute-start.12
  67.5 1.4 %contract.1.refs_3_ = f32[32,2048]{1,0:T(8,128)S(1)} custom-call(bf16[32,1792]{1,0:T(8,128)(2,1)S(1)} %gated.1.hidden, bf16[1792,2048]{1,0:T(8,128)(2,1)S(1)} %get-tuple-element.40.w), custom_call_target="tpu_custom_call" | custom-call | flops 234881024 | bytes 7340032 | tf_op jit(solution)/shard_map/contract/pallas_call | solution.py:548
  68.8 0.0 collective-permute-done.12.refs_1_
  68.8 1.9 %contract_last.1 = (f32[8,2048]{1,0:T(8,128)S(1)}, bf16[8,2048]{1,0:T(8,128)(2,1)S(1)}, bf16[8,2048]{1,0:T(8,128)(2,1)S(1)}, bf16[8,2048]{1,0:T(8,128)(2,1)S(1)}) custom-call(s32[4]{0:T(128)S(1)} %pad_add_fusion.refs_0_.at, bf16[32,1792]{1,0:T(8,128)(2,1)S(1)} %collective-permute-done.12.refs_1_, bf16[1792,2048]{1,0:T(8,128)(2,1)S(1)} %get-tuple-element.39.refs_2_, ...), custom_call_target="tpu_custom_call" | custom-call | flops 234881024 | bytes 7340032 | tf_op jit(solution)/shard_map/contract_last/pallas_call | solution.py:585
  70.8 0.5 collective-permute-start.13
  71.3 2.9 %collective-permute-start.14 = (bf16[8,2048]{1,0:T(8,128)(2,1)S(1)}, bf16[8,2048]{1,0:T(8,128)(2,1)S(1)}, u32[]{:S(2)}, u32[]{:S(2)}) collective-permute-start(bf16[8,2048]{1,0:T(8,128)(2,1)S(1)} %get-tuple-element.45), channel_id=1, source_target_pairs={{0,2},{1,3},{2,0},{3,1},{4,6},{5,7},{6,4},{7,5},{8,10},{9,11},{10,... | collective-permute-start | bytes 98312 | tf_op jit(solution)/shard_map/ppermute | solution.py:617
  74.1 1.1 %collective-permute-start.15 = (bf16[8,2048]{1,0:T(8,128)(2,1)S(1)}, bf16[8,2048]{1,0:T(8,128)(2,1)S(1)}, u32[]{:S(2)}, u32[]{:S(2)}) collective-permute-start(bf16[8,2048]{1,0:T(8,128)(2,1)S(1)} %get-tuple-element.46), channel_id=1, source_target_pairs={{0,3},{1,2},{2,1},{3,0},{4,7},{5,6},{6,5},{7,4},{8,11},{9,10},{10,... | collective-permute-start | bytes 98312 | tf_op jit(solution)/shard_map/ppermute | solution.py:617
  75.2 0.0 collective-permute-done.13
  75.2 0.9 %collective-permute-done.14 = bf16[8,2048]{1,0:T(8,128)(2,1)S(1)} collective-permute-done((bf16[8,2048]{1,0:T(8,128)(2,1)S(1)}, bf16[8,2048]{1,0:T(8,128)(2,1)S(1)}, u32[]{:S(2)}, u32[]{:S(2)}) %collective-permute-start.14) | collective-permute-done | bytes 32800 | tf_op jit(solution)/shard_map/ppermute | solution.py:617
  76.2 3.7 %collective-permute-done.15 = bf16[8,2048]{1,0:T(8,128)(2,1)S(1)} collective-permute-done((bf16[8,2048]{1,0:T(8,128)(2,1)S(1)}, bf16[8,2048]{1,0:T(8,128)(2,1)S(1)}, u32[]{:S(2)}, u32[]{:S(2)}) %collective-permute-start.15) | collective-permute-done | bytes 32800 | tf_op jit(solution)/shard_map/ppermute | solution.py:617
  79.8 0.6 add_convert_fusion
  (9 shorter events, 0.1 us)
Async XLA Ops:
  0.0 8.3 %copy-start.2 = (s32[8]{0:T(128)S(1)}, s32[8]{0:T(128)}, u32[]{:S(2)}) copy-start(s32[8]{0:T(128)} %param.24) | copy-start | bytes 100
  0.0 8.6 %copy-start.3 = (s32[8]{0:T(128)S(1)}, s32[8]{0:T(128)}, u32[]{:S(2)}) copy-start(s32[8]{0:T(128)} %param.25) | copy-start | bytes 100
  5.2 9.6 %collective-permute-start.1 = (bf16[32,2560]{1,0:T(8,128)(2,1)S(1)}, bf16[32,2560]{1,0:T(8,128)(2,1)S(1)}, u32[]{:S(2)}, u32[]{:S(2)}) collective-permute-start(bf16[32,2560]{1,0:T(8,128)(2,1)S(1)} %get-tuple-element.27.refs_1_.refs_4_), channel_id=1, source_target_pairs={{0,4},{4,0},{8,12},{12,8},{1,5},{5,1},{9,13},{13,9},{2,6},{6,2},{1... | collective-permute-start | bytes 491528 | tf_op jit(solution)/shard_map/ppermute | solution.py:617
  5.7 8.8 %collective-permute-start = (bf16[32,2560]{1,0:T(8,128)(2,1)S(1)}, bf16[32,2560]{1,0:T(8,128)(2,1)S(1)}, u32[]{:S(2)}, u32[]{:S(2)}) collective-permute-start(bf16[32,2560]{1,0:T(8,128)(2,1)S(1)} %get-tuple-element.27.refs_1_.refs_4_), channel_id=1, source_target_pairs={{0,8},{4,12},{8,0},{12,4},{1,9},{5,13},{9,1},{13,5},{2,10},{6,14},... | collective-permute-start | bytes 491528 | tf_op jit(solution)/shard_map/ppermute | solution.py:617
  8.8 30.6 %slice-start = ((s8[14680064]{0:T(1024)(128)(4,1)}), s8[4194304]{0:T(1024)(128)(4,1)S(1)}, s32[]{:S(2)}) async-start(s8[14680064]{0:T(1024)(128)(4,1)} %bitcast.8), calls=%async_computation | async-start | bytes 8388608
  8.8 30.6 %slice-start.1 = ((s8[14680064]{0:T(1024)(128)(4,1)}), s8[4194304]{0:T(1024)(128)(4,1)S(1)}, s32[]{:S(2)}) async-start(s8[14680064]{0:T(1024)(128)(4,1)} %bitcast.8), calls=%async_computation.1 | async-start | bytes 8388608
  14.5 1.5 %collective-permute-start.2 = (bf16[32,2560]{1,0:T(8,128)(2,1)S(1)}, bf16[32,2560]{1,0:T(8,128)(2,1)S(1)}, u32[]{:S(2)}, u32[]{:S(2)}) collective-permute-start(bf16[32,2560]{1,0:T(8,128)(2,1)S(1)} %hold.1.refs_5_), channel_id=1, source_target_pairs={{0,4},{4,0},{8,12},{12,8},{1,5},{5,1},{9,13},{13,9},{2,6},{6,2},{1... | collective-permute-start | bytes 491528 | tf_op jit(solution)/shard_map/ppermute | solution.py:617
  16.0 23.4 %slice-start.2 = ((s8[14680064]{0:T(1024)(128)(4,1)}), s8[4194304]{0:T(1024)(128)(4,1)S(1)}, s32[]{:S(2)}) async-start(s8[14680064]{0:T(1024)(128)(4,1)} %bitcast.8), calls=%async_computation.2 | async-start | bytes 8388608
  19.5 6.2 %collective-permute-start.3 = (bf16[32,2432]{1,0:T(8,128)(2,1)S(1)}, bf16[32,2432]{1,0:T(8,128)(2,1)S(1)}, u32[]{:S(2)}, u32[]{:S(2)}) collective-permute-start(bf16[32,2432]{1,0:T(8,128)(2,1)S(1)} %attend.1.refs_1_), channel_id=1, source_target_pairs={{0,8},{4,12},{8,0},{12,4},{1,9},{5,13},{9,1},{13,5},{2,10},{6,14},... | collective-permute-start | bytes 466952 | tf_op jit(solution)/shard_map/ppermute | solution.py:617
  19.8 5.8 %collective-permute-start.4 = (bf16[32,2432]{1,0:T(8,128)(2,1)S(1)}, bf16[32,2432]{1,0:T(8,128)(2,1)S(1)}, u32[]{:S(2)}, u32[]{:S(2)}) collective-permute-start(bf16[32,2432]{1,0:T(8,128)(2,1)S(1)} %attend.1.refs_1_), channel_id=1, source_target_pairs={{0,4},{4,0},{8,12},{12,8},{1,5},{5,1},{9,13},{13,9},{2,6},{6,2},{1... | collective-permute-start | bytes 466952 | tf_op jit(solution)/shard_map/ppermute | solution.py:617
  25.6 1.4 %collective-permute-start.5 = (bf16[32,2432]{1,0:T(8,128)(2,1)S(1)}, bf16[32,2432]{1,0:T(8,128)(2,1)S(1)}, u32[]{:S(2)}, u32[]{:S(2)}) collective-permute-start(bf16[32,2432]{1,0:T(8,128)(2,1)S(1)} %collective-permute-done.3.refs_2_), channel_id=1, source_target_pairs={{0,4},{4,0},{8,12},{12,8},{1,5},{5,1},{9,13},{13,9},{2,6},{6,2},{1... | collective-permute-start | bytes 466952 | tf_op jit(solution)/shard_map/ppermute | solution.py:617
  27.0 12.4 %slice-start.3 = ((s8[14680064]{0:T(1024)(128)(4,1)}), s8[2097152]{0:T(1024)(128)(4,1)S(1)}, s32[]{:S(2)}) async-start(s8[14680064]{0:T(1024)(128)(4,1)} %bitcast.8), calls=%async_computation.3 | async-start | bytes 4194304
  27.0 12.4 %copy-start = (bf16[2048,3584]{1,0:T(8,128)(2,1)S(1)}, bf16[2048,3584]{1,0:T(8,128)(2,1)}, u32[]{:S(2)}) copy-start(bf16[2048,3584]{1,0:T(8,128)(2,1)} %wu.1) | copy-start | bytes 44040196
  27.0 12.4 %copy-start.1 = (bf16[2048]{0:T(1024)(128)(2,1)S(1)}, bf16[2048]{0:T(1024)(128)(2,1)}, u32[]{:S(2)}) copy-start(bf16[2048]{0:T(1024)(128)(2,1)} %param.15) | copy-start | bytes 12292
  28.0 5.0 %collective-permute-start.6 = (bf16[32,1024]{1,0:T(8,128)(2,1)S(1)}, bf16[32,1024]{1,0:T(8,128)(2,1)S(1)}, u32[]{:S(2)}, u32[]{:S(2)}) collective-permute-start(bf16[32,1024]{1,0:T(8,128)(2,1)S(1)} %get-tuple-element.31.one), channel_id=1, source_target_pairs={{0,1},{1,0},{2,3},{3,2},{4,5},{5,4},{6,7},{7,6},{8,9},{9,8},{10,11... | collective-permute-start | bytes 196616 | tf_op jit(solution)/shard_map/ppermute | solution.py:617
  30.4 7.3 %collective-permute-start.8 = (bf16[32,1024]{1,0:T(8,128)(2,1)S(1)}, bf16[32,1024]{1,0:T(8,128)(2,1)S(1)}, u32[]{:S(2)}, u32[]{:S(2)}) collective-permute-start(bf16[32,1024]{1,0:T(8,128)(2,1)S(1)} %output_second.1.one), channel_id=1, source_target_pairs={{0,2},{1,3},{2,0},{3,1},{4,6},{5,7},{6,4},{7,5},{8,10},{9,11},{10,... | collective-permute-start | bytes 196616 | tf_op jit(solution)/shard_map/ppermute | solution.py:617
  33.0 6.4 %collective-permute-start.7 = (bf16[32,1024]{1,0:T(8,128)(2,1)S(1)}, bf16[32,1024]{1,0:T(8,128)(2,1)S(1)}, u32[]{:S(2)}, u32[]{:S(2)}) collective-permute-start(bf16[32,1024]{1,0:T(8,128)(2,1)S(1)} %add.41.refs_5_), channel_id=1, source_target_pairs={{0,2},{1,3},{2,0},{3,1},{4,6},{5,7},{6,4},{7,5},{8,10},{9,11},{10,... | collective-permute-start | bytes 196616 | tf_op jit(solution)/shard_map/ppermute | solution.py:617
  37.7 10.8 %collective-permute-start.9 = (bf16[32,1024]{1,0:T(8,128)(2,1)S(1)}, bf16[32,1024]{1,0:T(8,128)(2,1)S(1)}, u32[]{:S(2)}, u32[]{:S(2)}) collective-permute-start(bf16[32,1024]{1,0:T(8,128)(2,1)S(1)} %add.42.refs_7_), channel_id=1, source_target_pairs={{0,1},{1,0},{2,3},{3,2},{4,5},{5,4},{6,7},{7,6},{8,9},{9,8},{10,11... | collective-permute-start | bytes 196616 | tf_op jit(solution)/shard_map/ppermute | solution.py:617
  53.7 4.9 %collective-permute-start.10 = (bf16[32,3968]{1,0:T(8,128)(2,1)S(1)}, bf16[32,3968]{1,0:T(8,128)(2,1)S(1)}, u32[]{:S(2)}, u32[]{:S(2)}) collective-permute-start(bf16[32,3968]{1,0:T(8,128)(2,1)S(1)} %get-tuple-element.37.stats), channel_id=1, source_target_pairs={{0,4},{4,0},{8,12},{12,8},{1,5},{5,1},{9,13},{13,9},{2,6},{6,2},{1... | collective-permute-start | bytes 761864 | tf_op jit(solution)/shard_map/ppermute | solution.py:617
  58.7 8.6 %collective-permute-start.11 = (bf16[32,3968]{1,0:T(8,128)(2,1)S(1)}, bf16[32,3968]{1,0:T(8,128)(2,1)S(1)}, u32[]{:S(2)}, u32[]{:S(2)}) collective-permute-start(bf16[32,3968]{1,0:T(8,128)(2,1)S(1)} %pair.1.refs_1_.refs_0_), channel_id=1, source_target_pairs={{0,8},{4,12},{8,0},{12,4},{1,9},{5,13},{9,1},{13,5},{2,10},{6,14},... | collective-permute-start | bytes 761864 | tf_op jit(solution)/shard_map/ppermute | solution.py:617
  67.4 1.4 %collective-permute-start.12 = (bf16[32,1792]{1,0:T(8,128)(2,1)S(1)}, bf16[32,1792]{1,0:T(8,128)(2,1)S(1)}, u32[]{:S(2)}, u32[]{:S(2)}) collective-permute-start(bf16[32,1792]{1,0:T(8,128)(2,1)S(1)} %gated.1.hidden), channel_id=1, source_target_pairs={{0,4},{4,0},{8,12},{12,8},{1,5},{5,1},{9,13},{13,9},{2,6},{6,2},{1... | collective-permute-start | bytes 344072 | tf_op jit(solution)/shard_map/ppermute | solution.py:617
  70.8 4.5 %collective-permute-start.13 = (bf16[8,2048]{1,0:T(8,128)(2,1)S(1)}, bf16[8,2048]{1,0:T(8,128)(2,1)S(1)}, u32[]{:S(2)}, u32[]{:S(2)}) collective-permute-start(bf16[8,2048]{1,0:T(8,128)(2,1)S(1)} %get-tuple-element.44), channel_id=1, source_target_pairs={{0,1},{1,0},{2,3},{3,2},{4,5},{5,4},{6,7},{7,6},{8,9},{9,8},{10,11... | collective-permute-start | bytes 98312 | tf_op jit(solution)/shard_map/ppermute | solution.py:617
  71.3 4.9 %collective-permute-start.14 = (bf16[8,2048]{1,0:T(8,128)(2,1)S(1)}, bf16[8,2048]{1,0:T(8,128)(2,1)S(1)}, u32[]{:S(2)}, u32[]{:S(2)}) collective-permute-start(bf16[8,2048]{1,0:T(8,128)(2,1)S(1)} %get-tuple-element.45), channel_id=1, source_target_pairs={{0,2},{1,3},{2,0},{3,1},{4,6},{5,7},{6,4},{7,5},{8,10},{9,11},{10,... | collective-permute-start | bytes 98312 | tf_op jit(solution)/shard_map/ppermute | solution.py:617
  74.1 5.7 %collective-permute-start.15 = (bf16[8,2048]{1,0:T(8,128)(2,1)S(1)}, bf16[8,2048]{1,0:T(8,128)(2,1)S(1)}, u32[]{:S(2)}, u32[]{:S(2)}) collective-permute-start(bf16[8,2048]{1,0:T(8,128)(2,1)S(1)} %get-tuple-element.46), channel_id=1, source_target_pairs={{0,3},{1,2},{2,1},{3,0},{4,7},{5,6},{6,5},{7,4},{8,11},{9,10},{10,... | collective-permute-start | bytes 98312 | tf_op jit(solution)/shard_map/ppermute | solution.py:617

commit v10 on v9

--- a/solution.py
+++ b/solution.py
@@ -359,40 +359,43 @@
     )(attended, w)
 
 
-WIDE = 256
-AHEAD = 8
-
-
-def half_of(at, sides, x, row, wg, wu, held, sems, prepare=None):
-    half = wg.shape[1] // 2
-    jobs = []
-    for side, out, before in sides:
-        for base, w in ((0, wg), (half, wu)):
-            for start, size in blocks_of(half, WIDE):
-                n = len(jobs)
+def chunks_of(count):
+    return max(1, min(4, count // 256))
+
+
+def half_of(at, sides, x, row, weights, held, sems, prepare):
+    count, half = x.shape[1], weights[0].shape[1] // 2
+    chunks = chunks_of(count)
+    step = count // chunks
+    copies = [
+        pltpu.make_async_copy(
+            w.at[pl.ds(row + c * step, step)], h.at[pl.ds(c * step, step)], sems.at[i * chunks + c]
+        )
+        for i, (w, h) in enumerate(zip(weights, held))
+        for c in range(chunks)
+    ]
+    for copy in copies[:chunks]:
+        copy.start()
+    pl.when(at[2] >= 0)(prepare)
+    for n, copy in enumerate(copies):
+        copy.wait()
+        i, c = divmod(n, chunks)
+        part = slice(c * step, (c + 1) * step)
+        for side, out, total, before in sides:
+            for start, size in blocks_of(half, 512):
                 cols = pl.ds(pl.multiple_of(side * half + start, LANES), size)
-                copy = pltpu.make_async_copy(
-                    w.at[pl.ds(row, x.shape[1]), cols], held.at[n], sems.at[n]
-                )
-                jobs.append((copy, slice(base + start, base + start + size), out, before))
-    for copy, *_ in jobs[:AHEAD]:
-        copy.start()
-    if prepare is not None:
-        pl.when(at[2] >= 0)(prepare)
-    for n, (copy, cols, out, before) in enumerate(jobs):
-        copy.wait()
-        if n + AHEAD < len(jobs):
-            jobs[n + AHEAD][0].start()
-        term = jnp.dot(x[...], held[n], preferred_element_type=f32)
-        if before is not None:
-            term = before[:, cols] + term
-        out[:, cols] = term.astype(out.dtype)
-
-
-def block_scratch(sides, count, half):
-    blocks = blocks_of(half, WIDE)
-    number = sides * 2 * len(blocks)
-    return [pltpu.VMEM((number, count, blocks[0][1]), bf16), pltpu.SemaphoreType.DMA((number,))]
+                to = slice(i * half + start, i * half + start + size)
+                term = jnp.dot(x[:, part], held[i][part, cols], preferred_element_type=f32)
+                if c:
+                    term = total[:, to] + term
+                elif before is not None:
+                    term = before[:, to] + term
+                if c < chunks - 1:
+                    total[:, to] = term
+                else:
+                    out[:, to] = term.astype(out.dtype)
+        if n < chunks:
+            copies[n + chunks].start()
 
 
 def residual(which, own, gain, parts, resid, x, gain_f):
@@ -415,9 +418,8 @@
     def prepare():
         squares[...] = residual(0, own, gain, parts, resid, x, gain_f)
 
-    half_of(
-        at, [(1 - at[2], send, None), (at[2], keep, None)], x, 0, wg, wu, held, sems, prepare
-    )
+    sides = [(1 - at[2], send, send, None), (at[2], keep, keep, None)]
+    half_of(at, sides, x, 0, (wg, wu), (held, held), sems, prepare)
 
 
 def expand_first(at, own, gain, parts, wg, wu):
@@ -436,16 +438,17 @@
         scratch_shapes=[
             pltpu.VMEM((rows, depth // 2), bf16),
             pltpu.VMEM((depth // LANES, LANES), f32),
-        ]
-        + block_scratch(2, depth // 2, width // 2),
-        compiler_params=params(18),
+            pltpu.VMEM((depth // 2, width), bf16),
+            pltpu.SemaphoreType.DMA((2 * chunks_of(depth // 2),)),
+        ],
+        compiler_params=params(11),
         cost_estimate=cost(rows, wg, wu),
         name="expand_first",
     )(at, own, gain, wg, wu, *parts)
 
 
 def expand_send_kernel(n, at, own, gain, before, squares, wg, wu, *rest):
-    parts, (out, resid, x, gain_f, held, sems) = rest[:n], rest[n:]
+    parts, (out, resid, x, hg, hu, gain_f, total, sems) = rest[:n], rest[n:]
     width = wu.shape[1]
 
     def prepare():
@@ -454,41 +457,53 @@
         for p, term in enumerate(thirds(square)):
             out[:, width + p * LANES : width + (p + 1) * LANES] = term
 
-    half_of(at, [(1 - at[2], out, before)], x, x.shape[1], wg, wu, held, sems, prepare)
+    sides = [(1 - at[2], out, total, before)]
+    half_of(at, sides, x, x.shape[1], (wg, wu), (hg, hu), sems, prepare)
 
 
 def expand_send(at, own, gain, parts, wg, wu, before, squares):
     rows, depth = own.shape
+    width = wg.shape[1]
     return pl.pallas_call(
         lambda *refs: expand_send_kernel(len(parts), *refs),
         in_specs=[SMEM] + [VMEM] * 4 + [ANY] * 2 + [VMEM] * len(parts),
-        out_specs=[VMEM] * 3,
+        out_specs=[VMEM] * 5,
         out_shape=[
-            jax.ShapeDtypeStruct((rows, wu.shape[1] + 3 * LANES), bf16),
+            jax.ShapeDtypeStruct((rows, width + 3 * LANES), bf16),
             jax.ShapeDtypeStruct((rows, depth // 2), f32),
             jax.ShapeDtypeStruct((rows, depth // 2), bf16),
+            pltpu.VMEM((depth // 2, width), bf16),
+            pltpu.VMEM((depth // 2, width), bf16),
         ],
-        scratch_shapes=[pltpu.VMEM((depth // LANES, LANES), f32)]
-        + block_scratch(1, depth // 2, wu.shape[1] // 2),
-        compiler_params=params(10),
+        scratch_shapes=[
+            pltpu.VMEM((depth // LANES, LANES), f32),
+            pltpu.VMEM((rows, width), f32),
+            pltpu.SemaphoreType.DMA((2 * chunks_of(depth // 2),)),
+        ],
+        compiler_params=params(4),
         cost_estimate=cost(rows, wu),
         name="expand_send",
     )(at, own, gain, before, squares, wg, wu, *parts)
 
 
-def expand_keep_kernel(at, x, before, wg, wu, out, held, sems):
-    half_of(at, [(at[2], out, before)], x, x.shape[1], wg, wu, held, sems)
+def expand_keep_kernel(at, x, before, wg, wu, out):
+    half = wg.shape[1] // 2
+    for base, w in ((0, wg), (half, wu)):
+        for start, size in blocks_of(half, 512):
+            cols = pl.ds(pl.multiple_of(at[2] * half + start, LANES), size)
+            to = slice(base + start, base + start + size)
+            term = before[:, to] + jnp.dot(x[...], w[:, cols], preferred_element_type=f32)
+            out[:, to] = term.astype(out.dtype)
 
 
 def expand_keep(at, x, wg, wu, before):
     rows = x.shape[0]
     return pl.pallas_call(
         expand_keep_kernel,
-        in_specs=[SMEM] + [VMEM] * 2 + [ANY] * 2,
+        in_specs=[SMEM] + [VMEM] * 4,
         out_specs=VMEM,
         out_shape=jax.ShapeDtypeStruct((rows, wu.shape[1]), bf16),
-        scratch_shapes=block_scratch(1, x.shape[1], wu.shape[1] // 2),
-        compiler_params=params(10),
+        compiler_params=params(4),
         cost_estimate=cost(rows, wu),
         name="expand_keep",
     )(at, x, before, wg, wu)
@@ -670,9 +685,9 @@
     out_1 = output_second(attended, w_out)
     parts_0, parts_1 = summed(out_0, "head", 1), summed(out_1, "head", -1)
     send, keep, resid_0, squares = expand_first(at, own, gain, parts_0, w_gate, w_up)
-    send, resid_1, x = expand_send(at, own, gain, parts_1, w_gate, w_up, send, squares)
+    send, resid_1, x, gate_1, up_1 = expand_send(at, own, gain, parts_1, w_gate, w_up, send, squares)
     received = swap(send, "wide", 1)
-    total = pair(expand_keep(at, x, w_gate, w_up, keep), received, send)
+    total = pair(expand_keep(at, x, gate_1, up_1, keep), received, send)
     down_own, down_other, token = fetch(at, total, Part(w_down, side=0), Part(w_down, side=1))
     for bit in bits_of("wide")[1:-1]:
         there = swap(total, "wide", bit)

time: 80.6 us -> 71.6 us (0.89)
  Pallas kernels: 44.6 us -> 35.6 us
    pallas_call x1, Pallas kernels: 9.05 us -> 4.42 us  [expand_first(): pl.pallas_call(lambda *refs: expand_first_kernel(len(parts), *refs), in_s...]
    pallas_call x1, Pallas kernels: 4.83 us -> 1.91 us  [expand_keep(): pl.pallas_call(expand_keep_kernel, in_specs=[SMEM] + [VMEM] * 4, out_spec...]
    pallas_call x1, Pallas kernels: 5.15 us -> 3.72 us  [expand_send(): pl.pallas_call(lambda *refs: expand_send_kernel(len(parts), *refs), in_sp...]
  transfers between devices with their start and end apart: 16 -> 16, of which waited for: 8 -> 8; matrix products, arithmetic and copies ran while one was open for 1% -> 1% of each run, Pallas kernels for 35% -> 28%
where the time goes in v10:
time: 71.6 us; the launch traced here: 71.5 us
  Pallas kernels  35.6 us (50%)
  waiting for transfers between devices  18.8 us (26%)
  starting transfers between devices  15.6 us (22%)
  other arithmetic  1.02 us (1%)
    ppermute x16, waiting for transfers between devices, swap(): return lax.ppermute(x, axis, [(i, i ^ bit) for i in range(n)])  18.8 us
    ppermute x16, starting transfers between devices, swap(): return lax.ppermute(x, axis, [(i, i ^ bit) for i in range(n)])  15.6 us
    pallas_call x2, Pallas kernels, fetch(): pl.pallas_call(lambda *refs: fetch_kernel(wanted, len(after), *refs), in_...  11.7 us
    pallas_call x1, Pallas kernels, project(): pl.pallas_call(lambda *refs: project_kernel(chunks, *refs), in_specs=[SME...  5.11 us
    pallas_call x1, Pallas kernels, expand_first(): pl.pallas_call(lambda *refs: expand_first_kernel(len(parts), *refs), in_s...  4.42 us
    pallas_call x1, Pallas kernels, expand_send(): pl.pallas_call(lambda *refs: expand_send_kernel(len(parts), *refs), in_sp...  3.72 us
    pallas_call x1, Pallas kernels, attend(): pl.pallas_call(lambda *refs: attend_kernel(len(parts), *refs), in_specs=[...  3.46 us
    pallas_call x1, Pallas kernels, contract_last(): pl.pallas_call(lambda *refs: contract_last_kernel(n, *refs), in_specs=[SM...  1.93 us
  transfers between devices with their start and end apart: 16, of which 8 were waited for; matrix products, arithmetic and copies ran while one was open for 1% of the time, Pallas kernels for 28%

profile of v10, /device:TPU:0, one launch (start us, length us, event | category | flops | bytes accessed | tf_op | source)
XLA Modules:
  0.0 71.5 jit_solution(4153352359798431378)
XLA Ops:
  0.0 0.0 copy-start.2
  0.0 0.0 copy-start.3
  0.0 0.1 pad_add_fusion.refs_0_.at
  0.1 5.1 %project.1 = (bf16[32,2560]{1,0:T(8,128)(2,1)S(1)}, bf16[32,2048]{1,0:T(8,128)(2,1)S(1)}) custom-call(s32[4]{0:T(128)S(1)} %pad_add_fusion.refs_0_.at, bf16[32,8192]{1,0:T(8,128)(2,1)} %refs_1_.1, bf16[64,128]{1,0:T(8,128)(2,1)} %bitcast.14, bf16[2048,2048]{1,0:T(8,128)(2,1)} %refs_3_.3, bf16[2048,256]{1,0:T(8,128)(2,1)} %refs_4_.2, bf16[2048,256]{1,0:T(8,128)(2,1)} %refs_5_.2), custom_call_target="tpu_custom_call" | custom-call | flops 335544320 | bytes 10485760 | tf_op jit(solution)/shard_map/project/pallas_call | solution.py:178
  5.2 0.5 collective-permute-start.1
  5.7 2.6 %collective-permute-start = (bf16[32,2560]{1,0:T(8,128)(2,1)S(1)}, bf16[32,2560]{1,0:T(8,128)(2,1)S(1)}, u32[]{:S(2)}, u32[]{:S(2)}) collective-permute-start(bf16[32,2560]{1,0:T(8,128)(2,1)S(1)} %get-tuple-element.29.refs_1_.refs_4_), channel_id=1, source_target_pairs={{0,8},{4,12},{8,0},{12,4},{1,9},{5,13},{9,1},{13,5},{2,10},{6,14},... | collective-permute-start | bytes 491528 | tf_op jit(solution)/shard_map/ppermute | solution.py:632
  8.3 0.0 copy-done.2
  8.3 0.1 add_convert_fusion.1
  8.4 0.1 convert_element_type.24
  8.5 0.1 fusion
  8.6 0.0 copy-done.3
  8.6 0.1 concatenate.10.refs_2_.refs_0_
  8.7 0.1 pad_maximum_fusion
  8.8 0.0 slice-start
  8.8 0.0 slice-start.1
  8.8 5.7 %fetch.2 = (bf16[16,512,256]{2,1,0:T(8,128)(2,1)S(1)}, bf16[2048,2048]{1,0:T(8,128)(2,1)S(1)}, f32[8,128]{1,0:T(8,128)S(1)}) custom-call(s32[4]{0:T(128)S(1)} %pad_add_fusion.refs_0_.at, bf16[32,2560]{1,0:T(8,128)(2,1)S(1)} %get-tuple-element.29.refs_1_.refs_4_, s32[20]{0:T(128)S(1)} %concatenate.10.refs_2_.refs_0_, ...), custom_call_target="tpu_custom_call" | custom-call | bytes 25165824 | tf_op jit(solution)/shard_map/fetch/pallas_call | solution.py:94
  14.5 0.0 collective-permute-done.__0_
  14.5 0.2 collective-permute-start.2
  14.8 0.0 collective-permute-done.1.refs_6_
  14.8 1.2 %collective-permute-done.2.refs_7_ = bf16[32,2560]{1,0:T(8,128)(2,1)S(1)} collective-permute-done((bf16[32,2560]{1,0:T(8,128)(2,1)S(1)}, bf16[32,2560]{1,0:T(8,128)(2,1)S(1)}, u32[]{:S(2)}, u32[]{:S(2)}) %collective-permute-start.2) | collective-permute-done | bytes 163872 | tf_op jit(solution)/shard_map/ppermute | solution.py:632
  16.0 3.5 %attend.1.refs_1_ = bf16[32,2432]{1,0:T(8,128)(2,1)S(1)} custom-call(s32[20]{0:T(128)S(1)} %concatenate.10.refs_2_.refs_0_, f32[32,128]{1,0:T(8,128)S(1)} %get-tuple-element.54.refs_3_.refs_1_, f32[32,128]{1,0:T(8,128)S(1)} %get-tuple-element.55.refs_4_.refs_2_, bf16[2,8,512,256]{3,2,1,0:T(8,128)(2,1)S(1)} %bitcast.10, ...), custom_call_target="tpu_custom_call" | custom-call | flops 134217728 | bytes 4194304 | tf_op jit(solution)/shard_map/attend/pallas_call | solution.py:289
  19.5 0.3 collective-permute-start.3
  19.8 0.0 collective-permute-start.4
  19.8 5.8 %collective-permute-done.3.refs_2_ = bf16[32,2432]{1,0:T(8,128)(2,1)S(1)} collective-permute-done((bf16[32,2432]{1,0:T(8,128)(2,1)S(1)}, bf16[32,2432]{1,0:T(8,128)(2,1)S(1)}, u32[]{:S(2)}, u32[]{:S(2)}) %collective-permute-start.3) | collective-permute-done | bytes 155680 | tf_op jit(solution)/shard_map/ppermute | solution.py:632
  25.6 0.0 collective-permute-start.5
  25.6 0.0 collective-permute-done.4.refs_3_
  25.6 1.4 %collective-permute-done.5.refs_4_ = bf16[32,2432]{1,0:T(8,128)(2,1)S(1)} collective-permute-done((bf16[32,2432]{1,0:T(8,128)(2,1)S(1)}, bf16[32,2432]{1,0:T(8,128)(2,1)S(1)}, u32[]{:S(2)}, u32[]{:S(2)}) %collective-permute-start.5) | collective-permute-done | bytes 155680 | tf_op jit(solution)/shard_map/ppermute | solution.py:632
  27.0 1.0 %output_first.1 = (bf16[32,1024]{1,0:T(8,128)(2,1)S(1)}, bf16[32,2048]{1,0:T(8,128)(2,1)S(1)}) custom-call(bf16[2048,2048]{1,0:T(8,128)(2,1)S(1)} %get-tuple-element.30.refs_0_.w, bf16[32,2432]{1,0:T(8,128)(2,1)S(1)} %attend.1.refs_1_, bf16[32,2432]{1,0:T(8,128)(2,1)S(1)} %collective-permute-done.3.refs_2_, ...), custom_call_target="tpu_custom_call" | custom-call | flops 268435456 | bytes 8388608 | tf_op jit(solution)/shard_map/output_first/pallas_call | solution.py:335
  28.0 1.6 %collective-permute-start.6 = (bf16[32,1024]{1,0:T(8,128)(2,1)S(1)}, bf16[32,1024]{1,0:T(8,128)(2,1)S(1)}, u32[]{:S(2)}, u32[]{:S(2)}) collective-permute-start(bf16[32,1024]{1,0:T(8,128)(2,1)S(1)} %get-tuple-element.33.one), channel_id=1, source_target_pairs={{0,1},{1,0},{2,3},{3,2},{4,5},{5,4},{6,7},{7,6},{8,9},{9,8},{10,11... | collective-permute-start | bytes 196616 | tf_op jit(solution)/shard_map/ppermute | solution.py:632
  29.6 0.8 %output_second.1.one = bf16[32,1024]{1,0:T(8,128)(2,1)S(1)} custom-call(bf16[32,2048]{1,0:T(8,128)(2,1)S(1)} %get-tuple-element.36.x, bf16[2048,2048]{1,0:T(8,128)(2,1)S(1)} %get-tuple-element.30.refs_0_.w), custom_call_target="tpu_custom_call" | custom-call | flops 268435456 | bytes 8388608 | tf_op jit(solution)/shard_map/output_second/pallas_call | solution.py:351
  30.4 2.6 %collective-permute-start.8 = (bf16[32,1024]{1,0:T(8,128)(2,1)S(1)}, bf16[32,1024]{1,0:T(8,128)(2,1)S(1)}, u32[]{:S(2)}, u32[]{:S(2)}) collective-permute-start(bf16[32,1024]{1,0:T(8,128)(2,1)S(1)} %output_second.1.one), channel_id=1, source_target_pairs={{0,2},{1,3},{2,0},{3,1},{4,6},{5,7},{6,4},{7,5},{8,10},{9,11},{10,... | collective-permute-start | bytes 196616 | tf_op jit(solution)/shard_map/ppermute | solution.py:632
  33.0 0.0 collective-permute-done.6.two
  33.0 2.5 %collective-permute-start.7 = (bf16[32,1024]{1,0:T(8,128)(2,1)S(1)}, bf16[32,1024]{1,0:T(8,128)(2,1)S(1)}, u32[]{:S(2)}, u32[]{:S(2)}) collective-permute-start(bf16[32,1024]{1,0:T(8,128)(2,1)S(1)} %add.41.refs_5_), channel_id=1, source_target_pairs={{0,2},{1,3},{2,0},{3,1},{4,6},{5,7},{6,4},{7,5},{8,10},{9,11},{10,... | collective-permute-start | bytes 196616 | tf_op jit(solution)/shard_map/ppermute | solution.py:632
  35.6 2.1 %collective-permute-done.8.two = bf16[32,1024]{1,0:T(8,128)(2,1)S(1)} collective-permute-done((bf16[32,1024]{1,0:T(8,128)(2,1)S(1)}, bf16[32,1024]{1,0:T(8,128)(2,1)S(1)}, u32[]{:S(2)}, u32[]{:S(2)}) %collective-permute-start.8) | collective-permute-done | bytes 65568 | tf_op jit(solution)/shard_map/ppermute | solution.py:632
  37.7 0.1 collective-permute-start.9
  37.8 1.6 %collective-permute-done.7.refs_6_ = bf16[32,1024]{1,0:T(8,128)(2,1)S(1)} collective-permute-done((bf16[32,1024]{1,0:T(8,128)(2,1)S(1)}, bf16[32,1024]{1,0:T(8,128)(2,1)S(1)}, u32[]{:S(2)}, u32[]{:S(2)}) %collective-permute-start.7) | collective-permute-done | bytes 65568 | tf_op jit(solution)/shard_map/ppermute | solution.py:632
  39.4 0.0 slice-done
  39.4 0.0 slice-done.1
  39.4 0.0 slice-done.2
  39.4 0.0 slice-done.3
  39.4 0.0 copy-done
  39.4 0.0 copy-done.1
  39.4 4.4 %expand_first.1 = (f32[32,3584]{1,0:T(8,128)S(1)}, f32[32,3584]{1,0:T(8,128)S(1)}, f32[32,1024]{1,0:T(8,128)S(1)}, f32[32,128]{1,0:T(8,128)S(1)}) custom-call(s32[4]{0:T(128)S(1)} %pad_add_fusion.refs_0_.at, bf16[32,2048]{1,0:T(8,128)(2,1)S(1)} %get-tuple-element.28.refs_1_, bf16[16,128]{1,0:T(8,128)(2,1)S(1)} %bitcast.11, bf16[2048,3584]{1,0:T(8,128)(2,1)S(1)} %bitcast.9, ...), custom_call_target="tpu_custom_call" | custom-call | flops 939524096 | bytes 29360128 | tf_op jit(solution)/shard_map/expand_first/pallas_call | solution.py:428
  43.9 0.0 collective-permute-done.9.refs_8_
  43.9 3.7 %expand_send.1 = (bf16[32,3968]{1,0:T(8,128)(2,1)S(1)}, f32[32,1024]{1,0:T(8,128)S(1)}, bf16[32,1024]{1,0:T(8,128)(2,1)S(1)}, bf16[1024,3584]{1,0:T(8,128)(2,1)S(1)}, bf16[1024,3584]{1,0:T(8,128)(2,1)S(1)}) custom-call(s32[4]{0:T(128)S(1)} %pad_add_fusion.refs_0_.at, bf16[32,2048]{1,0:T(8,128)(2,1)S(1)} %get-tuple-element.28.refs_1_, ...), custom_call_target="tpu_custom_call" | custom-call | flops 469762048 | bytes 14680064 | tf_op jit(solution)/shard_map/expand_send/pallas_call | solution.py:467
  47.6 0.1 collective-permute-start.10
  47.7 1.9 %expand_keep.1.keep = bf16[32,3584]{1,0:T(8,128)(2,1)S(1)} custom-call(s32[4]{0:T(128)S(1)} %pad_add_fusion.refs_0_.at, bf16[32,1024]{1,0:T(8,128)(2,1)S(1)} %get-tuple-element.37.x, f32[32,3584]{1,0:T(8,128)S(1)} %get-tuple-element.38.before, bf16[1024,3584]{1,0:T(8,128)(2,1)S(1)} %get-tuple-element.39.wg, bf16[1024,3584]{1,0:T(8,128)(2,1)S(1)} %get-tuple-element.40.wu), custom_call_target="tpu_custom_call" | custom-call | flops 234881024 | bytes 7340032 | tf_op jit(solution)/shard_map/expand_keep/pallas_call | solution.py:501
  49.6 0.0 collective-permute-done.10.received
  49.6 0.1 pair.1.refs_1_.refs_0_
  49.7 0.5 collective-permute-start.11
  50.2 6.0 %fetch.3 = (bf16[1792,2048]{1,0:T(8,128)(2,1)S(1)}, bf16[1792,2048]{1,0:T(8,128)(2,1)S(1)}, f32[8,128]{1,0:T(8,128)S(1)}) custom-call(s32[4]{0:T(128)S(1)} %pad_add_fusion.refs_0_.at, bf16[32,3968]{1,0:T(8,128)(2,1)S(1)} %pair.1.refs_1_.refs_0_, bf16[3584,2048]{1,0:T(8,128)(2,1)} %refs_3_.5, bf16[3584,2048]{1,0:T(8,128)(2,1)} %refs_3_.5), custom_call_target="tpu_custom_call" | custom-call | bytes 29360128 | tf_op jit(solution)/shard_map/fetch/pallas_call | solution.py:94
  56.3 2.0 %collective-permute-done.11.refs_1_ = bf16[32,3968]{1,0:T(8,128)(2,1)S(1)} collective-permute-done((bf16[32,3968]{1,0:T(8,128)(2,1)S(1)}, bf16[32,3968]{1,0:T(8,128)(2,1)S(1)}, u32[]{:S(2)}, u32[]{:S(2)}) %collective-permute-start.11) | collective-permute-done | bytes 253984 | tf_op jit(solution)/shard_map/ppermute | solution.py:632
  58.3 0.1 gated.1.hidden
  58.4 0.1 collective-permute-start.12
  58.5 1.4 %contract.1.refs_3_ = f32[32,2048]{1,0:T(8,128)S(1)} custom-call(bf16[32,1792]{1,0:T(8,128)(2,1)S(1)} %gated.1.hidden, bf16[1792,2048]{1,0:T(8,128)(2,1)S(1)} %get-tuple-element.44.w), custom_call_target="tpu_custom_call" | custom-call | flops 234881024 | bytes 7340032 | tf_op jit(solution)/shard_map/contract/pallas_call | solution.py:563
  59.9 0.0 collective-permute-done.12.refs_1_
  59.9 1.9 %contract_last.1 = (f32[8,2048]{1,0:T(8,128)S(1)}, bf16[8,2048]{1,0:T(8,128)(2,1)S(1)}, bf16[8,2048]{1,0:T(8,128)(2,1)S(1)}, bf16[8,2048]{1,0:T(8,128)(2,1)S(1)}) custom-call(s32[4]{0:T(128)S(1)} %pad_add_fusion.refs_0_.at, bf16[32,1792]{1,0:T(8,128)(2,1)S(1)} %collective-permute-done.12.refs_1_, bf16[1792,2048]{1,0:T(8,128)(2,1)S(1)} %get-tuple-element.43.refs_2_, ...), custom_call_target="tpu_custom_call" | custom-call | flops 234881024 | bytes 7340032 | tf_op jit(solution)/shard_map/contract_last/pallas_call | solution.py:600
  61.8 0.5 collective-permute-start.13
  62.3 2.8 %collective-permute-start.14 = (bf16[8,2048]{1,0:T(8,128)(2,1)S(1)}, bf16[8,2048]{1,0:T(8,128)(2,1)S(1)}, u32[]{:S(2)}, u32[]{:S(2)}) collective-permute-start(bf16[8,2048]{1,0:T(8,128)(2,1)S(1)} %get-tuple-element.49), channel_id=1, source_target_pairs={{0,2},{1,3},{2,0},{3,1},{4,6},{5,7},{6,4},{7,5},{8,10},{9,11},{10,... | collective-permute-start | bytes 98312 | tf_op jit(solution)/shard_map/ppermute | solution.py:632
  65.1 1.1 %collective-permute-start.15 = (bf16[8,2048]{1,0:T(8,128)(2,1)S(1)}, bf16[8,2048]{1,0:T(8,128)(2,1)S(1)}, u32[]{:S(2)}, u32[]{:S(2)}) collective-permute-start(bf16[8,2048]{1,0:T(8,128)(2,1)S(1)} %get-tuple-element.50), channel_id=1, source_target_pairs={{0,3},{1,2},{2,1},{3,0},{4,7},{5,6},{6,5},{7,4},{8,11},{9,10},{10,... | collective-permute-start | bytes 98312 | tf_op jit(solution)/shard_map/ppermute | solution.py:632
  66.3 0.0 collective-permute-done.13
  66.3 0.9 %collective-permute-done.14 = bf16[8,2048]{1,0:T(8,128)(2,1)S(1)} collective-permute-done((bf16[8,2048]{1,0:T(8,128)(2,1)S(1)}, bf16[8,2048]{1,0:T(8,128)(2,1)S(1)}, u32[]{:S(2)}, u32[]{:S(2)}) %collective-permute-start.14) | collective-permute-done | bytes 32800 | tf_op jit(solution)/shard_map/ppermute | solution.py:632
  67.2 3.7 %collective-permute-done.15 = bf16[8,2048]{1,0:T(8,128)(2,1)S(1)} collective-permute-done((bf16[8,2048]{1,0:T(8,128)(2,1)S(1)}, bf16[8,2048]{1,0:T(8,128)(2,1)S(1)}, u32[]{:S(2)}, u32[]{:S(2)}) %collective-permute-start.15) | collective-permute-done | bytes 32800 | tf_op jit(solution)/shard_map/ppermute | solution.py:632
  70.8 0.6 add_convert_fusion
  (9 shorter events, 0.1 us)
Async XLA Ops:
  0.0 8.3 %copy-start.2 = (s32[8]{0:T(128)S(1)}, s32[8]{0:T(128)}, u32[]{:S(2)}) copy-start(s32[8]{0:T(128)} %param.24) | copy-start | bytes 100
  0.0 8.6 %copy-start.3 = (s32[8]{0:T(128)S(1)}, s32[8]{0:T(128)}, u32[]{:S(2)}) copy-start(s32[8]{0:T(128)} %param.25) | copy-start | bytes 100
  5.2 9.6 %collective-permute-start.1 = (bf16[32,2560]{1,0:T(8,128)(2,1)S(1)}, bf16[32,2560]{1,0:T(8,128)(2,1)S(1)}, u32[]{:S(2)}, u32[]{:S(2)}) collective-permute-start(bf16[32,2560]{1,0:T(8,128)(2,1)S(1)} %get-tuple-element.29.refs_1_.refs_4_), channel_id=1, source_target_pairs={{0,4},{4,0},{8,12},{12,8},{1,5},{5,1},{9,13},{13,9},{2,6},{6,2},{1... | collective-permute-start | bytes 491528 | tf_op jit(solution)/shard_map/ppermute | solution.py:632
  5.7 8.8 %collective-permute-start = (bf16[32,2560]{1,0:T(8,128)(2,1)S(1)}, bf16[32,2560]{1,0:T(8,128)(2,1)S(1)}, u32[]{:S(2)}, u32[]{:S(2)}) collective-permute-start(bf16[32,2560]{1,0:T(8,128)(2,1)S(1)} %get-tuple-element.29.refs_1_.refs_4_), channel_id=1, source_target_pairs={{0,8},{4,12},{8,0},{12,4},{1,9},{5,13},{9,1},{13,5},{2,10},{6,14},... | collective-permute-start | bytes 491528 | tf_op jit(solution)/shard_map/ppermute | solution.py:632
  8.8 30.6 %slice-start = ((s8[14680064]{0:T(1024)(128)(4,1)}), s8[4194304]{0:T(1024)(128)(4,1)S(1)}, s32[]{:S(2)}) async-start(s8[14680064]{0:T(1024)(128)(4,1)} %bitcast.8), calls=%async_computation | async-start | bytes 8388608
  8.8 30.6 %slice-start.1 = ((s8[14680064]{0:T(1024)(128)(4,1)}), s8[4194304]{0:T(1024)(128)(4,1)S(1)}, s32[]{:S(2)}) async-start(s8[14680064]{0:T(1024)(128)(4,1)} %bitcast.8), calls=%async_computation.1 | async-start | bytes 8388608
  14.5 1.5 %collective-permute-start.2 = (bf16[32,2560]{1,0:T(8,128)(2,1)S(1)}, bf16[32,2560]{1,0:T(8,128)(2,1)S(1)}, u32[]{:S(2)}, u32[]{:S(2)}) collective-permute-start(bf16[32,2560]{1,0:T(8,128)(2,1)S(1)} %hold.1.refs_5_), channel_id=1, source_target_pairs={{0,4},{4,0},{8,12},{12,8},{1,5},{5,1},{9,13},{13,9},{2,6},{6,2},{1... | collective-permute-start | bytes 491528 | tf_op jit(solution)/shard_map/ppermute | solution.py:632
  16.0 23.4 %slice-start.2 = ((s8[14680064]{0:T(1024)(128)(4,1)}), s8[4194304]{0:T(1024)(128)(4,1)S(1)}, s32[]{:S(2)}) async-start(s8[14680064]{0:T(1024)(128)(4,1)} %bitcast.8), calls=%async_computation.2 | async-start | bytes 8388608
  19.5 6.2 %collective-permute-start.3 = (bf16[32,2432]{1,0:T(8,128)(2,1)S(1)}, bf16[32,2432]{1,0:T(8,128)(2,1)S(1)}, u32[]{:S(2)}, u32[]{:S(2)}) collective-permute-start(bf16[32,2432]{1,0:T(8,128)(2,1)S(1)} %attend.1.refs_1_), channel_id=1, source_target_pairs={{0,8},{4,12},{8,0},{12,4},{1,9},{5,13},{9,1},{13,5},{2,10},{6,14},... | collective-permute-start | bytes 466952 | tf_op jit(solution)/shard_map/ppermute | solution.py:632
  19.8 5.8 %collective-permute-start.4 = (bf16[32,2432]{1,0:T(8,128)(2,1)S(1)}, bf16[32,2432]{1,0:T(8,128)(2,1)S(1)}, u32[]{:S(2)}, u32[]{:S(2)}) collective-permute-start(bf16[32,2432]{1,0:T(8,128)(2,1)S(1)} %attend.1.refs_1_), channel_id=1, source_target_pairs={{0,4},{4,0},{8,12},{12,8},{1,5},{5,1},{9,13},{13,9},{2,6},{6,2},{1... | collective-permute-start | bytes 466952 | tf_op jit(solution)/shard_map/ppermute | solution.py:632
  25.6 1.4 %collective-permute-start.5 = (bf16[32,2432]{1,0:T(8,128)(2,1)S(1)}, bf16[32,2432]{1,0:T(8,128)(2,1)S(1)}, u32[]{:S(2)}, u32[]{:S(2)}) collective-permute-start(bf16[32,2432]{1,0:T(8,128)(2,1)S(1)} %collective-permute-done.3.refs_2_), channel_id=1, source_target_pairs={{0,4},{4,0},{8,12},{12,8},{1,5},{5,1},{9,13},{13,9},{2,6},{6,2},{1... | collective-permute-start | bytes 466952 | tf_op jit(solution)/shard_map/ppermute | solution.py:632
  27.0 12.4 %slice-start.3 = ((s8[14680064]{0:T(1024)(128)(4,1)}), s8[2097152]{0:T(1024)(128)(4,1)S(1)}, s32[]{:S(2)}) async-start(s8[14680064]{0:T(1024)(128)(4,1)} %bitcast.8), calls=%async_computation.3 | async-start | bytes 4194304
  27.0 12.4 %copy-start = (bf16[2048,3584]{1,0:T(8,128)(2,1)S(1)}, bf16[2048,3584]{1,0:T(8,128)(2,1)}, u32[]{:S(2)}) copy-start(bf16[2048,3584]{1,0:T(8,128)(2,1)} %refs_6_.3) | copy-start | bytes 44040196
  27.0 12.4 %copy-start.1 = (bf16[2048]{0:T(1024)(128)(2,1)S(1)}, bf16[2048]{0:T(1024)(128)(2,1)}, u32[]{:S(2)}) copy-start(bf16[2048]{0:T(1024)(128)(2,1)} %param.15) | copy-start | bytes 12292
  28.0 5.0 %collective-permute-start.6 = (bf16[32,1024]{1,0:T(8,128)(2,1)S(1)}, bf16[32,1024]{1,0:T(8,128)(2,1)S(1)}, u32[]{:S(2)}, u32[]{:S(2)}) collective-permute-start(bf16[32,1024]{1,0:T(8,128)(2,1)S(1)} %get-tuple-element.33.one), channel_id=1, source_target_pairs={{0,1},{1,0},{2,3},{3,2},{4,5},{5,4},{6,7},{7,6},{8,9},{9,8},{10,11... | collective-permute-start | bytes 196616 | tf_op jit(solution)/shard_map/ppermute | solution.py:632
  30.4 7.3 %collective-permute-start.8 = (bf16[32,1024]{1,0:T(8,128)(2,1)S(1)}, bf16[32,1024]{1,0:T(8,128)(2,1)S(1)}, u32[]{:S(2)}, u32[]{:S(2)}) collective-permute-start(bf16[32,1024]{1,0:T(8,128)(2,1)S(1)} %output_second.1.one), channel_id=1, source_target_pairs={{0,2},{1,3},{2,0},{3,1},{4,6},{5,7},{6,4},{7,5},{8,10},{9,11},{10,... | collective-permute-start | bytes 196616 | tf_op jit(solution)/shard_map/ppermute | solution.py:632
  33.0 6.4 %collective-permute-start.7 = (bf16[32,1024]{1,0:T(8,128)(2,1)S(1)}, bf16[32,1024]{1,0:T(8,128)(2,1)S(1)}, u32[]{:S(2)}, u32[]{:S(2)}) collective-permute-start(bf16[32,1024]{1,0:T(8,128)(2,1)S(1)} %add.41.refs_5_), channel_id=1, source_target_pairs={{0,2},{1,3},{2,0},{3,1},{4,6},{5,7},{6,4},{7,5},{8,10},{9,11},{10,... | collective-permute-start | bytes 196616 | tf_op jit(solution)/shard_map/ppermute | solution.py:632
  37.7 6.2 %collective-permute-start.9 = (bf16[32,1024]{1,0:T(8,128)(2,1)S(1)}, bf16[32,1024]{1,0:T(8,128)(2,1)S(1)}, u32[]{:S(2)}, u32[]{:S(2)}) collective-permute-start(bf16[32,1024]{1,0:T(8,128)(2,1)S(1)} %add.42.refs_7_), channel_id=1, source_target_pairs={{0,1},{1,0},{2,3},{3,2},{4,5},{5,4},{6,7},{7,6},{8,9},{9,8},{10,11... | collective-permute-start | bytes 196616 | tf_op jit(solution)/shard_map/ppermute | solution.py:632
  47.6 2.0 %collective-permute-start.10 = (bf16[32,3968]{1,0:T(8,128)(2,1)S(1)}, bf16[32,3968]{1,0:T(8,128)(2,1)S(1)}, u32[]{:S(2)}, u32[]{:S(2)}) collective-permute-start(bf16[32,3968]{1,0:T(8,128)(2,1)S(1)} %get-tuple-element.41.stats), channel_id=1, source_target_pairs={{0,4},{4,0},{8,12},{12,8},{1,5},{5,1},{9,13},{13,9},{2,6},{6,2},{1... | collective-permute-start | bytes 761864 | tf_op jit(solution)/shard_map/ppermute | solution.py:632
  49.7 8.6 %collective-permute-start.11 = (bf16[32,3968]{1,0:T(8,128)(2,1)S(1)}, bf16[32,3968]{1,0:T(8,128)(2,1)S(1)}, u32[]{:S(2)}, u32[]{:S(2)}) collective-permute-start(bf16[32,3968]{1,0:T(8,128)(2,1)S(1)} %pair.1.refs_1_.refs_0_), channel_id=1, source_target_pairs={{0,8},{4,12},{8,0},{12,4},{1,9},{5,13},{9,1},{13,5},{2,10},{6,14},... | collective-permute-start | bytes 761864 | tf_op jit(solution)/shard_map/ppermute | solution.py:632
  58.4 1.4 %collective-permute-start.12 = (bf16[32,1792]{1,0:T(8,128)(2,1)S(1)}, bf16[32,1792]{1,0:T(8,128)(2,1)S(1)}, u32[]{:S(2)}, u32[]{:S(2)}) collective-permute-start(bf16[32,1792]{1,0:T(8,128)(2,1)S(1)} %gated.1.hidden), channel_id=1, source_target_pairs={{0,4},{4,0},{8,12},{12,8},{1,5},{5,1},{9,13},{13,9},{2,6},{6,2},{1... | collective-permute-start | bytes 344072 | tf_op jit(solution)/shard_map/ppermute | solution.py:632
  61.8 4.5 %collective-permute-start.13 = (bf16[8,2048]{1,0:T(8,128)(2,1)S(1)}, bf16[8,2048]{1,0:T(8,128)(2,1)S(1)}, u32[]{:S(2)}, u32[]{:S(2)}) collective-permute-start(bf16[8,2048]{1,0:T(8,128)(2,1)S(1)} %get-tuple-element.48), channel_id=1, source_target_pairs={{0,1},{1,0},{2,3},{3,2},{4,5},{5,4},{6,7},{7,6},{8,9},{9,8},{10,11... | collective-permute-start | bytes 98312 | tf_op jit(solution)/shard_map/ppermute | solution.py:632
  62.3 4.9 %collective-permute-start.14 = (bf16[8,2048]{1,0:T(8,128)(2,1)S(1)}, bf16[8,2048]{1,0:T(8,128)(2,1)S(1)}, u32[]{:S(2)}, u32[]{:S(2)}) collective-permute-start(bf16[8,2048]{1,0:T(8,128)(2,1)S(1)} %get-tuple-element.49), channel_id=1, source_target_pairs={{0,2},{1,3},{2,0},{3,1},{4,6},{5,7},{6,4},{7,5},{8,10},{9,11},{10,... | collective-permute-start | bytes 98312 | tf_op jit(solution)/shard_map/ppermute | solution.py:632
  65.1 5.7 %collective-permute-start.15 = (bf16[8,2048]{1,0:T(8,128)(2,1)S(1)}, bf16[8,2048]{1,0:T(8,128)(2,1)S(1)}, u32[]{:S(2)}, u32[]{:S(2)}) collective-permute-start(bf16[8,2048]{1,0:T(8,128)(2,1)S(1)} %get-tuple-element.50), channel_id=1, source_target_pairs={{0,3},{1,2},{2,1},{3,0},{4,7},{5,6},{6,5},{7,4},{8,11},{9,10},{10,... | collective-permute-start | bytes 98312 | tf_op jit(solution)/shard_map/ppermute | solution.py:632

commit v11 on v10

--- a/solution.py
+++ b/solution.py
@@ -359,43 +359,15 @@
     )(attended, w)
 
 
-def chunks_of(count):
-    return max(1, min(4, count // 256))
-
-
-def half_of(at, sides, x, row, weights, held, sems, prepare):
-    count, half = x.shape[1], weights[0].shape[1] // 2
-    chunks = chunks_of(count)
-    step = count // chunks
-    copies = [
-        pltpu.make_async_copy(
-            w.at[pl.ds(row + c * step, step)], h.at[pl.ds(c * step, step)], sems.at[i * chunks + c]
-        )
-        for i, (w, h) in enumerate(zip(weights, held))
-        for c in range(chunks)
-    ]
-    for copy in copies[:chunks]:
-        copy.start()
-    pl.when(at[2] >= 0)(prepare)
-    for n, copy in enumerate(copies):
-        copy.wait()
-        i, c = divmod(n, chunks)
-        part = slice(c * step, (c + 1) * step)
-        for side, out, total, before in sides:
-            for start, size in blocks_of(half, 512):
-                cols = pl.ds(pl.multiple_of(side * half + start, LANES), size)
-                to = slice(i * half + start, i * half + start + size)
-                term = jnp.dot(x[:, part], held[i][part, cols], preferred_element_type=f32)
-                if c:
-                    term = total[:, to] + term
-                elif before is not None:
-                    term = before[:, to] + term
-                if c < chunks - 1:
-                    total[:, to] = term
-                else:
-                    out[:, to] = term.astype(out.dtype)
-        if n < chunks:
-            copies[n + chunks].start()
+def side_of(side, x, w, base, out, before=None):
+    half = w.shape[1] // 2
+    for start, size in blocks_of(half, 512):
+        cols = pl.ds(pl.multiple_of(side * half + start, LANES), size)
+        to = slice(base + start, base + start + size)
+        term = jnp.dot(x[...], w[:, cols], preferred_element_type=f32)
+        if before is not None:
+            term = before[:, to] + term
+        out[:, to] = term.astype(out.dtype)
 
 
 def residual(which, own, gain, parts, resid, x, gain_f):
@@ -412,88 +384,103 @@
     return square
 
 
-def expand_first_kernel(n, at, own, gain, wg, wu, *rest):
-    parts, (send, keep, resid, squares, x, gain_f, held, sems) = rest[:n], rest[n:]
-
-    def prepare():
+def expand_first_kernel(n, parts_of, at, own, gain, wu, *rest):
+    sources, parts, (send, keep, resid, squares, up, wg, x, gain_f, *sems) = rest[:2], rest[2 : 2 + n], rest[2 + n :]
+    gate_copies, up_copies = (
+        p.copies(at, source, held, sem) for p, source, held, sem in zip(parts_of, sources, (wg, up), sems)
+    )
+    sides = ((1 - at[2], send), (at[2], keep))
+    half = wu.shape[1] // 2
+    for copy in gate_copies + up_copies:
+        copy.start()
+
+    @pl.when(at[2] >= 0)
+    def _():
         squares[...] = residual(0, own, gain, parts, resid, x, gain_f)
-
-    sides = [(1 - at[2], send, send, None), (at[2], keep, keep, None)]
-    half_of(at, sides, x, 0, (wg, wu), (held, held), sems, prepare)
-
-
-def expand_first(at, own, gain, parts, wg, wu):
+        for side, out in sides:
+            side_of(side, x, wu, half, out)
+
+    for copy in gate_copies:
+        copy.wait()
+    for side, out in sides:
+        side_of(side, x, wg, 0, out)
+    for copy in up_copies:
+        copy.wait()
+
+
+def expand_first(at, own, gain, parts, gate, wu, up):
     rows, depth = own.shape
-    width = wg.shape[1]
-    return pl.pallas_call(
-        lambda *refs: expand_first_kernel(len(parts), *refs),
-        in_specs=[SMEM] + [VMEM] * 2 + [ANY] * 2 + [VMEM] * len(parts),
-        out_specs=[VMEM] * 4,
+    width = wu.shape[1]
+    return pl.pallas_call(
+        lambda *refs: expand_first_kernel(len(parts), (gate, up), *refs),
+        in_specs=[SMEM] + [VMEM] * 3 + [ANY, HBM] + [VMEM] * len(parts),
+        out_specs=[VMEM] * 5,
         out_shape=[
             jax.ShapeDtypeStruct((rows, width), f32),
             jax.ShapeDtypeStruct((rows, width), f32),
             jax.ShapeDtypeStruct((rows, depth // 2), f32),
             jax.ShapeDtypeStruct((rows, LANES), f32),
+            up.out,
         ],
         scratch_shapes=[
+            pltpu.VMEM(gate.shape, bf16),
             pltpu.VMEM((rows, depth // 2), bf16),
             pltpu.VMEM((depth // LANES, LANES), f32),
-            pltpu.VMEM((depth // 2, width), bf16),
-            pltpu.SemaphoreType.DMA((2 * chunks_of(depth // 2),)),
+            pltpu.SemaphoreType.DMA((2 * PIECES,)),
+            pltpu.SemaphoreType.DMA((2 * PIECES,)),
         ],
         compiler_params=params(11),
-        cost_estimate=cost(rows, wg, wu),
+        cost_estimate=cost(rows, wu, wu),
         name="expand_first",
-    )(at, own, gain, wg, wu, *parts)
-
-
-def expand_send_kernel(n, at, own, gain, before, squares, wg, wu, *rest):
-    parts, (out, resid, x, hg, hu, gain_f, total, sems) = rest[:n], rest[n:]
-    width = wu.shape[1]
-
-    def prepare():
+    )(at, own, gain, wu, gate.array, in_hbm(up.array), *parts)
+
+
+def expand_send_kernel(n, gate, at, own, gain, before, squares, wu, source, *rest):
+    parts, (out, resid, x, wg, gain_f, sems) = rest[:n], rest[n:]
+    side, width = 1 - at[2], wu.shape[1]
+    copies = gate.copies(at, source, wg, sems)
+    for copy in copies:
+        copy.start()
+
+    @pl.when(at[2] >= 0)
+    def _():
         square = squares[...] + residual(1, own, gain, parts, resid, x, gain_f)
         square = jnp.broadcast_to(jnp.sum(square, axis=1, keepdims=True), square.shape)
         for p, term in enumerate(thirds(square)):
             out[:, width + p * LANES : width + (p + 1) * LANES] = term
-
-    sides = [(1 - at[2], out, total, before)]
-    half_of(at, sides, x, x.shape[1], (wg, wu), (hg, hu), sems, prepare)
-
-
-def expand_send(at, own, gain, parts, wg, wu, before, squares):
+        side_of(side, x, wu, width // 2, out, before)
+
+    for copy in copies:
+        copy.wait()
+    side_of(side, x, wg, 0, out, before)
+
+
+def expand_send(at, own, gain, parts, gate, wu, before, squares):
     rows, depth = own.shape
-    width = wg.shape[1]
-    return pl.pallas_call(
-        lambda *refs: expand_send_kernel(len(parts), *refs),
-        in_specs=[SMEM] + [VMEM] * 4 + [ANY] * 2 + [VMEM] * len(parts),
-        out_specs=[VMEM] * 5,
+    width = wu.shape[1]
+    return pl.pallas_call(
+        lambda *refs: expand_send_kernel(len(parts), gate, *refs),
+        in_specs=[SMEM] + [VMEM] * 5 + [ANY] + [VMEM] * len(parts),
+        out_specs=[VMEM] * 4,
         out_shape=[
             jax.ShapeDtypeStruct((rows, width + 3 * LANES), bf16),
             jax.ShapeDtypeStruct((rows, depth // 2), f32),
             jax.ShapeDtypeStruct((rows, depth // 2), bf16),
-            pltpu.VMEM((depth // 2, width), bf16),
-            pltpu.VMEM((depth // 2, width), bf16),
+            gate.out,
         ],
         scratch_shapes=[
             pltpu.VMEM((depth // LANES, LANES), f32),
-            pltpu.VMEM((rows, width), f32),
-            pltpu.SemaphoreType.DMA((2 * chunks_of(depth // 2),)),
+            pltpu.SemaphoreType.DMA((2 * PIECES,)),
         ],
         compiler_params=params(4),
         cost_estimate=cost(rows, wu),
         name="expand_send",
-    )(at, own, gain, before, squares, wg, wu, *parts)
+    )(at, own, gain, before, squares, wu, gate.array, *parts)
 
 
 def expand_keep_kernel(at, x, before, wg, wu, out):
-    half = wg.shape[1] // 2
-    for base, w in ((0, wg), (half, wu)):
-        for start, size in blocks_of(half, 512):
-            cols = pl.ds(pl.multiple_of(at[2] * half + start, LANES), size)
-            to = slice(base + start, base + start + size)
-            term = before[:, to] + jnp.dot(x[...], w[:, cols], preferred_element_type=f32)
-            out[:, to] = term.astype(out.dtype)
+    side_of(at[2], x, wg, 0, out, before)
+    side_of(at[2], x, wu, wu.shape[1] // 2, out, before)
 
 
 def expand_keep(at, x, wg, wu, before):
@@ -681,11 +668,16 @@
     cache, w_out, token = fetch(at, (qkv, meta, cos, sin), Part(flat_cache), Part(w_out))
     cache = cache.reshape(kv_cache.shape)
     value = attend(meta, cos, sin, cache, gathered(qkv, "wide", token))
-    out_0, attended = output_first(gathered(value, "wide"), w_out)
+    up_0, token = fetch(at, value, Part(w_up, 0, half))
+    out_0, attended = output_first(gathered(value, "wide", token), w_out)
     out_1 = output_second(attended, w_out)
     parts_0, parts_1 = summed(out_0, "head", 1), summed(out_1, "head", -1)
-    send, keep, resid_0, squares = expand_first(at, own, gain, parts_0, w_gate, w_up)
-    send, resid_1, x, gate_1, up_1 = expand_send(at, own, gain, parts_1, w_gate, w_up, send, squares)
+    send, keep, resid_0, squares, up_1 = expand_first(
+        at, own, gain, parts_0, Part(w_gate, 0, half), up_0, Part(w_up, half, half)
+    )
+    send, resid_1, x, gate_1 = expand_send(
+        at, own, gain, parts_1, Part(w_gate, half, half), up_1, send, squares
+    )
     received = swap(send, "wide", 1)
     total = pair(expand_keep(at, x, gate_1, up_1, keep), received, send)
     down_own, down_other, token = fetch(at, total, Part(w_down, side=0), Part(w_down, side=1))

time: 71.6 us -> 73.1 us (1.021)
  Pallas kernels: 35.6 us -> 41.1 us
  waiting for transfers between devices: 18.8 us -> 14.5 us
    ppermute x16, waiting for transfers between devices: 18.8 us -> 14.5 us  [swap(): return lax.ppermute(x, axis, [(i, i ^ bit) for i in range(n)])]
    pallas_call x2 -> x3, Pallas kernels: 11.7 us -> 15.5 us  [fetch(): pl.pallas_call(lambda *refs: fetch_kernel(wanted, len(after), *refs), in_...]
    pallas_call x2, Pallas kernels: 8.15 us -> 9.84 us  [the longest x1 5.72 us: expand_first(): pl.pallas_call(lambda *refs: expand_first_kernel(len(parts), (gate, up),...]
  transfers between devices with their start and end apart: 16 -> 16, of which waited for: 8 -> 8; matrix products, arithmetic and copies ran while one was open for 1% -> 1% of each run, Pallas kernels for 28% -> 35%
where the time goes in v11:
time: 73.1 us; the launch traced here: 73 us
  Pallas kernels  41.1 us (56%)
  starting transfers between devices  15.9 us (22%)
  waiting for transfers between devices  14.5 us (20%)
  other arithmetic  1.02 us (1%)
    ppermute x16, starting transfers between devices, swap(): return lax.ppermute(x, axis, [(i, i ^ bit) for i in range(n)])  15.9 us
    pallas_call x3, Pallas kernels, fetch(): pl.pallas_call(lambda *refs: fetch_kernel(wanted, len(after), *refs), in_...  15.5 us
    ppermute x16, waiting for transfers between devices, swap(): return lax.ppermute(x, axis, [(i, i ^ bit) for i in range(n)])  14.5 us
    pallas_call x1, Pallas kernels, expand_first(): pl.pallas_call(lambda *refs: expand_first_kernel(len(parts), (gate, up),...  5.72 us
    pallas_call x1, Pallas kernels, project(): pl.pallas_call(lambda *refs: project_kernel(chunks, *refs), in_specs=[SME...  5.11 us
    pallas_call x1, Pallas kernels, expand_send(): pl.pallas_call(lambda *refs: expand_send_kernel(len(parts), gate, *refs),...  4.12 us
    pallas_call x1, Pallas kernels, attend(): pl.pallas_call(lambda *refs: attend_kernel(len(parts), *refs), in_specs=[...  3.45 us
    pallas_call x1, Pallas kernels, contract_last(): pl.pallas_call(lambda *refs: contract_last_kernel(n, *refs), in_specs=[SM...  1.94 us
  transfers between devices with their start and end apart: 16, of which 8 were waited for; matrix products, arithmetic and copies ran while one was open for 1% of the time, Pallas kernels for 35%

profile of v11, /device:TPU:0, one launch (start us, length us, event | category | flops | bytes accessed | tf_op | source)
XLA Modules:
  0.0 73.0 jit_solution(6108455801298341217)
XLA Ops:
  0.0 0.0 copy-start.1
  0.0 0.0 copy-start.2
  0.0 0.1 pad_add_fusion.refs_0_.at
  0.1 5.1 %project.1 = (bf16[32,2560]{1,0:T(8,128)(2,1)S(1)}, bf16[32,2048]{1,0:T(8,128)(2,1)S(1)}) custom-call(s32[4]{0:T(128)S(1)} %pad_add_fusion.refs_0_.at, bf16[32,8192]{1,0:T(8,128)(2,1)} %refs_1_.1, bf16[64,128]{1,0:T(8,128)(2,1)} %bitcast.14, bf16[2048,2048]{1,0:T(8,128)(2,1)} %refs_3_.2, bf16[2048,256]{1,0:T(8,128)(2,1)} %refs_4_.2, bf16[2048,256]{1,0:T(8,128)(2,1)} %refs_5_.2), custom_call_target="tpu_custom_call" | custom-call | flops 335544320 | bytes 10485760 | tf_op jit(solution)/shard_map/project/pallas_call | solution.py:178
  5.2 0.5 collective-permute-start.1
  5.7 2.6 %collective-permute-start = (bf16[32,2560]{1,0:T(8,128)(2,1)S(1)}, bf16[32,2560]{1,0:T(8,128)(2,1)S(1)}, u32[]{:S(2)}, u32[]{:S(2)}) collective-permute-start(bf16[32,2560]{1,0:T(8,128)(2,1)S(1)} %get-tuple-element.31.refs_1_.refs_4_), channel_id=1, source_target_pairs={{0,8},{4,12},{8,0},{12,4},{1,9},{5,13},{9,1},{13,5},{2,10},{6,14},... | collective-permute-start | bytes 491528 | tf_op jit(solution)/shard_map/ppermute | solution.py:619
  8.3 0.0 copy-done.1
  8.3 0.1 add_convert_fusion.1
  8.4 0.1 convert_element_type.24
  8.5 0.1 fusion
  8.6 0.0 copy-done.2
  8.6 0.1 concatenate.10.refs_2_.refs_0_
  8.7 0.1 pad_maximum_fusion
  8.8 5.4 %fetch.3 = (bf16[16,512,256]{2,1,0:T(8,128)(2,1)S(1)}, bf16[2048,2048]{1,0:T(8,128)(2,1)S(1)}, f32[8,128]{1,0:T(8,128)S(1)}) custom-call(s32[4]{0:T(128)S(1)} %pad_add_fusion.refs_0_.at, bf16[32,2560]{1,0:T(8,128)(2,1)S(1)} %get-tuple-element.31.refs_1_.refs_4_, s32[20]{0:T(128)S(1)} %concatenate.10.refs_2_.refs_0_, ...), custom_call_target="tpu_custom_call" | custom-call | bytes 25165824 | tf_op jit(solution)/shard_map/fetch/pallas_call | solution.py:94
  14.3 0.0 collective-permute-done.__0_
  14.3 0.2 collective-permute-start.2
  14.5 0.0 collective-permute-done.1.refs_6_
  14.5 1.2 %collective-permute-done.2.refs_7_ = bf16[32,2560]{1,0:T(8,128)(2,1)S(1)} collective-permute-done((bf16[32,2560]{1,0:T(8,128)(2,1)S(1)}, bf16[32,2560]{1,0:T(8,128)(2,1)S(1)}, u32[]{:S(2)}, u32[]{:S(2)}) %collective-permute-start.2) | collective-permute-done | bytes 163872 | tf_op jit(solution)/shard_map/ppermute | solution.py:619
  15.7 3.5 %attend.1.refs_1_ = bf16[32,2432]{1,0:T(8,128)(2,1)S(1)} custom-call(s32[20]{0:T(128)S(1)} %concatenate.10.refs_2_.refs_0_, f32[32,128]{1,0:T(8,128)S(1)} %get-tuple-element.58.refs_3_.refs_1_, f32[32,128]{1,0:T(8,128)S(1)} %get-tuple-element.59.refs_4_.refs_2_, bf16[2,8,512,256]{3,2,1,0:T(8,128)(2,1)S(1)} %bitcast.10, ...), custom_call_target="tpu_custom_call" | custom-call | flops 134217728 | bytes 4194304 | tf_op jit(solution)/shard_map/attend/pallas_call | solution.py:289
  19.2 0.6 collective-permute-start.3
  19.8 0.0 collective-permute-start.4
  19.8 0.0 slice-start
  19.8 0.0 slice-start.1
  19.8 4.0 %fetch.4 = (bf16[1024,3584]{1,0:T(8,128)(2,1)S(1)}, f32[8,128]{1,0:T(8,128)S(1)}) custom-call(s32[4]{0:T(128)S(1)} %pad_add_fusion.refs_0_.at, bf16[32,2432]{1,0:T(8,128)(2,1)S(1)} %attend.1.refs_1_, bf16[2048,3584]{1,0:T(8,128)(2,1)} %refs_5_.3), custom_call_target="tpu_custom_call" | custom-call | bytes 14680064 | tf_op jit(solution)/shard_map/fetch/pallas_call | solution.py:94
  23.8 1.5 %collective-permute-done.3.__0_ = bf16[32,2432]{1,0:T(8,128)(2,1)S(1)} collective-permute-done((bf16[32,2432]{1,0:T(8,128)(2,1)S(1)}, bf16[32,2432]{1,0:T(8,128)(2,1)S(1)}, u32[]{:S(2)}, u32[]{:S(2)}) %collective-permute-start.3) | collective-permute-done | bytes 155680 | tf_op jit(solution)/shard_map/ppermute | solution.py:619
  25.4 0.0 collective-permute-start.5
  25.4 0.0 collective-permute-done.4.refs_3_
  25.4 1.4 %collective-permute-done.5.refs_4_ = bf16[32,2432]{1,0:T(8,128)(2,1)S(1)} collective-permute-done((bf16[32,2432]{1,0:T(8,128)(2,1)S(1)}, bf16[32,2432]{1,0:T(8,128)(2,1)S(1)}, u32[]{:S(2)}, u32[]{:S(2)}) %collective-permute-start.5) | collective-permute-done | bytes 155680 | tf_op jit(solution)/shard_map/ppermute | solution.py:619
  26.7 1.0 %output_first.1 = (bf16[32,1024]{1,0:T(8,128)(2,1)S(1)}, bf16[32,2048]{1,0:T(8,128)(2,1)S(1)}) custom-call(bf16[2048,2048]{1,0:T(8,128)(2,1)S(1)} %get-tuple-element.35.refs_0_.w, bf16[32,2432]{1,0:T(8,128)(2,1)S(1)} %attend.1.refs_1_, bf16[32,2432]{1,0:T(8,128)(2,1)S(1)} %hold.3.refs_2_, bf16[32,2432]{1,0:T(8,128)(2,1)S(1)} %collective-permute-done.4.refs_3_, ...), custom_call_target="tpu_custom_call" | custom-call | flops 268435456 | bytes 8388608 | tf_op jit(solution)/shard_map/output_first/pallas_call | solution.py:335
  27.7 1.6 %collective-permute-start.6 = (bf16[32,1024]{1,0:T(8,128)(2,1)S(1)}, bf16[32,1024]{1,0:T(8,128)(2,1)S(1)}, u32[]{:S(2)}, u32[]{:S(2)}) collective-permute-start(bf16[32,1024]{1,0:T(8,128)(2,1)S(1)} %get-tuple-element.37.one), channel_id=1, source_target_pairs={{0,1},{1,0},{2,3},{3,2},{4,5},{5,4},{6,7},{7,6},{8,9},{9,8},{10,11... | collective-permute-start | bytes 196616 | tf_op jit(solution)/shard_map/ppermute | solution.py:619
  29.3 0.8 %output_second.1.one = bf16[32,1024]{1,0:T(8,128)(2,1)S(1)} custom-call(bf16[32,2048]{1,0:T(8,128)(2,1)S(1)} %get-tuple-element.41.x, bf16[2048,2048]{1,0:T(8,128)(2,1)S(1)} %get-tuple-element.35.refs_0_.w), custom_call_target="tpu_custom_call" | custom-call | flops 268435456 | bytes 8388608 | tf_op jit(solution)/shard_map/output_second/pallas_call | solution.py:351
  30.1 2.6 %collective-permute-start.8 = (bf16[32,1024]{1,0:T(8,128)(2,1)S(1)}, bf16[32,1024]{1,0:T(8,128)(2,1)S(1)}, u32[]{:S(2)}, u32[]{:S(2)}) collective-permute-start(bf16[32,1024]{1,0:T(8,128)(2,1)S(1)} %output_second.1.one), channel_id=1, source_target_pairs={{0,2},{1,3},{2,0},{3,1},{4,6},{5,7},{6,4},{7,5},{8,10},{9,11},{10,... | collective-permute-start | bytes 196616 | tf_op jit(solution)/shard_map/ppermute | solution.py:619
  32.8 0.0 collective-permute-done.6.two
  32.8 2.5 %collective-permute-start.7 = (bf16[32,1024]{1,0:T(8,128)(2,1)S(1)}, bf16[32,1024]{1,0:T(8,128)(2,1)S(1)}, u32[]{:S(2)}, u32[]{:S(2)}) collective-permute-start(bf16[32,1024]{1,0:T(8,128)(2,1)S(1)} %add.41.refs_6_), channel_id=1, source_target_pairs={{0,2},{1,3},{2,0},{3,1},{4,6},{5,7},{6,4},{7,5},{8,10},{9,11},{10,... | collective-permute-start | bytes 196616 | tf_op jit(solution)/shard_map/ppermute | solution.py:619
  35.3 2.1 %collective-permute-done.8.two = bf16[32,1024]{1,0:T(8,128)(2,1)S(1)} collective-permute-done((bf16[32,1024]{1,0:T(8,128)(2,1)S(1)}, bf16[32,1024]{1,0:T(8,128)(2,1)S(1)}, u32[]{:S(2)}, u32[]{:S(2)}) %collective-permute-start.8) | collective-permute-done | bytes 65568 | tf_op jit(solution)/shard_map/ppermute | solution.py:619
  37.5 0.1 collective-permute-start.9
  37.5 1.6 %collective-permute-done.7.refs_7_ = bf16[32,1024]{1,0:T(8,128)(2,1)S(1)} collective-permute-done((bf16[32,1024]{1,0:T(8,128)(2,1)S(1)}, bf16[32,1024]{1,0:T(8,128)(2,1)S(1)}, u32[]{:S(2)}, u32[]{:S(2)}) %collective-permute-start.7) | collective-permute-done | bytes 65568 | tf_op jit(solution)/shard_map/ppermute | solution.py:619
  39.1 0.0 slice-done
  39.1 0.0 slice-done.1
  39.1 0.0 slice-done.2
  39.1 0.0 copy-done
  39.2 0.0 slice-done.3
  39.2 5.7 %expand_first.1 = (f32[32,3584]{1,0:T(8,128)S(1)}, f32[32,3584]{1,0:T(8,128)S(1)}, f32[32,1024]{1,0:T(8,128)S(1)}, f32[32,128]{1,0:T(8,128)S(1)}, bf16[1024,3584]{1,0:T(8,128)(2,1)S(1)}) custom-call(s32[4]{0:T(128)S(1)} %pad_add_fusion.refs_0_.at, bf16[32,2048]{1,0:T(8,128)(2,1)S(1)} %get-tuple-element.30.refs_1_, bf16[16,128]{1,0:T(8,128)(2,1)S(1)} %bitcast.11, ...), custom_call_target="tpu_custom_call" | custom-call | flops 469762048 | bytes 14680064 | tf_op jit(solution)/shard_map/expand_first/pallas_call | solution.py:414
  44.9 0.0 collective-permute-done.9.refs_8_
  44.9 4.1 %expand_send.1 = (bf16[32,3968]{1,0:T(8,128)(2,1)S(1)}, f32[32,1024]{1,0:T(8,128)S(1)}, bf16[32,1024]{1,0:T(8,128)(2,1)S(1)}, bf16[1024,3584]{1,0:T(8,128)(2,1)S(1)}) custom-call(s32[4]{0:T(128)S(1)} %pad_add_fusion.refs_0_.at, bf16[32,2048]{1,0:T(8,128)(2,1)S(1)} %get-tuple-element.30.refs_1_, bf16[16,128]{1,0:T(8,128)(2,1)S(1)} %bitcast.12, ...), custom_call_target="tpu_custom_call" | custom-call | flops 234881024 | bytes 7340032 | tf_op jit(solution)/shard_map/expand_send/pallas_call | solution.py:461
  49.0 0.1 collective-permute-start.10
  49.1 1.9 %expand_keep.1.keep = bf16[32,3584]{1,0:T(8,128)(2,1)S(1)} custom-call(s32[4]{0:T(128)S(1)} %pad_add_fusion.refs_0_.at, bf16[32,1024]{1,0:T(8,128)(2,1)S(1)} %get-tuple-element.42.x, f32[32,3584]{1,0:T(8,128)S(1)} %get-tuple-element.43.before, bf16[1024,3584]{1,0:T(8,128)(2,1)S(1)} %get-tuple-element.44.wg, bf16[1024,3584]{1,0:T(8,128)(2,1)S(1)} %get-tuple-element.40.refs_5_.wu), custom_call_target="tpu_custom_call" | custom-call | flops 234881024 | bytes 7340032 | tf_op jit(solution)/shard_map/expand_keep/pallas_call | solution.py:488
  51.0 0.0 collective-permute-done.10.received
  51.0 0.1 pair.1.refs_1_.refs_0_
  51.1 0.6 collective-permute-start.11
  51.7 6.0 %fetch.5 = (bf16[1792,2048]{1,0:T(8,128)(2,1)S(1)}, bf16[1792,2048]{1,0:T(8,128)(2,1)S(1)}, f32[8,128]{1,0:T(8,128)S(1)}) custom-call(s32[4]{0:T(128)S(1)} %pad_add_fusion.refs_0_.at, bf16[32,3968]{1,0:T(8,128)(2,1)S(1)} %pair.1.refs_1_.refs_0_, bf16[3584,2048]{1,0:T(8,128)(2,1)} %refs_3_.3, bf16[3584,2048]{1,0:T(8,128)(2,1)} %refs_3_.3), custom_call_target="tpu_custom_call" | custom-call | bytes 29360128 | tf_op jit(solution)/shard_map/fetch/pallas_call | solution.py:94
  57.7 2.0 %collective-permute-done.11.refs_1_ = bf16[32,3968]{1,0:T(8,128)(2,1)S(1)} collective-permute-done((bf16[32,3968]{1,0:T(8,128)(2,1)S(1)}, bf16[32,3968]{1,0:T(8,128)(2,1)S(1)}, u32[]{:S(2)}, u32[]{:S(2)}) %collective-permute-start.11) | collective-permute-done | bytes 253984 | tf_op jit(solution)/shard_map/ppermute | solution.py:619
  59.7 0.1 gated.1.hidden
  59.9 0.1 collective-permute-start.12
  59.9 1.4 %contract.1.refs_3_ = f32[32,2048]{1,0:T(8,128)S(1)} custom-call(bf16[32,1792]{1,0:T(8,128)(2,1)S(1)} %gated.1.hidden, bf16[1792,2048]{1,0:T(8,128)(2,1)S(1)} %get-tuple-element.48.w), custom_call_target="tpu_custom_call" | custom-call | flops 234881024 | bytes 7340032 | tf_op jit(solution)/shard_map/contract/pallas_call | solution.py:550
  61.3 0.0 collective-permute-done.12.refs_1_
  61.3 1.9 %contract_last.1 = (f32[8,2048]{1,0:T(8,128)S(1)}, bf16[8,2048]{1,0:T(8,128)(2,1)S(1)}, bf16[8,2048]{1,0:T(8,128)(2,1)S(1)}, bf16[8,2048]{1,0:T(8,128)(2,1)S(1)}) custom-call(s32[4]{0:T(128)S(1)} %pad_add_fusion.refs_0_.at, bf16[32,1792]{1,0:T(8,128)(2,1)S(1)} %collective-permute-done.12.refs_1_, bf16[1792,2048]{1,0:T(8,128)(2,1)S(1)} %get-tuple-element.47.refs_2_, ...), custom_call_target="tpu_custom_call" | custom-call | flops 234881024 | bytes 7340032 | tf_op jit(solution)/shard_map/contract_last/pallas_call | solution.py:587
  63.2 0.5 collective-permute-start.13
  63.7 2.9 %collective-permute-start.14 = (bf16[8,2048]{1,0:T(8,128)(2,1)S(1)}, bf16[8,2048]{1,0:T(8,128)(2,1)S(1)}, u32[]{:S(2)}, u32[]{:S(2)}) collective-permute-start(bf16[8,2048]{1,0:T(8,128)(2,1)S(1)} %get-tuple-element.53), channel_id=1, source_target_pairs={{0,2},{1,3},{2,0},{3,1},{4,6},{5,7},{6,4},{7,5},{8,10},{9,11},{10,... | collective-permute-start | bytes 98312 | tf_op jit(solution)/shard_map/ppermute | solution.py:619
  66.6 1.1 %collective-permute-start.15 = (bf16[8,2048]{1,0:T(8,128)(2,1)S(1)}, bf16[8,2048]{1,0:T(8,128)(2,1)S(1)}, u32[]{:S(2)}, u32[]{:S(2)}) collective-permute-start(bf16[8,2048]{1,0:T(8,128)(2,1)S(1)} %get-tuple-element.54), channel_id=1, source_target_pairs={{0,3},{1,2},{2,1},{3,0},{4,7},{5,6},{6,5},{7,4},{8,11},{9,10},{10,... | collective-permute-start | bytes 98312 | tf_op jit(solution)/shard_map/ppermute | solution.py:619
  67.7 0.0 collective-permute-done.13
  67.7 0.9 %collective-permute-done.14 = bf16[8,2048]{1,0:T(8,128)(2,1)S(1)} collective-permute-done((bf16[8,2048]{1,0:T(8,128)(2,1)S(1)}, bf16[8,2048]{1,0:T(8,128)(2,1)S(1)}, u32[]{:S(2)}, u32[]{:S(2)}) %collective-permute-start.14) | collective-permute-done | bytes 32800 | tf_op jit(solution)/shard_map/ppermute | solution.py:619
  68.6 3.7 %collective-permute-done.15 = bf16[8,2048]{1,0:T(8,128)(2,1)S(1)} collective-permute-done((bf16[8,2048]{1,0:T(8,128)(2,1)S(1)}, bf16[8,2048]{1,0:T(8,128)(2,1)S(1)}, u32[]{:S(2)}, u32[]{:S(2)}) %collective-permute-start.15) | collective-permute-done | bytes 32800 | tf_op jit(solution)/shard_map/ppermute | solution.py:619
  72.3 0.6 add_convert_fusion
  (9 shorter events, 0.1 us)
Async XLA Ops:
  0.0 8.3 %copy-start.1 = (s32[8]{0:T(128)S(1)}, s32[8]{0:T(128)}, u32[]{:S(2)}) copy-start(s32[8]{0:T(128)} %param.24) | copy-start | bytes 100
  0.0 8.6 %copy-start.2 = (s32[8]{0:T(128)S(1)}, s32[8]{0:T(128)}, u32[]{:S(2)}) copy-start(s32[8]{0:T(128)} %param.25) | copy-start | bytes 100
  5.2 9.3 %collective-permute-start.1 = (bf16[32,2560]{1,0:T(8,128)(2,1)S(1)}, bf16[32,2560]{1,0:T(8,128)(2,1)S(1)}, u32[]{:S(2)}, u32[]{:S(2)}) collective-permute-start(bf16[32,2560]{1,0:T(8,128)(2,1)S(1)} %get-tuple-element.31.refs_1_.refs_4_), channel_id=1, source_target_pairs={{0,4},{4,0},{8,12},{12,8},{1,5},{5,1},{9,13},{13,9},{2,6},{6,2},{1... | collective-permute-start | bytes 491528 | tf_op jit(solution)/shard_map/ppermute | solution.py:619
  5.7 8.5 %collective-permute-start = (bf16[32,2560]{1,0:T(8,128)(2,1)S(1)}, bf16[32,2560]{1,0:T(8,128)(2,1)S(1)}, u32[]{:S(2)}, u32[]{:S(2)}) collective-permute-start(bf16[32,2560]{1,0:T(8,128)(2,1)S(1)} %get-tuple-element.31.refs_1_.refs_4_), channel_id=1, source_target_pairs={{0,8},{4,12},{8,0},{12,4},{1,9},{5,13},{9,1},{13,5},{2,10},{6,14},... | collective-permute-start | bytes 491528 | tf_op jit(solution)/shard_map/ppermute | solution.py:619
  14.3 1.5 %collective-permute-start.2 = (bf16[32,2560]{1,0:T(8,128)(2,1)S(1)}, bf16[32,2560]{1,0:T(8,128)(2,1)S(1)}, u32[]{:S(2)}, u32[]{:S(2)}) collective-permute-start(bf16[32,2560]{1,0:T(8,128)(2,1)S(1)} %hold.2.refs_5_), channel_id=1, source_target_pairs={{0,4},{4,0},{8,12},{12,8},{1,5},{5,1},{9,13},{13,9},{2,6},{6,2},{1... | collective-permute-start | bytes 491528 | tf_op jit(solution)/shard_map/ppermute | solution.py:619
  19.2 6.2 %collective-permute-start.3 = (bf16[32,2432]{1,0:T(8,128)(2,1)S(1)}, bf16[32,2432]{1,0:T(8,128)(2,1)S(1)}, u32[]{:S(2)}, u32[]{:S(2)}) collective-permute-start(bf16[32,2432]{1,0:T(8,128)(2,1)S(1)} %attend.1.refs_1_), channel_id=1, source_target_pairs={{0,8},{4,12},{8,0},{12,4},{1,9},{5,13},{9,1},{13,5},{2,10},{6,14},... | collective-permute-start | bytes 466952 | tf_op jit(solution)/shard_map/ppermute | solution.py:619
  19.8 5.6 %collective-permute-start.4 = (bf16[32,2432]{1,0:T(8,128)(2,1)S(1)}, bf16[32,2432]{1,0:T(8,128)(2,1)S(1)}, u32[]{:S(2)}, u32[]{:S(2)}) collective-permute-start(bf16[32,2432]{1,0:T(8,128)(2,1)S(1)} %attend.1.refs_1_), channel_id=1, source_target_pairs={{0,4},{4,0},{8,12},{12,8},{1,5},{5,1},{9,13},{13,9},{2,6},{6,2},{1... | collective-permute-start | bytes 466952 | tf_op jit(solution)/shard_map/ppermute | solution.py:619
  19.8 19.4 %slice-start = ((s8[14680064]{0:T(1024)(128)(4,1)}), s8[4194304]{0:T(1024)(128)(4,1)S(1)}, s32[]{:S(2)}) async-start(s8[14680064]{0:T(1024)(128)(4,1)} %bitcast.8), calls=%async_computation | async-start | bytes 8388608
  19.8 19.4 %slice-start.1 = ((s8[14680064]{0:T(1024)(128)(4,1)}), s8[4194304]{0:T(1024)(128)(4,1)S(1)}, s32[]{:S(2)}) async-start(s8[14680064]{0:T(1024)(128)(4,1)} %bitcast.8), calls=%async_computation.1 | async-start | bytes 8388608
  25.4 1.4 %collective-permute-start.5 = (bf16[32,2432]{1,0:T(8,128)(2,1)S(1)}, bf16[32,2432]{1,0:T(8,128)(2,1)S(1)}, u32[]{:S(2)}, u32[]{:S(2)}) collective-permute-start(bf16[32,2432]{1,0:T(8,128)(2,1)S(1)} %hold.3.refs_2_), channel_id=1, source_target_pairs={{0,4},{4,0},{8,12},{12,8},{1,5},{5,1},{9,13},{13,9},{2,6},{6,2},{1... | collective-permute-start | bytes 466952 | tf_op jit(solution)/shard_map/ppermute | solution.py:619
  26.7 12.4 %slice-start.2 = ((s8[14680064]{0:T(1024)(128)(4,1)}), s8[4194304]{0:T(1024)(128)(4,1)S(1)}, s32[]{:S(2)}) async-start(s8[14680064]{0:T(1024)(128)(4,1)} %bitcast.8), calls=%async_computation.2 | async-start | bytes 8388608
  26.7 12.4 %copy-start = (bf16[2048]{0:T(1024)(128)(2,1)S(1)}, bf16[2048]{0:T(1024)(128)(2,1)}, u32[]{:S(2)}) copy-start(bf16[2048]{0:T(1024)(128)(2,1)} %param.15) | copy-start | bytes 12292
  27.7 5.0 %collective-permute-start.6 = (bf16[32,1024]{1,0:T(8,128)(2,1)S(1)}, bf16[32,1024]{1,0:T(8,128)(2,1)S(1)}, u32[]{:S(2)}, u32[]{:S(2)}) collective-permute-start(bf16[32,1024]{1,0:T(8,128)(2,1)S(1)} %get-tuple-element.37.one), channel_id=1, source_target_pairs={{0,1},{1,0},{2,3},{3,2},{4,5},{5,4},{6,7},{7,6},{8,9},{9,8},{10,11... | collective-permute-start | bytes 196616 | tf_op jit(solution)/shard_map/ppermute | solution.py:619
  29.3 9.8 %slice-start.3 = ((s8[14680064]{0:T(1024)(128)(4,1)}), s8[2097152]{0:T(1024)(128)(4,1)S(1)}, s32[]{:S(2)}) async-start(s8[14680064]{0:T(1024)(128)(4,1)} %bitcast.8), calls=%async_computation.3 | async-start | bytes 4194304
  30.1 7.3 %collective-permute-start.8 = (bf16[32,1024]{1,0:T(8,128)(2,1)S(1)}, bf16[32,1024]{1,0:T(8,128)(2,1)S(1)}, u32[]{:S(2)}, u32[]{:S(2)}) collective-permute-start(bf16[32,1024]{1,0:T(8,128)(2,1)S(1)} %output_second.1.one), channel_id=1, source_target_pairs={{0,2},{1,3},{2,0},{3,1},{4,6},{5,7},{6,4},{7,5},{8,10},{9,11},{10,... | collective-permute-start | bytes 196616 | tf_op jit(solution)/shard_map/ppermute | solution.py:619
  32.8 6.4 %collective-permute-start.7 = (bf16[32,1024]{1,0:T(8,128)(2,1)S(1)}, bf16[32,1024]{1,0:T(8,128)(2,1)S(1)}, u32[]{:S(2)}, u32[]{:S(2)}) collective-permute-start(bf16[32,1024]{1,0:T(8,128)(2,1)S(1)} %add.41.refs_6_), channel_id=1, source_target_pairs={{0,2},{1,3},{2,0},{3,1},{4,6},{5,7},{6,4},{7,5},{8,10},{9,11},{10,... | collective-permute-start | bytes 196616 | tf_op jit(solution)/shard_map/ppermute | solution.py:619
  37.5 7.5 %collective-permute-start.9 = (bf16[32,1024]{1,0:T(8,128)(2,1)S(1)}, bf16[32,1024]{1,0:T(8,128)(2,1)S(1)}, u32[]{:S(2)}, u32[]{:S(2)}) collective-permute-start(bf16[32,1024]{1,0:T(8,128)(2,1)S(1)} %add.42.refs_7_), channel_id=1, source_target_pairs={{0,1},{1,0},{2,3},{3,2},{4,5},{5,4},{6,7},{7,6},{8,9},{9,8},{10,11... | collective-permute-start | bytes 196616 | tf_op jit(solution)/shard_map/ppermute | solution.py:619
  49.0 2.0 %collective-permute-start.10 = (bf16[32,3968]{1,0:T(8,128)(2,1)S(1)}, bf16[32,3968]{1,0:T(8,128)(2,1)S(1)}, u32[]{:S(2)}, u32[]{:S(2)}) collective-permute-start(bf16[32,3968]{1,0:T(8,128)(2,1)S(1)} %get-tuple-element.45.stats), channel_id=1, source_target_pairs={{0,4},{4,0},{8,12},{12,8},{1,5},{5,1},{9,13},{13,9},{2,6},{6,2},{1... | collective-permute-start | bytes 761864 | tf_op jit(solution)/shard_map/ppermute | solution.py:619
  51.1 8.6 %collective-permute-start.11 = (bf16[32,3968]{1,0:T(8,128)(2,1)S(1)}, bf16[32,3968]{1,0:T(8,128)(2,1)S(1)}, u32[]{:S(2)}, u32[]{:S(2)}) collective-permute-start(bf16[32,3968]{1,0:T(8,128)(2,1)S(1)} %pair.1.refs_1_.refs_0_), channel_id=1, source_target_pairs={{0,8},{4,12},{8,0},{12,4},{1,9},{5,13},{9,1},{13,5},{2,10},{6,14},... | collective-permute-start | bytes 761864 | tf_op jit(solution)/shard_map/ppermute | solution.py:619
  59.9 1.4 %collective-permute-start.12 = (bf16[32,1792]{1,0:T(8,128)(2,1)S(1)}, bf16[32,1792]{1,0:T(8,128)(2,1)S(1)}, u32[]{:S(2)}, u32[]{:S(2)}) collective-permute-start(bf16[32,1792]{1,0:T(8,128)(2,1)S(1)} %gated.1.hidden), channel_id=1, source_target_pairs={{0,4},{4,0},{8,12},{12,8},{1,5},{5,1},{9,13},{13,9},{2,6},{6,2},{1... | collective-permute-start | bytes 344072 | tf_op jit(solution)/shard_map/ppermute | solution.py:619
  63.2 4.5 %collective-permute-start.13 = (bf16[8,2048]{1,0:T(8,128)(2,1)S(1)}, bf16[8,2048]{1,0:T(8,128)(2,1)S(1)}, u32[]{:S(2)}, u32[]{:S(2)}) collective-permute-start(bf16[8,2048]{1,0:T(8,128)(2,1)S(1)} %get-tuple-element.52), channel_id=1, source_target_pairs={{0,1},{1,0},{2,3},{3,2},{4,5},{5,4},{6,7},{7,6},{8,9},{9,8},{10,11... | collective-permute-start | bytes 98312 | tf_op jit(solution)/shard_map/ppermute | solution.py:619
  63.7 4.9 %collective-permute-start.14 = (bf16[8,2048]{1,0:T(8,128)(2,1)S(1)}, bf16[8,2048]{1,0:T(8,128)(2,1)S(1)}, u32[]{:S(2)}, u32[]{:S(2)}) collective-permute-start(bf16[8,2048]{1,0:T(8,128)(2,1)S(1)} %get-tuple-element.53), channel_id=1, source_target_pairs={{0,2},{1,3},{2,0},{3,1},{4,6},{5,7},{6,4},{7,5},{8,10},{9,11},{10,... | collective-permute-start | bytes 98312 | tf_op jit(solution)/shard_map/ppermute | solution.py:619
  66.6 5.7 %collective-permute-start.15 = (bf16[8,2048]{1,0:T(8,128)(2,1)S(1)}, bf16[8,2048]{1,0:T(8,128)(2,1)S(1)}, u32[]{:S(2)}, u32[]{:S(2)}) collective-permute-start(bf16[8,2048]{1,0:T(8,128)(2,1)S(1)} %get-tuple-element.54), channel_id=1, source_target_pairs={{0,3},{1,2},{2,1},{3,0},{4,7},{5,6},{6,5},{7,4},{8,11},{9,10},{10,... | collective-permute-start | bytes 98312 | tf_op jit(solution)/shard_map/ppermute | solution.py:619

commit v12 on v5

--- a/solution.py
+++ b/solution.py
@@ -330,12 +330,8 @@
         ).astype(out.dtype)
 
 
-def output_first_kernel(n, part, at, w, source, *rest):
-    values, (out, attended, held, sems) = rest[:n], rest[n:]
-    beside(part.copies(at, source, held, sems), at, lambda: combine(w, values, out, attended))
-
-
-def combine(w, values, out, attended):
+def output_first_kernel(n, w, *rest):
+    values, (out, attended) = rest[:n], rest[n:]
     heads = attended.shape[1] // HEAD_WIDTH
     stats = [joined(v, attended.shape[1]) for v in values]
     top = stats[0]
@@ -351,22 +347,20 @@
     product(attended, w, out, 0, out.shape[1])
 
 
-def output_first(at, values, w, part):
+def output_first(values, w):
     rows, half = values[0].shape[0], w.shape[1] // 2
     return pl.pallas_call(
-        lambda *refs: output_first_kernel(len(values), part, *refs),
-        in_specs=[SMEM, VMEM, HBM] + [VMEM] * len(values),
-        out_specs=[VMEM] * 3,
+        lambda *refs: output_first_kernel(len(values), *refs),
+        in_specs=[VMEM] * (1 + len(values)),
+        out_specs=[VMEM] * 2,
         out_shape=[
             jax.ShapeDtypeStruct((rows, half), bf16),
             jax.ShapeDtypeStruct((rows, w.shape[0]), bf16),
-            part.out,
         ],
-        scratch_shapes=[pltpu.SemaphoreType.DMA((2 * PIECES,))],
         compiler_params=params(4),
         cost_estimate=cost(rows, w),
         name="output_first",
-    )(at, w, in_hbm(part.array), *values)
+    )(w, *values)
 
 
 def output_second(attended, w):
@@ -589,21 +583,22 @@
     )(at, hidden, w, before, *resid)
 
 
-def add_kernel(one, two, out):
+def add_kernel(one, two, *rest):
+    out = rest[-1]
     for start, size in blocks_of(out.shape[1], 512):
         cols = slice(start, start + size)
         out[:, cols] = (one[:, cols].astype(f32) + two[:, cols].astype(f32)).astype(bf16)
 
 
-def add(one, two):
+def add(one, two, *tokens):
     return pl.pallas_call(
         add_kernel,
-        in_specs=[VMEM] * 2,
+        in_specs=[VMEM] * 2 + [ANY] * len(tokens),
         out_specs=VMEM,
         out_shape=jax.ShapeDtypeStruct(one.shape, bf16),
         compiler_params=params(4),
         name="add",
-    )(one, two)
+    )(one, two, *tokens)
 
 
 def swap(x, axis, bit):
@@ -625,10 +620,10 @@
     return parts
 
 
-def summed(x, axis, order):
+def summed(x, axis, order, *tokens):
     *bits, last = bits_of(axis)[::order]
     for bit in bits:
-        x = add(x, swap(x, axis, bit))
+        x = add(x, swap(x, axis, bit), *(tokens if bit == bits[-1] else ()))
     return x, swap(x, axis, last)
 
 
@@ -663,11 +658,11 @@
 
     quarter = half // 2
     up_0, gate_1, token = fetch(at, value, Part(w_up, 0, half), Part(w_gate, half, quarter))
-    out_0, attended, gate_2 = output_first(
-        at, gathered(value, "wide", token), w_out, Part(w_gate, half + quarter, quarter)
-    )
+    out_0, attended = output_first(gathered(value, "wide", token), w_out)
     out_1 = output_second(attended, w_out)
-    parts_0, parts_1 = summed(out_0, "head", 1), summed(out_1, "head", -1)
+    parts_0 = summed(out_0, "head", 1)
+    gate_2, token = fetch(at, parts_0[0], Part(w_gate, half + quarter, quarter))
+    parts_1 = summed(out_1, "head", -1, token)
     send, keep, resid_0, squares, up_1 = expand_first(
         at, own, gain, parts_0, gate_0, up_0, Part(w_up, half, half)
     )

time: 71.2 us -> 69.3 us (0.973)
  waiting for transfers between devices: 12.7 us -> 8.87 us
  Pallas kernels: 39.9 us -> 40.9 us
  starting transfers between devices: 17.1 us -> 18.1 us
    ppermute x16, waiting for transfers between devices: 12.7 us -> 8.87 us  [swap(): return lax.ppermute(x, axis, [(i, i ^ bit) for i in range(n)])]
    pallas_call x3 -> x4, Pallas kernels: 16.1 us -> 18.7 us  [fetch(): pl.pallas_call(lambda *refs: fetch_kernel(wanted, len(after), *refs), in_...]
    pallas_call x3, Pallas kernels: 2.71 us -> 1 us  [the longest x1 0.96 us: output_first(): pl.pallas_call(lambda *refs: output_first_kernel(len(values), *refs), in_...]
    ppermute x16, starting transfers between devices: 17.1 us -> 18.1 us  [swap(): return lax.ppermute(x, axis, [(i, i ^ bit) for i in range(n)])]
  transfers between devices with their start and end apart: 16 -> 16, of which waited for: 8 -> 7; matrix products, arithmetic and copies ran while one was open for 1% -> 1% of each run, Pallas kernels for 34% -> 39%
where the time goes in v12:
time: 69.3 us; the launch traced here: 69.2 us
  Pallas kernels  40.9 us (59%)
  starting transfers between devices  18.1 us (26%)
  waiting for transfers between devices  8.87 us (13%)
  other arithmetic  1.02 us (1%)
    pallas_call x4, Pallas kernels, fetch(): pl.pallas_call(lambda *refs: fetch_kernel(wanted, len(after), *refs), in_...  18.7 us
    ppermute x16, starting transfers between devices, swap(): return lax.ppermute(x, axis, [(i, i ^ bit) for i in range(n)])  18.1 us
    ppermute x16, waiting for transfers between devices, swap(): return lax.ppermute(x, axis, [(i, i ^ bit) for i in range(n)])  8.87 us
    pallas_call x1, Pallas kernels, project(): pl.pallas_call(lambda *refs: project_kernel(chunks, *refs), in_specs=[SME...  5.11 us
    pallas_call x1, Pallas kernels, attend(): pl.pallas_call(lambda *refs: attend_kernel(len(parts), part, *refs), in_s...  4.09 us
    pallas_call x1, Pallas kernels, expand_first(): pl.pallas_call(lambda *refs: expand_first_kernel(len(parts), part, *refs)...  3.79 us
    pallas_call x1, Pallas kernels, contract_last(): pl.pallas_call(lambda *refs: contract_last_kernel(n, *refs), in_specs=[SM...  1.94 us
    pallas_call x1, Pallas kernels, expand_send(): pl.pallas_call(lambda *refs: expand_send_kernel(len(parts), len(wg), *ref...  1.91 us
  transfers between devices with their start and end apart: 16, of which 7 were waited for; matrix products, arithmetic and copies ran while one was open for 1% of the time, Pallas kernels for 39%

profile of v12, /device:TPU:0, one launch (start us, length us, event | category | flops | bytes accessed | tf_op | source)
XLA Modules:
  0.0 69.2 jit_solution(17955058338768606998)
XLA Ops:
  0.0 0.0 copy-start.1
  0.0 0.0 copy-start.2
  0.0 0.1 pad_add_fusion.refs_0_.at
  0.1 5.1 %project.1 = (bf16[32,2560]{1,0:T(8,128)(2,1)S(1)}, bf16[32,2048]{1,0:T(8,128)(2,1)S(1)}) custom-call(s32[4]{0:T(128)S(1)} %pad_add_fusion.refs_0_.at, bf16[32,8192]{1,0:T(8,128)(2,1)} %refs_1_.1, bf16[64,128]{1,0:T(8,128)(2,1)} %bitcast.12, bf16[2048,2048]{1,0:T(8,128)(2,1)} %refs_3_.3, bf16[2048,256]{1,0:T(8,128)(2,1)} %refs_4_.2, bf16[2048,256]{1,0:T(8,128)(2,1)} %refs_5_.2), custom_call_target="tpu_custom_call" | custom-call | flops 335544320 | bytes 10485760 | tf_op jit(solution)/shard_map/project/pallas_call | solution.py:186
  5.2 0.5 collective-permute-start.1
  5.7 2.6 %collective-permute-start = (bf16[32,2560]{1,0:T(8,128)(2,1)S(1)}, bf16[32,2560]{1,0:T(8,128)(2,1)S(1)}, u32[]{:S(2)}, u32[]{:S(2)}) collective-permute-start(bf16[32,2560]{1,0:T(8,128)(2,1)S(1)} %get-tuple-element.35.refs_1_.refs_5_), channel_id=1, source_target_pairs={{0,8},{4,12},{8,0},{12,4},{1,9},{5,13},{9,1},{13,5},{2,10},{6,14},... | collective-permute-start | bytes 491528 | tf_op jit(solution)/shard_map/ppermute | solution.py:606
  8.3 0.0 copy-done.1
  8.3 0.1 add_convert_fusion.1
  8.4 0.1 convert_element_type.24
  8.5 0.1 fusion
  8.6 0.0 copy-done.2
  8.6 0.1 concatenate.10.refs_2_.refs_0_
  8.7 0.1 pad_maximum_fusion
  8.8 5.1 %fetch.4 = (bf16[16,512,256]{2,1,0:T(8,128)(2,1)S(1)}, bf16[1024,3584]{1,0:T(8,128)(2,1)S(1)}, f32[8,128]{1,0:T(8,128)S(1)}) custom-call(s32[4]{0:T(128)S(1)} %pad_add_fusion.refs_0_.at, bf16[32,2560]{1,0:T(8,128)(2,1)S(1)} %get-tuple-element.35.refs_1_.refs_5_, s32[20]{0:T(128)S(1)} %concatenate.10.refs_2_.refs_0_, ...), custom_call_target="tpu_custom_call" | custom-call | bytes 23068672 | tf_op jit(solution)/shard_map/fetch/pallas_call | solution.py:102
  13.9 0.0 collective-permute-done.__0_
  14.0 0.2 collective-permute-start.2
  14.2 0.0 collective-permute-done.1.refs_7_
  14.2 1.2 %collective-permute-done.2.refs_8_ = bf16[32,2560]{1,0:T(8,128)(2,1)S(1)} collective-permute-done((bf16[32,2560]{1,0:T(8,128)(2,1)S(1)}, bf16[32,2560]{1,0:T(8,128)(2,1)S(1)}, u32[]{:S(2)}, u32[]{:S(2)}) %collective-permute-start.2) | collective-permute-done | bytes 163872 | tf_op jit(solution)/shard_map/ppermute | solution.py:606
  15.4 4.1 %attend.1 = (bf16[32,2432]{1,0:T(8,128)(2,1)S(1)}, bf16[2048,2048]{1,0:T(8,128)(2,1)S(1)}) custom-call(s32[20]{0:T(128)S(1)} %concatenate.10.refs_2_.refs_0_, f32[32,128]{1,0:T(8,128)S(1)} %get-tuple-element.66.refs_3_.refs_1_, f32[32,128]{1,0:T(8,128)S(1)} %get-tuple-element.67.refs_4_.refs_2_, bf16[2,8,512,256]{3,2,1,0:T(8,128)(2,1)S(1)} %bitcast.8, ...), custom_call_target="tpu_custom_call" | custom-call | flops 134217728 | bytes 4194304 | tf_op jit(solution)/shard_map/attend/pallas_call | solution.py:305
  19.5 0.9 %collective-permute-start.3 = (bf16[32,2432]{1,0:T(8,128)(2,1)S(1)}, bf16[32,2432]{1,0:T(8,128)(2,1)S(1)}, u32[]{:S(2)}, u32[]{:S(2)}) collective-permute-start(bf16[32,2432]{1,0:T(8,128)(2,1)S(1)} %get-tuple-element.39.refs_1_), channel_id=1, source_target_pairs={{0,8},{4,12},{8,0},{12,4},{1,9},{5,13},{9,1},{13,5},{2,10},{6,14},... | collective-permute-start | bytes 466952 | tf_op jit(solution)/shard_map/ppermute | solution.py:606
  20.4 0.0 collective-permute-start.4
  20.4 4.9 %fetch.5 = (bf16[1024,3584]{1,0:T(8,128)(2,1)S(1)}, bf16[512,3584]{1,0:T(8,128)(2,1)S(1)}, f32[8,128]{1,0:T(8,128)S(1)}) custom-call(s32[4]{0:T(128)S(1)} %pad_add_fusion.refs_0_.at, bf16[32,2432]{1,0:T(8,128)(2,1)S(1)} %get-tuple-element.39.refs_1_, bf16[2048,3584]{1,0:T(8,128)(2,1)} %refs_5_.3, bf16[2048,3584]{1,0:T(8,128)(2,1)} %refs_2_.4), custom_call_target="tpu_custom_call" | custom-call | bytes 22020096 | tf_op jit(solution)/shard_map/fetch/pallas_call | solution.py:102
  25.4 0.3 collective-permute-done.3.__0_
  25.7 0.3 collective-permute-start.5
  25.9 0.0 collective-permute-done.4.refs_3_
  26.0 1.1 %collective-permute-done.5.refs_4_ = bf16[32,2432]{1,0:T(8,128)(2,1)S(1)} collective-permute-done((bf16[32,2432]{1,0:T(8,128)(2,1)S(1)}, bf16[32,2432]{1,0:T(8,128)(2,1)S(1)}, u32[]{:S(2)}, u32[]{:S(2)}) %collective-permute-start.5) | collective-permute-done | bytes 155680 | tf_op jit(solution)/shard_map/ppermute | solution.py:606
  27.1 1.0 %output_first.1 = (bf16[32,1024]{1,0:T(8,128)(2,1)S(1)}, bf16[32,2048]{1,0:T(8,128)(2,1)S(1)}) custom-call(bf16[2048,2048]{1,0:T(8,128)(2,1)S(1)} %get-tuple-element.41.refs_0_.w, bf16[32,2432]{1,0:T(8,128)(2,1)S(1)} %get-tuple-element.39.refs_1_, bf16[32,2432]{1,0:T(8,128)(2,1)S(1)} %hold.3.refs_2_, bf16[32,2432]{1,0:T(8,128)(2,1)S(1)} %collective-permute-done.4.refs_3_, ...), custom_call_target="tpu_custom_call" | custom-call | flops 268435456 | bytes 8388608 | tf_op jit(solution)/shard_map/output_first/pallas_call | solution.py:352
  28.0 1.6 %collective-permute-start.6 = (bf16[32,1024]{1,0:T(8,128)(2,1)S(1)}, bf16[32,1024]{1,0:T(8,128)(2,1)S(1)}, u32[]{:S(2)}, u32[]{:S(2)}) collective-permute-start(bf16[32,1024]{1,0:T(8,128)(2,1)S(1)} %get-tuple-element.43.one), channel_id=1, source_target_pairs={{0,1},{1,0},{2,3},{3,2},{4,5},{5,4},{6,7},{7,6},{8,9},{9,8},{10,11... | collective-permute-start | bytes 196616 | tf_op jit(solution)/shard_map/ppermute | solution.py:606
  29.6 0.8 %output_second.1.one = bf16[32,1024]{1,0:T(8,128)(2,1)S(1)} custom-call(bf16[32,2048]{1,0:T(8,128)(2,1)S(1)} %get-tuple-element.49.x, bf16[2048,2048]{1,0:T(8,128)(2,1)S(1)} %get-tuple-element.41.refs_0_.w), custom_call_target="tpu_custom_call" | custom-call | flops 268435456 | bytes 8388608 | tf_op jit(solution)/shard_map/output_second/pallas_call | solution.py:368
  30.4 2.6 %collective-permute-start.8 = (bf16[32,1024]{1,0:T(8,128)(2,1)S(1)}, bf16[32,1024]{1,0:T(8,128)(2,1)S(1)}, u32[]{:S(2)}, u32[]{:S(2)}) collective-permute-start(bf16[32,1024]{1,0:T(8,128)(2,1)S(1)} %output_second.1.one), channel_id=1, source_target_pairs={{0,2},{1,3},{2,0},{3,1},{4,6},{5,7},{6,4},{7,5},{8,10},{9,11},{10,... | collective-permute-start | bytes 196616 | tf_op jit(solution)/shard_map/ppermute | solution.py:606
  33.0 0.0 collective-permute-done.6.two
  33.1 0.0 copy-start
  33.1 2.4 %collective-permute-start.7 = (bf16[32,1024]{1,0:T(8,128)(2,1)S(1)}, bf16[32,1024]{1,0:T(8,128)(2,1)S(1)}, u32[]{:S(2)}, u32[]{:S(2)}) collective-permute-start(bf16[32,1024]{1,0:T(8,128)(2,1)S(1)} %add.41.refs_6_.refs_1_), channel_id=1, source_target_pairs={{0,2},{1,3},{2,0},{3,1},{4,6},{5,7},{6,4},{7,5},{8,10},{9,11},{10,... | collective-permute-start | bytes 196616 | tf_op jit(solution)/shard_map/ppermute | solution.py:606
  35.5 2.7 %fetch.6 = (bf16[512,3584]{1,0:T(8,128)(2,1)S(1)}, f32[8,128]{1,0:T(8,128)S(1)}) custom-call(s32[4]{0:T(128)S(1)} %pad_add_fusion.refs_0_.at, bf16[32,1024]{1,0:T(8,128)(2,1)S(1)} %add.41.refs_6_.refs_1_, bf16[2048,3584]{1,0:T(8,128)(2,1)} %refs_2_.4), custom_call_target="tpu_custom_call" | custom-call | bytes 7340032 | tf_op jit(solution)/shard_map/fetch/pallas_call | solution.py:102
  38.2 0.0 collective-permute-done.8.two
  38.2 1.1 %collective-permute-start.9 = (bf16[32,1024]{1,0:T(8,128)(2,1)S(1)}, bf16[32,1024]{1,0:T(8,128)(2,1)S(1)}, u32[]{:S(2)}, u32[]{:S(2)}) collective-permute-start(bf16[32,1024]{1,0:T(8,128)(2,1)S(1)} %add.42.refs_8_), channel_id=1, source_target_pairs={{0,1},{1,0},{2,3},{3,2},{4,5},{5,4},{6,7},{7,6},{8,9},{9,8},{10,11... | collective-permute-start | bytes 196616 | tf_op jit(solution)/shard_map/ppermute | solution.py:606
  39.4 0.2 collective-permute-done.7.refs_7_
  39.5 0.0 copy-done
  39.5 3.8 %expand_first.1 = (f32[32,3584]{1,0:T(8,128)S(1)}, f32[32,3584]{1,0:T(8,128)S(1)}, f32[32,1024]{1,0:T(8,128)S(1)}, f32[32,128]{1,0:T(8,128)S(1)}, bf16[1024,3584]{1,0:T(8,128)(2,1)S(1)}) custom-call(s32[4]{0:T(128)S(1)} %pad_add_fusion.refs_0_.at, bf16[32,2048]{1,0:T(8,128)(2,1)S(1)} %get-tuple-element.34.refs_1_, bf16[16,128]{1,0:T(8,128)(2,1)S(1)} %bitcast.9, ...), custom_call_target="tpu_custom_call" | custom-call | flops 469762048 | bytes 14680064 | tf_op jit(solution)/shard_map/expand_first/pallas_call | solution.py:422
  43.3 0.0 collective-permute-done.9.refs_9_
  43.3 1.9 %expand_send.1 = (bf16[32,3968]{1,0:T(8,128)(2,1)S(1)}, f32[32,1024]{1,0:T(8,128)S(1)}, bf16[32,1024]{1,0:T(8,128)(2,1)S(1)}) custom-call(s32[4]{0:T(128)S(1)} %pad_add_fusion.refs_0_.at, bf16[32,2048]{1,0:T(8,128)(2,1)S(1)} %get-tuple-element.34.refs_1_, bf16[16,128]{1,0:T(8,128)(2,1)S(1)} %bitcast.10, f32[32,3584]{1,0:T(8,128)S(1)} %get-tuple-element.44.refs_3_, ...), custom_call_target="tpu_custom_call" | custom-call | flops 234881024 | bytes 7340032 | tf_op jit(solution)/shard_map/expand_send/pallas_call | solution.py:456
  45.3 0.1 collective-permute-start.10
  45.3 1.9 %expand_keep.1.keep = bf16[32,3584]{1,0:T(8,128)(2,1)S(1)} custom-call(s32[4]{0:T(128)S(1)} %pad_add_fusion.refs_0_.at, bf16[32,1024]{1,0:T(8,128)(2,1)S(1)} %get-tuple-element.51.x, f32[32,3584]{1,0:T(8,128)S(1)} %get-tuple-element.52.before, bf16[512,3584]{1,0:T(8,128)(2,1)S(1)} %get-tuple-element.46.refs_5_.refs_0_, ...), custom_call_target="tpu_custom_call" | custom-call | flops 234881024 | bytes 7340032 | tf_op jit(solution)/shard_map/expand_keep/pallas_call | solution.py:474
  47.2 0.0 collective-permute-done.10.received
  47.2 0.1 pair.1.refs_1_.refs_0_
  47.3 1.2 %collective-permute-start.11 = (bf16[32,3968]{1,0:T(8,128)(2,1)S(1)}, bf16[32,3968]{1,0:T(8,128)(2,1)S(1)}, u32[]{:S(2)}, u32[]{:S(2)}) collective-permute-start(bf16[32,3968]{1,0:T(8,128)(2,1)S(1)} %pair.1.refs_1_.refs_0_), channel_id=1, source_target_pairs={{0,8},{4,12},{8,0},{12,4},{1,9},{5,13},{9,1},{13,5},{2,10},{6,14},... | collective-permute-start | bytes 761864 | tf_op jit(solution)/shard_map/ppermute | solution.py:606
  48.5 6.0 %fetch.7 = (bf16[1792,2048]{1,0:T(8,128)(2,1)S(1)}, bf16[1792,2048]{1,0:T(8,128)(2,1)S(1)}, f32[8,128]{1,0:T(8,128)S(1)}) custom-call(s32[4]{0:T(128)S(1)} %pad_add_fusion.refs_0_.at, bf16[32,3968]{1,0:T(8,128)(2,1)S(1)} %pair.1.refs_1_.refs_0_, bf16[3584,2048]{1,0:T(8,128)(2,1)} %refs_3_.5, bf16[3584,2048]{1,0:T(8,128)(2,1)} %refs_3_.5), custom_call_target="tpu_custom_call" | custom-call | bytes 29360128 | tf_op jit(solution)/shard_map/fetch/pallas_call | solution.py:102
  54.6 1.3 %collective-permute-done.11.refs_1_ = bf16[32,3968]{1,0:T(8,128)(2,1)S(1)} collective-permute-done((bf16[32,3968]{1,0:T(8,128)(2,1)S(1)}, bf16[32,3968]{1,0:T(8,128)(2,1)S(1)}, u32[]{:S(2)}, u32[]{:S(2)}) %collective-permute-start.11) | collective-permute-done | bytes 253984 | tf_op jit(solution)/shard_map/ppermute | solution.py:606
  55.9 0.1 gated.1.hidden
  56.1 0.1 collective-permute-start.12
  56.1 1.4 %contract.1.refs_3_ = f32[32,2048]{1,0:T(8,128)S(1)} custom-call(bf16[32,1792]{1,0:T(8,128)(2,1)S(1)} %gated.1.hidden, bf16[1792,2048]{1,0:T(8,128)(2,1)S(1)} %get-tuple-element.56.w), custom_call_target="tpu_custom_call" | custom-call | flops 234881024 | bytes 7340032 | tf_op jit(solution)/shard_map/contract/pallas_call | solution.py:536
  57.5 0.0 collective-permute-done.12.refs_1_
  57.5 1.9 %contract_last.1 = (f32[8,2048]{1,0:T(8,128)S(1)}, bf16[8,2048]{1,0:T(8,128)(2,1)S(1)}, bf16[8,2048]{1,0:T(8,128)(2,1)S(1)}, bf16[8,2048]{1,0:T(8,128)(2,1)S(1)}) custom-call(s32[4]{0:T(128)S(1)} %pad_add_fusion.refs_0_.at, bf16[32,1792]{1,0:T(8,128)(2,1)S(1)} %collective-permute-done.12.refs_1_, bf16[1792,2048]{1,0:T(8,128)(2,1)S(1)} %get-tuple-element.55.refs_2_, ...), custom_call_target="tpu_custom_call" | custom-call | flops 234881024 | bytes 7340032 | tf_op jit(solution)/shard_map/contract_last/pallas_call | solution.py:573
  59.4 0.8 %collective-permute-start.13 = (bf16[8,2048]{1,0:T(8,128)(2,1)S(1)}, bf16[8,2048]{1,0:T(8,128)(2,1)S(1)}, u32[]{:S(2)}, u32[]{:S(2)}) collective-permute-start(bf16[8,2048]{1,0:T(8,128)(2,1)S(1)} %get-tuple-element.60), channel_id=1, source_target_pairs={{0,1},{1,0},{2,3},{3,2},{4,5},{5,4},{6,7},{7,6},{8,9},{9,8},{10,11... | collective-permute-start | bytes 98312 | tf_op jit(solution)/shard_map/ppermute | solution.py:606
  60.3 2.6 %collective-permute-start.14 = (bf16[8,2048]{1,0:T(8,128)(2,1)S(1)}, bf16[8,2048]{1,0:T(8,128)(2,1)S(1)}, u32[]{:S(2)}, u32[]{:S(2)}) collective-permute-start(bf16[8,2048]{1,0:T(8,128)(2,1)S(1)} %get-tuple-element.61), channel_id=1, source_target_pairs={{0,2},{1,3},{2,0},{3,1},{4,6},{5,7},{6,4},{7,5},{8,10},{9,11},{10,... | collective-permute-start | bytes 98312 | tf_op jit(solution)/shard_map/ppermute | solution.py:606
  62.9 1.0 %collective-permute-start.15 = (bf16[8,2048]{1,0:T(8,128)(2,1)S(1)}, bf16[8,2048]{1,0:T(8,128)(2,1)S(1)}, u32[]{:S(2)}, u32[]{:S(2)}) collective-permute-start(bf16[8,2048]{1,0:T(8,128)(2,1)S(1)} %get-tuple-element.62), channel_id=1, source_target_pairs={{0,3},{1,2},{2,1},{3,0},{4,7},{5,6},{6,5},{7,4},{8,11},{9,10},{10,... | collective-permute-start | bytes 98312 | tf_op jit(solution)/shard_map/ppermute | solution.py:606
  63.9 0.0 collective-permute-done.13
  63.9 2.0 %collective-permute-done.14 = bf16[8,2048]{1,0:T(8,128)(2,1)S(1)} collective-permute-done((bf16[8,2048]{1,0:T(8,128)(2,1)S(1)}, bf16[8,2048]{1,0:T(8,128)(2,1)S(1)}, u32[]{:S(2)}, u32[]{:S(2)}) %collective-permute-start.14) | collective-permute-done | bytes 32800 | tf_op jit(solution)/shard_map/ppermute | solution.py:606
  65.9 2.7 %collective-permute-done.15 = bf16[8,2048]{1,0:T(8,128)(2,1)S(1)} collective-permute-done((bf16[8,2048]{1,0:T(8,128)(2,1)S(1)}, bf16[8,2048]{1,0:T(8,128)(2,1)S(1)}, u32[]{:S(2)}, u32[]{:S(2)}) %collective-permute-start.15) | collective-permute-done | bytes 32800 | tf_op jit(solution)/shard_map/ppermute | solution.py:606
  68.6 0.6 add_convert_fusion
  (5 shorter events, 0.1 us)
Async XLA Ops:
  0.0 8.3 %copy-start.1 = (s32[8]{0:T(128)S(1)}, s32[8]{0:T(128)}, u32[]{:S(2)}) copy-start(s32[8]{0:T(128)} %param.24) | copy-start | bytes 100
  0.0 8.6 %copy-start.2 = (s32[8]{0:T(128)S(1)}, s32[8]{0:T(128)}, u32[]{:S(2)}) copy-start(s32[8]{0:T(128)} %param.25) | copy-start | bytes 100
  5.2 9.0 %collective-permute-start.1 = (bf16[32,2560]{1,0:T(8,128)(2,1)S(1)}, bf16[32,2560]{1,0:T(8,128)(2,1)S(1)}, u32[]{:S(2)}, u32[]{:S(2)}) collective-permute-start(bf16[32,2560]{1,0:T(8,128)(2,1)S(1)} %get-tuple-element.35.refs_1_.refs_5_), channel_id=1, source_target_pairs={{0,4},{4,0},{8,12},{12,8},{1,5},{5,1},{9,13},{13,9},{2,6},{6,2},{1... | collective-permute-start | bytes 491528 | tf_op jit(solution)/shard_map/ppermute | solution.py:606
  5.7 8.2 %collective-permute-start = (bf16[32,2560]{1,0:T(8,128)(2,1)S(1)}, bf16[32,2560]{1,0:T(8,128)(2,1)S(1)}, u32[]{:S(2)}, u32[]{:S(2)}) collective-permute-start(bf16[32,2560]{1,0:T(8,128)(2,1)S(1)} %get-tuple-element.35.refs_1_.refs_5_), channel_id=1, source_target_pairs={{0,8},{4,12},{8,0},{12,4},{1,9},{5,13},{9,1},{13,5},{2,10},{6,14},... | collective-permute-start | bytes 491528 | tf_op jit(solution)/shard_map/ppermute | solution.py:606
  14.0 1.5 %collective-permute-start.2 = (bf16[32,2560]{1,0:T(8,128)(2,1)S(1)}, bf16[32,2560]{1,0:T(8,128)(2,1)S(1)}, u32[]{:S(2)}, u32[]{:S(2)}) collective-permute-start(bf16[32,2560]{1,0:T(8,128)(2,1)S(1)} %hold.2.refs_6_), channel_id=1, source_target_pairs={{0,4},{4,0},{8,12},{12,8},{1,5},{5,1},{9,13},{13,9},{2,6},{6,2},{1... | collective-permute-start | bytes 491528 | tf_op jit(solution)/shard_map/ppermute | solution.py:606
  19.5 6.2 %collective-permute-start.3 = (bf16[32,2432]{1,0:T(8,128)(2,1)S(1)}, bf16[32,2432]{1,0:T(8,128)(2,1)S(1)}, u32[]{:S(2)}, u32[]{:S(2)}) collective-permute-start(bf16[32,2432]{1,0:T(8,128)(2,1)S(1)} %get-tuple-element.39.refs_1_), channel_id=1, source_target_pairs={{0,8},{4,12},{8,0},{12,4},{1,9},{5,13},{9,1},{13,5},{2,10},{6,14},... | collective-permute-start | bytes 466952 | tf_op jit(solution)/shard_map/ppermute | solution.py:606
  20.4 5.5 %collective-permute-start.4 = (bf16[32,2432]{1,0:T(8,128)(2,1)S(1)}, bf16[32,2432]{1,0:T(8,128)(2,1)S(1)}, u32[]{:S(2)}, u32[]{:S(2)}) collective-permute-start(bf16[32,2432]{1,0:T(8,128)(2,1)S(1)} %get-tuple-element.39.refs_1_), channel_id=1, source_target_pairs={{0,4},{4,0},{8,12},{12,8},{1,5},{5,1},{9,13},{13,9},{2,6},{6,2},{1... | collective-permute-start | bytes 466952 | tf_op jit(solution)/shard_map/ppermute | solution.py:606
  25.7 1.4 %collective-permute-start.5 = (bf16[32,2432]{1,0:T(8,128)(2,1)S(1)}, bf16[32,2432]{1,0:T(8,128)(2,1)S(1)}, u32[]{:S(2)}, u32[]{:S(2)}) collective-permute-start(bf16[32,2432]{1,0:T(8,128)(2,1)S(1)} %hold.3.refs_2_), channel_id=1, source_target_pairs={{0,4},{4,0},{8,12},{12,8},{1,5},{5,1},{9,13},{13,9},{2,6},{6,2},{1... | collective-permute-start | bytes 466952 | tf_op jit(solution)/shard_map/ppermute | solution.py:606
  28.0 5.0 %collective-permute-start.6 = (bf16[32,1024]{1,0:T(8,128)(2,1)S(1)}, bf16[32,1024]{1,0:T(8,128)(2,1)S(1)}, u32[]{:S(2)}, u32[]{:S(2)}) collective-permute-start(bf16[32,1024]{1,0:T(8,128)(2,1)S(1)} %get-tuple-element.43.one), channel_id=1, source_target_pairs={{0,1},{1,0},{2,3},{3,2},{4,5},{5,4},{6,7},{7,6},{8,9},{9,8},{10,11... | collective-permute-start | bytes 196616 | tf_op jit(solution)/shard_map/ppermute | solution.py:606
  30.4 7.7 %collective-permute-start.8 = (bf16[32,1024]{1,0:T(8,128)(2,1)S(1)}, bf16[32,1024]{1,0:T(8,128)(2,1)S(1)}, u32[]{:S(2)}, u32[]{:S(2)}) collective-permute-start(bf16[32,1024]{1,0:T(8,128)(2,1)S(1)} %output_second.1.one), channel_id=1, source_target_pairs={{0,2},{1,3},{2,0},{3,1},{4,6},{5,7},{6,4},{7,5},{8,10},{9,11},{10,... | collective-permute-start | bytes 196616 | tf_op jit(solution)/shard_map/ppermute | solution.py:606
  33.1 6.5 %copy-start = (bf16[2048]{0:T(1024)(128)(2,1)S(1)}, bf16[2048]{0:T(1024)(128)(2,1)}, u32[]{:S(2)}) copy-start(bf16[2048]{0:T(1024)(128)(2,1)} %param.15) | copy-start | bytes 12292
  33.1 6.4 %collective-permute-start.7 = (bf16[32,1024]{1,0:T(8,128)(2,1)S(1)}, bf16[32,1024]{1,0:T(8,128)(2,1)S(1)}, u32[]{:S(2)}, u32[]{:S(2)}) collective-permute-start(bf16[32,1024]{1,0:T(8,128)(2,1)S(1)} %add.41.refs_6_.refs_1_), channel_id=1, source_target_pairs={{0,2},{1,3},{2,0},{3,1},{4,6},{5,7},{6,4},{7,5},{8,10},{9,11},{10,... | collective-permute-start | bytes 196616 | tf_op jit(solution)/shard_map/ppermute | solution.py:606
  38.2 5.1 %collective-permute-start.9 = (bf16[32,1024]{1,0:T(8,128)(2,1)S(1)}, bf16[32,1024]{1,0:T(8,128)(2,1)S(1)}, u32[]{:S(2)}, u32[]{:S(2)}) collective-permute-start(bf16[32,1024]{1,0:T(8,128)(2,1)S(1)} %add.42.refs_8_), channel_id=1, source_target_pairs={{0,1},{1,0},{2,3},{3,2},{4,5},{5,4},{6,7},{7,6},{8,9},{9,8},{10,11... | collective-permute-start | bytes 196616 | tf_op jit(solution)/shard_map/ppermute | solution.py:606
  45.3 2.0 %collective-permute-start.10 = (bf16[32,3968]{1,0:T(8,128)(2,1)S(1)}, bf16[32,3968]{1,0:T(8,128)(2,1)S(1)}, u32[]{:S(2)}, u32[]{:S(2)}) collective-permute-start(bf16[32,3968]{1,0:T(8,128)(2,1)S(1)} %get-tuple-element.53.stats), channel_id=1, source_target_pairs={{0,4},{4,0},{8,12},{12,8},{1,5},{5,1},{9,13},{13,9},{2,6},{6,2},{1... | collective-permute-start | bytes 761864 | tf_op jit(solution)/shard_map/ppermute | solution.py:606
  47.3 8.6 %collective-permute-start.11 = (bf16[32,3968]{1,0:T(8,128)(2,1)S(1)}, bf16[32,3968]{1,0:T(8,128)(2,1)S(1)}, u32[]{:S(2)}, u32[]{:S(2)}) collective-permute-start(bf16[32,3968]{1,0:T(8,128)(2,1)S(1)} %pair.1.refs_1_.refs_0_), channel_id=1, source_target_pairs={{0,8},{4,12},{8,0},{12,4},{1,9},{5,13},{9,1},{13,5},{2,10},{6,14},... | collective-permute-start | bytes 761864 | tf_op jit(solution)/shard_map/ppermute | solution.py:606
  56.1 1.4 %collective-permute-start.12 = (bf16[32,1792]{1,0:T(8,128)(2,1)S(1)}, bf16[32,1792]{1,0:T(8,128)(2,1)S(1)}, u32[]{:S(2)}, u32[]{:S(2)}) collective-permute-start(bf16[32,1792]{1,0:T(8,128)(2,1)S(1)} %gated.1.hidden), channel_id=1, source_target_pairs={{0,4},{4,0},{8,12},{12,8},{1,5},{5,1},{9,13},{13,9},{2,6},{6,2},{1... | collective-permute-start | bytes 344072 | tf_op jit(solution)/shard_map/ppermute | solution.py:606
  59.4 4.5 %collective-permute-start.13 = (bf16[8,2048]{1,0:T(8,128)(2,1)S(1)}, bf16[8,2048]{1,0:T(8,128)(2,1)S(1)}, u32[]{:S(2)}, u32[]{:S(2)}) collective-permute-start(bf16[8,2048]{1,0:T(8,128)(2,1)S(1)} %get-tuple-element.60), channel_id=1, source_target_pairs={{0,1},{1,0},{2,3},{3,2},{4,5},{5,4},{6,7},{7,6},{8,9},{9,8},{10,11... | collective-permute-start | bytes 98312 | tf_op jit(solution)/shard_map/ppermute | solution.py:606
  60.3 5.6 %collective-permute-start.14 = (bf16[8,2048]{1,0:T(8,128)(2,1)S(1)}, bf16[8,2048]{1,0:T(8,128)(2,1)S(1)}, u32[]{:S(2)}, u32[]{:S(2)}) collective-permute-start(bf16[8,2048]{1,0:T(8,128)(2,1)S(1)} %get-tuple-element.61), channel_id=1, source_target_pairs={{0,2},{1,3},{2,0},{3,1},{4,6},{5,7},{6,4},{7,5},{8,10},{9,11},{10,... | collective-permute-start | bytes 98312 | tf_op jit(solution)/shard_map/ppermute | solution.py:606
  62.9 5.7 %collective-permute-start.15 = (bf16[8,2048]{1,0:T(8,128)(2,1)S(1)}, bf16[8,2048]{1,0:T(8,128)(2,1)S(1)}, u32[]{:S(2)}, u32[]{:S(2)}) collective-permute-start(bf16[8,2048]{1,0:T(8,128)(2,1)S(1)} %get-tuple-element.62), channel_id=1, source_target_pairs={{0,3},{1,2},{2,1},{3,0},{4,7},{5,6},{6,5},{7,4},{8,11},{9,10},{10,... | collective-permute-start | bytes 98312 | tf_op jit(solution)/shard_map/ppermute | solution.py:606

commit v13 on v12

--- a/solution.py
+++ b/solution.py
@@ -679,7 +679,7 @@
     total, *sends = contract_last(
         head_size, at, other, down_other, contract(hidden, down_own), resid_0, resid_1
     )
-    for s, send in enumerate(sends, 1):
+    for s, send in reversed(list(enumerate(sends, 1))):
         total = total + swap(send, "head", s).astype(f32)
     return total.astype(bf16)
 

time: 69.3 us -> 67.9 us (0.980)
  waiting for transfers between devices: 8.87 us -> 7.41 us
    ppermute x16, waiting for transfers between devices: 8.87 us -> 7.41 us  [swap(): return lax.ppermute(x, axis, [(i, i ^ bit) for i in range(n)])]
where the time goes in v13:
time: 67.9 us; the launch traced here: 67.7 us
  Pallas kernels  40.9 us (60%)
  starting transfers between devices  18.1 us (27%)
  waiting for transfers between devices  7.41 us (11%)
  other arithmetic  1.02 us (2%)
    pallas_call x4, Pallas kernels, fetch(): pl.pallas_call(lambda *refs: fetch_kernel(wanted, len(after), *refs), in_...  18.7 us
    ppermute x16, starting transfers between devices, swap(): return lax.ppermute(x, axis, [(i, i ^ bit) for i in range(n)])  18.1 us
    ppermute x16, waiting for transfers between devices, swap(): return lax.ppermute(x, axis, [(i, i ^ bit) for i in range(n)])  7.41 us
    pallas_call x1, Pallas kernels, project(): pl.pallas_call(lambda *refs: project_kernel(chunks, *refs), in_specs=[SME...  5.11 us
    pallas_call x1, Pallas kernels, attend(): pl.pallas_call(lambda *refs: attend_kernel(len(parts), part, *refs), in_s...  4.09 us
    pallas_call x1, Pallas kernels, expand_first(): pl.pallas_call(lambda *refs: expand_first_kernel(len(parts), part, *refs)...  3.79 us
    pallas_call x1, Pallas kernels, contract_last(): pl.pallas_call(lambda *refs: contract_last_kernel(n, *refs), in_specs=[SM...  1.94 us
    pallas_call x1, Pallas kernels, expand_send(): pl.pallas_call(lambda *refs: expand_send_kernel(len(parts), len(wg), *ref...  1.91 us
  transfers between devices with their start and end apart: 16, of which 7 were waited for; matrix products, arithmetic and copies ran while one was open for 1% of the time, Pallas kernels for 39%

profile of v13, /device:TPU:0, one launch (start us, length us, event | category | flops | bytes accessed | tf_op | source)
XLA Modules:
  0.0 67.7 jit_solution(14750843114069458052)
XLA Ops:
  0.0 0.0 copy-start.1
  0.0 0.0 copy-start.2
  0.0 0.1 pad_add_fusion.refs_0_.at
  0.1 5.1 %project.1 = (bf16[32,2560]{1,0:T(8,128)(2,1)S(1)}, bf16[32,2048]{1,0:T(8,128)(2,1)S(1)}) custom-call(s32[4]{0:T(128)S(1)} %pad_add_fusion.refs_0_.at, bf16[32,8192]{1,0:T(8,128)(2,1)} %refs_1_.1, bf16[64,128]{1,0:T(8,128)(2,1)} %bitcast.12, bf16[2048,2048]{1,0:T(8,128)(2,1)} %refs_3_.3, bf16[2048,256]{1,0:T(8,128)(2,1)} %refs_4_.2, bf16[2048,256]{1,0:T(8,128)(2,1)} %refs_5_.2), custom_call_target="tpu_custom_call" | custom-call | flops 335544320 | bytes 10485760 | tf_op jit(solution)/shard_map/project/pallas_call | solution.py:186
  5.2 0.5 collective-permute-start.1
  5.7 2.6 %collective-permute-start = (bf16[32,2560]{1,0:T(8,128)(2,1)S(1)}, bf16[32,2560]{1,0:T(8,128)(2,1)S(1)}, u32[]{:S(2)}, u32[]{:S(2)}) collective-permute-start(bf16[32,2560]{1,0:T(8,128)(2,1)S(1)} %get-tuple-element.35.refs_1_.refs_5_), channel_id=1, source_target_pairs={{0,8},{4,12},{8,0},{12,4},{1,9},{5,13},{9,1},{13,5},{2,10},{6,14},... | collective-permute-start | bytes 491528 | tf_op jit(solution)/shard_map/ppermute | solution.py:606
  8.3 0.0 copy-done.1
  8.3 0.1 add_convert_fusion.1
  8.4 0.1 convert_element_type.24
  8.5 0.1 fusion
  8.6 0.0 copy-done.2
  8.6 0.1 concatenate.10.refs_2_.refs_0_
  8.7 0.1 pad_maximum_fusion
  8.8 5.1 %fetch.4 = (bf16[16,512,256]{2,1,0:T(8,128)(2,1)S(1)}, bf16[1024,3584]{1,0:T(8,128)(2,1)S(1)}, f32[8,128]{1,0:T(8,128)S(1)}) custom-call(s32[4]{0:T(128)S(1)} %pad_add_fusion.refs_0_.at, bf16[32,2560]{1,0:T(8,128)(2,1)S(1)} %get-tuple-element.35.refs_1_.refs_5_, s32[20]{0:T(128)S(1)} %concatenate.10.refs_2_.refs_0_, ...), custom_call_target="tpu_custom_call" | custom-call | bytes 23068672 | tf_op jit(solution)/shard_map/fetch/pallas_call | solution.py:102
  13.9 0.0 collective-permute-done.__0_
  14.0 0.2 collective-permute-start.2
  14.2 0.0 collective-permute-done.1.refs_7_
  14.2 1.2 %collective-permute-done.2.refs_8_ = bf16[32,2560]{1,0:T(8,128)(2,1)S(1)} collective-permute-done((bf16[32,2560]{1,0:T(8,128)(2,1)S(1)}, bf16[32,2560]{1,0:T(8,128)(2,1)S(1)}, u32[]{:S(2)}, u32[]{:S(2)}) %collective-permute-start.2) | collective-permute-done | bytes 163872 | tf_op jit(solution)/shard_map/ppermute | solution.py:606
  15.4 4.1 %attend.1 = (bf16[32,2432]{1,0:T(8,128)(2,1)S(1)}, bf16[2048,2048]{1,0:T(8,128)(2,1)S(1)}) custom-call(s32[20]{0:T(128)S(1)} %concatenate.10.refs_2_.refs_0_, f32[32,128]{1,0:T(8,128)S(1)} %get-tuple-element.66.refs_3_.refs_1_, f32[32,128]{1,0:T(8,128)S(1)} %get-tuple-element.67.refs_4_.refs_2_, bf16[2,8,512,256]{3,2,1,0:T(8,128)(2,1)S(1)} %bitcast.8, ...), custom_call_target="tpu_custom_call" | custom-call | flops 134217728 | bytes 4194304 | tf_op jit(solution)/shard_map/attend/pallas_call | solution.py:305
  19.5 0.9 %collective-permute-start.3 = (bf16[32,2432]{1,0:T(8,128)(2,1)S(1)}, bf16[32,2432]{1,0:T(8,128)(2,1)S(1)}, u32[]{:S(2)}, u32[]{:S(2)}) collective-permute-start(bf16[32,2432]{1,0:T(8,128)(2,1)S(1)} %get-tuple-element.39.refs_1_), channel_id=1, source_target_pairs={{0,8},{4,12},{8,0},{12,4},{1,9},{5,13},{9,1},{13,5},{2,10},{6,14},... | collective-permute-start | bytes 466952 | tf_op jit(solution)/shard_map/ppermute | solution.py:606
  20.4 0.0 collective-permute-start.4
  20.4 4.9 %fetch.5 = (bf16[1024,3584]{1,0:T(8,128)(2,1)S(1)}, bf16[512,3584]{1,0:T(8,128)(2,1)S(1)}, f32[8,128]{1,0:T(8,128)S(1)}) custom-call(s32[4]{0:T(128)S(1)} %pad_add_fusion.refs_0_.at, bf16[32,2432]{1,0:T(8,128)(2,1)S(1)} %get-tuple-element.39.refs_1_, bf16[2048,3584]{1,0:T(8,128)(2,1)} %refs_5_.3, bf16[2048,3584]{1,0:T(8,128)(2,1)} %refs_2_.4), custom_call_target="tpu_custom_call" | custom-call | bytes 22020096 | tf_op jit(solution)/shard_map/fetch/pallas_call | solution.py:102
  25.4 0.3 collective-permute-done.3.__0_
  25.7 0.3 collective-permute-start.5
  25.9 0.0 collective-permute-done.4.refs_3_
  26.0 1.1 %collective-permute-done.5.refs_4_ = bf16[32,2432]{1,0:T(8,128)(2,1)S(1)} collective-permute-done((bf16[32,2432]{1,0:T(8,128)(2,1)S(1)}, bf16[32,2432]{1,0:T(8,128)(2,1)S(1)}, u32[]{:S(2)}, u32[]{:S(2)}) %collective-permute-start.5) | collective-permute-done | bytes 155680 | tf_op jit(solution)/shard_map/ppermute | solution.py:606
  27.1 1.0 %output_first.1 = (bf16[32,1024]{1,0:T(8,128)(2,1)S(1)}, bf16[32,2048]{1,0:T(8,128)(2,1)S(1)}) custom-call(bf16[2048,2048]{1,0:T(8,128)(2,1)S(1)} %get-tuple-element.41.refs_0_.w, bf16[32,2432]{1,0:T(8,128)(2,1)S(1)} %get-tuple-element.39.refs_1_, bf16[32,2432]{1,0:T(8,128)(2,1)S(1)} %hold.3.refs_2_, bf16[32,2432]{1,0:T(8,128)(2,1)S(1)} %collective-permute-done.4.refs_3_, ...), custom_call_target="tpu_custom_call" | custom-call | flops 268435456 | bytes 8388608 | tf_op jit(solution)/shard_map/output_first/pallas_call | solution.py:352
  28.0 1.6 %collective-permute-start.6 = (bf16[32,1024]{1,0:T(8,128)(2,1)S(1)}, bf16[32,1024]{1,0:T(8,128)(2,1)S(1)}, u32[]{:S(2)}, u32[]{:S(2)}) collective-permute-start(bf16[32,1024]{1,0:T(8,128)(2,1)S(1)} %get-tuple-element.43.one), channel_id=1, source_target_pairs={{0,1},{1,0},{2,3},{3,2},{4,5},{5,4},{6,7},{7,6},{8,9},{9,8},{10,11... | collective-permute-start | bytes 196616 | tf_op jit(solution)/shard_map/ppermute | solution.py:606
  29.6 0.8 %output_second.1.one = bf16[32,1024]{1,0:T(8,128)(2,1)S(1)} custom-call(bf16[32,2048]{1,0:T(8,128)(2,1)S(1)} %get-tuple-element.49.x, bf16[2048,2048]{1,0:T(8,128)(2,1)S(1)} %get-tuple-element.41.refs_0_.w), custom_call_target="tpu_custom_call" | custom-call | flops 268435456 | bytes 8388608 | tf_op jit(solution)/shard_map/output_second/pallas_call | solution.py:368
  30.4 2.6 %collective-permute-start.8 = (bf16[32,1024]{1,0:T(8,128)(2,1)S(1)}, bf16[32,1024]{1,0:T(8,128)(2,1)S(1)}, u32[]{:S(2)}, u32[]{:S(2)}) collective-permute-start(bf16[32,1024]{1,0:T(8,128)(2,1)S(1)} %output_second.1.one), channel_id=1, source_target_pairs={{0,2},{1,3},{2,0},{3,1},{4,6},{5,7},{6,4},{7,5},{8,10},{9,11},{10,... | collective-permute-start | bytes 196616 | tf_op jit(solution)/shard_map/ppermute | solution.py:606
  33.0 0.0 collective-permute-done.6.two
  33.1 0.0 copy-start
  33.1 2.4 %collective-permute-start.7 = (bf16[32,1024]{1,0:T(8,128)(2,1)S(1)}, bf16[32,1024]{1,0:T(8,128)(2,1)S(1)}, u32[]{:S(2)}, u32[]{:S(2)}) collective-permute-start(bf16[32,1024]{1,0:T(8,128)(2,1)S(1)} %add.41.refs_6_.refs_1_), channel_id=1, source_target_pairs={{0,2},{1,3},{2,0},{3,1},{4,6},{5,7},{6,4},{7,5},{8,10},{9,11},{10,... | collective-permute-start | bytes 196616 | tf_op jit(solution)/shard_map/ppermute | solution.py:606
  35.5 2.7 %fetch.6 = (bf16[512,3584]{1,0:T(8,128)(2,1)S(1)}, f32[8,128]{1,0:T(8,128)S(1)}) custom-call(s32[4]{0:T(128)S(1)} %pad_add_fusion.refs_0_.at, bf16[32,1024]{1,0:T(8,128)(2,1)S(1)} %add.41.refs_6_.refs_1_, bf16[2048,3584]{1,0:T(8,128)(2,1)} %refs_2_.4), custom_call_target="tpu_custom_call" | custom-call | bytes 7340032 | tf_op jit(solution)/shard_map/fetch/pallas_call | solution.py:102
  38.2 0.0 collective-permute-done.8.two
  38.2 1.1 %collective-permute-start.9 = (bf16[32,1024]{1,0:T(8,128)(2,1)S(1)}, bf16[32,1024]{1,0:T(8,128)(2,1)S(1)}, u32[]{:S(2)}, u32[]{:S(2)}) collective-permute-start(bf16[32,1024]{1,0:T(8,128)(2,1)S(1)} %add.42.refs_8_), channel_id=1, source_target_pairs={{0,1},{1,0},{2,3},{3,2},{4,5},{5,4},{6,7},{7,6},{8,9},{9,8},{10,11... | collective-permute-start | bytes 196616 | tf_op jit(solution)/shard_map/ppermute | solution.py:606
  39.4 0.2 collective-permute-done.7.refs_7_
  39.5 0.0 copy-done
  39.5 3.8 %expand_first.1 = (f32[32,3584]{1,0:T(8,128)S(1)}, f32[32,3584]{1,0:T(8,128)S(1)}, f32[32,1024]{1,0:T(8,128)S(1)}, f32[32,128]{1,0:T(8,128)S(1)}, bf16[1024,3584]{1,0:T(8,128)(2,1)S(1)}) custom-call(s32[4]{0:T(128)S(1)} %pad_add_fusion.refs_0_.at, bf16[32,2048]{1,0:T(8,128)(2,1)S(1)} %get-tuple-element.34.refs_1_, bf16[16,128]{1,0:T(8,128)(2,1)S(1)} %bitcast.9, ...), custom_call_target="tpu_custom_call" | custom-call | flops 469762048 | bytes 14680064 | tf_op jit(solution)/shard_map/expand_first/pallas_call | solution.py:422
  43.3 0.0 collective-permute-done.9.refs_9_
  43.3 1.9 %expand_send.1 = (bf16[32,3968]{1,0:T(8,128)(2,1)S(1)}, f32[32,1024]{1,0:T(8,128)S(1)}, bf16[32,1024]{1,0:T(8,128)(2,1)S(1)}) custom-call(s32[4]{0:T(128)S(1)} %pad_add_fusion.refs_0_.at, bf16[32,2048]{1,0:T(8,128)(2,1)S(1)} %get-tuple-element.34.refs_1_, bf16[16,128]{1,0:T(8,128)(2,1)S(1)} %bitcast.10, f32[32,3584]{1,0:T(8,128)S(1)} %get-tuple-element.44.refs_3_, ...), custom_call_target="tpu_custom_call" | custom-call | flops 234881024 | bytes 7340032 | tf_op jit(solution)/shard_map/expand_send/pallas_call | solution.py:456
  45.3 0.1 collective-permute-start.10
  45.3 1.9 %expand_keep.1.keep = bf16[32,3584]{1,0:T(8,128)(2,1)S(1)} custom-call(s32[4]{0:T(128)S(1)} %pad_add_fusion.refs_0_.at, bf16[32,1024]{1,0:T(8,128)(2,1)S(1)} %get-tuple-element.51.x, f32[32,3584]{1,0:T(8,128)S(1)} %get-tuple-element.52.before, bf16[512,3584]{1,0:T(8,128)(2,1)S(1)} %get-tuple-element.46.refs_5_.refs_0_, ...), custom_call_target="tpu_custom_call" | custom-call | flops 234881024 | bytes 7340032 | tf_op jit(solution)/shard_map/expand_keep/pallas_call | solution.py:474
  47.2 0.0 collective-permute-done.10.received
  47.2 0.1 pair.1.refs_1_.refs_0_
  47.3 1.2 %collective-permute-start.11 = (bf16[32,3968]{1,0:T(8,128)(2,1)S(1)}, bf16[32,3968]{1,0:T(8,128)(2,1)S(1)}, u32[]{:S(2)}, u32[]{:S(2)}) collective-permute-start(bf16[32,3968]{1,0:T(8,128)(2,1)S(1)} %pair.1.refs_1_.refs_0_), channel_id=1, source_target_pairs={{0,8},{4,12},{8,0},{12,4},{1,9},{5,13},{9,1},{13,5},{2,10},{6,14},... | collective-permute-start | bytes 761864 | tf_op jit(solution)/shard_map/ppermute | solution.py:606
  48.5 6.0 %fetch.7 = (bf16[1792,2048]{1,0:T(8,128)(2,1)S(1)}, bf16[1792,2048]{1,0:T(8,128)(2,1)S(1)}, f32[8,128]{1,0:T(8,128)S(1)}) custom-call(s32[4]{0:T(128)S(1)} %pad_add_fusion.refs_0_.at, bf16[32,3968]{1,0:T(8,128)(2,1)S(1)} %pair.1.refs_1_.refs_0_, bf16[3584,2048]{1,0:T(8,128)(2,1)} %refs_3_.5, bf16[3584,2048]{1,0:T(8,128)(2,1)} %refs_3_.5), custom_call_target="tpu_custom_call" | custom-call | bytes 29360128 | tf_op jit(solution)/shard_map/fetch/pallas_call | solution.py:102
  54.6 1.3 %collective-permute-done.11.refs_1_ = bf16[32,3968]{1,0:T(8,128)(2,1)S(1)} collective-permute-done((bf16[32,3968]{1,0:T(8,128)(2,1)S(1)}, bf16[32,3968]{1,0:T(8,128)(2,1)S(1)}, u32[]{:S(2)}, u32[]{:S(2)}) %collective-permute-start.11) | collective-permute-done | bytes 253984 | tf_op jit(solution)/shard_map/ppermute | solution.py:606
  55.9 0.1 gated.1.hidden
  56.1 0.1 collective-permute-start.12
  56.1 1.4 %contract.1.refs_3_ = f32[32,2048]{1,0:T(8,128)S(1)} custom-call(bf16[32,1792]{1,0:T(8,128)(2,1)S(1)} %gated.1.hidden, bf16[1792,2048]{1,0:T(8,128)(2,1)S(1)} %get-tuple-element.56.w), custom_call_target="tpu_custom_call" | custom-call | flops 234881024 | bytes 7340032 | tf_op jit(solution)/shard_map/contract/pallas_call | solution.py:536
  57.5 0.0 collective-permute-done.12.refs_1_
  57.5 1.9 %contract_last.1 = (f32[8,2048]{1,0:T(8,128)S(1)}, bf16[8,2048]{1,0:T(8,128)(2,1)S(1)}, bf16[8,2048]{1,0:T(8,128)(2,1)S(1)}, bf16[8,2048]{1,0:T(8,128)(2,1)S(1)}) custom-call(s32[4]{0:T(128)S(1)} %pad_add_fusion.refs_0_.at, bf16[32,1792]{1,0:T(8,128)(2,1)S(1)} %collective-permute-done.12.refs_1_, bf16[1792,2048]{1,0:T(8,128)(2,1)S(1)} %get-tuple-element.55.refs_2_, ...), custom_call_target="tpu_custom_call" | custom-call | flops 234881024 | bytes 7340032 | tf_op jit(solution)/shard_map/contract_last/pallas_call | solution.py:573
  59.4 2.8 %collective-permute-start.13 = (bf16[8,2048]{1,0:T(8,128)(2,1)S(1)}, bf16[8,2048]{1,0:T(8,128)(2,1)S(1)}, u32[]{:S(2)}, u32[]{:S(2)}) collective-permute-start(bf16[8,2048]{1,0:T(8,128)(2,1)S(1)} %get-tuple-element.60), channel_id=1, source_target_pairs={{0,3},{1,2},{2,1},{3,0},{4,7},{5,6},{6,5},{7,4},{8,11},{9,10},{10,... | collective-permute-start | bytes 98312 | tf_op jit(solution)/shard_map/ppermute | solution.py:606
  62.3 0.0 collective-permute-start.14
  62.3 1.6 %collective-permute-start.15 = (bf16[8,2048]{1,0:T(8,128)(2,1)S(1)}, bf16[8,2048]{1,0:T(8,128)(2,1)S(1)}, u32[]{:S(2)}, u32[]{:S(2)}) collective-permute-start(bf16[8,2048]{1,0:T(8,128)(2,1)S(1)} %get-tuple-element.62), channel_id=1, source_target_pairs={{0,1},{1,0},{2,3},{3,2},{4,5},{5,4},{6,7},{7,6},{8,9},{9,8},{10,11... | collective-permute-start | bytes 98312 | tf_op jit(solution)/shard_map/ppermute | solution.py:606
  63.9 1.6 %collective-permute-done.13 = bf16[8,2048]{1,0:T(8,128)(2,1)S(1)} collective-permute-done((bf16[8,2048]{1,0:T(8,128)(2,1)S(1)}, bf16[8,2048]{1,0:T(8,128)(2,1)S(1)}, u32[]{:S(2)}, u32[]{:S(2)}) %collective-permute-start.13) | collective-permute-done | bytes 32800 | tf_op jit(solution)/shard_map/ppermute | solution.py:606
  65.5 1.6 %collective-permute-done.14 = bf16[8,2048]{1,0:T(8,128)(2,1)S(1)} collective-permute-done((bf16[8,2048]{1,0:T(8,128)(2,1)S(1)}, bf16[8,2048]{1,0:T(8,128)(2,1)S(1)}, u32[]{:S(2)}, u32[]{:S(2)}) %collective-permute-start.14) | collective-permute-done | bytes 32800 | tf_op jit(solution)/shard_map/ppermute | solution.py:606
  67.1 0.0 collective-permute-done.15
  67.1 0.6 add_convert_fusion
  (5 shorter events, 0.1 us)
Async XLA Ops:
  0.0 8.3 %copy-start.1 = (s32[8]{0:T(128)S(1)}, s32[8]{0:T(128)}, u32[]{:S(2)}) copy-start(s32[8]{0:T(128)} %param.24) | copy-start | bytes 100
  0.0 8.6 %copy-start.2 = (s32[8]{0:T(128)S(1)}, s32[8]{0:T(128)}, u32[]{:S(2)}) copy-start(s32[8]{0:T(128)} %param.25) | copy-start | bytes 100
  5.2 9.0 %collective-permute-start.1 = (bf16[32,2560]{1,0:T(8,128)(2,1)S(1)}, bf16[32,2560]{1,0:T(8,128)(2,1)S(1)}, u32[]{:S(2)}, u32[]{:S(2)}) collective-permute-start(bf16[32,2560]{1,0:T(8,128)(2,1)S(1)} %get-tuple-element.35.refs_1_.refs_5_), channel_id=1, source_target_pairs={{0,4},{4,0},{8,12},{12,8},{1,5},{5,1},{9,13},{13,9},{2,6},{6,2},{1... | collective-permute-start | bytes 491528 | tf_op jit(solution)/shard_map/ppermute | solution.py:606
  5.7 8.2 %collective-permute-start = (bf16[32,2560]{1,0:T(8,128)(2,1)S(1)}, bf16[32,2560]{1,0:T(8,128)(2,1)S(1)}, u32[]{:S(2)}, u32[]{:S(2)}) collective-permute-start(bf16[32,2560]{1,0:T(8,128)(2,1)S(1)} %get-tuple-element.35.refs_1_.refs_5_), channel_id=1, source_target_pairs={{0,8},{4,12},{8,0},{12,4},{1,9},{5,13},{9,1},{13,5},{2,10},{6,14},... | collective-permute-start | bytes 491528 | tf_op jit(solution)/shard_map/ppermute | solution.py:606
  14.0 1.5 %collective-permute-start.2 = (bf16[32,2560]{1,0:T(8,128)(2,1)S(1)}, bf16[32,2560]{1,0:T(8,128)(2,1)S(1)}, u32[]{:S(2)}, u32[]{:S(2)}) collective-permute-start(bf16[32,2560]{1,0:T(8,128)(2,1)S(1)} %hold.2.refs_6_), channel_id=1, source_target_pairs={{0,4},{4,0},{8,12},{12,8},{1,5},{5,1},{9,13},{13,9},{2,6},{6,2},{1... | collective-permute-start | bytes 491528 | tf_op jit(solution)/shard_map/ppermute | solution.py:606
  19.5 6.2 %collective-permute-start.3 = (bf16[32,2432]{1,0:T(8,128)(2,1)S(1)}, bf16[32,2432]{1,0:T(8,128)(2,1)S(1)}, u32[]{:S(2)}, u32[]{:S(2)}) collective-permute-start(bf16[32,2432]{1,0:T(8,128)(2,1)S(1)} %get-tuple-element.39.refs_1_), channel_id=1, source_target_pairs={{0,8},{4,12},{8,0},{12,4},{1,9},{5,13},{9,1},{13,5},{2,10},{6,14},... | collective-permute-start | bytes 466952 | tf_op jit(solution)/shard_map/ppermute | solution.py:606
  20.4 5.5 %collective-permute-start.4 = (bf16[32,2432]{1,0:T(8,128)(2,1)S(1)}, bf16[32,2432]{1,0:T(8,128)(2,1)S(1)}, u32[]{:S(2)}, u32[]{:S(2)}) collective-permute-start(bf16[32,2432]{1,0:T(8,128)(2,1)S(1)} %get-tuple-element.39.refs_1_), channel_id=1, source_target_pairs={{0,4},{4,0},{8,12},{12,8},{1,5},{5,1},{9,13},{13,9},{2,6},{6,2},{1... | collective-permute-start | bytes 466952 | tf_op jit(solution)/shard_map/ppermute | solution.py:606
  25.7 1.4 %collective-permute-start.5 = (bf16[32,2432]{1,0:T(8,128)(2,1)S(1)}, bf16[32,2432]{1,0:T(8,128)(2,1)S(1)}, u32[]{:S(2)}, u32[]{:S(2)}) collective-permute-start(bf16[32,2432]{1,0:T(8,128)(2,1)S(1)} %hold.3.refs_2_), channel_id=1, source_target_pairs={{0,4},{4,0},{8,12},{12,8},{1,5},{5,1},{9,13},{13,9},{2,6},{6,2},{1... | collective-permute-start | bytes 466952 | tf_op jit(solution)/shard_map/ppermute | solution.py:606
  28.0 5.0 %collective-permute-start.6 = (bf16[32,1024]{1,0:T(8,128)(2,1)S(1)}, bf16[32,1024]{1,0:T(8,128)(2,1)S(1)}, u32[]{:S(2)}, u32[]{:S(2)}) collective-permute-start(bf16[32,1024]{1,0:T(8,128)(2,1)S(1)} %get-tuple-element.43.one), channel_id=1, source_target_pairs={{0,1},{1,0},{2,3},{3,2},{4,5},{5,4},{6,7},{7,6},{8,9},{9,8},{10,11... | collective-permute-start | bytes 196616 | tf_op jit(solution)/shard_map/ppermute | solution.py:606
  30.4 7.7 %collective-permute-start.8 = (bf16[32,1024]{1,0:T(8,128)(2,1)S(1)}, bf16[32,1024]{1,0:T(8,128)(2,1)S(1)}, u32[]{:S(2)}, u32[]{:S(2)}) collective-permute-start(bf16[32,1024]{1,0:T(8,128)(2,1)S(1)} %output_second.1.one), channel_id=1, source_target_pairs={{0,2},{1,3},{2,0},{3,1},{4,6},{5,7},{6,4},{7,5},{8,10},{9,11},{10,... | collective-permute-start | bytes 196616 | tf_op jit(solution)/shard_map/ppermute | solution.py:606
  33.1 6.5 %copy-start = (bf16[2048]{0:T(1024)(128)(2,1)S(1)}, bf16[2048]{0:T(1024)(128)(2,1)}, u32[]{:S(2)}) copy-start(bf16[2048]{0:T(1024)(128)(2,1)} %param.15) | copy-start | bytes 12292
  33.1 6.4 %collective-permute-start.7 = (bf16[32,1024]{1,0:T(8,128)(2,1)S(1)}, bf16[32,1024]{1,0:T(8,128)(2,1)S(1)}, u32[]{:S(2)}, u32[]{:S(2)}) collective-permute-start(bf16[32,1024]{1,0:T(8,128)(2,1)S(1)} %add.41.refs_6_.refs_1_), channel_id=1, source_target_pairs={{0,2},{1,3},{2,0},{3,1},{4,6},{5,7},{6,4},{7,5},{8,10},{9,11},{10,... | collective-permute-start | bytes 196616 | tf_op jit(solution)/shard_map/ppermute | solution.py:606
  38.2 5.1 %collective-permute-start.9 = (bf16[32,1024]{1,0:T(8,128)(2,1)S(1)}, bf16[32,1024]{1,0:T(8,128)(2,1)S(1)}, u32[]{:S(2)}, u32[]{:S(2)}) collective-permute-start(bf16[32,1024]{1,0:T(8,128)(2,1)S(1)} %add.42.refs_8_), channel_id=1, source_target_pairs={{0,1},{1,0},{2,3},{3,2},{4,5},{5,4},{6,7},{7,6},{8,9},{9,8},{10,11... | collective-permute-start | bytes 196616 | tf_op jit(solution)/shard_map/ppermute | solution.py:606
  45.3 2.0 %collective-permute-start.10 = (bf16[32,3968]{1,0:T(8,128)(2,1)S(1)}, bf16[32,3968]{1,0:T(8,128)(2,1)S(1)}, u32[]{:S(2)}, u32[]{:S(2)}) collective-permute-start(bf16[32,3968]{1,0:T(8,128)(2,1)S(1)} %get-tuple-element.53.stats), channel_id=1, source_target_pairs={{0,4},{4,0},{8,12},{12,8},{1,5},{5,1},{9,13},{13,9},{2,6},{6,2},{1... | collective-permute-start | bytes 761864 | tf_op jit(solution)/shard_map/ppermute | solution.py:606
  47.3 8.6 %collective-permute-start.11 = (bf16[32,3968]{1,0:T(8,128)(2,1)S(1)}, bf16[32,3968]{1,0:T(8,128)(2,1)S(1)}, u32[]{:S(2)}, u32[]{:S(2)}) collective-permute-start(bf16[32,3968]{1,0:T(8,128)(2,1)S(1)} %pair.1.refs_1_.refs_0_), channel_id=1, source_target_pairs={{0,8},{4,12},{8,0},{12,4},{1,9},{5,13},{9,1},{13,5},{2,10},{6,14},... | collective-permute-start | bytes 761864 | tf_op jit(solution)/shard_map/ppermute | solution.py:606
  56.1 1.4 %collective-permute-start.12 = (bf16[32,1792]{1,0:T(8,128)(2,1)S(1)}, bf16[32,1792]{1,0:T(8,128)(2,1)S(1)}, u32[]{:S(2)}, u32[]{:S(2)}) collective-permute-start(bf16[32,1792]{1,0:T(8,128)(2,1)S(1)} %gated.1.hidden), channel_id=1, source_target_pairs={{0,4},{4,0},{8,12},{12,8},{1,5},{5,1},{9,13},{13,9},{2,6},{6,2},{1... | collective-permute-start | bytes 344072 | tf_op jit(solution)/shard_map/ppermute | solution.py:606
  59.4 6.1 %collective-permute-start.13 = (bf16[8,2048]{1,0:T(8,128)(2,1)S(1)}, bf16[8,2048]{1,0:T(8,128)(2,1)S(1)}, u32[]{:S(2)}, u32[]{:S(2)}) collective-permute-start(bf16[8,2048]{1,0:T(8,128)(2,1)S(1)} %get-tuple-element.60), channel_id=1, source_target_pairs={{0,3},{1,2},{2,1},{3,0},{4,7},{5,6},{6,5},{7,4},{8,11},{9,10},{10,... | collective-permute-start | bytes 98312 | tf_op jit(solution)/shard_map/ppermute | solution.py:606
  62.3 4.8 %collective-permute-start.14 = (bf16[8,2048]{1,0:T(8,128)(2,1)S(1)}, bf16[8,2048]{1,0:T(8,128)(2,1)S(1)}, u32[]{:S(2)}, u32[]{:S(2)}) collective-permute-start(bf16[8,2048]{1,0:T(8,128)(2,1)S(1)} %get-tuple-element.61), channel_id=1, source_target_pairs={{0,2},{1,3},{2,0},{3,1},{4,6},{5,7},{6,4},{7,5},{8,10},{9,11},{10,... | collective-permute-start | bytes 98312 | tf_op jit(solution)/shard_map/ppermute | solution.py:606
  62.3 4.8 %collective-permute-start.15 = (bf16[8,2048]{1,0:T(8,128)(2,1)S(1)}, bf16[8,2048]{1,0:T(8,128)(2,1)S(1)}, u32[]{:S(2)}, u32[]{:S(2)}) collective-permute-start(bf16[8,2048]{1,0:T(8,128)(2,1)S(1)} %get-tuple-element.62), channel_id=1, source_target_pairs={{0,1},{1,0},{2,3},{3,2},{4,5},{5,4},{6,7},{7,6},{8,9},{9,8},{10,11... | collective-permute-start | bytes 98312 | tf_op jit(solution)/shard_map/ppermute | solution.py:606

commit v14 on v13

--- a/solution.py
+++ b/solution.py
@@ -660,9 +660,9 @@
     up_0, gate_1, token = fetch(at, value, Part(w_up, 0, half), Part(w_gate, half, quarter))
     out_0, attended = output_first(gathered(value, "wide", token), w_out)
     out_1 = output_second(attended, w_out)
-    parts_0 = summed(out_0, "head", 1)
+    parts_0 = summed(out_0, "head", -1)
     gate_2, token = fetch(at, parts_0[0], Part(w_gate, half + quarter, quarter))
-    parts_1 = summed(out_1, "head", -1, token)
+    parts_1 = summed(out_1, "head", 1, token)
     send, keep, resid_0, squares, up_1 = expand_first(
         at, own, gain, parts_0, gate_0, up_0, Part(w_up, half, half)
     )

time: 67.9 us -> 69.4 us (1.022)
  starting transfers between devices: 18.1 us -> 18.9 us
    ppermute x16, starting transfers between devices: 18.1 us -> 18.9 us  [swap(): return lax.ppermute(x, axis, [(i, i ^ bit) for i in range(n)])]
  transfers between devices with their start and end apart: 16 -> 16, of which waited for: 7 -> 7; matrix products, arithmetic and copies ran while one was open for 1% -> 1% of each run, Pallas kernels for 39% -> 38%
where the time goes in v14:
time: 69.4 us; the launch traced here: 69.3 us
  Pallas kernels  40.9 us (59%)
  starting transfers between devices  18.9 us (27%)
  waiting for transfers between devices  8.07 us (12%)
  other arithmetic  1.02 us (1%)
    ppermute x16, starting transfers between devices, swap(): return lax.ppermute(x, axis, [(i, i ^ bit) for i in range(n)])  18.9 us
    pallas_call x4, Pallas kernels, fetch(): pl.pallas_call(lambda *refs: fetch_kernel(wanted, len(after), *refs), in_...  18.7 us
    ppermute x16, waiting for transfers between devices, swap(): return lax.ppermute(x, axis, [(i, i ^ bit) for i in range(n)])  8.07 us
    pallas_call x1, Pallas kernels, project(): pl.pallas_call(lambda *refs: project_kernel(chunks, *refs), in_specs=[SME...  5.11 us
    pallas_call x1, Pallas kernels, attend(): pl.pallas_call(lambda *refs: attend_kernel(len(parts), part, *refs), in_s...  4.09 us
    pallas_call x1, Pallas kernels, expand_first(): pl.pallas_call(lambda *refs: expand_first_kernel(len(parts), part, *refs)...  3.79 us
    pallas_call x1, Pallas kernels, contract_last(): pl.pallas_call(lambda *refs: contract_last_kernel(n, *refs), in_specs=[SM...  1.94 us
    pallas_call x1, Pallas kernels, expand_send(): pl.pallas_call(lambda *refs: expand_send_kernel(len(parts), len(wg), *ref...  1.91 us
  transfers between devices with their start and end apart: 16, of which 7 were waited for; matrix products, arithmetic and copies ran while one was open for 1% of the time, Pallas kernels for 38%

profile of v14, /device:TPU:0, one launch (start us, length us, event | category | flops | bytes accessed | tf_op | source)
XLA Modules:
  0.0 69.3 jit_solution(5003301041943399651)
XLA Ops:
  0.0 0.0 copy-start.1
  0.0 0.0 copy-start.2
  0.0 0.1 pad_add_fusion.refs_0_.at
  0.1 5.1 %project.1 = (bf16[32,2560]{1,0:T(8,128)(2,1)S(1)}, bf16[32,2048]{1,0:T(8,128)(2,1)S(1)}) custom-call(s32[4]{0:T(128)S(1)} %pad_add_fusion.refs_0_.at, bf16[32,8192]{1,0:T(8,128)(2,1)} %refs_1_.1, bf16[64,128]{1,0:T(8,128)(2,1)} %bitcast.12, bf16[2048,2048]{1,0:T(8,128)(2,1)} %refs_3_.3, bf16[2048,256]{1,0:T(8,128)(2,1)} %refs_4_.2, bf16[2048,256]{1,0:T(8,128)(2,1)} %refs_5_.2), custom_call_target="tpu_custom_call" | custom-call | flops 335544320 | bytes 10485760 | tf_op jit(solution)/shard_map/project/pallas_call | solution.py:186
  5.2 0.5 collective-permute-start.1
  5.7 2.6 %collective-permute-start = (bf16[32,2560]{1,0:T(8,128)(2,1)S(1)}, bf16[32,2560]{1,0:T(8,128)(2,1)S(1)}, u32[]{:S(2)}, u32[]{:S(2)}) collective-permute-start(bf16[32,2560]{1,0:T(8,128)(2,1)S(1)} %get-tuple-element.35.refs_1_.refs_5_), channel_id=1, source_target_pairs={{0,8},{4,12},{8,0},{12,4},{1,9},{5,13},{9,1},{13,5},{2,10},{6,14},... | collective-permute-start | bytes 491528 | tf_op jit(solution)/shard_map/ppermute | solution.py:606
  8.3 0.0 copy-done.1
  8.3 0.1 add_convert_fusion.1
  8.4 0.1 convert_element_type.24
  8.5 0.1 fusion
  8.6 0.0 copy-done.2
  8.6 0.1 concatenate.10.refs_2_.refs_0_
  8.7 0.1 pad_maximum_fusion
  8.8 5.1 %fetch.4 = (bf16[16,512,256]{2,1,0:T(8,128)(2,1)S(1)}, bf16[1024,3584]{1,0:T(8,128)(2,1)S(1)}, f32[8,128]{1,0:T(8,128)S(1)}) custom-call(s32[4]{0:T(128)S(1)} %pad_add_fusion.refs_0_.at, bf16[32,2560]{1,0:T(8,128)(2,1)S(1)} %get-tuple-element.35.refs_1_.refs_5_, s32[20]{0:T(128)S(1)} %concatenate.10.refs_2_.refs_0_, ...), custom_call_target="tpu_custom_call" | custom-call | bytes 23068672 | tf_op jit(solution)/shard_map/fetch/pallas_call | solution.py:102
  13.9 0.0 collective-permute-done.__0_
  14.0 0.2 collective-permute-start.2
  14.2 0.0 collective-permute-done.1.refs_7_
  14.2 1.2 %collective-permute-done.2.refs_8_ = bf16[32,2560]{1,0:T(8,128)(2,1)S(1)} collective-permute-done((bf16[32,2560]{1,0:T(8,128)(2,1)S(1)}, bf16[32,2560]{1,0:T(8,128)(2,1)S(1)}, u32[]{:S(2)}, u32[]{:S(2)}) %collective-permute-start.2) | collective-permute-done | bytes 163872 | tf_op jit(solution)/shard_map/ppermute | solution.py:606
  15.4 4.1 %attend.1 = (bf16[32,2432]{1,0:T(8,128)(2,1)S(1)}, bf16[2048,2048]{1,0:T(8,128)(2,1)S(1)}) custom-call(s32[20]{0:T(128)S(1)} %concatenate.10.refs_2_.refs_0_, f32[32,128]{1,0:T(8,128)S(1)} %get-tuple-element.66.refs_3_.refs_1_, f32[32,128]{1,0:T(8,128)S(1)} %get-tuple-element.67.refs_4_.refs_2_, bf16[2,8,512,256]{3,2,1,0:T(8,128)(2,1)S(1)} %bitcast.8, ...), custom_call_target="tpu_custom_call" | custom-call | flops 134217728 | bytes 4194304 | tf_op jit(solution)/shard_map/attend/pallas_call | solution.py:305
  19.5 0.9 %collective-permute-start.3 = (bf16[32,2432]{1,0:T(8,128)(2,1)S(1)}, bf16[32,2432]{1,0:T(8,128)(2,1)S(1)}, u32[]{:S(2)}, u32[]{:S(2)}) collective-permute-start(bf16[32,2432]{1,0:T(8,128)(2,1)S(1)} %get-tuple-element.39.refs_1_), channel_id=1, source_target_pairs={{0,8},{4,12},{8,0},{12,4},{1,9},{5,13},{9,1},{13,5},{2,10},{6,14},... | collective-permute-start | bytes 466952 | tf_op jit(solution)/shard_map/ppermute | solution.py:606
  20.4 0.0 collective-permute-start.4
  20.4 4.9 %fetch.5 = (bf16[1024,3584]{1,0:T(8,128)(2,1)S(1)}, bf16[512,3584]{1,0:T(8,128)(2,1)S(1)}, f32[8,128]{1,0:T(8,128)S(1)}) custom-call(s32[4]{0:T(128)S(1)} %pad_add_fusion.refs_0_.at, bf16[32,2432]{1,0:T(8,128)(2,1)S(1)} %get-tuple-element.39.refs_1_, bf16[2048,3584]{1,0:T(8,128)(2,1)} %refs_5_.3, bf16[2048,3584]{1,0:T(8,128)(2,1)} %refs_2_.4), custom_call_target="tpu_custom_call" | custom-call | bytes 22020096 | tf_op jit(solution)/shard_map/fetch/pallas_call | solution.py:102
  25.4 0.3 collective-permute-done.3.__0_
  25.7 0.3 collective-permute-start.5
  25.9 0.0 collective-permute-done.4.refs_3_
  26.0 1.1 %collective-permute-done.5.refs_4_ = bf16[32,2432]{1,0:T(8,128)(2,1)S(1)} collective-permute-done((bf16[32,2432]{1,0:T(8,128)(2,1)S(1)}, bf16[32,2432]{1,0:T(8,128)(2,1)S(1)}, u32[]{:S(2)}, u32[]{:S(2)}) %collective-permute-start.5) | collective-permute-done | bytes 155680 | tf_op jit(solution)/shard_map/ppermute | solution.py:606
  27.1 1.0 %output_first.1 = (bf16[32,1024]{1,0:T(8,128)(2,1)S(1)}, bf16[32,2048]{1,0:T(8,128)(2,1)S(1)}) custom-call(bf16[2048,2048]{1,0:T(8,128)(2,1)S(1)} %get-tuple-element.41.refs_0_.w, bf16[32,2432]{1,0:T(8,128)(2,1)S(1)} %get-tuple-element.39.refs_1_, bf16[32,2432]{1,0:T(8,128)(2,1)S(1)} %hold.3.refs_2_, bf16[32,2432]{1,0:T(8,128)(2,1)S(1)} %collective-permute-done.4.refs_3_, ...), custom_call_target="tpu_custom_call" | custom-call | flops 268435456 | bytes 8388608 | tf_op jit(solution)/shard_map/output_first/pallas_call | solution.py:352
  28.0 2.6 %collective-permute-start.6 = (bf16[32,1024]{1,0:T(8,128)(2,1)S(1)}, bf16[32,1024]{1,0:T(8,128)(2,1)S(1)}, u32[]{:S(2)}, u32[]{:S(2)}) collective-permute-start(bf16[32,1024]{1,0:T(8,128)(2,1)S(1)} %get-tuple-element.43.one), channel_id=1, source_target_pairs={{0,2},{1,3},{2,0},{3,1},{4,6},{5,7},{6,4},{7,5},{8,10},{9,11},{10,... | collective-permute-start | bytes 196616 | tf_op jit(solution)/shard_map/ppermute | solution.py:606
  30.6 0.8 %output_second.1.one = bf16[32,1024]{1,0:T(8,128)(2,1)S(1)} custom-call(bf16[32,2048]{1,0:T(8,128)(2,1)S(1)} %get-tuple-element.49.x, bf16[2048,2048]{1,0:T(8,128)(2,1)S(1)} %get-tuple-element.41.refs_0_.w), custom_call_target="tpu_custom_call" | custom-call | flops 268435456 | bytes 8388608 | tf_op jit(solution)/shard_map/output_second/pallas_call | solution.py:368
  31.5 1.6 %collective-permute-start.8 = (bf16[32,1024]{1,0:T(8,128)(2,1)S(1)}, bf16[32,1024]{1,0:T(8,128)(2,1)S(1)}, u32[]{:S(2)}, u32[]{:S(2)}) collective-permute-start(bf16[32,1024]{1,0:T(8,128)(2,1)S(1)} %output_second.1.one), channel_id=1, source_target_pairs={{0,1},{1,0},{2,3},{3,2},{4,5},{5,4},{6,7},{7,6},{8,9},{9,8},{10,11... | collective-permute-start | bytes 196616 | tf_op jit(solution)/shard_map/ppermute | solution.py:606
  33.0 1.5 %collective-permute-done.6.two = bf16[32,1024]{1,0:T(8,128)(2,1)S(1)} collective-permute-done((bf16[32,1024]{1,0:T(8,128)(2,1)S(1)}, bf16[32,1024]{1,0:T(8,128)(2,1)S(1)}, u32[]{:S(2)}, u32[]{:S(2)}) %collective-permute-start.6) | collective-permute-done | bytes 65568 | tf_op jit(solution)/shard_map/ppermute | solution.py:606
  34.5 0.0 copy-start
  34.6 0.9 %collective-permute-start.7 = (bf16[32,1024]{1,0:T(8,128)(2,1)S(1)}, bf16[32,1024]{1,0:T(8,128)(2,1)S(1)}, u32[]{:S(2)}, u32[]{:S(2)}) collective-permute-start(bf16[32,1024]{1,0:T(8,128)(2,1)S(1)} %add.41.refs_6_.refs_1_), channel_id=1, source_target_pairs={{0,1},{1,0},{2,3},{3,2},{4,5},{5,4},{6,7},{7,6},{8,9},{9,8},{10,11... | collective-permute-start | bytes 196616 | tf_op jit(solution)/shard_map/ppermute | solution.py:606
  35.4 2.7 %fetch.6 = (bf16[512,3584]{1,0:T(8,128)(2,1)S(1)}, f32[8,128]{1,0:T(8,128)S(1)}) custom-call(s32[4]{0:T(128)S(1)} %pad_add_fusion.refs_0_.at, bf16[32,1024]{1,0:T(8,128)(2,1)S(1)} %add.41.refs_6_.refs_1_, bf16[2048,3584]{1,0:T(8,128)(2,1)} %refs_2_.4), custom_call_target="tpu_custom_call" | custom-call | bytes 7340032 | tf_op jit(solution)/shard_map/fetch/pallas_call | solution.py:102
  38.1 0.0 collective-permute-done.8.two
  38.2 3.5 %collective-permute-start.9 = (bf16[32,1024]{1,0:T(8,128)(2,1)S(1)}, bf16[32,1024]{1,0:T(8,128)(2,1)S(1)}, u32[]{:S(2)}, u32[]{:S(2)}) collective-permute-start(bf16[32,1024]{1,0:T(8,128)(2,1)S(1)} %add.42.refs_8_), channel_id=1, source_target_pairs={{0,2},{1,3},{2,0},{3,1},{4,6},{5,7},{6,4},{7,5},{8,10},{9,11},{10,... | collective-permute-start | bytes 196616 | tf_op jit(solution)/shard_map/ppermute | solution.py:606
  41.7 0.0 collective-permute-done.7.refs_7_
  41.7 0.0 copy-done
  41.7 3.8 %expand_first.1 = (f32[32,3584]{1,0:T(8,128)S(1)}, f32[32,3584]{1,0:T(8,128)S(1)}, f32[32,1024]{1,0:T(8,128)S(1)}, f32[32,128]{1,0:T(8,128)S(1)}, bf16[1024,3584]{1,0:T(8,128)(2,1)S(1)}) custom-call(s32[4]{0:T(128)S(1)} %pad_add_fusion.refs_0_.at, bf16[32,2048]{1,0:T(8,128)(2,1)S(1)} %get-tuple-element.34.refs_1_, bf16[16,128]{1,0:T(8,128)(2,1)S(1)} %bitcast.9, ...), custom_call_target="tpu_custom_call" | custom-call | flops 469762048 | bytes 14680064 | tf_op jit(solution)/shard_map/expand_first/pallas_call | solution.py:422
  45.5 0.0 collective-permute-done.9.refs_9_
  45.5 1.9 %expand_send.1 = (bf16[32,3968]{1,0:T(8,128)(2,1)S(1)}, f32[32,1024]{1,0:T(8,128)S(1)}, bf16[32,1024]{1,0:T(8,128)(2,1)S(1)}) custom-call(s32[4]{0:T(128)S(1)} %pad_add_fusion.refs_0_.at, bf16[32,2048]{1,0:T(8,128)(2,1)S(1)} %get-tuple-element.34.refs_1_, bf16[16,128]{1,0:T(8,128)(2,1)S(1)} %bitcast.10, f32[32,3584]{1,0:T(8,128)S(1)} %get-tuple-element.44.refs_3_, ...), custom_call_target="tpu_custom_call" | custom-call | flops 234881024 | bytes 7340032 | tf_op jit(solution)/shard_map/expand_send/pallas_call | solution.py:456
  47.4 0.1 collective-permute-start.10
  47.4 1.9 %expand_keep.1.keep = bf16[32,3584]{1,0:T(8,128)(2,1)S(1)} custom-call(s32[4]{0:T(128)S(1)} %pad_add_fusion.refs_0_.at, bf16[32,1024]{1,0:T(8,128)(2,1)S(1)} %get-tuple-element.51.x, f32[32,3584]{1,0:T(8,128)S(1)} %get-tuple-element.52.before, bf16[512,3584]{1,0:T(8,128)(2,1)S(1)} %get-tuple-element.46.refs_5_.refs_0_, ...), custom_call_target="tpu_custom_call" | custom-call | flops 234881024 | bytes 7340032 | tf_op jit(solution)/shard_map/expand_keep/pallas_call | solution.py:474
  49.4 0.0 collective-permute-done.10.received
  49.4 0.1 pair.1.refs_1_.refs_0_
  49.4 1.3 %collective-permute-start.11 = (bf16[32,3968]{1,0:T(8,128)(2,1)S(1)}, bf16[32,3968]{1,0:T(8,128)(2,1)S(1)}, u32[]{:S(2)}, u32[]{:S(2)}) collective-permute-start(bf16[32,3968]{1,0:T(8,128)(2,1)S(1)} %pair.1.refs_1_.refs_0_), channel_id=1, source_target_pairs={{0,8},{4,12},{8,0},{12,4},{1,9},{5,13},{9,1},{13,5},{2,10},{6,14},... | collective-permute-start | bytes 761864 | tf_op jit(solution)/shard_map/ppermute | solution.py:606
  50.7 6.0 %fetch.7 = (bf16[1792,2048]{1,0:T(8,128)(2,1)S(1)}, bf16[1792,2048]{1,0:T(8,128)(2,1)S(1)}, f32[8,128]{1,0:T(8,128)S(1)}) custom-call(s32[4]{0:T(128)S(1)} %pad_add_fusion.refs_0_.at, bf16[32,3968]{1,0:T(8,128)(2,1)S(1)} %pair.1.refs_1_.refs_0_, bf16[3584,2048]{1,0:T(8,128)(2,1)} %refs_3_.5, bf16[3584,2048]{1,0:T(8,128)(2,1)} %refs_3_.5), custom_call_target="tpu_custom_call" | custom-call | bytes 29360128 | tf_op jit(solution)/shard_map/fetch/pallas_call | solution.py:102
  56.7 1.3 %collective-permute-done.11.refs_1_ = bf16[32,3968]{1,0:T(8,128)(2,1)S(1)} collective-permute-done((bf16[32,3968]{1,0:T(8,128)(2,1)S(1)}, bf16[32,3968]{1,0:T(8,128)(2,1)S(1)}, u32[]{:S(2)}, u32[]{:S(2)}) %collective-permute-start.11) | collective-permute-done | bytes 253984 | tf_op jit(solution)/shard_map/ppermute | solution.py:606
  58.0 0.1 gated.1.hidden
  58.2 0.1 collective-permute-start.12
  58.3 1.4 %contract.1.refs_3_ = f32[32,2048]{1,0:T(8,128)S(1)} custom-call(bf16[32,1792]{1,0:T(8,128)(2,1)S(1)} %gated.1.hidden, bf16[1792,2048]{1,0:T(8,128)(2,1)S(1)} %get-tuple-element.56.w), custom_call_target="tpu_custom_call" | custom-call | flops 234881024 | bytes 7340032 | tf_op jit(solution)/shard_map/contract/pallas_call | solution.py:536
  59.6 0.0 collective-permute-done.12.refs_1_
  59.6 1.9 %contract_last.1 = (f32[8,2048]{1,0:T(8,128)S(1)}, bf16[8,2048]{1,0:T(8,128)(2,1)S(1)}, bf16[8,2048]{1,0:T(8,128)(2,1)S(1)}, bf16[8,2048]{1,0:T(8,128)(2,1)S(1)}) custom-call(s32[4]{0:T(128)S(1)} %pad_add_fusion.refs_0_.at, bf16[32,1792]{1,0:T(8,128)(2,1)S(1)} %collective-permute-done.12.refs_1_, bf16[1792,2048]{1,0:T(8,128)(2,1)S(1)} %get-tuple-element.55.refs_2_, ...), custom_call_target="tpu_custom_call" | custom-call | flops 234881024 | bytes 7340032 | tf_op jit(solution)/shard_map/contract_last/pallas_call | solution.py:573
  61.6 1.6 %collective-permute-start.13 = (bf16[8,2048]{1,0:T(8,128)(2,1)S(1)}, bf16[8,2048]{1,0:T(8,128)(2,1)S(1)}, u32[]{:S(2)}, u32[]{:S(2)}) collective-permute-start(bf16[8,2048]{1,0:T(8,128)(2,1)S(1)} %get-tuple-element.60), channel_id=1, source_target_pairs={{0,3},{1,2},{2,1},{3,0},{4,7},{5,6},{6,5},{7,4},{8,11},{9,10},{10,... | collective-permute-start | bytes 98312 | tf_op jit(solution)/shard_map/ppermute | solution.py:606
  63.1 0.0 collective-permute-start.14
  63.1 2.9 %collective-permute-start.15 = (bf16[8,2048]{1,0:T(8,128)(2,1)S(1)}, bf16[8,2048]{1,0:T(8,128)(2,1)S(1)}, u32[]{:S(2)}, u32[]{:S(2)}) collective-permute-start(bf16[8,2048]{1,0:T(8,128)(2,1)S(1)} %get-tuple-element.62), channel_id=1, source_target_pairs={{0,1},{1,0},{2,3},{3,2},{4,5},{5,4},{6,7},{7,6},{8,9},{9,8},{10,11... | collective-permute-start | bytes 98312 | tf_op jit(solution)/shard_map/ppermute | solution.py:606
  66.0 1.6 %collective-permute-done.13 = bf16[8,2048]{1,0:T(8,128)(2,1)S(1)} collective-permute-done((bf16[8,2048]{1,0:T(8,128)(2,1)S(1)}, bf16[8,2048]{1,0:T(8,128)(2,1)S(1)}, u32[]{:S(2)}, u32[]{:S(2)}) %collective-permute-start.13) | collective-permute-done | bytes 32800 | tf_op jit(solution)/shard_map/ppermute | solution.py:606
  67.7 1.0 %collective-permute-done.14 = bf16[8,2048]{1,0:T(8,128)(2,1)S(1)} collective-permute-done((bf16[8,2048]{1,0:T(8,128)(2,1)S(1)}, bf16[8,2048]{1,0:T(8,128)(2,1)S(1)}, u32[]{:S(2)}, u32[]{:S(2)}) %collective-permute-start.14) | collective-permute-done | bytes 32800 | tf_op jit(solution)/shard_map/ppermute | solution.py:606
  68.6 0.0 collective-permute-done.15
  68.6 0.6 add_convert_fusion
  (5 shorter events, 0.1 us)
Async XLA Ops:
  0.0 8.3 %copy-start.1 = (s32[8]{0:T(128)S(1)}, s32[8]{0:T(128)}, u32[]{:S(2)}) copy-start(s32[8]{0:T(128)} %param.24) | copy-start | bytes 100
  0.0 8.6 %copy-start.2 = (s32[8]{0:T(128)S(1)}, s32[8]{0:T(128)}, u32[]{:S(2)}) copy-start(s32[8]{0:T(128)} %param.25) | copy-start | bytes 100
  5.2 9.0 %collective-permute-start.1 = (bf16[32,2560]{1,0:T(8,128)(2,1)S(1)}, bf16[32,2560]{1,0:T(8,128)(2,1)S(1)}, u32[]{:S(2)}, u32[]{:S(2)}) collective-permute-start(bf16[32,2560]{1,0:T(8,128)(2,1)S(1)} %get-tuple-element.35.refs_1_.refs_5_), channel_id=1, source_target_pairs={{0,4},{4,0},{8,12},{12,8},{1,5},{5,1},{9,13},{13,9},{2,6},{6,2},{1... | collective-permute-start | bytes 491528 | tf_op jit(solution)/shard_map/ppermute | solution.py:606
  5.7 8.2 %collective-permute-start = (bf16[32,2560]{1,0:T(8,128)(2,1)S(1)}, bf16[32,2560]{1,0:T(8,128)(2,1)S(1)}, u32[]{:S(2)}, u32[]{:S(2)}) collective-permute-start(bf16[32,2560]{1,0:T(8,128)(2,1)S(1)} %get-tuple-element.35.refs_1_.refs_5_), channel_id=1, source_target_pairs={{0,8},{4,12},{8,0},{12,4},{1,9},{5,13},{9,1},{13,5},{2,10},{6,14},... | collective-permute-start | bytes 491528 | tf_op jit(solution)/shard_map/ppermute | solution.py:606
  14.0 1.5 %collective-permute-start.2 = (bf16[32,2560]{1,0:T(8,128)(2,1)S(1)}, bf16[32,2560]{1,0:T(8,128)(2,1)S(1)}, u32[]{:S(2)}, u32[]{:S(2)}) collective-permute-start(bf16[32,2560]{1,0:T(8,128)(2,1)S(1)} %hold.2.refs_6_), channel_id=1, source_target_pairs={{0,4},{4,0},{8,12},{12,8},{1,5},{5,1},{9,13},{13,9},{2,6},{6,2},{1... | collective-permute-start | bytes 491528 | tf_op jit(solution)/shard_map/ppermute | solution.py:606
  19.5 6.2 %collective-permute-start.3 = (bf16[32,2432]{1,0:T(8,128)(2,1)S(1)}, bf16[32,2432]{1,0:T(8,128)(2,1)S(1)}, u32[]{:S(2)}, u32[]{:S(2)}) collective-permute-start(bf16[32,2432]{1,0:T(8,128)(2,1)S(1)} %get-tuple-element.39.refs_1_), channel_id=1, source_target_pairs={{0,8},{4,12},{8,0},{12,4},{1,9},{5,13},{9,1},{13,5},{2,10},{6,14},... | collective-permute-start | bytes 466952 | tf_op jit(solution)/shard_map/ppermute | solution.py:606
  20.4 5.5 %collective-permute-start.4 = (bf16[32,2432]{1,0:T(8,128)(2,1)S(1)}, bf16[32,2432]{1,0:T(8,128)(2,1)S(1)}, u32[]{:S(2)}, u32[]{:S(2)}) collective-permute-start(bf16[32,2432]{1,0:T(8,128)(2,1)S(1)} %get-tuple-element.39.refs_1_), channel_id=1, source_target_pairs={{0,4},{4,0},{8,12},{12,8},{1,5},{5,1},{9,13},{13,9},{2,6},{6,2},{1... | collective-permute-start | bytes 466952 | tf_op jit(solution)/shard_map/ppermute | solution.py:606
  25.7 1.4 %collective-permute-start.5 = (bf16[32,2432]{1,0:T(8,128)(2,1)S(1)}, bf16[32,2432]{1,0:T(8,128)(2,1)S(1)}, u32[]{:S(2)}, u32[]{:S(2)}) collective-permute-start(bf16[32,2432]{1,0:T(8,128)(2,1)S(1)} %hold.3.refs_2_), channel_id=1, source_target_pairs={{0,4},{4,0},{8,12},{12,8},{1,5},{5,1},{9,13},{13,9},{2,6},{6,2},{1... | collective-permute-start | bytes 466952 | tf_op jit(solution)/shard_map/ppermute | solution.py:606
  28.0 6.5 %collective-permute-start.6 = (bf16[32,1024]{1,0:T(8,128)(2,1)S(1)}, bf16[32,1024]{1,0:T(8,128)(2,1)S(1)}, u32[]{:S(2)}, u32[]{:S(2)}) collective-permute-start(bf16[32,1024]{1,0:T(8,128)(2,1)S(1)} %get-tuple-element.43.one), channel_id=1, source_target_pairs={{0,2},{1,3},{2,0},{3,1},{4,6},{5,7},{6,4},{7,5},{8,10},{9,11},{10,... | collective-permute-start | bytes 196616 | tf_op jit(solution)/shard_map/ppermute | solution.py:606
  31.5 6.7 %collective-permute-start.8 = (bf16[32,1024]{1,0:T(8,128)(2,1)S(1)}, bf16[32,1024]{1,0:T(8,128)(2,1)S(1)}, u32[]{:S(2)}, u32[]{:S(2)}) collective-permute-start(bf16[32,1024]{1,0:T(8,128)(2,1)S(1)} %output_second.1.one), channel_id=1, source_target_pairs={{0,1},{1,0},{2,3},{3,2},{4,5},{5,4},{6,7},{7,6},{8,9},{9,8},{10,11... | collective-permute-start | bytes 196616 | tf_op jit(solution)/shard_map/ppermute | solution.py:606
  34.5 7.1 %copy-start = (bf16[2048]{0:T(1024)(128)(2,1)S(1)}, bf16[2048]{0:T(1024)(128)(2,1)}, u32[]{:S(2)}) copy-start(bf16[2048]{0:T(1024)(128)(2,1)} %param.15) | copy-start | bytes 12292
  34.6 7.1 %collective-permute-start.7 = (bf16[32,1024]{1,0:T(8,128)(2,1)S(1)}, bf16[32,1024]{1,0:T(8,128)(2,1)S(1)}, u32[]{:S(2)}, u32[]{:S(2)}) collective-permute-start(bf16[32,1024]{1,0:T(8,128)(2,1)S(1)} %add.41.refs_6_.refs_1_), channel_id=1, source_target_pairs={{0,1},{1,0},{2,3},{3,2},{4,5},{5,4},{6,7},{7,6},{8,9},{9,8},{10,11... | collective-permute-start | bytes 196616 | tf_op jit(solution)/shard_map/ppermute | solution.py:606
  38.2 7.3 %collective-permute-start.9 = (bf16[32,1024]{1,0:T(8,128)(2,1)S(1)}, bf16[32,1024]{1,0:T(8,128)(2,1)S(1)}, u32[]{:S(2)}, u32[]{:S(2)}) collective-permute-start(bf16[32,1024]{1,0:T(8,128)(2,1)S(1)} %add.42.refs_8_), channel_id=1, source_target_pairs={{0,2},{1,3},{2,0},{3,1},{4,6},{5,7},{6,4},{7,5},{8,10},{9,11},{10,... | collective-permute-start | bytes 196616 | tf_op jit(solution)/shard_map/ppermute | solution.py:606
  47.4 2.0 %collective-permute-start.10 = (bf16[32,3968]{1,0:T(8,128)(2,1)S(1)}, bf16[32,3968]{1,0:T(8,128)(2,1)S(1)}, u32[]{:S(2)}, u32[]{:S(2)}) collective-permute-start(bf16[32,3968]{1,0:T(8,128)(2,1)S(1)} %get-tuple-element.53.stats), channel_id=1, source_target_pairs={{0,4},{4,0},{8,12},{12,8},{1,5},{5,1},{9,13},{13,9},{2,6},{6,2},{1... | collective-permute-start | bytes 761864 | tf_op jit(solution)/shard_map/ppermute | solution.py:606
  49.4 8.6 %collective-permute-start.11 = (bf16[32,3968]{1,0:T(8,128)(2,1)S(1)}, bf16[32,3968]{1,0:T(8,128)(2,1)S(1)}, u32[]{:S(2)}, u32[]{:S(2)}) collective-permute-start(bf16[32,3968]{1,0:T(8,128)(2,1)S(1)} %pair.1.refs_1_.refs_0_), channel_id=1, source_target_pairs={{0,8},{4,12},{8,0},{12,4},{1,9},{5,13},{9,1},{13,5},{2,10},{6,14},... | collective-permute-start | bytes 761864 | tf_op jit(solution)/shard_map/ppermute | solution.py:606
  58.2 1.4 %collective-permute-start.12 = (bf16[32,1792]{1,0:T(8,128)(2,1)S(1)}, bf16[32,1792]{1,0:T(8,128)(2,1)S(1)}, u32[]{:S(2)}, u32[]{:S(2)}) collective-permute-start(bf16[32,1792]{1,0:T(8,128)(2,1)S(1)} %gated.1.hidden), channel_id=1, source_target_pairs={{0,4},{4,0},{8,12},{12,8},{1,5},{5,1},{9,13},{13,9},{2,6},{6,2},{1... | collective-permute-start | bytes 344072 | tf_op jit(solution)/shard_map/ppermute | solution.py:606
  61.6 6.1 %collective-permute-start.13 = (bf16[8,2048]{1,0:T(8,128)(2,1)S(1)}, bf16[8,2048]{1,0:T(8,128)(2,1)S(1)}, u32[]{:S(2)}, u32[]{:S(2)}) collective-permute-start(bf16[8,2048]{1,0:T(8,128)(2,1)S(1)} %get-tuple-element.60), channel_id=1, source_target_pairs={{0,3},{1,2},{2,1},{3,0},{4,7},{5,6},{6,5},{7,4},{8,11},{9,10},{10,... | collective-permute-start | bytes 98312 | tf_op jit(solution)/shard_map/ppermute | solution.py:606
  63.1 5.5 %collective-permute-start.14 = (bf16[8,2048]{1,0:T(8,128)(2,1)S(1)}, bf16[8,2048]{1,0:T(8,128)(2,1)S(1)}, u32[]{:S(2)}, u32[]{:S(2)}) collective-permute-start(bf16[8,2048]{1,0:T(8,128)(2,1)S(1)} %get-tuple-element.61), channel_id=1, source_target_pairs={{0,2},{1,3},{2,0},{3,1},{4,6},{5,7},{6,4},{7,5},{8,10},{9,11},{10,... | collective-permute-start | bytes 98312 | tf_op jit(solution)/shard_map/ppermute | solution.py:606
  63.1 5.5 %collective-permute-start.15 = (bf16[8,2048]{1,0:T(8,128)(2,1)S(1)}, bf16[8,2048]{1,0:T(8,128)(2,1)S(1)}, u32[]{:S(2)}, u32[]{:S(2)}) collective-permute-start(bf16[8,2048]{1,0:T(8,128)(2,1)S(1)} %get-tuple-element.62), channel_id=1, source_target_pairs={{0,1},{1,0},{2,3},{3,2},{4,5},{5,4},{6,7},{7,6},{8,9},{9,8},{10,11... | collective-permute-start | bytes 98312 | tf_op jit(solution)/shard_map/ppermute | solution.py:606

commit v15 on v13

--- a/solution.py
+++ b/solution.py
@@ -10,6 +10,7 @@
 HEAD_WIDTH = 128
 DRAFT_TOKENS = 4
 LANES = 128
+GAP = 32
 MIB = 1 << 20
 
 epsilon = 1e-05
@@ -47,6 +48,21 @@
     rest = x - high.astype(f32)
     middle = rest.astype(bf16)
     return high, middle, (rest - middle.astype(f32)).astype(bf16)
+
+
+def packed(x, gap):
+    high, middle, low = (term.astype(f32) for term in thirds(x))
+    lane = lax.broadcasted_iota(jnp.int32, x.shape, 1)
+    if gap > 1:
+        middle, low = pltpu.roll(middle, gap, 1), pltpu.roll(low, 2 * gap, 1)
+    return jnp.where(lane < gap, high, jnp.where(lane < 2 * gap, middle, low)).astype(bf16)
+
+
+def joined(ref, start, gap):
+    tile = ref[:, start : start + LANES].astype(f32)
+    if gap == 1:
+        return tile[:, 0:1] + tile[:, 1:2] + tile[:, 2:3]
+    return tile + pltpu.roll(tile, LANES - gap, 1) + pltpu.roll(tile, LANES - 2 * gap, 1)
 
 
 def lanes(at):
@@ -295,8 +311,7 @@
                 stats = jnp.where(lane == k * group + g, lse[at_rows], stats)
         stats_f[tile * i : tile * (i + 1), :] = stats
     out[:, :q_cols] = total[...].astype(bf16)
-    for p, term in enumerate(thirds(stats_f[...])):
-        out[:, q_cols + p * LANES : q_cols + (p + 1) * LANES] = term
+    out[:, q_cols : q_cols + LANES] = packed(stats_f[...], GAP)
 
 
 def attend(at, cos, sin, cache, parts, part):
@@ -306,7 +321,7 @@
         lambda *refs: attend_kernel(len(parts), part, *refs),
         in_specs=[SMEM] + [VMEM] * 3 + [HBM] + [VMEM] * len(parts),
         out_specs=[VMEM, VMEM],
-        out_shape=[jax.ShapeDtypeStruct((rows, q_cols + 3 * LANES), bf16), part.out],
+        out_shape=[jax.ShapeDtypeStruct((rows, q_cols + LANES), bf16), part.out],
         scratch_shapes=[
             pltpu.VMEM((rows, q_cols), f32),
             pltpu.VMEM((rows, q_cols), f32),
@@ -319,10 +334,6 @@
     )(at, cos, sin, cache, in_hbm(part.array), *parts)
 
 
-def joined(ref, start):
-    return sum(ref[:, start + p * LANES : start + (p + 1) * LANES].astype(f32) for p in range(3))
-
-
 def product(x, w, out, base, width):
     for start, size in blocks_of(width, 512):
         out[:, start : start + size] = jnp.dot(
@@ -333,7 +344,7 @@
 def output_first_kernel(n, w, *rest):
     values, (out, attended) = rest[:n], rest[n:]
     heads = attended.shape[1] // HEAD_WIDTH
-    stats = [joined(v, attended.shape[1]) for v in values]
+    stats = [joined(v, attended.shape[1], GAP) for v in values]
     top = stats[0]
     for s in stats[1:]:
         top = jnp.maximum(top, s)
@@ -446,8 +457,7 @@
     square = squares[...] + residual(1, own, gain, parts, resid, x, gain_f)
     square = jnp.broadcast_to(jnp.sum(square, axis=1, keepdims=True), square.shape)
     width = wu[0].shape[1]
-    for p, term in enumerate(thirds(square)):
-        out[:, width + p * LANES : width + (p + 1) * LANES] = term
+    out[:, width : width + LANES] = packed(square, 1)
     half_of(1 - at[2], x, wg, wu, out, before)
 
 
@@ -458,7 +468,7 @@
         in_specs=[SMEM] + [VMEM] * (5 + len(wg) + len(parts)),
         out_specs=[VMEM] * 3,
         out_shape=[
-            jax.ShapeDtypeStruct((rows, wu.shape[1] + 3 * LANES), bf16),
+            jax.ShapeDtypeStruct((rows, wu.shape[1] + LANES), bf16),
             jax.ShapeDtypeStruct((rows, depth // 2), f32),
             jax.ShapeDtypeStruct((rows, depth // 2), bf16),
         ],
@@ -483,12 +493,12 @@
 
 
 def pair_kernel(keep, received, stats, out):
-    width = out.shape[1] - 3 * LANES
+    width = out.shape[1] - LANES
     for start, size in blocks_of(width, 512):
         cols = slice(start, start + size)
         out[:, cols] = (keep[:, cols].astype(f32) + received[:, cols].astype(f32)).astype(bf16)
-    for p, term in enumerate(thirds(joined(stats, width) + joined(received, width))):
-        out[:, width + p * LANES : width + (p + 1) * LANES] = term
+    square = joined(stats, width, 1) + joined(received, width, 1)
+    out[:, width : width + LANES] = packed(jnp.broadcast_to(square, (square.shape[0], LANES)), 1)
 
 
 def pair(keep, received, stats):
@@ -504,7 +514,7 @@
 
 def gated_kernel(model, one, two, out):
     half = out.shape[1]
-    scale = lax.rsqrt((joined(one, 2 * half) + joined(two, 2 * half)) / model + epsilon)
+    scale = lax.rsqrt((joined(one, 2 * half, 1) + joined(two, 2 * half, 1)) / model + epsilon)
     for c in range(half // LANES):
         gate, up = (
             scale * (one[:, lanes(at)].astype(f32) + two[:, lanes(at)].astype(f32))
@@ -519,7 +529,7 @@
         lambda _, *refs: gated_kernel(model, *refs),
         in_specs=[ANY] + [VMEM] * 2,
         out_specs=VMEM,
-        out_shape=jax.ShapeDtypeStruct((rows, (width - 3 * LANES) // 2), bf16),
+        out_shape=jax.ShapeDtypeStruct((rows, (width - LANES) // 2), bf16),
         compiler_params=params(4),
         name="gated",
     )(after, one, two)

time: 67.9 us -> 67.7 us (level)
  waiting for transfers between devices: 7.41 us -> 6.53 us
    ppermute x16, waiting for transfers between devices: 7.41 us -> 6.53 us  [swap(): return lax.ppermute(x, axis, [(i, i ^ bit) for i in range(n)])]
  transfers between devices with their start and end apart: 16 -> 16, of which waited for: 7 -> 6; matrix products, arithmetic and copies ran while one was open for 1% -> 1% of each run, Pallas kernels for 39% -> 39%
where the time goes in v15:
time: 67.7 us; the launch traced here: 67.5 us
  Pallas kernels  41.1 us (61%)
  starting transfers between devices  18.5 us (27%)
  waiting for transfers between devices  6.53 us (10%)
  other arithmetic  1.02 us (2%)
    pallas_call x4, Pallas kernels, fetch(): pl.pallas_call(lambda *refs: fetch_kernel(wanted, len(after), *refs), in_...  18.7 us
    ppermute x16, starting transfers between devices, swap(): return lax.ppermute(x, axis, [(i, i ^ bit) for i in range(n)])  18.5 us
    ppermute x16, waiting for transfers between devices, swap(): return lax.ppermute(x, axis, [(i, i ^ bit) for i in range(n)])  6.53 us
    pallas_call x1, Pallas kernels, project(): pl.pallas_call(lambda *refs: project_kernel(chunks, *refs), in_specs=[SME...  5.11 us
    pallas_call x1, Pallas kernels, attend(): pl.pallas_call(lambda *refs: attend_kernel(len(parts), part, *refs), in_s...  4.09 us
    pallas_call x1, Pallas kernels, expand_first(): pl.pallas_call(lambda *refs: expand_first_kernel(len(parts), part, *refs)...  3.79 us
    pallas_call x1, Pallas kernels, contract_last(): pl.pallas_call(lambda *refs: contract_last_kernel(n, *refs), in_specs=[SM...  1.94 us
    pallas_call x1, Pallas kernels, expand_send(): pl.pallas_call(lambda *refs: expand_send_kernel(len(parts), len(wg), *ref...  1.91 us
  transfers between devices with their start and end apart: 16, of which 6 were waited for; matrix products, arithmetic and copies ran while one was open for 1% of the time, Pallas kernels for 39%

profile of v15, /device:TPU:0, one launch (start us, length us, event | category | flops | bytes accessed | tf_op | source)
XLA Modules:
  0.0 67.5 jit_solution(1771505657961965977)
XLA Ops:
  0.0 0.0 copy-start.1
  0.0 0.0 copy-start.2
  0.0 0.1 pad_add_fusion.refs_0_.at
  0.1 5.1 %project.1 = (bf16[32,2560]{1,0:T(8,128)(2,1)S(1)}, bf16[32,2048]{1,0:T(8,128)(2,1)S(1)}) custom-call(s32[4]{0:T(128)S(1)} %pad_add_fusion.refs_0_.at, bf16[32,8192]{1,0:T(8,128)(2,1)} %refs_1_.1, bf16[64,128]{1,0:T(8,128)(2,1)} %bitcast.12, bf16[2048,2048]{1,0:T(8,128)(2,1)} %refs_3_.3, bf16[2048,256]{1,0:T(8,128)(2,1)} %refs_4_.2, bf16[2048,256]{1,0:T(8,128)(2,1)} %refs_5_.2), custom_call_target="tpu_custom_call" | custom-call | flops 335544320 | bytes 10485760 | tf_op jit(solution)/shard_map/project/pallas_call | solution.py:202
  5.2 0.5 collective-permute-start.1
  5.7 2.6 %collective-permute-start = (bf16[32,2560]{1,0:T(8,128)(2,1)S(1)}, bf16[32,2560]{1,0:T(8,128)(2,1)S(1)}, u32[]{:S(2)}, u32[]{:S(2)}) collective-permute-start(bf16[32,2560]{1,0:T(8,128)(2,1)S(1)} %get-tuple-element.35.refs_1_.refs_5_), channel_id=1, source_target_pairs={{0,8},{4,12},{8,0},{12,4},{1,9},{5,13},{9,1},{13,5},{2,10},{6,14},... | collective-permute-start | bytes 491528 | tf_op jit(solution)/shard_map/ppermute | solution.py:616
  8.3 0.0 copy-done.1
  8.3 0.1 add_convert_fusion.1
  8.4 0.1 convert_element_type.24
  8.5 0.1 fusion
  8.6 0.0 copy-done.2
  8.6 0.1 concatenate.10.refs_2_.refs_0_
  8.7 0.1 pad_maximum_fusion
  8.8 5.1 %fetch.4 = (bf16[16,512,256]{2,1,0:T(8,128)(2,1)S(1)}, bf16[1024,3584]{1,0:T(8,128)(2,1)S(1)}, f32[8,128]{1,0:T(8,128)S(1)}) custom-call(s32[4]{0:T(128)S(1)} %pad_add_fusion.refs_0_.at, bf16[32,2560]{1,0:T(8,128)(2,1)S(1)} %get-tuple-element.35.refs_1_.refs_5_, s32[20]{0:T(128)S(1)} %concatenate.10.refs_2_.refs_0_, ...), custom_call_target="tpu_custom_call" | custom-call | bytes 23068672 | tf_op jit(solution)/shard_map/fetch/pallas_call | solution.py:118
  13.9 0.0 collective-permute-done.__0_
  14.0 0.2 collective-permute-start.2
  14.2 0.0 collective-permute-done.1.refs_7_
  14.2 1.2 %collective-permute-done.2.refs_8_ = bf16[32,2560]{1,0:T(8,128)(2,1)S(1)} collective-permute-done((bf16[32,2560]{1,0:T(8,128)(2,1)S(1)}, bf16[32,2560]{1,0:T(8,128)(2,1)S(1)}, u32[]{:S(2)}, u32[]{:S(2)}) %collective-permute-start.2) | collective-permute-done | bytes 163872 | tf_op jit(solution)/shard_map/ppermute | solution.py:616
  15.4 4.1 %attend.1 = (bf16[32,2176]{1,0:T(8,128)(2,1)S(1)}, bf16[2048,2048]{1,0:T(8,128)(2,1)S(1)}) custom-call(s32[20]{0:T(128)S(1)} %concatenate.10.refs_2_.refs_0_, f32[32,128]{1,0:T(8,128)S(1)} %get-tuple-element.66.refs_3_.refs_1_, f32[32,128]{1,0:T(8,128)S(1)} %get-tuple-element.67.refs_4_.refs_2_, bf16[2,8,512,256]{3,2,1,0:T(8,128)(2,1)S(1)} %bitcast.8, ...), custom_call_target="tpu_custom_call" | custom-call | flops 134217728 | bytes 4194304 | tf_op jit(solution)/shard_map/attend/pallas_call | solution.py:320
  19.5 0.9 %collective-permute-start.3 = (bf16[32,2176]{1,0:T(8,128)(2,1)S(1)}, bf16[32,2176]{1,0:T(8,128)(2,1)S(1)}, u32[]{:S(2)}, u32[]{:S(2)}) collective-permute-start(bf16[32,2176]{1,0:T(8,128)(2,1)S(1)} %get-tuple-element.39.refs_1_), channel_id=1, source_target_pairs={{0,8},{4,12},{8,0},{12,4},{1,9},{5,13},{9,1},{13,5},{2,10},{6,14},... | collective-permute-start | bytes 417800 | tf_op jit(solution)/shard_map/ppermute | solution.py:616
  20.4 0.0 collective-permute-start.4
  20.4 4.9 %fetch.5 = (bf16[1024,3584]{1,0:T(8,128)(2,1)S(1)}, bf16[512,3584]{1,0:T(8,128)(2,1)S(1)}, f32[8,128]{1,0:T(8,128)S(1)}) custom-call(s32[4]{0:T(128)S(1)} %pad_add_fusion.refs_0_.at, bf16[32,2176]{1,0:T(8,128)(2,1)S(1)} %get-tuple-element.39.refs_1_, bf16[2048,3584]{1,0:T(8,128)(2,1)} %refs_5_.3, bf16[2048,3584]{1,0:T(8,128)(2,1)} %refs_2_.4), custom_call_target="tpu_custom_call" | custom-call | bytes 22020096 | tf_op jit(solution)/shard_map/fetch/pallas_call | solution.py:118
  25.4 0.0 collective-permute-done.3.__0_
  25.4 0.6 collective-permute-start.5
  25.9 0.0 collective-permute-done.4.refs_3_
  26.0 1.0 %collective-permute-done.5.refs_4_ = bf16[32,2176]{1,0:T(8,128)(2,1)S(1)} collective-permute-done((bf16[32,2176]{1,0:T(8,128)(2,1)S(1)}, bf16[32,2176]{1,0:T(8,128)(2,1)S(1)}, u32[]{:S(2)}, u32[]{:S(2)}) %collective-permute-start.5) | collective-permute-done | bytes 139296 | tf_op jit(solution)/shard_map/ppermute | solution.py:616
  26.9 1.0 %output_first.1 = (bf16[32,1024]{1,0:T(8,128)(2,1)S(1)}, bf16[32,2048]{1,0:T(8,128)(2,1)S(1)}) custom-call(bf16[2048,2048]{1,0:T(8,128)(2,1)S(1)} %get-tuple-element.41.refs_0_.w, bf16[32,2176]{1,0:T(8,128)(2,1)S(1)} %get-tuple-element.39.refs_1_, bf16[32,2176]{1,0:T(8,128)(2,1)S(1)} %hold.3.refs_2_, bf16[32,2176]{1,0:T(8,128)(2,1)S(1)} %collective-permute-done.4.refs_3_, ...), custom_call_target="tpu_custom_call" | custom-call | flops 268435456 | bytes 8388608 | tf_op jit(solution)/shard_map/output_first/pallas_call | solution.py:363
  28.0 1.6 %collective-permute-start.6 = (bf16[32,1024]{1,0:T(8,128)(2,1)S(1)}, bf16[32,1024]{1,0:T(8,128)(2,1)S(1)}, u32[]{:S(2)}, u32[]{:S(2)}) collective-permute-start(bf16[32,1024]{1,0:T(8,128)(2,1)S(1)} %get-tuple-element.43.one), channel_id=1, source_target_pairs={{0,1},{1,0},{2,3},{3,2},{4,5},{5,4},{6,7},{7,6},{8,9},{9,8},{10,11... | collective-permute-start | bytes 196616 | tf_op jit(solution)/shard_map/ppermute | solution.py:616
  29.6 0.8 %output_second.1.one = bf16[32,1024]{1,0:T(8,128)(2,1)S(1)} custom-call(bf16[32,2048]{1,0:T(8,128)(2,1)S(1)} %get-tuple-element.49.x, bf16[2048,2048]{1,0:T(8,128)(2,1)S(1)} %get-tuple-element.41.refs_0_.w), custom_call_target="tpu_custom_call" | custom-call | flops 268435456 | bytes 8388608 | tf_op jit(solution)/shard_map/output_second/pallas_call | solution.py:379
  30.4 2.6 %collective-permute-start.8 = (bf16[32,1024]{1,0:T(8,128)(2,1)S(1)}, bf16[32,1024]{1,0:T(8,128)(2,1)S(1)}, u32[]{:S(2)}, u32[]{:S(2)}) collective-permute-start(bf16[32,1024]{1,0:T(8,128)(2,1)S(1)} %output_second.1.one), channel_id=1, source_target_pairs={{0,2},{1,3},{2,0},{3,1},{4,6},{5,7},{6,4},{7,5},{8,10},{9,11},{10,... | collective-permute-start | bytes 196616 | tf_op jit(solution)/shard_map/ppermute | solution.py:616
  33.0 0.0 collective-permute-done.6.two
  33.0 0.0 copy-start
  33.1 2.5 %collective-permute-start.7 = (bf16[32,1024]{1,0:T(8,128)(2,1)S(1)}, bf16[32,1024]{1,0:T(8,128)(2,1)S(1)}, u32[]{:S(2)}, u32[]{:S(2)}) collective-permute-start(bf16[32,1024]{1,0:T(8,128)(2,1)S(1)} %add.41.refs_6_.refs_1_), channel_id=1, source_target_pairs={{0,2},{1,3},{2,0},{3,1},{4,6},{5,7},{6,4},{7,5},{8,10},{9,11},{10,... | collective-permute-start | bytes 196616 | tf_op jit(solution)/shard_map/ppermute | solution.py:616
  35.6 2.7 %fetch.6 = (bf16[512,3584]{1,0:T(8,128)(2,1)S(1)}, f32[8,128]{1,0:T(8,128)S(1)}) custom-call(s32[4]{0:T(128)S(1)} %pad_add_fusion.refs_0_.at, bf16[32,1024]{1,0:T(8,128)(2,1)S(1)} %add.41.refs_6_.refs_1_, bf16[2048,3584]{1,0:T(8,128)(2,1)} %refs_2_.4), custom_call_target="tpu_custom_call" | custom-call | bytes 7340032 | tf_op jit(solution)/shard_map/fetch/pallas_call | solution.py:118
  38.2 0.0 collective-permute-done.8.two
  38.3 1.1 %collective-permute-start.9 = (bf16[32,1024]{1,0:T(8,128)(2,1)S(1)}, bf16[32,1024]{1,0:T(8,128)(2,1)S(1)}, u32[]{:S(2)}, u32[]{:S(2)}) collective-permute-start(bf16[32,1024]{1,0:T(8,128)(2,1)S(1)} %add.42.refs_8_), channel_id=1, source_target_pairs={{0,1},{1,0},{2,3},{3,2},{4,5},{5,4},{6,7},{7,6},{8,9},{9,8},{10,11... | collective-permute-start | bytes 196616 | tf_op jit(solution)/shard_map/ppermute | solution.py:616
  39.4 0.1 collective-permute-done.7.refs_7_
  39.6 0.0 copy-done
  39.6 3.8 %expand_first.1 = (f32[32,3584]{1,0:T(8,128)S(1)}, f32[32,3584]{1,0:T(8,128)S(1)}, f32[32,1024]{1,0:T(8,128)S(1)}, f32[32,128]{1,0:T(8,128)S(1)}, bf16[1024,3584]{1,0:T(8,128)(2,1)S(1)}) custom-call(s32[4]{0:T(128)S(1)} %pad_add_fusion.refs_0_.at, bf16[32,2048]{1,0:T(8,128)(2,1)S(1)} %get-tuple-element.34.refs_1_, bf16[16,128]{1,0:T(8,128)(2,1)S(1)} %bitcast.9, ...), custom_call_target="tpu_custom_call" | custom-call | flops 469762048 | bytes 14680064 | tf_op jit(solution)/shard_map/expand_first/pallas_call | solution.py:433
  43.4 0.0 collective-permute-done.9.refs_9_
  43.4 1.9 %expand_send.1 = (bf16[32,3712]{1,0:T(8,128)(2,1)S(1)}, f32[32,1024]{1,0:T(8,128)S(1)}, bf16[32,1024]{1,0:T(8,128)(2,1)S(1)}) custom-call(s32[4]{0:T(128)S(1)} %pad_add_fusion.refs_0_.at, bf16[32,2048]{1,0:T(8,128)(2,1)S(1)} %get-tuple-element.34.refs_1_, bf16[16,128]{1,0:T(8,128)(2,1)S(1)} %bitcast.10, f32[32,3584]{1,0:T(8,128)S(1)} %get-tuple-element.44.refs_3_, ...), custom_call_target="tpu_custom_call" | custom-call | flops 234881024 | bytes 7340032 | tf_op jit(solution)/shard_map/expand_send/pallas_call | solution.py:466
  45.3 0.1 collective-permute-start.10
  45.3 1.9 %expand_keep.1.keep = bf16[32,3584]{1,0:T(8,128)(2,1)S(1)} custom-call(s32[4]{0:T(128)S(1)} %pad_add_fusion.refs_0_.at, bf16[32,1024]{1,0:T(8,128)(2,1)S(1)} %get-tuple-element.51.x, f32[32,3584]{1,0:T(8,128)S(1)} %get-tuple-element.52.before, bf16[512,3584]{1,0:T(8,128)(2,1)S(1)} %get-tuple-element.46.refs_5_.refs_0_, ...), custom_call_target="tpu_custom_call" | custom-call | flops 234881024 | bytes 7340032 | tf_op jit(solution)/shard_map/expand_keep/pallas_call | solution.py:484
  47.3 0.0 collective-permute-done.10.received
  47.3 0.2 pair.1.refs_1_.refs_0_
  47.4 1.2 %collective-permute-start.11 = (bf16[32,3712]{1,0:T(8,128)(2,1)S(1)}, bf16[32,3712]{1,0:T(8,128)(2,1)S(1)}, u32[]{:S(2)}, u32[]{:S(2)}) collective-permute-start(bf16[32,3712]{1,0:T(8,128)(2,1)S(1)} %pair.1.refs_1_.refs_0_), channel_id=1, source_target_pairs={{0,8},{4,12},{8,0},{12,4},{1,9},{5,13},{9,1},{13,5},{2,10},{6,14},... | collective-permute-start | bytes 712712 | tf_op jit(solution)/shard_map/ppermute | solution.py:616
  48.6 6.0 %fetch.7 = (bf16[1792,2048]{1,0:T(8,128)(2,1)S(1)}, bf16[1792,2048]{1,0:T(8,128)(2,1)S(1)}, f32[8,128]{1,0:T(8,128)S(1)}) custom-call(s32[4]{0:T(128)S(1)} %pad_add_fusion.refs_0_.at, bf16[32,3712]{1,0:T(8,128)(2,1)S(1)} %pair.1.refs_1_.refs_0_, bf16[3584,2048]{1,0:T(8,128)(2,1)} %refs_3_.5, bf16[3584,2048]{1,0:T(8,128)(2,1)} %refs_3_.5), custom_call_target="tpu_custom_call" | custom-call | bytes 29360128 | tf_op jit(solution)/shard_map/fetch/pallas_call | solution.py:118
  54.7 1.0 %collective-permute-done.11.refs_1_ = bf16[32,3712]{1,0:T(8,128)(2,1)S(1)} collective-permute-done((bf16[32,3712]{1,0:T(8,128)(2,1)S(1)}, bf16[32,3712]{1,0:T(8,128)(2,1)S(1)}, u32[]{:S(2)}, u32[]{:S(2)}) %collective-permute-start.11) | collective-permute-done | bytes 237600 | tf_op jit(solution)/shard_map/ppermute | solution.py:616
  55.6 0.2 gated.1.hidden
  55.9 0.1 collective-permute-start.12
  56.0 1.4 %contract.1.refs_3_ = f32[32,2048]{1,0:T(8,128)S(1)} custom-call(bf16[32,1792]{1,0:T(8,128)(2,1)S(1)} %gated.1.hidden, bf16[1792,2048]{1,0:T(8,128)(2,1)S(1)} %get-tuple-element.56.w), custom_call_target="tpu_custom_call" | custom-call | flops 234881024 | bytes 7340032 | tf_op jit(solution)/shard_map/contract/pallas_call | solution.py:546
  57.3 0.0 collective-permute-done.12.refs_1_
  57.3 1.9 %contract_last.1 = (f32[8,2048]{1,0:T(8,128)S(1)}, bf16[8,2048]{1,0:T(8,128)(2,1)S(1)}, bf16[8,2048]{1,0:T(8,128)(2,1)S(1)}, bf16[8,2048]{1,0:T(8,128)(2,1)S(1)}) custom-call(s32[4]{0:T(128)S(1)} %pad_add_fusion.refs_0_.at, bf16[32,1792]{1,0:T(8,128)(2,1)S(1)} %collective-permute-done.12.refs_1_, bf16[1792,2048]{1,0:T(8,128)(2,1)S(1)} %get-tuple-element.55.refs_2_, ...), custom_call_target="tpu_custom_call" | custom-call | flops 234881024 | bytes 7340032 | tf_op jit(solution)/shard_map/contract_last/pallas_call | solution.py:583
  59.3 2.8 %collective-permute-start.13 = (bf16[8,2048]{1,0:T(8,128)(2,1)S(1)}, bf16[8,2048]{1,0:T(8,128)(2,1)S(1)}, u32[]{:S(2)}, u32[]{:S(2)}) collective-permute-start(bf16[8,2048]{1,0:T(8,128)(2,1)S(1)} %get-tuple-element.60), channel_id=1, source_target_pairs={{0,3},{1,2},{2,1},{3,0},{4,7},{5,6},{6,5},{7,4},{8,11},{9,10},{10,... | collective-permute-start | bytes 98312 | tf_op jit(solution)/shard_map/ppermute | solution.py:616
  62.1 0.0 collective-permute-start.14
  62.1 1.6 %collective-permute-start.15 = (bf16[8,2048]{1,0:T(8,128)(2,1)S(1)}, bf16[8,2048]{1,0:T(8,128)(2,1)S(1)}, u32[]{:S(2)}, u32[]{:S(2)}) collective-permute-start(bf16[8,2048]{1,0:T(8,128)(2,1)S(1)} %get-tuple-element.62), channel_id=1, source_target_pairs={{0,1},{1,0},{2,3},{3,2},{4,5},{5,4},{6,7},{7,6},{8,9},{9,8},{10,11... | collective-permute-start | bytes 98312 | tf_op jit(solution)/shard_map/ppermute | solution.py:616
  63.7 1.7 %collective-permute-done.13 = bf16[8,2048]{1,0:T(8,128)(2,1)S(1)} collective-permute-done((bf16[8,2048]{1,0:T(8,128)(2,1)S(1)}, bf16[8,2048]{1,0:T(8,128)(2,1)S(1)}, u32[]{:S(2)}, u32[]{:S(2)}) %collective-permute-start.13) | collective-permute-done | bytes 32800 | tf_op jit(solution)/shard_map/ppermute | solution.py:616
  65.4 1.5 %collective-permute-done.14 = bf16[8,2048]{1,0:T(8,128)(2,1)S(1)} collective-permute-done((bf16[8,2048]{1,0:T(8,128)(2,1)S(1)}, bf16[8,2048]{1,0:T(8,128)(2,1)S(1)}, u32[]{:S(2)}, u32[]{:S(2)}) %collective-permute-start.14) | collective-permute-done | bytes 32800 | tf_op jit(solution)/shard_map/ppermute | solution.py:616
  66.9 0.0 collective-permute-done.15
  66.9 0.6 add_convert_fusion
  (5 shorter events, 0.1 us)
Async XLA Ops:
  0.0 8.3 %copy-start.1 = (s32[8]{0:T(128)S(1)}, s32[8]{0:T(128)}, u32[]{:S(2)}) copy-start(s32[8]{0:T(128)} %param.24) | copy-start | bytes 100
  0.0 8.6 %copy-start.2 = (s32[8]{0:T(128)S(1)}, s32[8]{0:T(128)}, u32[]{:S(2)}) copy-start(s32[8]{0:T(128)} %param.25) | copy-start | bytes 100
  5.2 9.0 %collective-permute-start.1 = (bf16[32,2560]{1,0:T(8,128)(2,1)S(1)}, bf16[32,2560]{1,0:T(8,128)(2,1)S(1)}, u32[]{:S(2)}, u32[]{:S(2)}) collective-permute-start(bf16[32,2560]{1,0:T(8,128)(2,1)S(1)} %get-tuple-element.35.refs_1_.refs_5_), channel_id=1, source_target_pairs={{0,4},{4,0},{8,12},{12,8},{1,5},{5,1},{9,13},{13,9},{2,6},{6,2},{1... | collective-permute-start | bytes 491528 | tf_op jit(solution)/shard_map/ppermute | solution.py:616
  5.7 8.2 %collective-permute-start = (bf16[32,2560]{1,0:T(8,128)(2,1)S(1)}, bf16[32,2560]{1,0:T(8,128)(2,1)S(1)}, u32[]{:S(2)}, u32[]{:S(2)}) collective-permute-start(bf16[32,2560]{1,0:T(8,128)(2,1)S(1)} %get-tuple-element.35.refs_1_.refs_5_), channel_id=1, source_target_pairs={{0,8},{4,12},{8,0},{12,4},{1,9},{5,13},{9,1},{13,5},{2,10},{6,14},... | collective-permute-start | bytes 491528 | tf_op jit(solution)/shard_map/ppermute | solution.py:616
  14.0 1.5 %collective-permute-start.2 = (bf16[32,2560]{1,0:T(8,128)(2,1)S(1)}, bf16[32,2560]{1,0:T(8,128)(2,1)S(1)}, u32[]{:S(2)}, u32[]{:S(2)}) collective-permute-start(bf16[32,2560]{1,0:T(8,128)(2,1)S(1)} %hold.2.refs_6_), channel_id=1, source_target_pairs={{0,4},{4,0},{8,12},{12,8},{1,5},{5,1},{9,13},{13,9},{2,6},{6,2},{1... | collective-permute-start | bytes 491528 | tf_op jit(solution)/shard_map/ppermute | solution.py:616
  19.5 5.8 %collective-permute-start.3 = (bf16[32,2176]{1,0:T(8,128)(2,1)S(1)}, bf16[32,2176]{1,0:T(8,128)(2,1)S(1)}, u32[]{:S(2)}, u32[]{:S(2)}) collective-permute-start(bf16[32,2176]{1,0:T(8,128)(2,1)S(1)} %get-tuple-element.39.refs_1_), channel_id=1, source_target_pairs={{0,8},{4,12},{8,0},{12,4},{1,9},{5,13},{9,1},{13,5},{2,10},{6,14},... | collective-permute-start | bytes 417800 | tf_op jit(solution)/shard_map/ppermute | solution.py:616
  20.4 5.5 %collective-permute-start.4 = (bf16[32,2176]{1,0:T(8,128)(2,1)S(1)}, bf16[32,2176]{1,0:T(8,128)(2,1)S(1)}, u32[]{:S(2)}, u32[]{:S(2)}) collective-permute-start(bf16[32,2176]{1,0:T(8,128)(2,1)S(1)} %get-tuple-element.39.refs_1_), channel_id=1, source_target_pairs={{0,4},{4,0},{8,12},{12,8},{1,5},{5,1},{9,13},{13,9},{2,6},{6,2},{1... | collective-permute-start | bytes 417800 | tf_op jit(solution)/shard_map/ppermute | solution.py:616
  25.4 1.6 %collective-permute-start.5 = (bf16[32,2176]{1,0:T(8,128)(2,1)S(1)}, bf16[32,2176]{1,0:T(8,128)(2,1)S(1)}, u32[]{:S(2)}, u32[]{:S(2)}) collective-permute-start(bf16[32,2176]{1,0:T(8,128)(2,1)S(1)} %hold.3.refs_2_), channel_id=1, source_target_pairs={{0,4},{4,0},{8,12},{12,8},{1,5},{5,1},{9,13},{13,9},{2,6},{6,2},{1... | collective-permute-start | bytes 417800 | tf_op jit(solution)/shard_map/ppermute | solution.py:616
  28.0 5.0 %collective-permute-start.6 = (bf16[32,1024]{1,0:T(8,128)(2,1)S(1)}, bf16[32,1024]{1,0:T(8,128)(2,1)S(1)}, u32[]{:S(2)}, u32[]{:S(2)}) collective-permute-start(bf16[32,1024]{1,0:T(8,128)(2,1)S(1)} %get-tuple-element.43.one), channel_id=1, source_target_pairs={{0,1},{1,0},{2,3},{3,2},{4,5},{5,4},{6,7},{7,6},{8,9},{9,8},{10,11... | collective-permute-start | bytes 196616 | tf_op jit(solution)/shard_map/ppermute | solution.py:616
  30.4 7.8 %collective-permute-start.8 = (bf16[32,1024]{1,0:T(8,128)(2,1)S(1)}, bf16[32,1024]{1,0:T(8,128)(2,1)S(1)}, u32[]{:S(2)}, u32[]{:S(2)}) collective-permute-start(bf16[32,1024]{1,0:T(8,128)(2,1)S(1)} %output_second.1.one), channel_id=1, source_target_pairs={{0,2},{1,3},{2,0},{3,1},{4,6},{5,7},{6,4},{7,5},{8,10},{9,11},{10,... | collective-permute-start | bytes 196616 | tf_op jit(solution)/shard_map/ppermute | solution.py:616
  33.0 6.5 %copy-start = (bf16[2048]{0:T(1024)(128)(2,1)S(1)}, bf16[2048]{0:T(1024)(128)(2,1)}, u32[]{:S(2)}) copy-start(bf16[2048]{0:T(1024)(128)(2,1)} %param.15) | copy-start | bytes 12292
  33.1 6.5 %collective-permute-start.7 = (bf16[32,1024]{1,0:T(8,128)(2,1)S(1)}, bf16[32,1024]{1,0:T(8,128)(2,1)S(1)}, u32[]{:S(2)}, u32[]{:S(2)}) collective-permute-start(bf16[32,1024]{1,0:T(8,128)(2,1)S(1)} %add.41.refs_6_.refs_1_), channel_id=1, source_target_pairs={{0,2},{1,3},{2,0},{3,1},{4,6},{5,7},{6,4},{7,5},{8,10},{9,11},{10,... | collective-permute-start | bytes 196616 | tf_op jit(solution)/shard_map/ppermute | solution.py:616
  38.3 5.1 %collective-permute-start.9 = (bf16[32,1024]{1,0:T(8,128)(2,1)S(1)}, bf16[32,1024]{1,0:T(8,128)(2,1)S(1)}, u32[]{:S(2)}, u32[]{:S(2)}) collective-permute-start(bf16[32,1024]{1,0:T(8,128)(2,1)S(1)} %add.42.refs_8_), channel_id=1, source_target_pairs={{0,1},{1,0},{2,3},{3,2},{4,5},{5,4},{6,7},{7,6},{8,9},{9,8},{10,11... | collective-permute-start | bytes 196616 | tf_op jit(solution)/shard_map/ppermute | solution.py:616
  45.3 2.0 %collective-permute-start.10 = (bf16[32,3712]{1,0:T(8,128)(2,1)S(1)}, bf16[32,3712]{1,0:T(8,128)(2,1)S(1)}, u32[]{:S(2)}, u32[]{:S(2)}) collective-permute-start(bf16[32,3712]{1,0:T(8,128)(2,1)S(1)} %get-tuple-element.53.stats), channel_id=1, source_target_pairs={{0,4},{4,0},{8,12},{12,8},{1,5},{5,1},{9,13},{13,9},{2,6},{6,2},{1... | collective-permute-start | bytes 712712 | tf_op jit(solution)/shard_map/ppermute | solution.py:616
  47.4 8.2 %collective-permute-start.11 = (bf16[32,3712]{1,0:T(8,128)(2,1)S(1)}, bf16[32,3712]{1,0:T(8,128)(2,1)S(1)}, u32[]{:S(2)}, u32[]{:S(2)}) collective-permute-start(bf16[32,3712]{1,0:T(8,128)(2,1)S(1)} %pair.1.refs_1_.refs_0_), channel_id=1, source_target_pairs={{0,8},{4,12},{8,0},{12,4},{1,9},{5,13},{9,1},{13,5},{2,10},{6,14},... | collective-permute-start | bytes 712712 | tf_op jit(solution)/shard_map/ppermute | solution.py:616
  55.9 1.4 %collective-permute-start.12 = (bf16[32,1792]{1,0:T(8,128)(2,1)S(1)}, bf16[32,1792]{1,0:T(8,128)(2,1)S(1)}, u32[]{:S(2)}, u32[]{:S(2)}) collective-permute-start(bf16[32,1792]{1,0:T(8,128)(2,1)S(1)} %gated.1.hidden), channel_id=1, source_target_pairs={{0,4},{4,0},{8,12},{12,8},{1,5},{5,1},{9,13},{13,9},{2,6},{6,2},{1... | collective-permute-start | bytes 344072 | tf_op jit(solution)/shard_map/ppermute | solution.py:616
  59.3 6.1 %collective-permute-start.13 = (bf16[8,2048]{1,0:T(8,128)(2,1)S(1)}, bf16[8,2048]{1,0:T(8,128)(2,1)S(1)}, u32[]{:S(2)}, u32[]{:S(2)}) collective-permute-start(bf16[8,2048]{1,0:T(8,128)(2,1)S(1)} %get-tuple-element.60), channel_id=1, source_target_pairs={{0,3},{1,2},{2,1},{3,0},{4,7},{5,6},{6,5},{7,4},{8,11},{9,10},{10,... | collective-permute-start | bytes 98312 | tf_op jit(solution)/shard_map/ppermute | solution.py:616
  62.1 4.8 %collective-permute-start.14 = (bf16[8,2048]{1,0:T(8,128)(2,1)S(1)}, bf16[8,2048]{1,0:T(8,128)(2,1)S(1)}, u32[]{:S(2)}, u32[]{:S(2)}) collective-permute-start(bf16[8,2048]{1,0:T(8,128)(2,1)S(1)} %get-tuple-element.61), channel_id=1, source_target_pairs={{0,2},{1,3},{2,0},{3,1},{4,6},{5,7},{6,4},{7,5},{8,10},{9,11},{10,... | collective-permute-start | bytes 98312 | tf_op jit(solution)/shard_map/ppermute | solution.py:616
  62.1 4.8 %collective-permute-start.15 = (bf16[8,2048]{1,0:T(8,128)(2,1)S(1)}, bf16[8,2048]{1,0:T(8,128)(2,1)S(1)}, u32[]{:S(2)}, u32[]{:S(2)}) collective-permute-start(bf16[8,2048]{1,0:T(8,128)(2,1)S(1)} %get-tuple-element.62), channel_id=1, source_target_pairs={{0,1},{1,0},{2,3},{3,2},{4,5},{5,4},{6,7},{7,6},{8,9},{9,8},{10,11... | collective-permute-start | bytes 98312 | tf_op jit(solution)/shard_map/ppermute | solution.py:616

commit v16 on v15

--- a/solution.py
+++ b/solution.py
@@ -69,7 +69,7 @@
     return slice(at * LANES, (at + 1) * LANES)
 
 
-PIECES = 8
+PIECES = 4
 
 
 class Part:

time: 67.7 us -> 67.5 us (level)
  no operation moved by 1% of the time
where the time goes in v16:
time: 67.5 us; the launch traced here: 67.4 us
  Pallas kernels  40.8 us (60%)
  starting transfers between devices  18.5 us (27%)
  waiting for transfers between devices  6.75 us (10%)
  other arithmetic  1.02 us (2%)
    ppermute x16, starting transfers between devices, swap(): return lax.ppermute(x, axis, [(i, i ^ bit) for i in range(n)])  18.5 us
    pallas_call x4, Pallas kernels, fetch(): pl.pallas_call(lambda *refs: fetch_kernel(wanted, len(after), *refs), in_...  18.4 us
    ppermute x16, waiting for transfers between devices, swap(): return lax.ppermute(x, axis, [(i, i ^ bit) for i in range(n)])  6.75 us
    pallas_call x1, Pallas kernels, project(): pl.pallas_call(lambda *refs: project_kernel(chunks, *refs), in_specs=[SME...  5.11 us
    pallas_call x1, Pallas kernels, attend(): pl.pallas_call(lambda *refs: attend_kernel(len(parts), part, *refs), in_s...  4.08 us
    pallas_call x1, Pallas kernels, expand_first(): pl.pallas_call(lambda *refs: expand_first_kernel(len(parts), part, *refs)...  3.76 us
    pallas_call x1, Pallas kernels, contract_last(): pl.pallas_call(lambda *refs: contract_last_kernel(n, *refs), in_specs=[SM...  1.94 us
    pallas_call x1, Pallas kernels, expand_send(): pl.pallas_call(lambda *refs: expand_send_kernel(len(parts), len(wg), *ref...  1.91 us
  transfers between devices with their start and end apart: 16, of which 6 were waited for; matrix products, arithmetic and copies ran while one was open for 1% of the time, Pallas kernels for 39%

profile of v16, /device:TPU:0, one launch (start us, length us, event | category | flops | bytes accessed | tf_op | source)
XLA Modules:
  0.0 67.4 jit_solution(2054022909622217582)
XLA Ops:
  0.0 0.0 copy-start.1
  0.0 0.0 copy-start.2
  0.0 0.1 pad_add_fusion.refs_0_.at
  0.1 5.1 %project.1 = (bf16[32,2560]{1,0:T(8,128)(2,1)S(1)}, bf16[32,2048]{1,0:T(8,128)(2,1)S(1)}) custom-call(s32[4]{0:T(128)S(1)} %pad_add_fusion.refs_0_.at, bf16[32,8192]{1,0:T(8,128)(2,1)} %refs_1_.1, bf16[64,128]{1,0:T(8,128)(2,1)} %bitcast.12, bf16[2048,2048]{1,0:T(8,128)(2,1)} %refs_3_.3, bf16[2048,256]{1,0:T(8,128)(2,1)} %refs_4_.2, bf16[2048,256]{1,0:T(8,128)(2,1)} %refs_5_.2), custom_call_target="tpu_custom_call" | custom-call | flops 335544320 | bytes 10485760 | tf_op jit(solution)/shard_map/project/pallas_call | solution.py:202
  5.2 0.5 collective-permute-start.1
  5.7 2.6 %collective-permute-start = (bf16[32,2560]{1,0:T(8,128)(2,1)S(1)}, bf16[32,2560]{1,0:T(8,128)(2,1)S(1)}, u32[]{:S(2)}, u32[]{:S(2)}) collective-permute-start(bf16[32,2560]{1,0:T(8,128)(2,1)S(1)} %get-tuple-element.35.refs_1_.refs_5_), channel_id=1, source_target_pairs={{0,8},{4,12},{8,0},{12,4},{1,9},{5,13},{9,1},{13,5},{2,10},{6,14},... | collective-permute-start | bytes 491528 | tf_op jit(solution)/shard_map/ppermute | solution.py:616
  8.3 0.0 copy-done.1
  8.3 0.1 add_convert_fusion.1
  8.4 0.1 convert_element_type.24
  8.5 0.1 fusion
  8.6 0.0 copy-done.2
  8.6 0.1 concatenate.10.refs_2_.refs_0_
  8.7 0.1 pad_maximum_fusion
  8.8 5.0 %fetch.4 = (bf16[16,512,256]{2,1,0:T(8,128)(2,1)S(1)}, bf16[1024,3584]{1,0:T(8,128)(2,1)S(1)}, f32[8,128]{1,0:T(8,128)S(1)}) custom-call(s32[4]{0:T(128)S(1)} %pad_add_fusion.refs_0_.at, bf16[32,2560]{1,0:T(8,128)(2,1)S(1)} %get-tuple-element.35.refs_1_.refs_5_, s32[20]{0:T(128)S(1)} %concatenate.10.refs_2_.refs_0_, ...), custom_call_target="tpu_custom_call" | custom-call | bytes 23068672 | tf_op jit(solution)/shard_map/fetch/pallas_call | solution.py:118
  13.9 0.0 collective-permute-done.__0_
  13.9 0.2 collective-permute-start.2
  14.1 0.0 collective-permute-done.1.refs_7_
  14.1 1.2 %collective-permute-done.2.refs_8_ = bf16[32,2560]{1,0:T(8,128)(2,1)S(1)} collective-permute-done((bf16[32,2560]{1,0:T(8,128)(2,1)S(1)}, bf16[32,2560]{1,0:T(8,128)(2,1)S(1)}, u32[]{:S(2)}, u32[]{:S(2)}) %collective-permute-start.2) | collective-permute-done | bytes 163872 | tf_op jit(solution)/shard_map/ppermute | solution.py:616
  15.3 4.1 %attend.1 = (bf16[32,2176]{1,0:T(8,128)(2,1)S(1)}, bf16[2048,2048]{1,0:T(8,128)(2,1)S(1)}) custom-call(s32[20]{0:T(128)S(1)} %concatenate.10.refs_2_.refs_0_, f32[32,128]{1,0:T(8,128)S(1)} %get-tuple-element.66.refs_3_.refs_1_, f32[32,128]{1,0:T(8,128)S(1)} %get-tuple-element.67.refs_4_.refs_2_, bf16[2,8,512,256]{3,2,1,0:T(8,128)(2,1)S(1)} %bitcast.8, ...), custom_call_target="tpu_custom_call" | custom-call | flops 134217728 | bytes 4194304 | tf_op jit(solution)/shard_map/attend/pallas_call | solution.py:320
  19.4 1.0 %collective-permute-start.3 = (bf16[32,2176]{1,0:T(8,128)(2,1)S(1)}, bf16[32,2176]{1,0:T(8,128)(2,1)S(1)}, u32[]{:S(2)}, u32[]{:S(2)}) collective-permute-start(bf16[32,2176]{1,0:T(8,128)(2,1)S(1)} %get-tuple-element.39.refs_1_), channel_id=1, source_target_pairs={{0,8},{4,12},{8,0},{12,4},{1,9},{5,13},{9,1},{13,5},{2,10},{6,14},... | collective-permute-start | bytes 417800 | tf_op jit(solution)/shard_map/ppermute | solution.py:616
  20.4 0.0 collective-permute-start.4
  20.4 4.8 %fetch.5 = (bf16[1024,3584]{1,0:T(8,128)(2,1)S(1)}, bf16[512,3584]{1,0:T(8,128)(2,1)S(1)}, f32[8,128]{1,0:T(8,128)S(1)}) custom-call(s32[4]{0:T(128)S(1)} %pad_add_fusion.refs_0_.at, bf16[32,2176]{1,0:T(8,128)(2,1)S(1)} %get-tuple-element.39.refs_1_, bf16[2048,3584]{1,0:T(8,128)(2,1)} %refs_5_.3, bf16[2048,3584]{1,0:T(8,128)(2,1)} %refs_2_.4), custom_call_target="tpu_custom_call" | custom-call | bytes 22020096 | tf_op jit(solution)/shard_map/fetch/pallas_call | solution.py:118
  25.2 0.0 collective-permute-done.3.__0_
  25.3 0.6 collective-permute-start.5
  25.8 0.0 collective-permute-done.4.refs_3_
  25.8 1.0 %collective-permute-done.5.refs_4_ = bf16[32,2176]{1,0:T(8,128)(2,1)S(1)} collective-permute-done((bf16[32,2176]{1,0:T(8,128)(2,1)S(1)}, bf16[32,2176]{1,0:T(8,128)(2,1)S(1)}, u32[]{:S(2)}, u32[]{:S(2)}) %collective-permute-start.5) | collective-permute-done | bytes 139296 | tf_op jit(solution)/shard_map/ppermute | solution.py:616
  26.8 1.0 %output_first.1 = (bf16[32,1024]{1,0:T(8,128)(2,1)S(1)}, bf16[32,2048]{1,0:T(8,128)(2,1)S(1)}) custom-call(bf16[2048,2048]{1,0:T(8,128)(2,1)S(1)} %get-tuple-element.41.refs_0_.w, bf16[32,2176]{1,0:T(8,128)(2,1)S(1)} %get-tuple-element.39.refs_1_, bf16[32,2176]{1,0:T(8,128)(2,1)S(1)} %hold.3.refs_2_, bf16[32,2176]{1,0:T(8,128)(2,1)S(1)} %collective-permute-done.4.refs_3_, ...), custom_call_target="tpu_custom_call" | custom-call | flops 268435456 | bytes 8388608 | tf_op jit(solution)/shard_map/output_first/pallas_call | solution.py:363
  27.9 1.6 %collective-permute-start.6 = (bf16[32,1024]{1,0:T(8,128)(2,1)S(1)}, bf16[32,1024]{1,0:T(8,128)(2,1)S(1)}, u32[]{:S(2)}, u32[]{:S(2)}) collective-permute-start(bf16[32,1024]{1,0:T(8,128)(2,1)S(1)} %get-tuple-element.43.one), channel_id=1, source_target_pairs={{0,1},{1,0},{2,3},{3,2},{4,5},{5,4},{6,7},{7,6},{8,9},{9,8},{10,11... | collective-permute-start | bytes 196616 | tf_op jit(solution)/shard_map/ppermute | solution.py:616
  29.5 0.8 %output_second.1.one = bf16[32,1024]{1,0:T(8,128)(2,1)S(1)} custom-call(bf16[32,2048]{1,0:T(8,128)(2,1)S(1)} %get-tuple-element.49.x, bf16[2048,2048]{1,0:T(8,128)(2,1)S(1)} %get-tuple-element.41.refs_0_.w), custom_call_target="tpu_custom_call" | custom-call | flops 268435456 | bytes 8388608 | tf_op jit(solution)/shard_map/output_second/pallas_call | solution.py:379
  30.3 2.6 %collective-permute-start.8 = (bf16[32,1024]{1,0:T(8,128)(2,1)S(1)}, bf16[32,1024]{1,0:T(8,128)(2,1)S(1)}, u32[]{:S(2)}, u32[]{:S(2)}) collective-permute-start(bf16[32,1024]{1,0:T(8,128)(2,1)S(1)} %output_second.1.one), channel_id=1, source_target_pairs={{0,2},{1,3},{2,0},{3,1},{4,6},{5,7},{6,4},{7,5},{8,10},{9,11},{10,... | collective-permute-start | bytes 196616 | tf_op jit(solution)/shard_map/ppermute | solution.py:616
  32.9 0.0 collective-permute-done.6.two
  32.9 0.0 copy-start
  32.9 2.5 %collective-permute-start.7 = (bf16[32,1024]{1,0:T(8,128)(2,1)S(1)}, bf16[32,1024]{1,0:T(8,128)(2,1)S(1)}, u32[]{:S(2)}, u32[]{:S(2)}) collective-permute-start(bf16[32,1024]{1,0:T(8,128)(2,1)S(1)} %add.41.refs_6_.refs_1_), channel_id=1, source_target_pairs={{0,2},{1,3},{2,0},{3,1},{4,6},{5,7},{6,4},{7,5},{8,10},{9,11},{10,... | collective-permute-start | bytes 196616 | tf_op jit(solution)/shard_map/ppermute | solution.py:616
  35.4 2.6 %fetch.6 = (bf16[512,3584]{1,0:T(8,128)(2,1)S(1)}, f32[8,128]{1,0:T(8,128)S(1)}) custom-call(s32[4]{0:T(128)S(1)} %pad_add_fusion.refs_0_.at, bf16[32,1024]{1,0:T(8,128)(2,1)S(1)} %add.41.refs_6_.refs_1_, bf16[2048,3584]{1,0:T(8,128)(2,1)} %refs_2_.4), custom_call_target="tpu_custom_call" | custom-call | bytes 7340032 | tf_op jit(solution)/shard_map/fetch/pallas_call | solution.py:118
  38.1 0.0 collective-permute-done.8.two
  38.1 1.1 %collective-permute-start.9 = (bf16[32,1024]{1,0:T(8,128)(2,1)S(1)}, bf16[32,1024]{1,0:T(8,128)(2,1)S(1)}, u32[]{:S(2)}, u32[]{:S(2)}) collective-permute-start(bf16[32,1024]{1,0:T(8,128)(2,1)S(1)} %add.42.refs_8_), channel_id=1, source_target_pairs={{0,1},{1,0},{2,3},{3,2},{4,5},{5,4},{6,7},{7,6},{8,9},{9,8},{10,11... | collective-permute-start | bytes 196616 | tf_op jit(solution)/shard_map/ppermute | solution.py:616
  39.2 0.2 collective-permute-done.7.refs_7_
  39.4 0.0 copy-done
  39.4 3.8 %expand_first.1 = (f32[32,3584]{1,0:T(8,128)S(1)}, f32[32,3584]{1,0:T(8,128)S(1)}, f32[32,1024]{1,0:T(8,128)S(1)}, f32[32,128]{1,0:T(8,128)S(1)}, bf16[1024,3584]{1,0:T(8,128)(2,1)S(1)}) custom-call(s32[4]{0:T(128)S(1)} %pad_add_fusion.refs_0_.at, bf16[32,2048]{1,0:T(8,128)(2,1)S(1)} %get-tuple-element.34.refs_1_, bf16[16,128]{1,0:T(8,128)(2,1)S(1)} %bitcast.9, ...), custom_call_target="tpu_custom_call" | custom-call | flops 469762048 | bytes 14680064 | tf_op jit(solution)/shard_map/expand_first/pallas_call | solution.py:433
  43.2 0.0 collective-permute-done.9.refs_9_
  43.2 1.9 %expand_send.1 = (bf16[32,3712]{1,0:T(8,128)(2,1)S(1)}, f32[32,1024]{1,0:T(8,128)S(1)}, bf16[32,1024]{1,0:T(8,128)(2,1)S(1)}) custom-call(s32[4]{0:T(128)S(1)} %pad_add_fusion.refs_0_.at, bf16[32,2048]{1,0:T(8,128)(2,1)S(1)} %get-tuple-element.34.refs_1_, bf16[16,128]{1,0:T(8,128)(2,1)S(1)} %bitcast.10, f32[32,3584]{1,0:T(8,128)S(1)} %get-tuple-element.44.refs_3_, ...), custom_call_target="tpu_custom_call" | custom-call | flops 234881024 | bytes 7340032 | tf_op jit(solution)/shard_map/expand_send/pallas_call | solution.py:466
  45.1 0.1 collective-permute-start.10
  45.2 1.9 %expand_keep.1.keep = bf16[32,3584]{1,0:T(8,128)(2,1)S(1)} custom-call(s32[4]{0:T(128)S(1)} %pad_add_fusion.refs_0_.at, bf16[32,1024]{1,0:T(8,128)(2,1)S(1)} %get-tuple-element.51.x, f32[32,3584]{1,0:T(8,128)S(1)} %get-tuple-element.52.before, bf16[512,3584]{1,0:T(8,128)(2,1)S(1)} %get-tuple-element.46.refs_5_.refs_0_, ...), custom_call_target="tpu_custom_call" | custom-call | flops 234881024 | bytes 7340032 | tf_op jit(solution)/shard_map/expand_keep/pallas_call | solution.py:484
  47.1 0.0 collective-permute-done.10.received
  47.1 0.2 pair.1.refs_1_.refs_0_
  47.3 1.1 %collective-permute-start.11 = (bf16[32,3712]{1,0:T(8,128)(2,1)S(1)}, bf16[32,3712]{1,0:T(8,128)(2,1)S(1)}, u32[]{:S(2)}, u32[]{:S(2)}) collective-permute-start(bf16[32,3712]{1,0:T(8,128)(2,1)S(1)} %pair.1.refs_1_.refs_0_), channel_id=1, source_target_pairs={{0,8},{4,12},{8,0},{12,4},{1,9},{5,13},{9,1},{13,5},{2,10},{6,14},... | collective-permute-start | bytes 712712 | tf_op jit(solution)/shard_map/ppermute | solution.py:616
  48.4 5.9 %fetch.7 = (bf16[1792,2048]{1,0:T(8,128)(2,1)S(1)}, bf16[1792,2048]{1,0:T(8,128)(2,1)S(1)}, f32[8,128]{1,0:T(8,128)S(1)}) custom-call(s32[4]{0:T(128)S(1)} %pad_add_fusion.refs_0_.at, bf16[32,3712]{1,0:T(8,128)(2,1)S(1)} %pair.1.refs_1_.refs_0_, bf16[3584,2048]{1,0:T(8,128)(2,1)} %refs_3_.5, bf16[3584,2048]{1,0:T(8,128)(2,1)} %refs_3_.5), custom_call_target="tpu_custom_call" | custom-call | bytes 29360128 | tf_op jit(solution)/shard_map/fetch/pallas_call | solution.py:118
  54.3 1.1 %collective-permute-done.11.refs_1_ = bf16[32,3712]{1,0:T(8,128)(2,1)S(1)} collective-permute-done((bf16[32,3712]{1,0:T(8,128)(2,1)S(1)}, bf16[32,3712]{1,0:T(8,128)(2,1)S(1)}, u32[]{:S(2)}, u32[]{:S(2)}) %collective-permute-start.11) | collective-permute-done | bytes 237600 | tf_op jit(solution)/shard_map/ppermute | solution.py:616
  55.5 0.2 gated.1.hidden
  55.7 0.1 collective-permute-start.12
  55.8 1.4 %contract.1.refs_3_ = f32[32,2048]{1,0:T(8,128)S(1)} custom-call(bf16[32,1792]{1,0:T(8,128)(2,1)S(1)} %gated.1.hidden, bf16[1792,2048]{1,0:T(8,128)(2,1)S(1)} %get-tuple-element.56.w), custom_call_target="tpu_custom_call" | custom-call | flops 234881024 | bytes 7340032 | tf_op jit(solution)/shard_map/contract/pallas_call | solution.py:546
  57.2 0.0 collective-permute-done.12.refs_1_
  57.2 1.9 %contract_last.1 = (f32[8,2048]{1,0:T(8,128)S(1)}, bf16[8,2048]{1,0:T(8,128)(2,1)S(1)}, bf16[8,2048]{1,0:T(8,128)(2,1)S(1)}, bf16[8,2048]{1,0:T(8,128)(2,1)S(1)}) custom-call(s32[4]{0:T(128)S(1)} %pad_add_fusion.refs_0_.at, bf16[32,1792]{1,0:T(8,128)(2,1)S(1)} %collective-permute-done.12.refs_1_, bf16[1792,2048]{1,0:T(8,128)(2,1)S(1)} %get-tuple-element.55.refs_2_, ...), custom_call_target="tpu_custom_call" | custom-call | flops 234881024 | bytes 7340032 | tf_op jit(solution)/shard_map/contract_last/pallas_call | solution.py:583
  59.1 2.8 %collective-permute-start.13 = (bf16[8,2048]{1,0:T(8,128)(2,1)S(1)}, bf16[8,2048]{1,0:T(8,128)(2,1)S(1)}, u32[]{:S(2)}, u32[]{:S(2)}) collective-permute-start(bf16[8,2048]{1,0:T(8,128)(2,1)S(1)} %get-tuple-element.60), channel_id=1, source_target_pairs={{0,3},{1,2},{2,1},{3,0},{4,7},{5,6},{6,5},{7,4},{8,11},{9,10},{10,... | collective-permute-start | bytes 98312 | tf_op jit(solution)/shard_map/ppermute | solution.py:616
  61.9 0.0 collective-permute-start.14
  61.9 1.6 %collective-permute-start.15 = (bf16[8,2048]{1,0:T(8,128)(2,1)S(1)}, bf16[8,2048]{1,0:T(8,128)(2,1)S(1)}, u32[]{:S(2)}, u32[]{:S(2)}) collective-permute-start(bf16[8,2048]{1,0:T(8,128)(2,1)S(1)} %get-tuple-element.62), channel_id=1, source_target_pairs={{0,1},{1,0},{2,3},{3,2},{4,5},{5,4},{6,7},{7,6},{8,9},{9,8},{10,11... | collective-permute-start | bytes 98312 | tf_op jit(solution)/shard_map/ppermute | solution.py:616
  63.6 1.7 %collective-permute-done.13 = bf16[8,2048]{1,0:T(8,128)(2,1)S(1)} collective-permute-done((bf16[8,2048]{1,0:T(8,128)(2,1)S(1)}, bf16[8,2048]{1,0:T(8,128)(2,1)S(1)}, u32[]{:S(2)}, u32[]{:S(2)}) %collective-permute-start.13) | collective-permute-done | bytes 32800 | tf_op jit(solution)/shard_map/ppermute | solution.py:616
  65.2 1.5 %collective-permute-done.14 = bf16[8,2048]{1,0:T(8,128)(2,1)S(1)} collective-permute-done((bf16[8,2048]{1,0:T(8,128)(2,1)S(1)}, bf16[8,2048]{1,0:T(8,128)(2,1)S(1)}, u32[]{:S(2)}, u32[]{:S(2)}) %collective-permute-start.14) | collective-permute-done | bytes 32800 | tf_op jit(solution)/shard_map/ppermute | solution.py:616
  66.7 0.0 collective-permute-done.15
  66.7 0.6 add_convert_fusion
  (5 shorter events, 0.1 us)
Async XLA Ops:
  0.0 8.3 %copy-start.1 = (s32[8]{0:T(128)S(1)}, s32[8]{0:T(128)}, u32[]{:S(2)}) copy-start(s32[8]{0:T(128)} %param.24) | copy-start | bytes 100
  0.0 8.6 %copy-start.2 = (s32[8]{0:T(128)S(1)}, s32[8]{0:T(128)}, u32[]{:S(2)}) copy-start(s32[8]{0:T(128)} %param.25) | copy-start | bytes 100
  5.2 8.9 %collective-permute-start.1 = (bf16[32,2560]{1,0:T(8,128)(2,1)S(1)}, bf16[32,2560]{1,0:T(8,128)(2,1)S(1)}, u32[]{:S(2)}, u32[]{:S(2)}) collective-permute-start(bf16[32,2560]{1,0:T(8,128)(2,1)S(1)} %get-tuple-element.35.refs_1_.refs_5_), channel_id=1, source_target_pairs={{0,4},{4,0},{8,12},{12,8},{1,5},{5,1},{9,13},{13,9},{2,6},{6,2},{1... | collective-permute-start | bytes 491528 | tf_op jit(solution)/shard_map/ppermute | solution.py:616
  5.7 8.1 %collective-permute-start = (bf16[32,2560]{1,0:T(8,128)(2,1)S(1)}, bf16[32,2560]{1,0:T(8,128)(2,1)S(1)}, u32[]{:S(2)}, u32[]{:S(2)}) collective-permute-start(bf16[32,2560]{1,0:T(8,128)(2,1)S(1)} %get-tuple-element.35.refs_1_.refs_5_), channel_id=1, source_target_pairs={{0,8},{4,12},{8,0},{12,4},{1,9},{5,13},{9,1},{13,5},{2,10},{6,14},... | collective-permute-start | bytes 491528 | tf_op jit(solution)/shard_map/ppermute | solution.py:616
  13.9 1.5 %collective-permute-start.2 = (bf16[32,2560]{1,0:T(8,128)(2,1)S(1)}, bf16[32,2560]{1,0:T(8,128)(2,1)S(1)}, u32[]{:S(2)}, u32[]{:S(2)}) collective-permute-start(bf16[32,2560]{1,0:T(8,128)(2,1)S(1)} %hold.2.refs_6_), channel_id=1, source_target_pairs={{0,4},{4,0},{8,12},{12,8},{1,5},{5,1},{9,13},{13,9},{2,6},{6,2},{1... | collective-permute-start | bytes 491528 | tf_op jit(solution)/shard_map/ppermute | solution.py:616
  19.4 5.8 %collective-permute-start.3 = (bf16[32,2176]{1,0:T(8,128)(2,1)S(1)}, bf16[32,2176]{1,0:T(8,128)(2,1)S(1)}, u32[]{:S(2)}, u32[]{:S(2)}) collective-permute-start(bf16[32,2176]{1,0:T(8,128)(2,1)S(1)} %get-tuple-element.39.refs_1_), channel_id=1, source_target_pairs={{0,8},{4,12},{8,0},{12,4},{1,9},{5,13},{9,1},{13,5},{2,10},{6,14},... | collective-permute-start | bytes 417800 | tf_op jit(solution)/shard_map/ppermute | solution.py:616
  20.4 5.4 %collective-permute-start.4 = (bf16[32,2176]{1,0:T(8,128)(2,1)S(1)}, bf16[32,2176]{1,0:T(8,128)(2,1)S(1)}, u32[]{:S(2)}, u32[]{:S(2)}) collective-permute-start(bf16[32,2176]{1,0:T(8,128)(2,1)S(1)} %get-tuple-element.39.refs_1_), channel_id=1, source_target_pairs={{0,4},{4,0},{8,12},{12,8},{1,5},{5,1},{9,13},{13,9},{2,6},{6,2},{1... | collective-permute-start | bytes 417800 | tf_op jit(solution)/shard_map/ppermute | solution.py:616
  25.3 1.6 %collective-permute-start.5 = (bf16[32,2176]{1,0:T(8,128)(2,1)S(1)}, bf16[32,2176]{1,0:T(8,128)(2,1)S(1)}, u32[]{:S(2)}, u32[]{:S(2)}) collective-permute-start(bf16[32,2176]{1,0:T(8,128)(2,1)S(1)} %hold.3.refs_2_), channel_id=1, source_target_pairs={{0,4},{4,0},{8,12},{12,8},{1,5},{5,1},{9,13},{13,9},{2,6},{6,2},{1... | collective-permute-start | bytes 417800 | tf_op jit(solution)/shard_map/ppermute | solution.py:616
  27.9 5.0 %collective-permute-start.6 = (bf16[32,1024]{1,0:T(8,128)(2,1)S(1)}, bf16[32,1024]{1,0:T(8,128)(2,1)S(1)}, u32[]{:S(2)}, u32[]{:S(2)}) collective-permute-start(bf16[32,1024]{1,0:T(8,128)(2,1)S(1)} %get-tuple-element.43.one), channel_id=1, source_target_pairs={{0,1},{1,0},{2,3},{3,2},{4,5},{5,4},{6,7},{7,6},{8,9},{9,8},{10,11... | collective-permute-start | bytes 196616 | tf_op jit(solution)/shard_map/ppermute | solution.py:616
  30.3 7.8 %collective-permute-start.8 = (bf16[32,1024]{1,0:T(8,128)(2,1)S(1)}, bf16[32,1024]{1,0:T(8,128)(2,1)S(1)}, u32[]{:S(2)}, u32[]{:S(2)}) collective-permute-start(bf16[32,1024]{1,0:T(8,128)(2,1)S(1)} %output_second.1.one), channel_id=1, source_target_pairs={{0,2},{1,3},{2,0},{3,1},{4,6},{5,7},{6,4},{7,5},{8,10},{9,11},{10,... | collective-permute-start | bytes 196616 | tf_op jit(solution)/shard_map/ppermute | solution.py:616
  32.9 6.5 %copy-start = (bf16[2048]{0:T(1024)(128)(2,1)S(1)}, bf16[2048]{0:T(1024)(128)(2,1)}, u32[]{:S(2)}) copy-start(bf16[2048]{0:T(1024)(128)(2,1)} %param.15) | copy-start | bytes 12292
  32.9 6.5 %collective-permute-start.7 = (bf16[32,1024]{1,0:T(8,128)(2,1)S(1)}, bf16[32,1024]{1,0:T(8,128)(2,1)S(1)}, u32[]{:S(2)}, u32[]{:S(2)}) collective-permute-start(bf16[32,1024]{1,0:T(8,128)(2,1)S(1)} %add.41.refs_6_.refs_1_), channel_id=1, source_target_pairs={{0,2},{1,3},{2,0},{3,1},{4,6},{5,7},{6,4},{7,5},{8,10},{9,11},{10,... | collective-permute-start | bytes 196616 | tf_op jit(solution)/shard_map/ppermute | solution.py:616
  38.1 5.1 %collective-permute-start.9 = (bf16[32,1024]{1,0:T(8,128)(2,1)S(1)}, bf16[32,1024]{1,0:T(8,128)(2,1)S(1)}, u32[]{:S(2)}, u32[]{:S(2)}) collective-permute-start(bf16[32,1024]{1,0:T(8,128)(2,1)S(1)} %add.42.refs_8_), channel_id=1, source_target_pairs={{0,1},{1,0},{2,3},{3,2},{4,5},{5,4},{6,7},{7,6},{8,9},{9,8},{10,11... | collective-permute-start | bytes 196616 | tf_op jit(solution)/shard_map/ppermute | solution.py:616
  45.1 2.0 %collective-permute-start.10 = (bf16[32,3712]{1,0:T(8,128)(2,1)S(1)}, bf16[32,3712]{1,0:T(8,128)(2,1)S(1)}, u32[]{:S(2)}, u32[]{:S(2)}) collective-permute-start(bf16[32,3712]{1,0:T(8,128)(2,1)S(1)} %get-tuple-element.53.stats), channel_id=1, source_target_pairs={{0,4},{4,0},{8,12},{12,8},{1,5},{5,1},{9,13},{13,9},{2,6},{6,2},{1... | collective-permute-start | bytes 712712 | tf_op jit(solution)/shard_map/ppermute | solution.py:616
  47.3 8.2 %collective-permute-start.11 = (bf16[32,3712]{1,0:T(8,128)(2,1)S(1)}, bf16[32,3712]{1,0:T(8,128)(2,1)S(1)}, u32[]{:S(2)}, u32[]{:S(2)}) collective-permute-start(bf16[32,3712]{1,0:T(8,128)(2,1)S(1)} %pair.1.refs_1_.refs_0_), channel_id=1, source_target_pairs={{0,8},{4,12},{8,0},{12,4},{1,9},{5,13},{9,1},{13,5},{2,10},{6,14},... | collective-permute-start | bytes 712712 | tf_op jit(solution)/shard_map/ppermute | solution.py:616
  55.7 1.4 %collective-permute-start.12 = (bf16[32,1792]{1,0:T(8,128)(2,1)S(1)}, bf16[32,1792]{1,0:T(8,128)(2,1)S(1)}, u32[]{:S(2)}, u32[]{:S(2)}) collective-permute-start(bf16[32,1792]{1,0:T(8,128)(2,1)S(1)} %gated.1.hidden), channel_id=1, source_target_pairs={{0,4},{4,0},{8,12},{12,8},{1,5},{5,1},{9,13},{13,9},{2,6},{6,2},{1... | collective-permute-start | bytes 344072 | tf_op jit(solution)/shard_map/ppermute | solution.py:616
  59.1 6.1 %collective-permute-start.13 = (bf16[8,2048]{1,0:T(8,128)(2,1)S(1)}, bf16[8,2048]{1,0:T(8,128)(2,1)S(1)}, u32[]{:S(2)}, u32[]{:S(2)}) collective-permute-start(bf16[8,2048]{1,0:T(8,128)(2,1)S(1)} %get-tuple-element.60), channel_id=1, source_target_pairs={{0,3},{1,2},{2,1},{3,0},{4,7},{5,6},{6,5},{7,4},{8,11},{9,10},{10,... | collective-permute-start | bytes 98312 | tf_op jit(solution)/shard_map/ppermute | solution.py:616
  61.9 4.8 %collective-permute-start.14 = (bf16[8,2048]{1,0:T(8,128)(2,1)S(1)}, bf16[8,2048]{1,0:T(8,128)(2,1)S(1)}, u32[]{:S(2)}, u32[]{:S(2)}) collective-permute-start(bf16[8,2048]{1,0:T(8,128)(2,1)S(1)} %get-tuple-element.61), channel_id=1, source_target_pairs={{0,2},{1,3},{2,0},{3,1},{4,6},{5,7},{6,4},{7,5},{8,10},{9,11},{10,... | collective-permute-start | bytes 98312 | tf_op jit(solution)/shard_map/ppermute | solution.py:616
  61.9 4.8 %collective-permute-start.15 = (bf16[8,2048]{1,0:T(8,128)(2,1)S(1)}, bf16[8,2048]{1,0:T(8,128)(2,1)S(1)}, u32[]{:S(2)}, u32[]{:S(2)}) collective-permute-start(bf16[8,2048]{1,0:T(8,128)(2,1)S(1)} %get-tuple-element.62), channel_id=1, source_target_pairs={{0,1},{1,0},{2,3},{3,2},{4,5},{5,4},{6,7},{7,6},{8,9},{9,8},{10,11... | collective-permute-start | bytes 98312 | tf_op jit(solution)/shard_map/ppermute | solution.py:616
